TPU v7x, 32 devices: a whole 2x2x4 slice. The times are simulated.
32 devices in a mesh: tok: 8 (over z, x), hd: 4 (over y, core).
Axes of the slice: x: 2, y: 2, z: 4, core: 2. Of those that a mesh axis runs over, the one named last changes fastest.
Arguments:
- hidden: bfloat16 [8192, 1024], P(('tok', 'hd')), may hold values from -6 to 6
- encoder: bfloat16 [1, 256, 1024], P(None, 'hd'), may hold values from -6 to 6
- cotangent: bfloat16 [8192, 1024], P(('tok', 'hd')), may hold values from -6 to 6
- block_ids: int32 [8192], P('tok'), may hold values from 0 to 63, as said below
- self_qkv: bfloat16 [1024, 3, 1024], P('tok', None, 'hd'), may hold values from -0.1875 to 0.1875
- self_out: bfloat16 [1024, 1024], P('hd', 'tok'), may hold values from -3 to 3
- cross_qkv: bfloat16 [1024, 3, 1024], P('tok', None, 'hd'), may hold values from -0.1875 to 0.1875
- cross_out: bfloat16 [1024, 1024], P('hd', 'tok'), may hold values from -3 to 3
- up_weight: bfloat16 [1024, 8192], P('tok', 'hd'), may hold values from -0.1875 to 0.1875
- down_weight: bfloat16 [8192, 1024], P('hd', 'tok'), may hold values from -0.0625 to 0.0625
- proj_bias: bfloat16 [1024, 7], P(('tok', 'hd')), may hold values from -1.796875 to 1.796875
- up_bias: bfloat16 [8192], P(('tok', 'hd')), may hold values from -1.796875 to 1.796875
- norm_gain: bfloat16 [1024, 3], P(('tok', 'hd')), may hold values from 0.5 to 1.5
- norm_shift: bfloat16 [1024, 3], P(('tok', 'hd')), may hold values from -1.796875 to 1.796875
Outputs:
- output: bfloat16 [8192, 1024], P(('tok', 'hd'))
- grad_hidden: float32 [8192, 1024], P(('tok', 'hd'))
- grad_encoder: float32 [1, 256, 1024], P(None, 'hd')
- grad_self_qkv: float32 [1024, 3, 1024], P('tok', None, 'hd')
- grad_self_out: float32 [1024, 1024], P('hd', 'tok')
- grad_cross_qkv: float32 [1024, 3, 1024], P('tok', None, 'hd')
- grad_cross_out: float32 [1024, 1024], P('hd', 'tok')
- grad_up_weight: float32 [1024, 8192], P('tok', 'hd')
- grad_down_weight: float32 [8192, 1024], P('hd', 'tok')
- grad_proj_bias: float32 [1024, 7], P(('tok', 'hd'))
- grad_up_bias: float32 [8192], P(('tok', 'hd'))
- grad_norm_gain: float32 [1024, 3], P(('tok', 'hd'))
- grad_norm_shift: float32 [1024, 3], P(('tok', 'hd'))
Inputs may be any that keep to these rules, and one draw needn't show every extreme that they name: block_ids never fall along the stream; each block has 1 to 256 tokens and lies within one aligned window of 256 tokens; one block has exactly 256.
All inputs are finite; a program needn't handle non-finite values.
Results may differ from a plain program's by a relative error of at most 0.03.
Values may be sent and summed in bfloat16 or wider, within the bound.
No kernel may reach another device: no remote copies, remote signals or barrier semaphores. Data moves between devices by JAX's collectives and lax.ppermute only.
A program may use at most 576 MiB of HBM per device.

v0:
```python
import jax
import jax.numpy as jnp
from jax import lax
from jax.sharding import PartitionSpec as P

HDIM = 64
SEQ = 8192
BLOCK = 256


norm_eps = 1e-05
neg_large = -1e30


def from_behind(shard, axis, by):
    length = lax.axis_size(axis)
    pairs = [(i, i + by) for i in range(length) if 0 <= i + by < length]
    return lax.ppermute(shard, axis, pairs)


def layer_norm(value, gain_vec, shift_vec):
    center = value - jnp.mean(value, axis=-1, keepdims=True)
    variance = jnp.mean(center * center, axis=-1, keepdims=True)
    return center * lax.rsqrt(variance + norm_eps) * gain_vec + shift_vec


def gelu_exact(value):
    return jax.nn.gelu(value, approximate=False)


def linear(left, right):
    return jnp.dot(left, right, preferred_element_type=jnp.float32)


def lead_product(left, right):
    return lax.dot_general(
        left, right, (((0,), (0,)), ((), ())), preferred_element_type=jnp.float32
    )


def trail_product(left, right):
    return lax.dot_general(
        left, right, (((1,), (1,)), ((), ())), preferred_element_type=jnp.float32
    )


def masked_scores(queries, key_rows, allowed):
    scores = jnp.einsum("qhd,khd->hqk", queries, key_rows, preferred_element_type=jnp.float32)
    return jnp.where(allowed[None], scores, neg_large)


def attend_forward(queries, key_rows, value_rows, allowed):
    scores = masked_scores(queries, key_rows, allowed)
    row_max = jnp.max(scores, axis=-1, keepdims=True)
    expo_val = jnp.exp(scores - row_max)
    row_total = jnp.sum(expo_val, axis=-1, keepdims=True)
    soft_probs = (expo_val / row_total).astype(jnp.bfloat16)
    context = jnp.einsum("hqk,khd->qhd", soft_probs, value_rows, preferred_element_type=jnp.float32)
    return (context, row_max + jnp.log(row_total))


def attend_backward(queries, key_rows, value_rows, allowed, log_total, grad_context):
    scores = masked_scores(queries, key_rows, allowed)
    soft_probs = jnp.exp(scores - log_total)
    grad_probs = jnp.einsum(
        "qhd,khd->hqk", grad_context, value_rows, preferred_element_type=jnp.float32
    )
    row_inner = jnp.sum(soft_probs * grad_probs, axis=-1, keepdims=True)
    grad_scores = (soft_probs * (grad_probs - row_inner)).astype(jnp.bfloat16)
    query_grad = jnp.einsum(
        "hqk,khd->qhd", grad_scores, key_rows, preferred_element_type=jnp.float32
    )
    key_grad = jnp.einsum("hqk,qhd->khd", grad_scores, queries, preferred_element_type=jnp.float32)
    value_grad = jnp.einsum(
        "hqk,qhd->khd",
        soft_probs.astype(jnp.bfloat16),
        grad_context,
        preferred_element_type=jnp.float32,
    )
    return (query_grad, key_grad, value_grad)


def local(
    hidden,
    encoder,
    cotangent,
    block_ids,
    self_qkv,
    self_out,
    cross_qkv,
    cross_out,
    up_weight,
    down_weight,
    proj_bias,
    up_bias,
    norm_gain,
    norm_shift,
):
    w_self, w_cross, w_up, w_self_out, w_cross_out, w_down = (
        lax.all_gather(self_qkv, "tok", axis=0, tiled=True),
        lax.all_gather(cross_qkv, "tok", axis=0, tiled=True),
        lax.all_gather(up_weight, "tok", axis=0, tiled=True),
        lax.all_gather(self_out, "tok", axis=1, tiled=True),
        lax.all_gather(cross_out, "tok", axis=1, tiled=True),
        lax.all_gather(down_weight, "tok", axis=1, tiled=True),
    )
    bias_all, bias_up, gain_all, shift_all = (
        lax.all_gather(proj_bias, ("tok", "hd"), axis=0, tiled=True),
        lax.all_gather(up_bias, ("tok", "hd"), axis=0, tiled=True),
        lax.all_gather(norm_gain, ("tok", "hd"), axis=0, tiled=True),
        lax.all_gather(norm_shift, ("tok", "hd"), axis=0, tiled=True),
    )
    bias_all = bias_all.astype(jnp.float32)
    bias_up = bias_up.astype(jnp.float32)
    gain_all = gain_all.astype(jnp.float32)
    shift_all = shift_all.astype(jnp.float32)
    tok_rows, model_width = hidden.shape
    group_size = lax.axis_size("hd")
    hd_index = lax.axis_index("hd")
    stretch_rows = tok_rows * group_size
    local_width = w_self.shape[2]
    ff_local = w_up.shape[1]
    ff_total = bias_up.shape[0]
    heads_local = local_width // HDIM
    col_start = hd_index * local_width
    ff_start = hd_index * ff_local
    back_count = SEQ // stretch_rows - 1
    seq_count = encoder.shape[0]
    stretch_start = lax.axis_index("tok") * stretch_rows
    own_seq = stretch_start // SEQ
    zeros_local = jnp.zeros((local_width,), jnp.float32)
    qkv_scale = jnp.array([0.125, 1.0, 1.0], jnp.float32)[:, None]
    w_self_flat = w_self.reshape(model_width, 3 * local_width)
    w_cross_query = w_cross[:, 0]
    w_cross_kv = w_cross[:, 1:].reshape(model_width, 2 * local_width)

    def local_cols(vector):
        return lax.dynamic_slice_in_dim(vector, col_start, local_width, 0)

    def place_cols(vector):
        return lax.dynamic_update_slice_in_dim(
            jnp.zeros((model_width,), jnp.float32), vector, col_start, 0
        )

    def split_heads(block_rows):
        return block_rows.reshape(block_rows.shape[0], heads_local, HDIM)

    def group_rows(block_rows):
        return lax.all_gather(block_rows, "hd", axis=0, tiled=True)

    def group_sums(left, right, product):
        return lax.psum_scatter(
            product(left, right).astype(jnp.bfloat16), "hd", scatter_dimension=0, tiled=True
        ).astype(jnp.float32)

    resid_zero = hidden.astype(jnp.float32)
    norm_one, norm_pull_one = jax.vjp(layer_norm, resid_zero, gain_all[:, 0], shift_all[:, 0])
    h_one_all = group_rows(norm_one.astype(jnp.bfloat16))
    self_bias = jnp.stack([local_cols(bias_all[:, 0]), zeros_local, local_cols(bias_all[:, 1])])
    qkv_heads = (
        (linear(h_one_all, w_self_flat).reshape(stretch_rows, 3, local_width) + self_bias)
        * qkv_scale
    ).astype(jnp.bfloat16)
    queries = split_heads(qkv_heads[:, 0])
    own_keys = qkv_heads[:, 1]
    own_values = qkv_heads[:, 2]
    own_kv = qkv_heads[:, 1:]
    prior_keys = []
    prior_values = []
    prior_allowed = []
    for back_step in range(back_count, 0, -1):
        received = from_behind(own_kv, "tok", back_step)
        prior_keys.append(received[:, 0])
        prior_values.append(received[:, 1])
        same_seq = (stretch_start - back_step * stretch_rows) // SEQ == own_seq
        prior_allowed.append(jnp.broadcast_to(same_seq, (stretch_rows,)))
    prior_key_rows = jnp.concatenate(prior_keys, 0)
    prior_value_rows = jnp.concatenate(prior_values, 0)
    prior_mask = jnp.concatenate(prior_allowed, 0)
    prior_span = back_count * stretch_rows
    tile_rows = min(512, stretch_rows)
    tile_total = stretch_rows // tile_rows

    def tile_inputs(tile_index):
        first_row = tile_index * tile_rows
        own_end = min(stretch_rows, first_row + tile_rows + BLOCK)
        key_rows = split_heads(jnp.concatenate([prior_key_rows, own_keys[:own_end]], 0))
        value_rows = split_heads(jnp.concatenate([prior_value_rows, own_values[:own_end]], 0))
        tile_ids = block_ids[first_row : first_row + tile_rows]
        own_mask = block_ids[None, :own_end] <= tile_ids[:, None]
        allowed = jnp.concatenate(
            [jnp.broadcast_to(prior_mask[None], (tile_rows, prior_span)), own_mask], 1
        )
        return (queries[first_row : first_row + tile_rows], key_rows, value_rows, allowed, own_end)

    context_tiles = []
    log_tiles = []
    for tile_index in range(tile_total):
        tile_query, key_rows, value_rows, allowed, own_end = tile_inputs(tile_index)
        context_tile, log_tile = attend_forward(tile_query, key_rows, value_rows, allowed)
        context_tiles.append(context_tile)
        log_tiles.append(log_tile)
    context_heads = (
        jnp.concatenate(context_tiles, 0).astype(jnp.bfloat16).reshape(stretch_rows, local_width)
    )
    resid_one = resid_zero + group_sums(context_heads, w_self_out, linear) + bias_all[:, 2]
    norm_two, norm_pull_two = jax.vjp(layer_norm, resid_one, gain_all[:, 1], shift_all[:, 1])
    h_two_all = group_rows(norm_two.astype(jnp.bfloat16))
    query_two = ((linear(h_two_all, w_cross_query) + local_cols(bias_all[:, 3])) * 0.125).astype(
        jnp.bfloat16
    )
    enc_rows = lax.all_gather(
        lax.dynamic_index_in_dim(encoder, own_seq, 0, keepdims=False), "hd", axis=0, tiled=True
    )
    cross_bias = jnp.concatenate([zeros_local, local_cols(bias_all[:, 4])])
    kv_two = (linear(enc_rows, w_cross_kv) + cross_bias).astype(jnp.bfloat16)
    enc_total = kv_two.shape[0]
    keys_two = split_heads(kv_two[:, :local_width])
    values_two = split_heads(kv_two[:, local_width:])
    queries_two = split_heads(query_two)
    cross_mask = jnp.ones((stretch_rows, enc_total), jnp.bool_)
    context_two, log_two = attend_forward(queries_two, keys_two, values_two, cross_mask)
    context_two = context_two.astype(jnp.bfloat16).reshape(stretch_rows, local_width)
    resid_two = resid_one + group_sums(context_two, w_cross_out, linear) + bias_all[:, 5]
    norm_three, norm_pull_three = jax.vjp(layer_norm, resid_two, gain_all[:, 2], shift_all[:, 2])
    h_three_all = group_rows(norm_three.astype(jnp.bfloat16))
    inner_pre = linear(h_three_all, w_up) + lax.dynamic_slice_in_dim(bias_up, ff_start, ff_local, 0)
    gelu_value, gelu_pull = jax.vjp(gelu_exact, inner_pre)
    act_low = gelu_value.astype(jnp.bfloat16)
    final_rows = resid_two + group_sums(act_low, w_down, linear) + bias_all[:, 6]
    output = final_rows.astype(jnp.bfloat16)
    cot_all = group_rows(cotangent)
    grad_down = lead_product(act_low, cot_all)
    bias_six = jnp.sum(cotangent.astype(jnp.float32), 0)
    grad_act = trail_product(cot_all, w_down)
    grad_inner = gelu_pull(grad_act)[0].astype(jnp.bfloat16)
    grad_up = lead_product(h_three_all, grad_inner)
    grad_bias_up = lax.dynamic_update_slice_in_dim(
        jnp.zeros((ff_total,), jnp.float32), jnp.sum(grad_inner.astype(jnp.float32), 0), ff_start, 0
    )
    grad_h_three = group_sums(grad_inner, w_up, trail_product)
    back_three, gain_three, shift_three = norm_pull_three(grad_h_three)
    grad_two = cotangent.astype(jnp.float32) + back_three
    grad_att_two = grad_two.astype(jnp.bfloat16)
    bias_five = jnp.sum(grad_att_two.astype(jnp.float32), 0)
    grad_two_all = group_rows(grad_att_two)
    grad_cross_out = lead_product(context_two, grad_two_all)
    grad_context_two = split_heads(trail_product(grad_two_all, w_cross_out).astype(jnp.bfloat16))
    grad_q_two, grad_k_two, grad_v_two = attend_backward(
        queries_two, keys_two, values_two, cross_mask, log_two, grad_context_two
    )
    grad_q_low = (grad_q_two.reshape(stretch_rows, local_width) * 0.125).astype(jnp.bfloat16)
    grad_cross_query = lead_product(h_two_all, grad_q_low)
    bias_three = place_cols(jnp.sum(grad_q_low.astype(jnp.float32), 0))
    grad_h_two = group_sums(grad_q_low, w_cross_query, trail_product)
    kv_grad_part = jnp.concatenate(
        [grad_k_two.reshape(enc_total, local_width), grad_v_two.reshape(enc_total, local_width)], 1
    )
    seq_pick = jnp.arange(seq_count) == own_seq
    placed = jnp.where(seq_pick[:, None, None], kv_grad_part[None], 0.0)
    kv_grad_all = lax.psum(placed.astype(jnp.bfloat16), "tok")
    enc_partial = jnp.einsum(
        "sre,de->srd", kv_grad_all, w_cross_kv, preferred_element_type=jnp.float32
    )
    grad_encoder = lax.psum_scatter(
        enc_partial.astype(jnp.bfloat16), "hd", scatter_dimension=1, tiled=True
    ).astype(jnp.float32)
    first_stretch = (stretch_start % SEQ == 0).astype(jnp.float32)
    own_kv_low = lax.dynamic_index_in_dim(kv_grad_all, own_seq, 0, keepdims=False)
    grad_cross_kv = lead_product(enc_rows, own_kv_low) * first_stretch
    bias_four = (
        place_cols(jnp.sum(own_kv_low[:, local_width:].astype(jnp.float32), 0)) * first_stretch
    )
    grad_cross_qkv = jnp.concatenate(
        [grad_cross_query[:, None], grad_cross_kv.reshape(model_width, 2, local_width)], 1
    )
    back_two, gain_two, shift_two = norm_pull_two(grad_h_two)
    grad_one = grad_two + back_two
    grad_att_one = grad_one.astype(jnp.bfloat16)
    bias_two = jnp.sum(grad_att_one.astype(jnp.float32), 0)
    grad_one_all = group_rows(grad_att_one)
    grad_self_out = lead_product(context_heads, grad_one_all)
    grad_context = trail_product(grad_one_all, w_self_out).astype(jnp.bfloat16)
    query_tiles = []
    own_kv_grad = jnp.zeros((stretch_rows, 2, local_width), jnp.float32)
    prior_kv_grad = jnp.zeros((prior_span, 2, local_width), jnp.float32)
    for tile_index in range(tile_total):
        tile_query, key_rows, value_rows, allowed, own_end = tile_inputs(tile_index)
        first_row = tile_index * tile_rows
        tile_grad = split_heads(grad_context[first_row : first_row + tile_rows])
        query_grad, key_grad, value_grad = attend_backward(
            tile_query, key_rows, value_rows, allowed, log_tiles[tile_index], tile_grad
        )
        query_tiles.append(query_grad.reshape(tile_rows, 1, local_width))
        tile_kv = jnp.stack(
            [key_grad.reshape(-1, local_width), value_grad.reshape(-1, local_width)], 1
        )
        own_kv_grad = own_kv_grad + jnp.pad(
            tile_kv[prior_span:], ((0, stretch_rows - own_end), (0, 0), (0, 0))
        )
        prior_kv_grad = prior_kv_grad + tile_kv[:prior_span]
    for back_step in range(back_count, 0, -1):
        slot_index = back_count - back_step
        grad_piece = prior_kv_grad[slot_index * stretch_rows : (slot_index + 1) * stretch_rows]
        own_kv_grad = own_kv_grad + from_behind(
            grad_piece.astype(jnp.bfloat16), "tok", -back_step
        ).astype(grad_piece.dtype)
    grad_heads = jnp.concatenate([jnp.concatenate(query_tiles, 0), own_kv_grad], 1)
    grad_pre = (grad_heads * qkv_scale).astype(jnp.bfloat16)
    grad_pre_flat = grad_pre.reshape(stretch_rows, 3 * local_width)
    grad_self_qkv = lead_product(h_one_all, grad_pre_flat).reshape(model_width, 3, local_width)
    bias_zero = place_cols(jnp.sum(grad_pre[:, 0].astype(jnp.float32), 0))
    bias_one = place_cols(jnp.sum(grad_pre[:, 2].astype(jnp.float32), 0))
    grad_h_one = group_sums(grad_pre_flat, w_self_flat, trail_product)
    back_one, gain_one, shift_one = norm_pull_one(grad_h_one)
    grad_hidden = grad_one + back_one
    grad_bias = jnp.stack(
        [bias_zero, bias_one, bias_two, bias_three, bias_four, bias_five, bias_six], 1
    )
    grad_gain = jnp.stack([gain_one, gain_two, gain_three], 1)
    grad_shift = jnp.stack([shift_one, shift_two, shift_three], 1)
    sent_self_qkv, sent_cross_qkv, sent_up, sent_self_out, sent_cross_out, sent_down = (
        lax.psum_scatter(
            grad_self_qkv.astype(jnp.bfloat16), "tok", scatter_dimension=0, tiled=True
        ).astype(jnp.float32),
        lax.psum_scatter(
            grad_cross_qkv.astype(jnp.bfloat16), "tok", scatter_dimension=0, tiled=True
        ).astype(jnp.float32),
        lax.psum_scatter(
            grad_up.astype(jnp.bfloat16), "tok", scatter_dimension=0, tiled=True
        ).astype(jnp.float32),
        lax.psum_scatter(
            grad_self_out.astype(jnp.bfloat16), "tok", scatter_dimension=1, tiled=True
        ).astype(jnp.float32),
        lax.psum_scatter(
            grad_cross_out.astype(jnp.bfloat16), "tok", scatter_dimension=1, tiled=True
        ).astype(jnp.float32),
        lax.psum_scatter(
            grad_down.astype(jnp.bfloat16), "tok", scatter_dimension=1, tiled=True
        ).astype(jnp.float32),
    )
    sent_bias, sent_bias_up, sent_gain, sent_shift = (
        lax.psum_scatter(grad_bias, ("tok", "hd"), scatter_dimension=0, tiled=True),
        lax.psum_scatter(grad_bias_up, ("tok", "hd"), scatter_dimension=0, tiled=True),
        lax.psum_scatter(grad_gain, ("tok", "hd"), scatter_dimension=0, tiled=True),
        lax.psum_scatter(grad_shift, ("tok", "hd"), scatter_dimension=0, tiled=True),
    )
    return (
        output,
        grad_hidden,
        grad_encoder,
        sent_self_qkv,
        sent_self_out,
        sent_cross_qkv,
        sent_cross_out,
        sent_up,
        sent_down,
        sent_bias,
        sent_bias_up,
        sent_gain,
        sent_shift,
    )


def solution(mesh):
    in_specs = (
        P(("tok", "hd"), None),
        P(None, "hd", None),
        P(("tok", "hd"), None),
        P("tok"),
        P("tok", None, "hd"),
        P("hd", "tok"),
        P("tok", None, "hd"),
        P("hd", "tok"),
        P("tok", "hd"),
        P("hd", "tok"),
        P(("tok", "hd"), None),
        P(("tok", "hd")),
        P(("tok", "hd"), None),
        P(("tok", "hd"), None),
    )
    out_specs = (
        P(("tok", "hd"), None),
        P(("tok", "hd"), None),
        P(None, "hd", None),
        P("tok", None, "hd"),
        P("hd", "tok"),
        P("tok", None, "hd"),
        P("hd", "tok"),
        P("tok", "hd"),
        P("hd", "tok"),
        P(("tok", "hd"), None),
        P(("tok", "hd")),
        P(("tok", "hd"), None),
        P(("tok", "hd"), None),
    )
    return jax.shard_map(local, mesh=mesh, in_specs=in_specs, out_specs=out_specs, check_vma=False)
```

profile of v0, /device:TPU:0, one launch (start us, length us, event | category | flops | bytes accessed | tf_op | source)
XLA Modules:
  0.0 2221.6 jit_solution(9509138172984459463)
XLA Ops:
  8.0 43.6 %all-gather.1 = bf16[32,32,3]{1,2,0:T(4,128)(2,1)S(1)} all-gather(bf16[1,32,3]{1,2,0:T(4,128)(2,1)} %bitcast.324), channel_id=1, replica_groups=mesh['tok'=8,'hd'=4] {'tok','hd'}, dimensions={0}, use_global_device_ids=true | all-gather | bytes 6336 | tf_op jit(solution)/shard_map/all_gather | solution.py:110
  51.6 36.9 %all-gather.2 = bf16[32,32,3]{1,2,0:T(4,128)(2,1)S(1)} all-gather(bf16[1,32,3]{1,2,0:T(4,128)(2,1)} %bitcast.325), channel_id=1, replica_groups=mesh['tok'=8,'hd'=4] {'tok','hd'}, dimensions={0}, use_global_device_ids=true | all-gather | bytes 6336 | tf_op jit(solution)/shard_map/all_gather | solution.py:111
  95.1 38.6 %all-gather.3 = bf16[32,32,7]{1,2,0:T(8,128)(2,1)S(1)} all-gather(bf16[1,32,7]{1,2,0:T(8,128)(2,1)} %bitcast.323), channel_id=1, replica_groups=mesh['tok'=8,'hd'=4] {'tok','hd'}, dimensions={0}, use_global_device_ids=true | all-gather | bytes 14784 | tf_op jit(solution)/shard_map/all_gather | solution.py:108
  151.8 44.3 %all_gather.56 = bf16[256,1024]{1,0:T(8,128)(2,1)} all-gather(bf16[256,128]{1,0:T(8,128)(2,1)S(1)} %copy-done.45), channel_id=1, replica_groups=mesh['tok'=8,'hd'=4] {'tok'}, dimensions={1}, use_global_device_ids=true | all-gather | bytes 589824 | tf_op jit(solution)/shard_map/all_gather | solution.py:103
  209.9 39.6 %collective-permute-done.3 = bf16[1024,2,256]{0,2,1:T(8,128)(2,1)S(1)} collective-permute-done((bf16[1024,2,256]{0,2,1:T(8,128)(2,1)S(1)}, bf16[1024,2,256]{0,2,1:T(8,128)(2,1)S(1)}, u32[]{:S(2)}, u32[]{:S(2)}) %collective-permute-start.3) | collective-permute-done | bytes 1048608 | tf_op jit(solution)/shard_map/ppermute | solution.py:18
  249.5 109.3 %collective-permute-start.4 = (bf16[1024,2,256]{0,2,1:T(8,128)(2,1)S(1)}, bf16[1024,2,256]{0,2,1:T(8,128)(2,1)S(1)}, u32[]{:S(2)}, u32[]{:S(2)}) collective-permute-start(bf16[1024,2,256]{0,2,1:T(8,128)(2,1)S(1)} %slice.261), channel_id=1, source_target_pairs={{0,12},{4,16},{8,20},{12,24},{16,28},{1,13},{5,17},{9,21},{13,25},... | collective-permute-start | bytes 3145736 | tf_op jit(solution)/shard_map/ppermute | solution.py:18
  381.2 26.2 %select_reduce_fusion.1 = (f32[4,512]{1,0:T(4,128)S(1)}, f32[4,512,7936]{2,1,0:T(8,128)}) fusion(pred[512,7936]{1,0:T(8,128)(4,1)} %pad_add_fusion.1, bf16[512,4,64]{0,2,1:T(8,128)(2,1)S(1)} %bitcast.234, bf16[7936,4,64]{0,2,1:T(8,128)(2,1)} %constant_dynamic-update-slice_fusion.9), kind=kOutput, calls=%fused_computation.13 | convolution fusion | flops 2112878592 | bytes 73408512 | tf_op jit(solution)/shard_map/qhd,khd->hqk/dot_general | solution.py:48
  407.4 23.2 %fusion.1 = f32[4,512]{1,0:T(4,128)S(1)} fusion(f32[4,512,7936]{2,1,0:T(8,128)} %get-tuple-element.119, f32[4,512]{1,0:T(4,128)S(1)} %get-tuple-element.118, pred[512,7936]{1,0:T(8,128)(4,1)} %pad_add_fusion.1), kind=kLoop, calls=%fused_computation.11 | loop fusion | flops 48756736 | bytes 69091328 | tf_op jit(solution)/shard_map/reduce_sum | solution.py:56
  430.6 27.9 %fusion.66 = bf16[4,64,512]{2,1,0:T(8,128)(2,1)} fusion(bf16[7936,4,64]{0,2,1:T(8,128)(2,1)} %copy-done.13, f32[4,512,7936]{2,1,0:T(8,128)} %get-tuple-element.119, f32[4,512]{1,0:T(4,128)S(1)} %fusion.1, f32[4,512]{1,0:T(4,128)S(1)} %get-tuple-element.118, pred[512,7936]{1,0:T(8,128)(4,1)} %pad_add_fusion.1), kind=kOutput, calls=%fused_computation.133 | convolution fusion | flops 2145517568 | bytes 73416704 | tf_op jit(solution)/shard_map/hqk,khd->qhd/dot_general | solution.py:58
  458.6 26.8 %select_reduce_fusion = (f32[4,512]{1,0:T(4,128)S(1)}, f32[4,512,8192]{2,1,0:T(8,128)}) fusion(pred[512,8192]{1,0:T(8,128)(4,1)} %pad_add_fusion, bf16[512,4,64]{0,2,1:T(8,128)(2,1)S(1)} %bitcast.236, bf16[8192,4,64]{0,2,1:T(8,128)(2,1)} %constant_dynamic-update-slice_fusion.25), kind=kOutput, calls=%fused_computation.12 | convolution fusion | flops 2181036032 | bytes 75767808 | tf_op jit(solution)/shard_map/qhd,khd->hqk/dot_general | solution.py:48
  485.4 22.6 %fusion = f32[4,512]{1,0:T(4,128)S(1)} fusion(f32[4,512,8192]{2,1,0:T(8,128)} %get-tuple-element.117, f32[4,512]{1,0:T(4,128)S(1)} %get-tuple-element.116, pred[512,8192]{1,0:T(8,128)(4,1)} %pad_add_fusion), kind=kLoop, calls=%fused_computation.10 | loop fusion | flops 50329600 | bytes 71319552 | tf_op jit(solution)/shard_map/reduce_sum | solution.py:56
  508.0 28.5 %fusion.67 = bf16[4,64,512]{2,1,0:T(8,128)(2,1)S(1)} fusion(bf16[8192,4,64]{0,2,1:T(8,128)(2,1)} %copy-done.12, f32[4,512,8192]{2,1,0:T(8,128)} %get-tuple-element.117, f32[4,512]{1,0:T(4,128)S(1)} %fusion, f32[4,512]{1,0:T(4,128)S(1)} %get-tuple-element.116, pred[512,8192]{1,0:T(8,128)(4,1)} %pad_add_fusion), kind=kOutput, calls=%fused_computation.134 | convolution fusion | flops 2214723584 | bytes 75776000 | tf_op jit(solution)/shard_map/hqk,khd->qhd/dot_general | solution.py:58
  539.6 35.5 %reduce-scatter.29.cloned.1.call-done = bf16[256,1024]{1,0:T(8,128)(2,1)} async-done(((bf16[1024,1024]{1,0:T(8,128)(2,1)}), bf16[256,1024]{1,0:T(8,128)(2,1)}) %reduce-scatter.29.cloned.1.call-update) | async-done | bytes 524304 | tf_op jit(solution)/shard_map/reduce_scatter | solution.py:152
  588.2 29.8 %all_gather.60 = bf16[256,1024]{1,0:T(8,128)(2,1)S(1)} all-gather(bf16[256,128]{1,0:T(8,128)(2,1)S(1)} %copy-done.46), channel_id=1, replica_groups=mesh['tok'=8,'hd'=4] {'tok'}, dimensions={1}, use_global_device_ids=true | all-gather | bytes 589824 | tf_op jit(solution)/shard_map/all_gather | solution.py:104
  629.8 20.8 all-gather.22.cloned.1.call-done
  659.6 30.8 %reduce-scatter.31.cloned.1.call-done = bf16[256,1024]{1,0:T(8,128)(2,1)} async-done(((bf16[1024,1024]{1,0:T(8,128)(2,1)}), bf16[256,1024]{1,0:T(8,128)(2,1)}) %reduce-scatter.31.cloned.1.call-update) | async-done | bytes 524304 | tf_op jit(solution)/shard_map/reduce_scatter | solution.py:152
  694.6 41.2 %all-gather.4 = bf16[32,1,256]{2,1,0:T(2,128)(2,1)S(1)} all-gather(bf16[1,1,256]{2,1,0:T(2,128)(2,1)S(1)} %reshape.392), channel_id=1, replica_groups=mesh['tok'=8,'hd'=4] {'tok','hd'}, dimensions={0}, use_global_device_ids=true | all-gather | bytes 16896 | tf_op jit(solution)/shard_map/all_gather | solution.py:109
  735.9 30.2 %all-gather.26.cloned.1.call-done = bf16[1024,2048]{1,0:T(8,128)(2,1)} async-done(((bf16[128,2048]{1,0:T(8,128)(2,1)}), bf16[1024,2048]{1,0:T(8,128)(2,1)}) %all-gather.26.cloned.1.call-update) | async-done | bytes 4194320 | tf_op jit(solution)/shard_map/all_gather | solution.py:102
  766.0 23.0 %all-gather.24.cloned.1.call-done = bf16[1024,1024]{1,0:T(8,128)(2,1)} async-done(((bf16[256,1024]{1,0:T(8,128)(2,1)}), bf16[1024,1024]{1,0:T(8,128)(2,1)}) %all-gather.24.cloned.1.call-update) | async-done | bytes 2097168 | tf_op jit(solution)/shard_map/all_gather | solution.py:149
  789.1 10.7 fusion.121
  799.7 13.5 all-gather.30.cloned.1.call-done
  813.3 76.9 %all-gather.28.cloned.1.call-done = bf16[2048,1024]{1,0:T(8,128)(2,1)} async-done(((bf16[2048,128]{1,0:T(8,128)(2,1)}), bf16[2048,1024]{1,0:T(8,128)(2,1)}) %all-gather.28.cloned.1.call-update) | async-done | bytes 4194320 | tf_op jit(solution)/shard_map/all_gather | solution.py:105
  890.2 28.5 %convert_reduce_fusion = (f32[2048]{0:T(1024)}, bf16[1024,2048]{1,0:T(8,128)(2,1)S(1)}, f32[1024,2048]{1,0:T(8,128)}) fusion(f32[1024,2048]{1,0:T(8,128)} %fusion.121, f32[2048]{0:T(1024)S(1)} %dynamic_slice.26, bf16[1024,1024]{1,0:T(8,128)(2,1)} %all-gather.30.cloned.1.call-done, bf16[2048,1024]{1,0:T(8,128)(2,1)} %all-gather.28.cloned.1.call-done), kind=kOutput, calls=%fused_computation.34 | convolution fusion | flops 4452251648 | bytes 27279360 | tf_op jit(solution)/shard_map/dot_general | solution.py:42
  926.6 10.7 multiply_convert_fusion.2
  958.2 32.0 %reduce-scatter.33.cloned.1.call-done = bf16[256,1024]{1,0:T(8,128)(2,1)} async-done(((bf16[1024,1024]{1,0:T(8,128)(2,1)}), bf16[256,1024]{1,0:T(8,128)(2,1)}) %reduce-scatter.33.cloned.1.call-update) | async-done | bytes 524304 | tf_op jit(solution)/shard_map/reduce_scatter | solution.py:152
  995.4 22.7 %all-gather.32.cloned.1.call-done = bf16[1024,1024]{1,0:T(8,128)(2,1)} async-done(((bf16[256,1024]{1,0:T(8,128)(2,1)}), bf16[1024,1024]{1,0:T(8,128)(2,1)}) %all-gather.32.cloned.1.call-update) | async-done | bytes 2097168 | tf_op jit(solution)/shard_map/all_gather | solution.py:149
  1035.5 25.1 %reduce-scatter.37.cloned.1.call-done = bf16[256,1024]{1,0:T(8,128)(2,1)} async-done(((bf16[1024,1024]{1,0:T(8,128)(2,1)}), bf16[256,1024]{1,0:T(8,128)(2,1)}) %reduce-scatter.37.cloned.1.call-update) | async-done | bytes 524304 | tf_op jit(solution)/shard_map/reduce_scatter | solution.py:152
  1098.8 36.0 %all-reduce.5.cloned.1.call-done = bf16[256,512]{0,1:T(8,128)(2,1)} async-done(((bf16[256,512]{0,1:T(8,128)(2,1)}), bf16[256,512]{0,1:T(8,128)(2,1)}) %all-reduce.5.cloned.1.call-update) | async-done | bytes 262160 | tf_op jit(solution)/shard_map/psum | solution.py:261
  1145.8 12.9 all-gather.34.cloned.1.call-done
  1161.1 29.5 %fusion.10 = f32[4,64,7936]{2,1,0:T(8,128)} fusion(bf16[512,4,64]{0,2,1:T(8,128)(2,1)S(1)} %bitcast.231, f32[4,512,7936]{2,1,0:T(8,128)} %get-tuple-element.119, f32[4,512]{1,0:T(4,128)S(1)} %log_add_fusion.2, pred[512,7936]{1,0:T(8,128)(4,1)} %pad_add_fusion.1), kind=kOutput, calls=%fused_computation.21 | convolution fusion | flops 2129133568 | bytes 77471744 | tf_op jit(solution)/shard_map/hqk,qhd->khd/dot_general | solution.py:74
  1190.6 47.8 %multiply_reduce_fusion.1 = (f32[4,512]{1,0:T(4,128)S(1)}, f32[4,512,7936]{2,1,0:T(8,128)}) fusion(f32[4,512,7936]{2,1,0:T(8,128)} %get-tuple-element.119, f32[4,512]{1,0:T(4,128)S(1)} %log_add_fusion.2, pred[512,7936]{1,0:T(8,128)(4,1)} %pad_add_fusion.1, bf16[512,4,64]{0,2,1:T(8,128)(2,1)S(1)} %bitcast.232, bf16[7936,4,64]{0,2,1:T(8,128)(2,1)} %copy-done.13), kind=kOutput, calls=%fused_computation.6 | convolution fusion | flops 2145384448 | bytes 138428416 | tf_op jit(solution)/shard_map/qhd,khd->hqk/dot_general | solution.py:65
  1238.4 30.6 %fusion.4 = f32[4,64,8192]{2,1,0:T(8,128)} fusion(bf16[512,4,64]{0,2,1:T(8,128)(2,1)S(1)} %bitcast.229, f32[4,512,8192]{2,1,0:T(8,128)} %get-tuple-element.117, f32[4,512]{1,0:T(4,128)S(1)} %log_add_fusion.1, pred[512,8192]{1,0:T(8,128)(4,1)} %pad_add_fusion), kind=kOutput, calls=%fused_computation.16 | convolution fusion | flops 2197815296 | bytes 79962112 | tf_op jit(solution)/shard_map/hqk,qhd->khd/dot_general | solution.py:74
  1269.0 51.0 %multiply_reduce_fusion = (f32[4,512]{1,0:T(4,128)S(1)}, f32[4,512,8192]{2,1,0:T(8,128)}) fusion(f32[4,512,8192]{2,1,0:T(8,128)} %get-tuple-element.117, f32[4,512]{1,0:T(4,128)S(1)} %log_add_fusion.1, pred[512,8192]{1,0:T(8,128)(4,1)} %pad_add_fusion, bf16[512,4,64]{0,2,1:T(8,128)(2,1)S(1)} %bitcast.230, bf16[8192,4,64]{0,2,1:T(8,128)(2,1)} %copy-done.12), kind=kOutput, calls=%fused_computation.1 | convolution fusion | flops 2214590464 | bytes 142884864 | tf_op jit(solution)/shard_map/qhd,khd->hqk/dot_general | solution.py:65
  1320.0 54.0 %multiply_convert_fusion.1 = bf16[4,512,7936]{2,1,0:T(8,128)(2,1)} fusion(f32[4,512,7936]{2,1,0:T(8,128)} %get-tuple-element.127, f32[4,512,7936]{2,1,0:T(8,128)} %get-tuple-element.119, f32[4,512]{1,0:T(4,128)S(1)} %get-tuple-element.126, f32[4,512]{1,0:T(4,128)S(1)} %log_add_fusion.2, pred[512,7936]{1,0:T(8,128)(4,1)} %pad_add_fusion.1), kind=kLoop, calls=%fused_computation.5 | loop fusion | flops 81264640 | bytes 166608896 | tf_op jit(solution)/shard_map/convert_element_type | solution.py:69
  1374.0 19.2 fusion.124
  1393.3 55.2 %multiply_convert_fusion = bf16[4,512,8192]{2,1,0:T(8,128)(2,1)} fusion(f32[4,512,8192]{2,1,0:T(8,128)} %get-tuple-element.125, f32[4,512,8192]{2,1,0:T(8,128)} %get-tuple-element.117, f32[4,512]{1,0:T(4,128)S(1)} %get-tuple-element.124, f32[4,512]{1,0:T(4,128)S(1)} %log_add_fusion.1, pred[512,8192]{1,0:T(8,128)(4,1)} %pad_add_fusion), kind=kLoop, calls=%fused_computation | loop fusion | flops 83886080 | bytes 171982848 | tf_op jit(solution)/shard_map/convert_element_type | solution.py:69
  1448.5 20.1 fusion.125
  1483.5 16.7 fusion.122
  1504.1 13.7 collective-permute-done.7
  1519.1 14.7 collective-permute-done.13
  1535.2 17.2 fusion.123
  1562.0 116.5 %collective-permute-done.10 = bf16[1024,2,256]{0,2,1:T(8,128)(2,1)} collective-permute-done((bf16[1024,2,256]{0,2,1:T(8,128)(2,1)}, bf16[1024,2,256]{0,2,1:T(8,128)(2,1)}, u32[]{:S(2)}, u32[]{:S(2)}) %collective-permute-start.10) | collective-permute-done | bytes 1048608 | tf_op jit(solution)/shard_map/ppermute | solution.py:18
  1701.9 37.1 %all-reduce.2 = f32[8192]{0:T(1024)S(1)} all-reduce(f32[8192]{0:T(1024)S(1)} %dynamic_update_slice.22), channel_id=17, replica_groups=mesh['tok'=8,'hd'=4] {'tok','hd'}, use_global_device_ids=true, to_apply=%region_44.45.clone | all-reduce | flops 8192 | bytes 65536
  1750.8 93.9 %reduce-scatter.55.cloned.1.call-done = f32[32,7]{1,0:T(8,128)} async-done(((f32[1024,7]{1,0:T(8,128)}), f32[32,7]{1,0:T(8,128)}) %reduce-scatter.55.cloned.1.call-update) | async-done | bytes 912
  1846.0 63.7 %reduce-scatter.43.cloned.1.call-done = bf16[128,3,256]{2,0,1:T(8,128)(2,1)} async-done(((bf16[1024,3,256]{2,0,1:T(8,128)(2,1)}), bf16[128,3,256]{2,0,1:T(8,128)(2,1)}) %reduce-scatter.43.cloned.1.call-update) | async-done | bytes 196624 | tf_op jit(solution)/shard_map/reduce_scatter | solution.py:323
  1911.5 31.2 %reduce-scatter.39.cloned.1.call-done = bf16[256,1024]{1,0:T(8,128)(2,1)} async-done(((bf16[1024,1024]{1,0:T(8,128)(2,1)}), bf16[256,1024]{1,0:T(8,128)(2,1)}) %reduce-scatter.39.cloned.1.call-update) | async-done | bytes 524304 | tf_op jit(solution)/shard_map/reduce_scatter | solution.py:152
  1949.5 131.6 %reduce-scatter.57.cloned.1.call-done = f32[32,3]{1,0:T(8,128)} async-done(((f32[1024,3]{1,0:T(8,128)}), f32[32,3]{1,0:T(8,128)}) %reduce-scatter.57.cloned.1.call-update) | async-done | bytes 400
  2082.5 130.5 %reduce-scatter.59.cloned.1.call-done = f32[32,3]{1,0:T(8,128)} async-done(((f32[1024,3]{1,0:T(8,128)}), f32[32,3]{1,0:T(8,128)}) %reduce-scatter.59.cloned.1.call-update) | async-done | bytes 400
  (422 shorter events, 282.9 us)
Async XLA Ops:
  7.2 135.2 %all-gather.18.cloned.1.call-start = ((), (), s32[]{:S(2)}) async-start(), calls=%async_computation.17 | async-start | bytes 1769472 | tf_op jit(solution)/shard_map/all_gather | solution.py:100
  7.9 136.2 %all-gather.16.cloned.1.call-start = ((), (), s32[]{:S(2)}) async-start(), calls=%async_computation.16 | async-start | bytes 2621440 | tf_op jit(solution)/shard_map/all_gather | solution.py:149
  95.1 480.1 %reduce-scatter.29.cloned.1.call-start = ((), (), s32[]{:S(2)}) async-start(), calls=%async_computation.18 | async-start | bytes 2621440 | tf_op jit(solution)/shard_map/reduce_scatter | solution.py:152
  147.8 60.5 %collective-permute-start = (bf16[1024,2,256]{0,2,1:T(8,128)(2,1)S(1)}, bf16[1024,2,256]{0,2,1:T(8,128)(2,1)S(1)}, u32[]{:S(2)}, u32[]{:S(2)}) collective-permute-start(bf16[1024,2,256]{0,2,1:T(8,128)(2,1)S(1)} %slice.261), channel_id=1, source_target_pairs={{0,28},{1,29},{2,30},{3,31}} | collective-permute-start | bytes 3145736 | tf_op jit(solution)/shard_map/ppermute | solution.py:18
  196.1 175.4 %collective-permute-start.6 = (bf16[1024,2,256]{0,2,1:T(8,128)(2,1)S(1)}, bf16[1024,2,256]{0,2,1:T(8,128)(2,1)S(1)}, u32[]{:S(2)}, u32[]{:S(2)}) collective-permute-start(bf16[1024,2,256]{0,2,1:T(8,128)(2,1)S(1)} %slice.261), channel_id=1, source_target_pairs={{0,4},{4,8},{8,12},{12,16},{16,20},{20,24},{24,28},{1,5},{5,9},{9,... | collective-permute-start | bytes 3145736 | tf_op jit(solution)/shard_map/ppermute | solution.py:18
  200.7 170.6 %collective-permute-start.5 = (bf16[1024,2,256]{0,2,1:T(8,128)(2,1)S(1)}, bf16[1024,2,256]{0,2,1:T(8,128)(2,1)S(1)}, u32[]{:S(2)}, u32[]{:S(2)}) collective-permute-start(bf16[1024,2,256]{0,2,1:T(8,128)(2,1)S(1)} %slice.261), channel_id=1, source_target_pairs={{0,8},{4,12},{8,16},{12,20},{16,24},{20,28},{1,9},{5,13},{9,17},{1... | collective-permute-start | bytes 3145736 | tf_op jit(solution)/shard_map/ppermute | solution.py:18
  203.4 46.0 %collective-permute-start.3 = (bf16[1024,2,256]{0,2,1:T(8,128)(2,1)S(1)}, bf16[1024,2,256]{0,2,1:T(8,128)(2,1)S(1)}, u32[]{:S(2)}, u32[]{:S(2)}) collective-permute-start(bf16[1024,2,256]{0,2,1:T(8,128)(2,1)S(1)} %slice.261), channel_id=1, source_target_pairs={{0,16},{4,20},{8,24},{12,28},{1,17},{5,21},{9,25},{13,29},{2,18},{... | collective-permute-start | bytes 3145736 | tf_op jit(solution)/shard_map/ppermute | solution.py:18
  206.1 154.0 %collective-permute-start.1 = (bf16[1024,2,256]{0,2,1:T(8,128)(2,1)S(1)}, bf16[1024,2,256]{0,2,1:T(8,128)(2,1)S(1)}, u32[]{:S(2)}, u32[]{:S(2)}) collective-permute-start(bf16[1024,2,256]{0,2,1:T(8,128)(2,1)S(1)} %slice.261), channel_id=1, source_target_pairs={{0,24},{4,28},{1,25},{5,29},{2,26},{6,30},{3,27},{7,31}} | collective-permute-start | bytes 3145736 | tf_op jit(solution)/shard_map/ppermute | solution.py:18
  208.4 151.9 %collective-permute-start.2 = (bf16[1024,2,256]{0,2,1:T(8,128)(2,1)S(1)}, bf16[1024,2,256]{0,2,1:T(8,128)(2,1)S(1)}, u32[]{:S(2)}, u32[]{:S(2)}) collective-permute-start(bf16[1024,2,256]{0,2,1:T(8,128)(2,1)S(1)} %slice.261), channel_id=1, source_target_pairs={{0,20},{4,24},{8,28},{1,21},{5,25},{9,29},{2,22},{6,26},{10,30},{3... | collective-permute-start | bytes 3145736 | tf_op jit(solution)/shard_map/ppermute | solution.py:18
  249.5 121.6 %collective-permute-start.4 = (bf16[1024,2,256]{0,2,1:T(8,128)(2,1)S(1)}, bf16[1024,2,256]{0,2,1:T(8,128)(2,1)S(1)}, u32[]{:S(2)}, u32[]{:S(2)}) collective-permute-start(bf16[1024,2,256]{0,2,1:T(8,128)(2,1)S(1)} %slice.261), channel_id=1, source_target_pairs={{0,12},{4,16},{8,20},{12,24},{16,28},{1,13},{5,17},{9,21},{13,25},... | collective-permute-start | bytes 3145736 | tf_op jit(solution)/shard_map/ppermute | solution.py:18
  538.7 88.2 %all-gather.20.cloned.1.call-start = ((), (), s32[]{:S(2)}) async-start(), calls=%async_computation.19 | async-start | bytes 1769472 | tf_op jit(solution)/shard_map/all_gather | solution.py:101
  539.6 111.1 %all-gather.22.cloned.1.call-start = ((), (), s32[]{:S(2)}) async-start(), calls=%async_computation.20 | async-start | bytes 2621440 | tf_op jit(solution)/shard_map/all_gather | solution.py:149
  580.0 110.4 %reduce-scatter.31.cloned.1.call-start = ((), (), s32[]{:S(2)}) async-start(), calls=%async_computation.21 | async-start | bytes 2621440 | tf_op jit(solution)/shard_map/reduce_scatter | solution.py:152
  658.8 107.2 %all-gather.26.cloned.1.call-start = ((), (), s32[]{:S(2)}) async-start(), calls=%async_computation.23 | async-start | bytes 4718592 | tf_op jit(solution)/shard_map/all_gather | solution.py:102
  659.6 129.5 %all-gather.24.cloned.1.call-start = ((), (), s32[]{:S(2)}) async-start(), calls=%async_computation.22 | async-start | bytes 2621440 | tf_op jit(solution)/shard_map/all_gather | solution.py:149
  693.2 120.1 %all-gather.30.cloned.1.call-start = ((), (), s32[]{:S(2)}) async-start(), calls=%async_computation.26 | async-start | bytes 2621440 | tf_op jit(solution)/shard_map/all_gather | solution.py:149
  693.9 196.3 %all-gather.28.cloned.1.call-start = ((), (), s32[]{:S(2)}) async-start(), calls=%async_computation.24 | async-start | bytes 4718592 | tf_op jit(solution)/shard_map/all_gather | solution.py:105
  694.5 261.7 %reduce-scatter.35.cloned.1.call-start = ((), (), s32[]{:S(2)}) async-start(), calls=%async_computation.27 | async-start | bytes 2621440 | tf_op jit(solution)/shard_map/reduce_scatter | solution.py:152
  926.4 63.8 %reduce-scatter.33.cloned.1.call-start = ((), (), s32[]{:S(2)}) async-start(), calls=%async_computation.25 | async-start | bytes 2621440 | tf_op jit(solution)/shard_map/reduce_scatter | solution.py:152
  946.7 71.4 %all-gather.32.cloned.1.call-start = ((), (), s32[]{:S(2)}) async-start(), calls=%async_computation.28 | async-start | bytes 2621440 | tf_op jit(solution)/shard_map/all_gather | solution.py:149
  995.3 65.3 %reduce-scatter.37.cloned.1.call-start = ((), (), s32[]{:S(2)}) async-start(), calls=%async_computation.29 | async-start | bytes 2621440 | tf_op jit(solution)/shard_map/reduce_scatter | solution.py:152
  1029.0 105.7 %all-reduce.5.cloned.1.call-start = ((), (), s32[]{:S(2)}) async-start(), calls=%async_computation.32 | async-start | bytes 524288 | tf_op jit(solution)/shard_map/psum | solution.py:261
  1035.3 123.4 %all-gather.34.cloned.1.call-start = ((), (), s32[]{:S(2)}) async-start(), calls=%async_computation.30 | async-start | bytes 2621440 | tf_op jit(solution)/shard_map/all_gather | solution.py:149
  1068.5 671.1 %reduce-scatter.53.cloned.1.call-start = ((), (), s32[]{:S(2)}) async-start(), calls=%async_computation.39 | async-start | bytes 4718592
  1084.6 657.4 %reduce-scatter.51.cloned.1.call-start = ((), (), s32[]{:S(2)}) async-start(), calls=%async_computation.38 | async-start | bytes 589824
  1089.0 654.7 %reduce-scatter.47.cloned.1.call-start = ((), (), s32[]{:S(2)}) async-start(), calls=%async_computation.36 | async-start | bytes 4718592 | tf_op jit(solution)/shard_map/reduce_scatter | solution.py:329
  1097.4 648.4 %reduce-scatter.41.cloned.1.call-start = ((), (), s32[]{:S(2)}) async-start(), calls=%async_computation.33 | async-start | bytes 655360 | tf_op jit(solution)/shard_map/reduce_scatter | solution.py:265
  1137.1 610.3 %reduce-scatter.45.cloned.1.call-start = ((), (), s32[]{:S(2)}) async-start(), calls=%async_computation.35 | async-start | bytes 1769472 | tf_op jit(solution)/shard_map/reduce_scatter | solution.py:326
  1145.3 603.8 %reduce-scatter.49.cloned.1.call-start = ((), (), s32[]{:S(2)}) async-start(), calls=%async_computation.37 | async-start | bytes 589824
  1480.9 36.9 %collective-permute-start.7 = (bf16[1024,2,256]{0,2,1:T(8,128)(2,1)S(1)}, bf16[1024,2,256]{0,2,1:T(8,128)(2,1)S(1)}, u32[]{:S(2)}, u32[]{:S(2)}) collective-permute-start(bf16[1024,2,256]{0,2,1:T(8,128)(2,1)S(1)} %get-tuple-element.38), channel_id=1, source_target_pairs={{28,0},{29,1},{30,2},{31,3}} | collective-permute-start | bytes 3145736 | tf_op jit(solution)/shard_map/ppermute | solution.py:18
  1482.2 51.6 %collective-permute-start.13 = (bf16[1024,2,256]{0,2,1:T(8,128)(2,1)S(1)}, bf16[1024,2,256]{0,2,1:T(8,128)(2,1)S(1)}, u32[]{:S(2)}, u32[]{:S(2)}) collective-permute-start(bf16[1024,2,256]{0,2,1:T(8,128)(2,1)S(1)} %get-tuple-element.39), channel_id=1, source_target_pairs={{4,0},{8,4},{12,8},{16,12},{20,16},{24,20},{28,24},{5,1},{9,5},{13... | collective-permute-start | bytes 3145736 | tf_op jit(solution)/shard_map/ppermute | solution.py:18
  1500.2 57.8 %collective-permute-start.12 = (bf16[1024,2,256]{0,2,1:T(8,128)(2,1)}, bf16[1024,2,256]{0,2,1:T(8,128)(2,1)}, u32[]{:S(2)}, u32[]{:S(2)}) collective-permute-start(bf16[1024,2,256]{0,2,1:T(8,128)(2,1)} %get-tuple-element.40), channel_id=1, source_target_pairs={{8,0},{12,4},{16,8},{20,12},{24,16},{28,20},{9,1},{13,5},{17,9},{2... | collective-permute-start | bytes 3145736 | tf_op jit(solution)/shard_map/ppermute | solution.py:18
  1501.5 60.5 %collective-permute-start.11 = (bf16[1024,2,256]{0,2,1:T(8,128)(2,1)}, bf16[1024,2,256]{0,2,1:T(8,128)(2,1)}, u32[]{:S(2)}, u32[]{:S(2)}) collective-permute-start(bf16[1024,2,256]{0,2,1:T(8,128)(2,1)} %get-tuple-element.41), channel_id=1, source_target_pairs={{12,0},{16,4},{20,8},{24,12},{28,16},{13,1},{17,5},{21,9},{25,13},... | collective-permute-start | bytes 3145736 | tf_op jit(solution)/shard_map/ppermute | solution.py:18
  1502.8 175.7 %collective-permute-start.10 = (bf16[1024,2,256]{0,2,1:T(8,128)(2,1)}, bf16[1024,2,256]{0,2,1:T(8,128)(2,1)}, u32[]{:S(2)}, u32[]{:S(2)}) collective-permute-start(bf16[1024,2,256]{0,2,1:T(8,128)(2,1)} %get-tuple-element.42), channel_id=1, source_target_pairs={{16,0},{20,4},{24,8},{28,12},{17,1},{21,5},{25,9},{29,13},{18,2},{... | collective-permute-start | bytes 3145736 | tf_op jit(solution)/shard_map/ppermute | solution.py:18
  1517.8 160.8 %collective-permute-start.9 = (bf16[1024,2,256]{0,2,1:T(8,128)(2,1)S(1)}, bf16[1024,2,256]{0,2,1:T(8,128)(2,1)}, u32[]{:S(2)}, u32[]{:S(2)}) collective-permute-start(bf16[1024,2,256]{0,2,1:T(8,128)(2,1)S(1)} %get-tuple-element.43), channel_id=1, source_target_pairs={{20,0},{24,4},{28,8},{21,1},{25,5},{29,9},{22,2},{26,6},{30,10},{2... | collective-permute-start | bytes 3145736 | tf_op jit(solution)/shard_map/ppermute | solution.py:18
  1533.8 144.8 %collective-permute-start.8 = (bf16[1024,2,256]{0,2,1:T(8,128)(2,1)S(1)}, bf16[1024,2,256]{0,2,1:T(8,128)(2,1)}, u32[]{:S(2)}, u32[]{:S(2)}) collective-permute-start(bf16[1024,2,256]{0,2,1:T(8,128)(2,1)S(1)} %get-tuple-element.44), channel_id=1, source_target_pairs={{24,0},{28,4},{25,1},{29,5},{26,2},{30,6},{27,3},{31,7}} | collective-permute-start | bytes 3145736 | tf_op jit(solution)/shard_map/ppermute | solution.py:18
  1557.7 287.0 %reduce-scatter.55.cloned.1.call-start = ((), (), s32[]{:S(2)}) async-start(), calls=%async_computation.40 | async-start | bytes 540672
  1691.6 218.2 %reduce-scatter.43.cloned.1.call-start = ((), (), s32[]{:S(2)}) async-start(), calls=%async_computation.34 | async-start | bytes 1769472 | tf_op jit(solution)/shard_map/reduce_scatter | solution.py:323
  1696.8 245.9 %reduce-scatter.39.cloned.1.call-start = ((), (), s32[]{:S(2)}) async-start(), calls=%async_computation.31 | async-start | bytes 2621440 | tf_op jit(solution)/shard_map/reduce_scatter | solution.py:152
  1701.4 241.3 %copy-start.3 = (bf16[256,1024]{1,0:T(8,128)(2,1)S(1)}, bf16[256,1024]{1,0:T(8,128)(2,1)}, u32[]{:S(2)}) copy-start(bf16[256,1024]{1,0:T(8,128)(2,1)} %param.15) | copy-start | bytes 1572868
  1701.4 241.3 %copy-start.41 = (f32[1024,1]{0,1:T(1,128)S(1)}, f32[1024,1]{0,1:T(1,128)}, u32[]{:S(2)}) copy-start(f32[1024,1]{0,1:T(1,128)} %copy-done.40) | copy-start | bytes 12292
  1701.4 241.3 %copy-start.50 = (f32[256]{0:T(256)S(1)}, f32[256]{0:T(256)}, u32[]{:S(2)}) copy-start(f32[256]{0:T(256)} %copy-done.49) | copy-start | bytes 3076
  1701.4 242.8 %copy-start.71 = (f32[256]{0:T(256)S(1)}, f32[256]{0:T(256)}, u32[]{:S(2)}) copy-start(f32[256]{0:T(256)} %copy-done.70) | copy-start | bytes 3076
  1701.4 242.8 %copy-start.67 = (f32[256]{0:T(256)S(1)}, f32[256]{0:T(256)}, u32[]{:S(2)}) copy-start(f32[256]{0:T(256)} %copy-done.66) | copy-start | bytes 3076
  1701.5 379.7 %reduce-scatter.57.cloned.1.call-start = ((), (), s32[]{:S(2)}) async-start(), calls=%async_computation.41 | async-start | bytes 540672
  1739.6 206.3 %copy-start.55 = (f32[1024]{0:T(1024)S(1)}, f32[1024]{0:T(1024)}, u32[]{:S(2)}) copy-start(f32[1024]{0:T(1024)} %get-tuple-element.15) | copy-start | bytes 12292
  1739.6 206.3 %copy-start.57 = (f32[1024]{0:T(1024)S(1)}, f32[1024]{0:T(1024)}, u32[]{:S(2)}) copy-start(f32[1024]{0:T(1024)} %get-tuple-element.13) | copy-start | bytes 12292
  1947.0 266.0 %reduce-scatter.59.cloned.1.call-start = ((), (), s32[]{:S(2)}) async-start(), calls=%async_computation.42 | async-start | bytes 540672
  (73 other events, 2346.0 us)
Sparse Core Ops, SparseCore 0:
  10.2 46.9 all-gather.17
  95.2 20.3 all-gather.15
  538.8 36.2 reduce-scatter.28
  577.8 48.9 all-gather.19
  628.9 21.7 all-gather.21
  658.9 31.4 reduce-scatter.30
  692.5 73.4 all-gather.25
  768.2 20.8 all-gather.23
  790.7 22.5 all-gather.29
  815.2 75.0 all-gather.27
  926.5 29.6 reduce-scatter.34
  958.7 31.4 reduce-scatter.32
  995.4 22.5 all-gather.31
  1029.2 31.4 reduce-scatter.36
  1064.2 70.5 all-reduce.4
  1136.8 21.8 all-gather.33
  1162.2 88.0 reduce-scatter.52
  1253.8 61.6 reduce-scatter.50
  1319.2 86.8 reduce-scatter.46
  1408.6 21.4 reduce-scatter.40
  1433.5 72.0 reduce-scatter.44
  1557.8 151.7 reduce-scatter.48
  1711.8 132.8 reduce-scatter.54
  1848.3 61.3 reduce-scatter.42
  1912.3 30.3 reduce-scatter.38
  1947.1 133.9 reduce-scatter.56
  2083.2 129.7 reduce-scatter.58
where the time goes:
time: 2230 us; the launch traced here: 2220 us
  waiting for transfers between devices  1030 us (46%)
  matrix products  462 us (21%)
  blocking collectives  278 us (12%)
  other arithmetic  241 us (11%)
  starting transfers between devices  135 us (6%)
  local copies, waits for them, and re-layouts  58.5 us (3%)
    unnamed x33, waiting for transfers between devices  359 us
    ppermute x14, waiting for transfers between devices, from_behind(): return lax.ppermute(shard, axis, pairs)  199 us
    reduce_scatter x6, waiting for transfers between devices, group_sums(): lax.psum_scatter(product(left, right).astype(jnp.bfloat16), 'hd', scatter...  164 us
    ppermute x14, starting transfers between devices, from_behind(): return lax.ppermute(shard, axis, pairs)  133 us
    convert_element_type x3, other arithmetic, attend_backward(): grad_scores = (soft_probs * (grad_probs - row_inner)).astype(jnp.bfloat16)  110 us
    dot_general x3, matrix products, attend_backward(): jnp.einsum('qhd,khd->hqk', grad_context, value_rows, preferred_element_ty...  99.9 us
    all_gather x6, waiting for transfers between devices, group_rows(): return lax.all_gather(block_rows, 'hd', axis=0, tiled=True)  93 us
    all_gather x1, waiting for transfers between devices, local(): lax.all_gather(down_weight, 'tok', axis=1, tiled=True)  76.9 us
  transfers between devices with their start and end apart: 41, of which 26 were waited for; matrix products, arithmetic and copies ran while one was open for 23% of the time, Pallas kernels for 0%

commit v1 on v0

v1 whole, which is shorter than its diff:
```python
import functools

import jax
import jax.numpy as jnp
from jax import lax
from jax.experimental import pallas as pl
from jax.experimental.pallas import tpu as pltpu
from jax.sharding import PartitionSpec as P

HDIM = 64
SEQ = 8192
TILE = 512
norm_eps = 1e-05
neg_large = -1e30
f32 = jnp.float32
bf16 = jnp.bfloat16


def dot(left, right, left_dim, right_dim):
    return lax.dot_general(
        left, right, (((left_dim,), (right_dim,)), ((), ())), preferred_element_type=f32
    )


def swap(value, axis, mask):
    return lax.ppermute(value, axis, [(i, i ^ mask) for i in range(lax.axis_size(axis))])


def hd_masks():
    mask, masks = lax.axis_size("hd") // 2, []
    while mask:
        masks.append(mask)
        mask //= 2
    return masks


def gather_xor(value):
    have = {0: value}
    for mask in hd_masks():
        for index in list(have):
            have[index ^ mask] = swap(have[index], "hd", mask)
    return [have[index] for index in range(len(have))]


def reduce_xor(parts):
    have = dict(enumerate(parts))
    for mask in reversed(hd_masks()):
        for index in sorted(have, reverse=True):
            if index & mask:
                got = swap(have.pop(index).astype(bf16), "hd", mask)
                have[index ^ mask] = have[index ^ mask] + got.astype(f32)
    return have[0]


def exchange_xor(parts):
    have = {index: {0: part} for index, part in enumerate(parts)}
    for mask in hd_masks():
        gone = [index for index in have if index & mask]
        keys = [(index, source) for index in gone for source in have[index]]
        got = swap(jnp.stack([have[index][source] for index, source in keys]), "hd", mask)
        for slot, (index, source) in enumerate(keys):
            have[index ^ mask][source ^ mask] = got[slot]
        for index in gone:
            del have[index]
    return [have[0][index] for index in range(len(parts))]


def pick(stacked, index):
    return lax.dynamic_index_in_dim(stacked, index, 0, keepdims=False)


def normalize(value):
    center = value - jnp.mean(value, axis=-1, keepdims=True)
    inverse = lax.rsqrt(jnp.mean(center * center, axis=-1, keepdims=True) + norm_eps)
    return center * inverse, inverse


def norm_backward(grad, unit, inverse, gain):
    scaled = grad * gain
    back = (
        scaled
        - jnp.mean(scaled, axis=-1, keepdims=True)
        - unit * jnp.mean(scaled * unit, axis=-1, keepdims=True)
    ) * inverse
    return back, jnp.sum(grad * unit, axis=0), jnp.sum(grad, axis=0)


def column(row, rows):
    return jnp.swapaxes(jnp.broadcast_to(row, (128, rows)), 0, 1)[:, :1]


VMEM = pl.BlockSpec(memory_space=pltpu.VMEM)
LIMIT = 48 * 2**20


def self_forward_kernel(heads, others, info, *refs):
    refs = list(refs)
    q_refs = [refs.pop(0) for _ in range(heads)]
    kv_refs = [[refs.pop(0) for _ in range(heads)] for _ in range(others)]
    id_refs = [refs.pop(0) for _ in range(heads)]
    o_ref, l_ref, q_all, k_all, v_all, id_all = refs
    piece_rows = q_all.shape[2]
    per = piece_rows // TILE
    step = pl.program_id(0)
    at, beside = info[0], info[1]

    @pl.when(step == 0)
    def _():
        for slot in range(heads):
            q_all[slot] = q_refs[slot][...]
            id_all[slot] = id_refs[slot][...]
            for other in range(others):
                k_all[other, slot] = jnp.swapaxes(kv_refs[other][slot][0], 0, 1)
                v_all[other, slot] = kv_refs[other][slot][1]

    slot = step // per
    tile = lax.rem(step, per)
    piece = jnp.bitwise_xor(slot, at) * others + beside
    cols = pl.ds(pl.multiple_of(tile * TILE, TILE), TILE)
    q = q_all[slot, :, cols]

    def update(state, k, v, mask):
        top, total, acc = state
        scores = dot(k, q, 1, 0)
        if mask is not None:
            scores = jnp.where(mask, scores, neg_large)
        new_top = jnp.maximum(top, jnp.max(scores, axis=0, keepdims=True))
        probs = jnp.exp(scores - new_top)
        fade = jnp.exp(top - new_top)
        total = total * fade + jnp.sum(probs, axis=0, keepdims=True)
        acc = acc * fade + dot(v, probs.astype(bf16), 1, 0)
        return new_top, total, acc

    def earlier_piece(index, state):
        place = jnp.bitwise_xor(index // others, at)
        other = jnp.bitwise_xor(lax.rem(index, others), beside)
        return update(state, k_all[other, place], v_all[other, place], None)

    def earlier_tile(index, state):
        rows = pl.ds(pl.multiple_of(index * TILE, TILE), TILE)
        return update(state, k_all[0, slot, rows, :], v_all[0, slot, :, rows], None)

    state = (
        jnp.full((1, TILE), neg_large, f32),
        jnp.zeros((1, TILE), f32),
        jnp.zeros((HDIM, TILE), f32),
    )
    state = lax.fori_loop(0, piece, earlier_piece, state)
    state = lax.fori_loop(0, tile, earlier_tile, state)
    ids = id_all[slot, :, cols].astype(f32)
    mask = column(ids, TILE) <= ids
    top, total, acc = update(state, k_all[0, slot, cols, :], v_all[0, slot, :, cols], mask)
    o_ref[slot, :, cols] = (acc / total).astype(o_ref.dtype)
    l_ref[slot, :, cols] = top + jnp.log(total)


def self_forward(info, q, kv, ids):
    heads, others = len(q), len(kv)
    depth, rows = q[0].shape
    flat = list(q) + [block for line in kv for block in line] + list(ids)
    area = heads * rows * heads * others * rows // 2
    return pl.pallas_call(
        functools.partial(self_forward_kernel, heads, others),
        grid_spec=pltpu.PrefetchScalarGridSpec(
            num_scalar_prefetch=1,
            grid=(heads * rows // TILE,),
            in_specs=[VMEM] * len(flat),
            out_specs=[VMEM] * 2,
            scratch_shapes=[
                pltpu.VMEM((heads, depth, rows), bf16),
                pltpu.VMEM((others, heads, rows, depth), bf16),
                pltpu.VMEM((others, heads, depth, rows), bf16),
                pltpu.VMEM((heads, 1, rows), jnp.int32),
            ],
        ),
        out_shape=[
            jax.ShapeDtypeStruct((heads, depth, rows), bf16),
            jax.ShapeDtypeStruct((heads, 1, rows), f32),
        ],
        compiler_params=pltpu.CompilerParams(vmem_limit_bytes=LIMIT),
        cost_estimate=pl.CostEstimate(
            flops=area * 1024, bytes_accessed=8 * 2**20, transcendentals=area
        ),
        name="self_forward",
    )(info, *flat)


def self_backward_kernel(heads, others, info, *refs):
    refs = list(refs)
    q_refs = [refs.pop(0) for _ in range(heads)]
    kv_refs = [[refs.pop(0) for _ in range(heads)] for _ in range(others)]
    id_refs = [refs.pop(0) for _ in range(heads)]
    g_refs = [refs.pop(0) for _ in range(heads)]
    o_ref, l_ref, dq_ref, dkv_ref, q_all, g_all, id_all, kt_all, k_all, v_all, dk, dv = refs
    piece_rows = q_all.shape[2]
    per = piece_rows // TILE
    step = pl.program_id(0)
    at, beside = info[0], info[1]

    @pl.when(step == 0)
    def _():
        for slot in range(heads):
            q_all[slot] = q_refs[slot][...]
            g_all[slot] = g_refs[slot][...]
            id_all[slot] = id_refs[slot][...]
            for other in range(others):
                kt_all[other, slot] = kv_refs[other][slot][0]
                k_all[other, slot] = jnp.swapaxes(kv_refs[other][slot][0], 0, 1)
                v_all[other, slot] = jnp.swapaxes(kv_refs[other][slot][1], 0, 1)
        dk[...] = jnp.zeros_like(dk)
        dv[...] = jnp.zeros_like(dv)

    slot = step // per
    tile = lax.rem(step, per)
    piece = jnp.bitwise_xor(slot, at) * others + beside
    cols = pl.ds(pl.multiple_of(tile * TILE, TILE), TILE)
    q = q_all[slot, :, cols]
    grad = g_all[slot, :, cols]
    q_rows = jnp.swapaxes(q, 0, 1)
    grad_rows = jnp.swapaxes(grad, 0, 1)
    log_total = l_ref[slot, :, cols]
    inner = jnp.sum(o_ref[slot, :, cols].astype(f32) * grad.astype(f32), axis=0, keepdims=True)

    def update(dq, other, place, rows, mask):
        scores = dot(k_all[other, place, rows, :], q, 1, 0)
        if mask is not None:
            scores = jnp.where(mask, scores, neg_large)
        probs = jnp.exp(scores - log_total)
        grad_probs = dot(v_all[other, place, rows, :], grad, 1, 0)
        grad_scores = (probs * (grad_probs - inner)).astype(bf16)
        dv[other, place, rows, :] += dot(probs.astype(bf16), grad_rows, 1, 0)
        dk[other, place, rows, :] += dot(grad_scores, q_rows, 1, 0)
        return dq + dot(kt_all[other, place, :, rows], grad_scores, 1, 0)

    def earlier(index, dq):
        other_piece = index // per
        rows = pl.ds(pl.multiple_of(lax.rem(index, per) * TILE, TILE), TILE)
        place = jnp.bitwise_xor(other_piece // others, at)
        other = jnp.bitwise_xor(lax.rem(other_piece, others), beside)
        return update(dq, other, place, rows, None)

    dq = lax.fori_loop(0, piece * per + tile, earlier, jnp.zeros((HDIM, TILE), f32))
    ids = id_all[slot, :, cols].astype(f32)
    mask = column(ids, TILE) <= ids
    dq = update(dq, 0, slot, cols, mask)
    dq_ref[slot, :, cols] = (dq * 0.125).astype(dq_ref.dtype)

    @pl.when(step == heads * per - 1)
    def _():
        for other in range(others):
            for place in range(heads):
                dkv_ref[other, place, 0] = jnp.swapaxes(dk[other, place], 0, 1).astype(dkv_ref.dtype)
                dkv_ref[other, place, 1] = jnp.swapaxes(dv[other, place], 0, 1).astype(dkv_ref.dtype)


def self_backward(info, q, kv, ids, grad, context, log_total):
    heads, others = len(q), len(kv)
    depth, rows = q[0].shape
    flat = list(q) + [block for line in kv for block in line] + list(ids) + list(grad)
    flat += [context, log_total]
    area = heads * rows * heads * others * rows // 2
    return pl.pallas_call(
        functools.partial(self_backward_kernel, heads, others),
        grid_spec=pltpu.PrefetchScalarGridSpec(
            num_scalar_prefetch=1,
            grid=(heads * rows // TILE,),
            in_specs=[VMEM] * len(flat),
            out_specs=[VMEM] * 2,
            scratch_shapes=[
                pltpu.VMEM((heads, depth, rows), bf16),
                pltpu.VMEM((heads, depth, rows), bf16),
                pltpu.VMEM((heads, 1, rows), jnp.int32),
                pltpu.VMEM((others, heads, depth, rows), bf16),
                pltpu.VMEM((others, heads, rows, depth), bf16),
                pltpu.VMEM((others, heads, rows, depth), bf16),
                pltpu.VMEM((others, heads, rows, depth), f32),
                pltpu.VMEM((others, heads, rows, depth), f32),
            ],
        ),
        out_shape=[
            jax.ShapeDtypeStruct((heads, depth, rows), bf16),
            jax.ShapeDtypeStruct((others, heads, 2, depth, rows), bf16),
        ],
        compiler_params=pltpu.CompilerParams(vmem_limit_bytes=LIMIT),
        cost_estimate=pl.CostEstimate(
            flops=area * 2560, bytes_accessed=12 * 2**20, transcendentals=area
        ),
        name="self_backward",
    )(info, *flat)


def cross_forward_kernel(q_ref, kv_ref, o_ref, l_ref):
    def head(index, _):
        rows = pl.ds(pl.multiple_of(index * HDIM, HDIM), HDIM)
        scores = dot(jnp.swapaxes(kv_ref[0, rows, :], 0, 1), q_ref[rows, :], 1, 0)
        top = jnp.max(scores, axis=0, keepdims=True)
        probs = jnp.exp(scores - top)
        total = jnp.sum(probs, axis=0, keepdims=True)
        probs = (probs / total).astype(bf16)
        o_ref[rows, :] = dot(kv_ref[1, rows, :], probs, 1, 0).astype(bf16)
        l_ref[index] = top + jnp.log(total)
        return 0

    lax.fori_loop(0, q_ref.shape[0] // HDIM, head, 0)


def cross_forward(q, kv):
    width, rows = q.shape
    return pl.pallas_call(
        cross_forward_kernel,
        in_specs=[VMEM] * 2,
        out_specs=[VMEM] * 2,
        out_shape=[
            jax.ShapeDtypeStruct((width, rows), bf16),
            jax.ShapeDtypeStruct((width // HDIM, 1, rows), f32),
        ],
        compiler_params=pltpu.CompilerParams(vmem_limit_bytes=LIMIT),
        name="cross_forward",
    )(q, kv)


def cross_backward_kernel(q_ref, kv_ref, g_ref, o_ref, l_ref, dq_ref, dkv_ref):
    def head(index, _):
        rows = pl.ds(pl.multiple_of(index * HDIM, HDIM), HDIM)
        q, grad = q_ref[rows, :], g_ref[rows, :]
        inner = jnp.sum(o_ref[rows, :].astype(f32) * grad.astype(f32), axis=0, keepdims=True)
        k_t = kv_ref[0, rows, :]
        scores = dot(jnp.swapaxes(k_t, 0, 1), q, 1, 0)
        probs = jnp.exp(scores - l_ref[index])
        grad_probs = dot(jnp.swapaxes(kv_ref[1, rows, :], 0, 1), grad, 1, 0)
        grad_scores = (probs * (grad_probs - inner)).astype(bf16)
        dq_ref[rows, :] = (dot(k_t, grad_scores, 1, 0) * 0.125).astype(bf16)
        dkv_ref[0, rows, :] = dot(q, grad_scores, 1, 1)
        dkv_ref[1, rows, :] = dot(grad, probs.astype(bf16), 1, 1)
        return 0

    lax.fori_loop(0, q_ref.shape[0] // HDIM, head, 0)


def cross_backward(q, kv, grad, context, log_total):
    width, rows = q.shape
    return pl.pallas_call(
        cross_backward_kernel,
        in_specs=[VMEM] * 5,
        out_specs=[VMEM] * 2,
        out_shape=[jax.ShapeDtypeStruct((width, rows), bf16), jax.ShapeDtypeStruct(kv.shape, f32)],
        compiler_params=pltpu.CompilerParams(vmem_limit_bytes=LIMIT),
        name="cross_backward",
    )(q, kv, grad, context, log_total)


def gelu_parts(value):
    half = 0.5 * (1.0 + lax.erf(value * 0.7071067811865476))
    slope = half + value * jnp.exp(-0.5 * value * value) * 0.3989422804014327
    return value * half, slope


def local(
    hidden,
    encoder,
    cotangent,
    block_ids,
    self_qkv,
    self_out,
    cross_qkv,
    cross_out,
    up_weight,
    down_weight,
    proj_bias,
    up_bias,
    norm_gain,
    norm_shift,
):
    tok_size, group = lax.axis_size("tok"), lax.axis_size("hd")
    tok_index, me = lax.axis_index("tok"), lax.axis_index("hd")
    rows, model = hidden.shape
    shard = self_qkv.shape[0]
    width = self_qkv.shape[2]
    ff_local = up_weight.shape[1]
    piece_rows = rows * group
    span = SEQ // piece_rows
    heads = min(width // HDIM, span)
    others = span // heads
    assert heads * HDIM == width and heads * others == span
    seq_count, enc_rows, _ = encoder.shape
    enc_total = enc_rows * group
    own_seq = tok_index // span
    at = lax.rem(tok_index, span) // others
    beside = lax.rem(tok_index, others)
    info = jnp.stack([at, beside]).astype(jnp.int32)

    def natural(blocks):
        stacked = jnp.stack(blocks)
        return [pick(stacked, me ^ index) for index in range(group)]

    def gather_tok(block):
        return lax.all_gather(block, "tok", axis=0, tiled=True)

    w_self = gather_tok(self_qkv.reshape(shard, 3 * width))
    small = jnp.concatenate(
        [proj_bias.T.reshape(-1), norm_gain.T.reshape(-1), norm_shift.T.reshape(-1), up_bias]
    )
    total_devices = tok_size * group
    small_all = lax.all_to_all(
        jnp.broadcast_to(small[None], (total_devices, small.shape[0])),
        ("tok", "hd"), 0, 0, tiled=True,
    ).astype(f32)
    few = model // total_devices
    vectors = small_all[:, : 13 * few].reshape(total_devices, 13, few)
    vectors = vectors.transpose(1, 0, 2).reshape(13, model)
    bias, gain, shift = vectors[:7], vectors[7:10], vectors[10:13]
    bias_up = lax.dynamic_slice_in_dim(small_all[:, 13 * few :].reshape(-1), me * ff_local, ff_local)

    def own_columns(vector):
        return lax.dynamic_slice_in_dim(vector, me * width, width)

    def xor_columns(vector):
        return jnp.concatenate(
            [lax.dynamic_slice_in_dim(vector, (me ^ j) * width, width) for j in range(group)]
        )

    hidden_blocks = gather_xor(hidden)
    ids = [block_ids.reshape(1, piece_rows)]
    ids += [swap(ids[0], "tok", step * others) for step in range(1, heads)]

    w_mid = gather_tok(jnp.concatenate([self_out.T, cross_out.T, cross_qkv.reshape(shard, 3 * width)], 1))
    w_up = gather_tok(up_weight)
    w_down = gather_tok(down_weight.T)

    hidden_all = jnp.concatenate(hidden_blocks, 0).astype(f32)
    h_one = (normalize(hidden_all)[0] * gain[0] + shift[0]).astype(bf16)
    self_bias = jnp.concatenate(
        [own_columns(bias[0]), jnp.zeros((width,), f32), own_columns(bias[1])]
    )
    scale = jnp.concatenate([jnp.full((width,), 0.125, f32), jnp.ones((2 * width,), f32)])
    qkv = (dot(w_self, h_one, 0, 1) + self_bias[:, None]) * scale[:, None]
    qkv = qkv.astype(bf16).reshape(3, heads, HDIM, group, rows)

    def head_message(first, count, step):
        return jnp.concatenate(
            [
                lax.dynamic_slice(
                    qkv, (first, at ^ step, 0, me ^ j, 0), (count, 1, HDIM, 1, rows)
                ).reshape(count, HDIM, rows)
                for j in range(group)
            ],
            -1,
        )

    kv = [[head_message(1, 2, 0)]]
    q = [head_message(0, 1, 0)[0]]
    for step in range(1, heads):
        kv[0].append(swap(head_message(1, 2, step), "tok", step * others))
    for other in range(1, others):
        kv.append([swap(block, "tok", other) for block in kv[0]])
    for step in range(1, heads):
        q.append(swap(head_message(0, 1, step)[0], "tok", step * others))
    context, log_one = self_forward(info, q, kv, ids)

    def to_tokens(stacked):
        got = [stacked[0]] + [
            swap(stacked[step], "tok", step * others) for step in range(1, heads)
        ]
        got = jnp.stack(got)
        ordered = jnp.concatenate([pick(got, at ^ index) for index in range(heads)], 0)
        parts = [
            lax.dynamic_slice(ordered, (0, (me ^ j) * rows), (width, rows)) for j in range(group)
        ]
        return jnp.concatenate(exchange_xor(parts), 0)

    def to_heads(value):
        got = exchange_xor([value[j * width : (j + 1) * width] for j in range(group)])
        ordered = jnp.concatenate(natural(got), 1).reshape(heads, HDIM, piece_rows)
        return [pick(ordered, at)] + [
            swap(pick(ordered, at ^ step), "tok", step * others) for step in range(1, heads)
        ]

    out_blocks = gather_xor(
        jnp.stack([w_mid[:, :width], w_mid[:, width : 2 * width], w_mid[:, 2 * width : 3 * width]])
    )
    out_all = jnp.concatenate(out_blocks, 2)
    w_self_out, w_cross_out, w_cross_q = out_all[0], out_all[1], out_all[2]
    w_cross_kv = w_mid[:, 3 * width :]
    enc_all = jnp.concatenate(natural(gather_xor(encoder)), 1)
    kv_bias = jnp.concatenate([jnp.zeros((width,), f32), own_columns(bias[4])])
    kv_two = dot(w_cross_kv, pick(enc_all, own_seq), 0, 1) + kv_bias[:, None]
    kv_two = kv_two.astype(bf16).reshape(2, width, enc_total)
    kv_two = jnp.concatenate(gather_xor(kv_two), 1)

    ctx_one = to_tokens(context)
    resid_zero = hidden.astype(f32)
    resid_one = resid_zero + dot(ctx_one, w_self_out, 0, 1) + bias[2]
    unit_two, inverse_two = normalize(resid_one)
    h_two = (unit_two * gain[1] + shift[1]).astype(bf16)
    q_two = dot(w_cross_q, h_two, 0, 1) + xor_columns(bias[3])[:, None]
    q_two = (q_two * 0.125).astype(bf16)
    ctx_two, log_two = cross_forward(q_two, kv_two)
    resid_two = resid_one + dot(ctx_two, w_cross_out, 0, 1) + bias[5]
    unit_three, inverse_three = normalize(resid_two)
    h_three = (unit_three * gain[2] + shift[2]).astype(bf16)

    cot_all = jnp.concatenate(gather_xor(cotangent), 0)
    grad_act = dot(cot_all, w_down, 1, 0)
    h_three_all = jnp.concatenate(gather_xor(h_three), 0)
    inner_pre = dot(h_three_all, w_up, 1, 0) + bias_up
    act, slope = gelu_parts(inner_pre)
    act = act.astype(bf16)
    grad_inner = (slope * grad_act).astype(bf16)

    def block(array, index):
        return array[index * rows : (index + 1) * rows]

    grad_h_three = reduce_xor([dot(block(grad_inner, j), w_up, 1, 1) for j in range(group)])
    cot = cotangent.astype(f32)
    back, gain_three, shift_three = norm_backward(grad_h_three, unit_three, inverse_three, gain[2])
    grad_two = cot + back
    grad_two_low = grad_two.astype(bf16)
    final = reduce_xor([dot(block(act, j), w_down, 1, 1) for j in range(group)])
    output = (resid_two + final + bias[6]).astype(bf16)
    grad_up = dot(h_three_all, grad_inner, 0, 0).astype(bf16)
    grad_down = dot(cot_all, act, 0, 0).astype(bf16)

    def reduce_tok(value):
        return lax.psum_scatter(value, "tok", scatter_dimension=0, tiled=True).astype(f32)

    sent_up = reduce_tok(grad_up)
    sent_down = reduce_tok(grad_down).T

    grad_ctx_two = dot(w_cross_out, grad_two_low, 0, 1).astype(bf16)
    grad_q_two, grad_kv_two = cross_backward(q_two, kv_two, grad_ctx_two, ctx_two, log_two)
    grad_h_two = dot(grad_q_two, w_cross_q, 0, 1)
    back, gain_two, shift_two = norm_backward(grad_h_two, unit_two, inverse_two, gain[1])
    grad_one = grad_two + back
    grad_one_low = grad_one.astype(bf16)
    grad_ctx_one = dot(w_self_out, grad_one_low, 0, 1).astype(bf16)
    grad_heads = to_heads(grad_ctx_one)

    grad_mid = [
        dot(grad_one_low, ctx_one, 0, 1),
        dot(grad_two_low, ctx_two, 0, 1),
        dot(h_two, grad_q_two, 0, 1),
    ]
    grad_mid = reduce_xor(
        [
            jnp.concatenate([g[:, j * width : (j + 1) * width] for g in grad_mid], 1)
            for j in range(group)
        ]
    )
    sent_mid = reduce_tok(grad_mid.astype(bf16))
    kv_total = reduce_xor([grad_kv_two[:, j * width : (j + 1) * width] for j in range(group)])
    seq_pick = jnp.arange(seq_count) == own_seq
    kv_total = jnp.where(seq_pick[:, None, None, None], kv_total[None], 0.0).astype(bf16)
    mask = 1
    while mask < tok_size:
        kv_total = (kv_total.astype(f32) + swap(kv_total, "tok", mask).astype(f32)).astype(bf16)
        mask *= 2
    kv_flat = kv_total.reshape(seq_count, 2 * width, enc_total)
    own_enc = lax.dynamic_slice_in_dim(enc_all, tok_index * shard, shard, 2)
    sent_cross_kv = sum(dot(own_enc[n], kv_flat[n], 0, 1) for n in range(seq_count))

    def encoder_part(index):
        start = (me ^ index) * enc_rows
        return jnp.stack(
            [
                dot(lax.dynamic_slice_in_dim(kv_flat[n], start, enc_rows, 1), w_cross_kv, 0, 1)
                for n in range(seq_count)
            ]
        )

    grad_encoder = reduce_xor([encoder_part(j) for j in range(group)])

    grad_q, grad_kv = self_backward(info, q, kv, ids, grad_heads, context, log_one)
    messages = []
    for step in range(heads):
        total = grad_kv[0, step].astype(f32)
        for other in range(1, others):
            total = total + swap(grad_kv[other, step], "tok", other).astype(f32)
        message = jnp.concatenate([grad_q[step][None], total.astype(bf16)], 0)
        messages.append(swap(message, "tok", step * others) if step else message)
    messages = jnp.stack(messages)
    grad_qkv = jnp.stack([pick(messages, at ^ index) for index in range(heads)], 1)
    grad_qkv = grad_qkv.reshape(3 * width, piece_rows)
    grad_qkv = [
        lax.dynamic_slice(grad_qkv, (0, (me ^ j) * rows), (3 * width, rows)) for j in range(group)
    ]
    grad_h_one = reduce_xor([dot(grad_qkv[j], w_self, 0, 1) for j in range(group)])
    grad_qkv = jnp.concatenate(grad_qkv, 1)
    grad_self = dot(h_one, grad_qkv, 0, 1).astype(bf16)
    sent_self = reduce_tok(grad_self).reshape(shard, 3, width)
    unit_one, inverse_one = normalize(resid_zero)
    back, gain_one, shift_one = norm_backward(grad_h_one, unit_one, inverse_one, gain[0])
    grad_hidden = grad_one + back

    def place(vector):
        return lax.dynamic_update_slice_in_dim(jnp.zeros((model,), f32), vector, me * width, 0)

    def unxor(vector):
        return jnp.concatenate(natural([vector[j * width : (j + 1) * width] for j in range(group)]))

    qkv_sums = jnp.sum(grad_qkv.astype(f32), 1)
    once = (tok_index == 0).astype(f32)
    vectors = jnp.stack(
        [
            place(qkv_sums[:width]),
            place(qkv_sums[2 * width :]),
            jnp.sum(grad_one_low.astype(f32), 0),
            unxor(jnp.sum(grad_q_two.astype(f32), 1)),
            place(jnp.sum(kv_flat[:, width:].astype(f32), (0, 2)) * once),
            jnp.sum(grad_two_low.astype(f32), 0),
            jnp.sum(cot, 0),
            gain_one,
            gain_two,
            gain_three,
            shift_one,
            shift_two,
            shift_three,
        ]
    )
    vectors = vectors.reshape(13, total_devices, few).transpose(1, 0, 2).reshape(total_devices, -1)
    up_sums = lax.dynamic_update_slice_in_dim(
        jnp.zeros((group * ff_local,), f32), jnp.sum(grad_inner.astype(f32), 0), me * ff_local, 0
    )
    vectors = jnp.concatenate([vectors, up_sums.reshape(total_devices, -1)], 1)
    vectors = jnp.sum(lax.all_to_all(vectors, ("tok", "hd"), 0, 0, tiled=True), 0)
    columns = vectors[: 13 * few].reshape(13, few).T

    sent_mid = [sent_mid[:, j * width : (j + 1) * width] for j in range(3)]
    sent_cross = jnp.concatenate(
        [sent_mid[2][:, None], sent_cross_kv.reshape(shard, 2, width)], 1
    )
    return (
        output,
        grad_hidden,
        grad_encoder,
        sent_self,
        sent_mid[0].T,
        sent_cross,
        sent_mid[1].T,
        sent_up,
        sent_down,
        columns[:, :7],
        vectors[13 * few :],
        columns[:, 7:10],
        columns[:, 10:13],
    )


def solution(mesh):
    in_specs = (
        P(("tok", "hd"), None),
        P(None, "hd", None),
        P(("tok", "hd"), None),
        P("tok"),
        P("tok", None, "hd"),
        P("hd", "tok"),
        P("tok", None, "hd"),
        P("hd", "tok"),
        P("tok", "hd"),
        P("hd", "tok"),
        P(("tok", "hd"), None),
        P(("tok", "hd")),
        P(("tok", "hd"), None),
        P(("tok", "hd"), None),
    )
    out_specs = (
        P(("tok", "hd"), None),
        P(("tok", "hd"), None),
        P(None, "hd", None),
        P("tok", None, "hd"),
        P("hd", "tok"),
        P("tok", None, "hd"),
        P("hd", "tok"),
        P("tok", "hd"),
        P("hd", "tok"),
        P(("tok", "hd"), None),
        P(("tok", "hd")),
        P(("tok", "hd"), None),
        P(("tok", "hd"), None),
    )
    return jax.shard_map(local, mesh=mesh, in_specs=in_specs, out_specs=out_specs, check_vma=False)
```

time: 2230 us -> 860 us (0.39)
  waiting for transfers between devices: 1030 us -> 436 us
  matrix products: 462 us -> 88.2 us
  blocking collectives: 278 us -> 0 us
  other arithmetic: 241 us -> 52.1 us
  Pallas kernels: 0 us -> 101 us
  starting transfers between devices: 135 us -> 83.1 us
    dot_general x39 -> x33, matrix products: 462 us -> 88.2 us  [dot(): lax.dot_general(left, right, (((left_dim,), (right_dim,)), ((), ())), pre...]
    unnamed x33 -> x8, waiting for transfers between devices: 359 us -> 0.8 us
    all_gather x7 -> x0, blocking collectives: 241 us -> none  [the longest x1 44.3 us: local(): lax.all_gather(self_out, 'tok', axis=1, tiled=True)]
    all_gather x10 -> x4, waiting for transfers between devices: 209 us -> 56 us  [gather_tok(): return lax.all_gather(block, 'tok', axis=0, tiled=True)]
    convert_element_type x19 -> x11, other arithmetic: 139 us -> 12.4 us  [the longest x2 3.81 us: reduce_xor(): got = swap(have.pop(index).astype(bf16), 'hd', mask)]
    pallas_call x0 -> x4, Pallas kernels: none -> 101 us  [the longest x1 51.4 us: self_backward(): pl.pallas_call(functools.partial(self_backward_kernel, heads, others), gr...]
    reduce_scatter x10 -> x4, waiting for transfers between devices: 228 us -> 134 us  [reduce_tok(): lax.psum_scatter(value, 'tok', scatter_dimension=0, tiled=True).astype(f32)]
    reduce_sum x19 -> x14, other arithmetic: 71.6 us -> 11.2 us  [the longest x4 3.16 us: normalize(): jnp.mean(center * center, axis=-1, keepdims=True) + norm_eps]
  transfers between devices with their start and end apart: 41 -> 79, of which waited for: 26 -> 34; matrix products, arithmetic and copies ran while one was open for 23% -> 21% of each run, Pallas kernels for 0% -> 5%
where the time goes in v1:
time: 860 us; the launch traced here: 855 us
  waiting for transfers between devices  436 us (51%)
  Pallas kernels  101 us (12%)
  matrix products  88.2 us (10%)
  starting transfers between devices  83.1 us (10%)
  local copies, waits for them, and re-layouts  78.2 us (9%)
  other arithmetic  52.1 us (6%)
  between operations  17.3 us (2%)
    ppermute x69, waiting for transfers between devices, swap(): lax.ppermute(value, axis, [(i, i ^ mask) for i in range(lax.axis_size(axi...  230 us
    reduce_scatter x4, waiting for transfers between devices, reduce_tok(): lax.psum_scatter(value, 'tok', scatter_dimension=0, tiled=True).astype(f32)  134 us
    dot_general x33, matrix products, dot(): lax.dot_general(left, right, (((left_dim,), (right_dim,)), ((), ())), pre...  88.2 us
    ppermute x69, starting transfers between devices, swap(): lax.ppermute(value, axis, [(i, i ^ mask) for i in range(lax.axis_size(axi...  76.2 us
    all_gather x4, waiting for transfers between devices, gather_tok(): return lax.all_gather(block, 'tok', axis=0, tiled=True)  56 us
    pallas_call x1, Pallas kernels, self_backward(): pl.pallas_call(functools.partial(self_backward_kernel, heads, others), gr...  51.4 us
    pallas_call x1, Pallas kernels, self_forward(): pl.pallas_call(functools.partial(self_forward_kernel, heads, others), gri...  33.5 us
    unnamed x325, local copies, waits for them, and re-layouts  25.8 us
  transfers between devices with their start and end apart: 79, of which 34 were waited for; matrix products, arithmetic and copies ran while one was open for 21% of the time, Pallas kernels for 5%

profile of v1, /device:TPU:0, one launch (start us, length us, event | category | flops | bytes accessed | tf_op | source)
XLA Modules:
  0.0 855.1 jit_solution(3693476984672812724)
XLA Ops:
  11.8 3.0 collective-permute-start.1
  14.9 12.1 %collective-permute-done.1 = bf16[256,1024]{1,0:T(8,128)(2,1)S(1)} collective-permute-done((bf16[256,1024]{1,0:T(8,128)(2,1)}, bf16[256,1024]{1,0:T(8,128)(2,1)S(1)}, u32[]{:S(2)}, u32[]{:S(2)}) %collective-permute-start.1) | collective-permute-done | bytes 524320 | tf_op jit(solution)/shard_map/ppermute | solution.py:26
  40.4 6.5 all-to-all-done
  52.2 7.3 all-gather.5.cloned.1.call-done
  59.5 6.8 fusion.21
  83.1 21.7 %collective-permute-done.15.refs_15_ = s32[1,1024]{1,0:T(1,128)S(1)} collective-permute-done((s32[1,1024]{1,0:T(1,128)S(1)}, s32[1,1024]{1,0:T(1,128)S(1)}, u32[]{:S(2)}, u32[]{:S(2)}) %collective-permute-start.15) | collective-permute-done | bytes 4128 | tf_op jit(solution)/shard_map/ppermute | solution.py:26
  104.8 3.6 collective-permute-start.4
  112.4 35.9 %all-gather.7.cloned.1.call-done = bf16[1024,1280]{0,1:T(8,128)(2,1)} async-done(((bf16[128,1280]{0,1:T(8,128)(2,1)}), bf16[1024,1280]{0,1:T(8,128)(2,1)}) %all-gather.7.cloned.1.call-update) | async-done | bytes 2621456 | tf_op jit(solution)/shard_map/all_gather | solution.py:397
  152.7 4.2 collective-permute-done.5.refs_3_
  159.0 33.5 %self_forward.1 = (bf16[4,64,1024]{2,1,0:T(8,128)(2,1)S(1)}, f32[4,1,1024]{2,1,0:T(1,128)S(1)}) custom-call(s32[2]{0:T(128)S(1)} %pad_add_fusion.info, bf16[64,1024]{1,0:T(8,128)(2,1)S(1)} %maximum_bitcast_fusion.1.refs_0_, bf16[64,1024]{1,0:T(8,128)(2,1)S(1)} %collective-permute-done.3.refs_1_, bf16[64,1024]{1,0:T(8,128)(2,1)S(1)} %collective-permute-done.4.refs_2_, ...), custom_call_target="tpu_custom_call" | custom-call | flops 17179869184 | bytes 8388608 | tf_op jit(solution)/shard_map/self_forward/pallas_call | solution.py:162
  198.1 6.4 collective-permute-done.18
  204.4 17.4 %collective-permute-done.17 = bf16[64,1024]{1,0:T(8,128)(2,1)S(1)} collective-permute-done((bf16[64,1024]{1,0:T(8,128)(2,1)S(1)}, bf16[64,1024]{1,0:T(8,128)(2,1)S(1)}, u32[]{:S(2)}, u32[]{:S(2)}) %collective-permute-start.17) | collective-permute-done | bytes 131104 | tf_op jit(solution)/shard_map/ppermute | solution.py:26
  225.6 6.0 collective-permute-done.19
  235.2 5.7 collective-permute-done.28
  243.9 4.4 pad_maximum_fusion
  250.4 7.6 cross_forward.1
  263.0 10.6 %collective-permute-done.31 = bf16[256,1024]{1,0:T(8,128)(2,1)} collective-permute-done((bf16[256,1024]{1,0:T(8,128)(2,1)S(1)}, bf16[256,1024]{1,0:T(8,128)(2,1)}, u32[]{:S(2)}, u32[]{:S(2)}) %collective-permute-start.31) | collective-permute-done | bytes 524320 | tf_op jit(solution)/shard_map/ppermute | solution.py:26
  282.5 11.4 %multiply_convert_fusion = (bf16[1024,2048]{1,0:T(8,128)(2,1)}, f32[1024,2048]{1,0:T(8,128)}) fusion(f32[2048]{0:T(1024)} %dynamic_slice.289, bf16[1024,2048]{1,0:T(8,128)(2,1)} %all-gather.9.cloned.1.call-done, bf16[256,1024]{1,0:T(8,128)(2,1)} %collective-permute-done.32, bf16[256,1024]{1,0:T(8,128)(2,1)} %collective-permute-done.31, ...), kind=kOutput, calls=%fused_computation.8 | convolution fusion | flops 4315938816 | bytes 18882560 | tf_op jit(solution)/shard_map/dot_general | solution.py:20
  293.9 12.8 %all-gather.11.cloned.1.call-done = bf16[1024,2048]{0,1:T(8,128)(2,1)} async-done(((bf16[128,2048]{0,1:T(8,128)(2,1)}), bf16[1024,2048]{0,1:T(8,128)(2,1)}) %all-gather.11.cloned.1.call-update) | async-done | bytes 4194320 | tf_op jit(solution)/shard_map/all_gather | solution.py:397
  306.7 11.6 %convert_reduce_fusion = (f32[2048]{0:T(1024)}, bf16[1024,2048]{1,0:T(8,128)(2,1)S(1)}) fusion(bf16[1024,1024]{1,0:T(8,128)(2,1)} %constant_dynamic-update-slice_fusion.3, bf16[1024,2048]{0,1:T(8,128)(2,1)} %all-gather.11.cloned.1.call-done, f32[1024,2048]{1,0:T(8,128)} %get-tuple-element.243, f32[2048]{0:T(1024)S(1)} %copy-done.135), kind=kOutput, calls=%fused_computation.7 | convolution fusion | flops 4322228224 | bytes 18890752 | tf_op jit(solution)/shard_map/dot_general | solution.py:20
  333.8 10.1 %collective-permute-done.41 = bf16[256,1024]{1,0:T(8,128)(2,1)S(1)} collective-permute-done((bf16[256,1024]{1,0:T(8,128)(2,1)S(1)}, bf16[256,1024]{1,0:T(8,128)(2,1)S(1)}, u32[]{:S(2)}, u32[]{:S(2)}) %collective-permute-start.41) | collective-permute-done | bytes 524320 | tf_op jit(solution)/shard_map/ppermute | solution.py:26
  345.1 9.1 %collective-permute-done.35 = bf16[256,1024]{1,0:T(8,128)(2,1)S(1)} collective-permute-done((bf16[256,1024]{1,0:T(8,128)(2,1)S(1)}, bf16[256,1024]{1,0:T(8,128)(2,1)S(1)}, u32[]{:S(2)}, u32[]{:S(2)}) %collective-permute-start.35) | collective-permute-done | bytes 524320 | tf_op jit(solution)/shard_map/ppermute | solution.py:26
  354.2 3.1 convert_reduce_fusion.5
  358.5 8.1 cross_backward.1
  380.0 3.2 collective-permute-done.42
  389.8 3.5 collective-permute-done.44.refs_17_
  393.3 5.0 collective-permute-done.45.refs_18_
  398.5 51.4 %self_backward.1 = (bf16[4,64,1024]{2,1,0:T(8,128)(2,1)S(1)}, bf16[2,4,2,64,1024]{4,3,2,1,0:T(8,128)(2,1)}) custom-call(s32[2]{0:T(128)S(1)} %copy-done.37, bf16[64,1024]{1,0:T(8,128)(2,1)S(1)} %maximum_bitcast_fusion.1.refs_0_, bf16[64,1024]{1,0:T(8,128)(2,1)S(1)} %copy-done.23, bf16[64,1024]{1,0:T(8,128)(2,1)S(1)} %copy-done.25, ...), custom_call_target="tpu_custom_call" | custom-call | flops 42949672960 | bytes 12582912 | tf_op jit(solution)/shard_map/self_backward/pallas_call | solution.py:262
  451.4 13.7 %collective-permute-start.47 = (bf16[2,64,1024]{2,1,0:T(8,128)(2,1)S(1)}, bf16[2,64,1024]{2,1,0:T(8,128)(2,1)S(1)}, u32[]{:S(2)}, u32[]{:S(2)}) collective-permute-start(bf16[2,64,1024]{2,1,0:T(8,128)(2,1)S(1)} %get-tuple-element.131), channel_id=1, source_target_pairs={{0,4},{4,0},{8,12},{12,8},{16,20},{20,16},{24,28},{28,24},{1,5},{5... | collective-permute-start | bytes 786440 | tf_op jit(solution)/shard_map/ppermute | solution.py:26
  467.3 5.0 collective-permute-done.47
  472.3 5.6 collective-permute-done.52
  477.9 5.6 collective-permute-done.50
  483.5 3.4 collective-permute-done.48
  488.9 3.5 collective-permute-start.51
  495.6 5.9 collective-permute-done.53
  501.5 22.0 %collective-permute-done.51 = bf16[3,64,1024]{2,1,0:T(8,128)(2,1)S(1)} collective-permute-done((bf16[3,64,1024]{2,1,0:T(8,128)(2,1)S(1)}, bf16[3,64,1024]{2,1,0:T(8,128)(2,1)S(1)}, u32[]{:S(2)}, u32[]{:S(2)}) %collective-permute-start.51) | collective-permute-done | bytes 393248 | tf_op jit(solution)/shard_map/ppermute | solution.py:26
  525.6 3.5 convolution_convert_fusion.2
  537.2 34.8 %collective-permute-done.68 = bf16[1024,768]{0,1:T(8,128)(2,1)S(1)} collective-permute-done((bf16[1024,768]{0,1:T(8,128)(2,1)S(1)}, bf16[1024,768]{0,1:T(8,128)(2,1)S(1)}, u32[]{:S(2)}, u32[]{:S(2)}) %collective-permute-start.68) | collective-permute-done | bytes 1572896 | tf_op jit(solution)/shard_map/ppermute | solution.py:26
  572.1 3.5 fusion.13
  578.2 9.6 %convolution_convert_fusion = bf16[1024,2048]{1,0:T(8,128)(2,1)} fusion(bf16[1024,1024]{1,0:T(8,128)(2,1)} %constant_dynamic-update-slice_fusion.3, bf16[1024,2048]{1,0:T(8,128)(2,1)} %get-tuple-element.242), kind=kOutput, calls=%fused_computation.19 | convolution fusion | flops 4297064448 | bytes 10485760 | tf_op jit(solution)/shard_map/dot_general | solution.py:20
  588.9 9.3 %convolution_convert_fusion.1 = bf16[1024,2048]{1,0:T(8,128)(2,1)} fusion(bf16[1024,2048]{1,0:T(8,128)(2,1)} %copy-done.143, bf16[256,1024]{1,0:T(8,128)(2,1)} %collective-permute-done.32, bf16[256,1024]{1,0:T(8,128)(2,1)} %collective-permute-done.31, bf16[256,1024]{1,0:T(8,128)(2,1)} %collective-permute-done.30, bf16[256,1024]{1,0:T(8,128)(2,1)S(1)} %copy-done.83), kind=kOutput, calls=%fused_computation.20 | convolution fusion | flops 4305453056 | bytes 10485760 | tf_op jit(solution)/shard_map/dot_general | solution.py:20
  614.3 7.6 collective-permute-done.60
  638.5 7.3 collective-permute-done.62
  670.3 13.6 %collective-permute-done.65 = bf16[1,64,1024]{2,1,0:T(8,128)(2,1)S(1)} collective-permute-done((bf16[1,64,1024]{2,1,0:T(8,128)(2,1)S(1)}, bf16[1,64,1024]{2,1,0:T(8,128)(2,1)S(1)}, u32[]{:S(2)}, u32[]{:S(2)}) %collective-permute-start.65) | collective-permute-done | bytes 131104 | tf_op jit(solution)/shard_map/ppermute | solution.py:26
  688.9 3.6 all-to-all-start.1
  693.9 8.3 all-to-all-done.1
  709.4 44.6 %reduce-scatter.11.cloned.1.call-done = bf16[128,2048]{1,0:T(8,128)(2,1)} async-done(((bf16[1024,2048]{1,0:T(8,128)(2,1)}), bf16[128,2048]{1,0:T(8,128)(2,1)}) %reduce-scatter.11.cloned.1.call-update) | async-done | bytes 524304 | tf_op jit(solution)/shard_map/reduce_scatter | solution.py:524
  756.5 89.4 %reduce-scatter.9.cloned.1.call-done = bf16[128,2048]{1,0:T(8,128)(2,1)} async-done(((bf16[1024,2048]{1,0:T(8,128)(2,1)}), bf16[128,2048]{1,0:T(8,128)(2,1)}) %reduce-scatter.9.cloned.1.call-update) | async-done | bytes 524304 | tf_op jit(solution)/shard_map/reduce_scatter | solution.py:524
  (659 shorter events, 215.6 us)
Async XLA Ops:
  7.2 52.3 %all-gather.5.cloned.1.call-start = ((), (), s32[]{:S(2)}) async-start(), calls=%async_computation.6 | async-start | bytes 1769472 | tf_op jit(solution)/shard_map/all_gather | solution.py:397
  9.0 139.3 %all-gather.7.cloned.1.call-start = ((), (), s32[]{:S(2)}) async-start(), calls=%async_computation.7 | async-start | bytes 2949120 | tf_op jit(solution)/shard_map/all_gather | solution.py:397
  14.9 34.5 %collective-permute-start = (bf16[256,1024]{1,0:T(8,128)(2,1)}, bf16[256,1024]{1,0:T(8,128)(2,1)S(1)}, u32[]{:S(2)}, u32[]{:S(2)}) collective-permute-start(bf16[256,1024]{1,0:T(8,128)(2,1)} %param.14), channel_id=1, source_target_pairs={{0,1},{1,0},{2,3},{3,2},{4,5},{5,4},{6,7},{7,6},{8,9},{9,8},{10,11... | collective-permute-start | bytes 1572872 | tf_op jit(solution)/shard_map/ppermute | solution.py:26
  27.0 22.4 %collective-permute-start.2 = (bf16[256,1024]{1,0:T(8,128)(2,1)S(1)}, bf16[256,1024]{1,0:T(8,128)(2,1)S(1)}, u32[]{:S(2)}, u32[]{:S(2)}) collective-permute-start(bf16[256,1024]{1,0:T(8,128)(2,1)S(1)} %collective-permute-done.1), channel_id=1, source_target_pairs={{0,1},{1,0},{2,3},{3,2},{4,5},{5,4},{6,7},{7,6},{8,9},{9,8},{10,11... | collective-permute-start | bytes 1572872 | tf_op jit(solution)/shard_map/ppermute | solution.py:26
  27.0 53.8 %collective-permute-start.13 = (s32[1,1024]{1,0:T(1,128)}, s32[1,1024]{1,0:T(1,128)S(1)}, u32[]{:S(2)}, u32[]{:S(2)}) collective-permute-start(s32[1,1024]{1,0:T(1,128)} %bitcast.307), channel_id=1, source_target_pairs={{0,8},{4,12},{8,0},{12,4},{16,24},{20,28},{24,16},{28,20},{1,9},{5... | collective-permute-start | bytes 12296 | tf_op jit(solution)/shard_map/ppermute | solution.py:26
  28.8 52.1 %collective-permute-start.14 = (s32[1,1024]{1,0:T(1,128)}, s32[1,1024]{1,0:T(1,128)S(1)}, u32[]{:S(2)}, u32[]{:S(2)}) collective-permute-start(s32[1,1024]{1,0:T(1,128)} %bitcast.308), channel_id=1, source_target_pairs={{0,16},{4,20},{8,24},{12,28},{16,0},{20,4},{24,8},{28,12},{1,17},{... | collective-permute-start | bytes 12296 | tf_op jit(solution)/shard_map/ppermute | solution.py:26
  39.5 243.0 %all-gather.9.cloned.1.call-start = ((), (), s32[]{:S(2)}) async-start(), calls=%async_computation.8 | async-start | bytes 4718592 | tf_op jit(solution)/shard_map/all_gather | solution.py:397
  40.2 266.5 %all-gather.11.cloned.1.call-start = ((), (), s32[]{:S(2)}) async-start(), calls=%async_computation.9 | async-start | bytes 4718592 | tf_op jit(solution)/shard_map/all_gather | solution.py:397
  74.6 34.6 %collective-permute-start.6 = (bf16[2,64,1024]{2,1,0:T(8,128)(2,1)S(1)}, bf16[2,64,1024]{2,1,0:T(8,128)(2,1)S(1)}, u32[]{:S(2)}, u32[]{:S(2)}) collective-permute-start(bf16[2,64,1024]{2,1,0:T(8,128)(2,1)S(1)} %pad_maximum_fusion.26), channel_id=1, source_target_pairs={{0,8},{4,12},{8,0},{12,4},{16,24},{20,28},{24,16},{28,20},{1,9},{5... | collective-permute-start | bytes 786440 | tf_op jit(solution)/shard_map/ppermute | solution.py:26
  74.8 35.6 %collective-permute-start.7 = (bf16[2,64,1024]{2,1,0:T(8,128)(2,1)S(1)}, bf16[2,64,1024]{2,1,0:T(8,128)(2,1)S(1)}, u32[]{:S(2)}, u32[]{:S(2)}) collective-permute-start(bf16[2,64,1024]{2,1,0:T(8,128)(2,1)S(1)} %pad_maximum_fusion.27), channel_id=1, source_target_pairs={{0,16},{4,20},{8,24},{12,28},{16,0},{20,4},{24,8},{28,12},{1,17},{... | collective-permute-start | bytes 786440 | tf_op jit(solution)/shard_map/ppermute | solution.py:26
  76.8 34.5 %collective-permute-start.8 = (bf16[2,64,1024]{2,1,0:T(8,128)(2,1)S(1)}, bf16[2,64,1024]{2,1,0:T(8,128)(2,1)S(1)}, u32[]{:S(2)}, u32[]{:S(2)}) collective-permute-start(bf16[2,64,1024]{2,1,0:T(8,128)(2,1)S(1)} %pad_maximum_fusion.28), channel_id=1, source_target_pairs={{0,24},{4,28},{8,16},{12,20},{16,8},{20,12},{24,0},{28,4},{1,25},{... | collective-permute-start | bytes 786440 | tf_op jit(solution)/shard_map/ppermute | solution.py:26
  80.8 27.5 %collective-permute-start.3 = (bf16[64,1024]{1,0:T(8,128)(2,1)S(1)}, bf16[64,1024]{1,0:T(8,128)(2,1)S(1)}, u32[]{:S(2)}, u32[]{:S(2)}) collective-permute-start(bf16[64,1024]{1,0:T(8,128)(2,1)S(1)} %maximum_bitcast_fusion.2), channel_id=1, source_target_pairs={{0,8},{4,12},{8,0},{12,4},{16,24},{20,28},{24,16},{28,20},{1,9},{5... | collective-permute-start | bytes 393224 | tf_op jit(solution)/shard_map/ppermute | solution.py:26
  81.0 23.8 %collective-permute-start.15 = (s32[1,1024]{1,0:T(1,128)S(1)}, s32[1,1024]{1,0:T(1,128)S(1)}, u32[]{:S(2)}, u32[]{:S(2)}) collective-permute-start(s32[1,1024]{1,0:T(1,128)S(1)} %bitcast.309), channel_id=1, source_target_pairs={{0,24},{4,28},{8,16},{12,20},{16,8},{20,12},{24,0},{28,4},{1,25},{... | collective-permute-start | bytes 12296 | tf_op jit(solution)/shard_map/ppermute | solution.py:26
  104.8 45.1 %collective-permute-start.4 = (bf16[64,1024]{1,0:T(8,128)(2,1)S(1)}, bf16[64,1024]{1,0:T(8,128)(2,1)S(1)}, u32[]{:S(2)}, u32[]{:S(2)}) collective-permute-start(bf16[64,1024]{1,0:T(8,128)(2,1)S(1)} %maximum_bitcast_fusion.3), channel_id=1, source_target_pairs={{0,16},{4,20},{8,24},{12,28},{16,0},{20,4},{24,8},{28,12},{1,17},{... | collective-permute-start | bytes 393224 | tf_op jit(solution)/shard_map/ppermute | solution.py:26
  108.3 49.9 %collective-permute-start.9 = (bf16[2,64,1024]{2,1,0:T(8,128)(2,1)S(1)}, bf16[2,64,1024]{2,1,0:T(8,128)(2,1)S(1)}, u32[]{:S(2)}, u32[]{:S(2)}) collective-permute-start(bf16[2,64,1024]{2,1,0:T(8,128)(2,1)S(1)} %pad_maximum_fusion.25.refs_4_), channel_id=1, source_target_pairs={{0,4},{4,0},{8,12},{12,8},{16,20},{20,16},{24,28},{28,24},{1,5},{5... | collective-permute-start | bytes 786440 | tf_op jit(solution)/shard_map/ppermute | solution.py:26
  109.2 49.6 %collective-permute-start.10 = (bf16[2,64,1024]{2,1,0:T(8,128)(2,1)S(1)}, bf16[2,64,1024]{2,1,0:T(8,128)(2,1)S(1)}, u32[]{:S(2)}, u32[]{:S(2)}) collective-permute-start(bf16[2,64,1024]{2,1,0:T(8,128)(2,1)S(1)} %collective-permute-done.6.refs_5_), channel_id=1, source_target_pairs={{0,4},{4,0},{8,12},{12,8},{16,20},{20,16},{24,28},{28,24},{1,5},{5... | collective-permute-start | bytes 786440 | tf_op jit(solution)/shard_map/ppermute | solution.py:26
  110.4 48.5 %collective-permute-start.11 = (bf16[2,64,1024]{2,1,0:T(8,128)(2,1)S(1)}, bf16[2,64,1024]{2,1,0:T(8,128)(2,1)S(1)}, u32[]{:S(2)}, u32[]{:S(2)}) collective-permute-start(bf16[2,64,1024]{2,1,0:T(8,128)(2,1)S(1)} %collective-permute-done.7.refs_6_), channel_id=1, source_target_pairs={{0,4},{4,0},{8,12},{12,8},{16,20},{20,16},{24,28},{28,24},{1,5},{5... | collective-permute-start | bytes 786440 | tf_op jit(solution)/shard_map/ppermute | solution.py:26
  111.3 47.6 %collective-permute-start.12 = (bf16[2,64,1024]{2,1,0:T(8,128)(2,1)S(1)}, bf16[2,64,1024]{2,1,0:T(8,128)(2,1)S(1)}, u32[]{:S(2)}, u32[]{:S(2)}) collective-permute-start(bf16[2,64,1024]{2,1,0:T(8,128)(2,1)S(1)} %collective-permute-done.8.refs_7_), channel_id=1, source_target_pairs={{0,4},{4,0},{8,12},{12,8},{16,20},{20,16},{24,28},{28,24},{1,5},{5... | collective-permute-start | bytes 786440 | tf_op jit(solution)/shard_map/ppermute | solution.py:26
  156.9 41.1 %collective-permute-start.25 = (bf16[1,64,1024]{2,1,0:T(8,128)(2,1)}, bf16[1,64,1024]{2,1,0:T(8,128)(2,1)}, u32[]{:S(2)}, u32[]{:S(2)}) collective-permute-start(bf16[1,64,1024]{2,1,0:T(8,128)(2,1)} %param.15), channel_id=1, source_target_pairs={{0,2},{1,3},{2,0},{3,1},{4,6},{5,7},{6,4},{7,5},{8,10},{9,11},{10,... | collective-permute-start | bytes 393224 | tf_op jit(solution)/shard_map/ppermute | solution.py:26
  158.3 64.5 %collective-permute-start.22 = (bf16[3,1024,256]{1,2,0:T(8,128)(2,1)}, bf16[3,1024,256]{1,2,0:T(8,128)(2,1)}, u32[]{:S(2)}, u32[]{:S(2)}) collective-permute-start(bf16[3,1024,256]{1,2,0:T(8,128)(2,1)} %pad_maximum_fusion.3), channel_id=1, source_target_pairs={{0,2},{1,3},{2,0},{3,1},{4,6},{5,7},{6,4},{7,5},{8,10},{9,11},{10,... | collective-permute-start | bytes 4718600 | tf_op jit(solution)/shard_map/ppermute | solution.py:26
  195.0 26.9 %collective-permute-start.17 = (bf16[64,1024]{1,0:T(8,128)(2,1)S(1)}, bf16[64,1024]{1,0:T(8,128)(2,1)S(1)}, u32[]{:S(2)}, u32[]{:S(2)}) collective-permute-start(bf16[64,1024]{1,0:T(8,128)(2,1)S(1)} %get-tuple-element.209), channel_id=1, source_target_pairs={{0,16},{4,20},{8,24},{12,28},{16,0},{20,4},{24,8},{28,12},{1,17},{... | collective-permute-start | bytes 393224 | tf_op jit(solution)/shard_map/ppermute | solution.py:26
  195.9 26.0 %collective-permute-start.16 = (bf16[64,1024]{1,0:T(8,128)(2,1)S(1)}, bf16[64,1024]{1,0:T(8,128)(2,1)S(1)}, u32[]{:S(2)}, u32[]{:S(2)}) collective-permute-start(bf16[64,1024]{1,0:T(8,128)(2,1)S(1)} %get-tuple-element.210), channel_id=1, source_target_pairs={{0,8},{4,12},{8,0},{12,4},{16,24},{20,28},{24,16},{28,20},{1,9},{5... | collective-permute-start | bytes 393224 | tf_op jit(solution)/shard_map/ppermute | solution.py:26
  197.9 506.2 %reduce-scatter.7.cloned.1.call-start = ((), (), s32[]{:S(2)}) async-start(), calls=%async_computation.10 | async-start | bytes 1769472 | tf_op jit(solution)/shard_map/reduce_scatter | solution.py:524
  198.0 26.4 %collective-permute-start.24 = (bf16[1,64,1024]{2,1,0:T(8,128)(2,1)}, bf16[1,64,1024]{2,1,0:T(8,128)(2,1)S(1)}, u32[]{:S(2)}, u32[]{:S(2)}) collective-permute-start(bf16[1,64,1024]{2,1,0:T(8,128)(2,1)} %param.15), channel_id=1, source_target_pairs={{0,1},{1,0},{2,3},{3,2},{4,5},{5,4},{6,7},{7,6},{8,9},{9,8},{10,11... | collective-permute-start | bytes 393224 | tf_op jit(solution)/shard_map/ppermute | solution.py:26
  204.4 20.0 %collective-permute-start.26 = (bf16[1,64,1024]{2,1,0:T(8,128)(2,1)}, bf16[1,64,1024]{2,1,0:T(8,128)(2,1)S(1)}, u32[]{:S(2)}, u32[]{:S(2)}) collective-permute-start(bf16[1,64,1024]{2,1,0:T(8,128)(2,1)} %collective-permute-done.25), channel_id=1, source_target_pairs={{0,1},{1,0},{2,3},{3,2},{4,5},{5,4},{6,7},{7,6},{8,9},{9,8},{10,11... | collective-permute-start | bytes 393224 | tf_op jit(solution)/shard_map/ppermute | solution.py:26
  222.8 21.1 %collective-permute-start.21 = (bf16[3,1024,256]{1,2,0:T(8,128)(2,1)}, bf16[3,1024,256]{1,2,0:T(8,128)(2,1)}, u32[]{:S(2)}, u32[]{:S(2)}) collective-permute-start(bf16[3,1024,256]{1,2,0:T(8,128)(2,1)} %pad_maximum_fusion.3), channel_id=1, source_target_pairs={{0,1},{1,0},{2,3},{3,2},{4,5},{5,4},{6,7},{7,6},{8,9},{9,8},{10,11... | collective-permute-start | bytes 4718600 | tf_op jit(solution)/shard_map/ppermute | solution.py:26
  222.8 21.1 %collective-permute-start.23 = (bf16[3,1024,256]{1,2,0:T(8,128)(2,1)}, bf16[3,1024,256]{1,2,0:T(8,128)(2,1)}, u32[]{:S(2)}, u32[]{:S(2)}) collective-permute-start(bf16[3,1024,256]{1,2,0:T(8,128)(2,1)} %collective-permute-done.22), channel_id=1, source_target_pairs={{0,1},{1,0},{2,3},{3,2},{4,5},{5,4},{6,7},{7,6},{8,9},{9,8},{10,11... | collective-permute-start | bytes 4718600 | tf_op jit(solution)/shard_map/ppermute | solution.py:26
  241.4 19.2 %collective-permute-start.37 = (bf16[256,1024]{1,0:T(8,128)(2,1)}, bf16[256,1024]{1,0:T(8,128)(2,1)}, u32[]{:S(2)}, u32[]{:S(2)}) collective-permute-start(bf16[256,1024]{1,0:T(8,128)(2,1)} %param.16), channel_id=1, source_target_pairs={{0,2},{1,3},{2,0},{3,1},{4,6},{5,7},{6,4},{7,5},{8,10},{9,11},{10,... | collective-permute-start | bytes 1572872 | tf_op jit(solution)/shard_map/ppermute | solution.py:26
  260.6 21.1 %collective-permute-start.38 = (bf16[256,1024]{1,0:T(8,128)(2,1)}, bf16[256,1024]{1,0:T(8,128)(2,1)S(1)}, u32[]{:S(2)}, u32[]{:S(2)}) collective-permute-start(bf16[256,1024]{1,0:T(8,128)(2,1)} %collective-permute-done.37), channel_id=1, source_target_pairs={{0,1},{1,0},{2,3},{3,2},{4,5},{5,4},{6,7},{7,6},{8,9},{9,8},{10,11... | collective-permute-start | bytes 1572872 | tf_op jit(solution)/shard_map/ppermute | solution.py:26
  263.0 19.5 %collective-permute-start.30 = (bf16[256,1024]{1,0:T(8,128)(2,1)S(1)}, bf16[256,1024]{1,0:T(8,128)(2,1)}, u32[]{:S(2)}, u32[]{:S(2)}) collective-permute-start(bf16[256,1024]{1,0:T(8,128)(2,1)S(1)} %add_convert_fusion.4), channel_id=1, source_target_pairs={{0,1},{1,0},{2,3},{3,2},{4,5},{5,4},{6,7},{7,6},{8,9},{9,8},{10,11... | collective-permute-start | bytes 1572872 | tf_op jit(solution)/shard_map/ppermute | solution.py:26
  325.9 19.2 %collective-permute-start.33 = (bf16[256,1024]{1,0:T(8,128)(2,1)S(1)}, bf16[256,1024]{1,0:T(8,128)(2,1)S(1)}, u32[]{:S(2)}, u32[]{:S(2)}) collective-permute-start(bf16[256,1024]{1,0:T(8,128)(2,1)S(1)} %convolution_convert_fusion.8), channel_id=1, source_target_pairs={{0,1},{1,0},{2,3},{3,2},{4,5},{5,4},{6,7},{7,6},{8,9},{9,8},{10,11... | collective-permute-start | bytes 1572872 | tf_op jit(solution)/shard_map/ppermute | solution.py:26
  333.2 21.0 %collective-permute-start.35 = (bf16[256,1024]{1,0:T(8,128)(2,1)S(1)}, bf16[256,1024]{1,0:T(8,128)(2,1)S(1)}, u32[]{:S(2)}, u32[]{:S(2)}) collective-permute-start(bf16[256,1024]{1,0:T(8,128)(2,1)S(1)} %add_convert_fusion.3), channel_id=1, source_target_pairs={{0,2},{1,3},{2,0},{3,1},{4,6},{5,7},{6,4},{7,5},{8,10},{9,11},{10,... | collective-permute-start | bytes 1572872 | tf_op jit(solution)/shard_map/ppermute | solution.py:26
  451.4 21.0 %collective-permute-start.47 = (bf16[2,64,1024]{2,1,0:T(8,128)(2,1)S(1)}, bf16[2,64,1024]{2,1,0:T(8,128)(2,1)S(1)}, u32[]{:S(2)}, u32[]{:S(2)}) collective-permute-start(bf16[2,64,1024]{2,1,0:T(8,128)(2,1)S(1)} %get-tuple-element.131), channel_id=1, source_target_pairs={{0,4},{4,0},{8,12},{12,8},{16,20},{20,16},{24,28},{28,24},{1,5},{5... | collective-permute-start | bytes 786440 | tf_op jit(solution)/shard_map/ppermute | solution.py:26
  465.2 18.4 %collective-permute-start.50 = (bf16[2,64,1024]{2,1,0:T(8,128)(2,1)S(1)}, bf16[2,64,1024]{2,1,0:T(8,128)(2,1)S(1)}, u32[]{:S(2)}, u32[]{:S(2)}) collective-permute-start(bf16[2,64,1024]{2,1,0:T(8,128)(2,1)S(1)} %get-tuple-element.133), channel_id=1, source_target_pairs={{0,4},{4,0},{8,12},{12,8},{16,20},{20,16},{24,28},{28,24},{1,5},{5... | collective-permute-start | bytes 786440 | tf_op jit(solution)/shard_map/ppermute | solution.py:26
  467.1 19.8 %collective-permute-start.48 = (bf16[2,64,1024]{2,1,0:T(8,128)(2,1)S(1)}, bf16[2,64,1024]{2,1,0:T(8,128)(2,1)S(1)}, u32[]{:S(2)}, u32[]{:S(2)}) collective-permute-start(bf16[2,64,1024]{2,1,0:T(8,128)(2,1)S(1)} %get-tuple-element.134), channel_id=1, source_target_pairs={{0,4},{4,0},{8,12},{12,8},{16,20},{20,16},{24,28},{28,24},{1,5},{5... | collective-permute-start | bytes 786440 | tf_op jit(solution)/shard_map/ppermute | solution.py:26
  488.9 34.5 %collective-permute-start.51 = (bf16[3,64,1024]{2,1,0:T(8,128)(2,1)S(1)}, bf16[3,64,1024]{2,1,0:T(8,128)(2,1)S(1)}, u32[]{:S(2)}, u32[]{:S(2)}) collective-permute-start(bf16[3,64,1024]{2,1,0:T(8,128)(2,1)S(1)} %pad_maximum_fusion.18), channel_id=1, source_target_pairs={{0,16},{4,20},{8,24},{12,28},{16,0},{20,4},{24,8},{28,12},{1,17},{... | collective-permute-start | bytes 1179656 | tf_op jit(solution)/shard_map/ppermute | solution.py:26
  492.4 31.0 %collective-permute-start.49 = (bf16[3,64,1024]{2,1,0:T(8,128)(2,1)S(1)}, bf16[3,64,1024]{2,1,0:T(8,128)(2,1)S(1)}, u32[]{:S(2)}, u32[]{:S(2)}) collective-permute-start(bf16[3,64,1024]{2,1,0:T(8,128)(2,1)S(1)} %pad_maximum_fusion.17), channel_id=1, source_target_pairs={{0,8},{4,12},{8,0},{12,4},{16,24},{20,28},{24,16},{28,20},{1,9},{5... | collective-permute-start | bytes 1179656 | tf_op jit(solution)/shard_map/ppermute | solution.py:26
  493.8 39.8 %collective-permute-start.67 = (bf16[1024,768]{0,1:T(8,128)(2,1)}, bf16[1024,768]{0,1:T(8,128)(2,1)}, u32[]{:S(2)}, u32[]{:S(2)}) collective-permute-start(bf16[1024,768]{0,1:T(8,128)(2,1)} %pad_maximum_fusion.8), channel_id=1, source_target_pairs={{0,1},{1,0},{2,3},{3,2},{4,5},{5,4},{6,7},{7,6},{8,9},{9,8},{10,11... | collective-permute-start | bytes 4718600 | tf_op jit(solution)/shard_map/ppermute | solution.py:26
  495.0 42.2 %collective-permute-start.66 = (bf16[1024,768]{0,1:T(8,128)(2,1)}, bf16[1024,768]{0,1:T(8,128)(2,1)}, u32[]{:S(2)}, u32[]{:S(2)}) collective-permute-start(bf16[1024,768]{0,1:T(8,128)(2,1)} %pad_maximum_fusion.7), channel_id=1, source_target_pairs={{0,1},{1,0},{2,3},{3,2},{4,5},{5,4},{6,7},{7,6},{8,9},{9,8},{10,11... | collective-permute-start | bytes 4718600 | tf_op jit(solution)/shard_map/ppermute | solution.py:26
  529.1 177.0 %reduce-scatter.13.cloned.1.call-start = ((), (), s32[]{:S(2)}) async-start(), calls=%async_computation.13 | async-start | bytes 1769472 | tf_op jit(solution)/shard_map/reduce_scatter | solution.py:524
  535.7 36.3 %collective-permute-start.68 = (bf16[1024,768]{0,1:T(8,128)(2,1)S(1)}, bf16[1024,768]{0,1:T(8,128)(2,1)S(1)}, u32[]{:S(2)}, u32[]{:S(2)}) collective-permute-start(bf16[1024,768]{0,1:T(8,128)(2,1)S(1)} %fusion.14), channel_id=1, source_target_pairs={{0,2},{1,3},{2,0},{3,1},{4,6},{5,7},{6,4},{7,5},{8,10},{9,11},{10,... | collective-permute-start | bytes 4718600 | tf_op jit(solution)/shard_map/ppermute | solution.py:26
  578.2 175.9 %reduce-scatter.11.cloned.1.call-start = ((), (), s32[]{:S(2)}) async-start(), calls=%async_computation.12 | async-start | bytes 4718592 | tf_op jit(solution)/shard_map/reduce_scatter | solution.py:524
  587.9 258.1 %reduce-scatter.9.cloned.1.call-start = ((), (), s32[]{:S(2)}) async-start(), calls=%async_computation.11 | async-start | bytes 4718592 | tf_op jit(solution)/shard_map/reduce_scatter | solution.py:524
  636.6 28.7 %collective-permute-start.55 = (bf16[256,1024]{1,0:T(8,128)(2,1)}, bf16[256,1024]{1,0:T(8,128)(2,1)}, u32[]{:S(2)}, u32[]{:S(2)}) collective-permute-start(bf16[256,1024]{1,0:T(8,128)(2,1)} %convolution_convert_fusion.3), channel_id=1, source_target_pairs={{0,1},{1,0},{2,3},{3,2},{4,5},{5,4},{6,7},{7,6},{8,9},{9,8},{10,11... | collective-permute-start | bytes 1572872 | tf_op jit(solution)/shard_map/ppermute | solution.py:26
  638.0 47.5 %collective-permute-start.54 = (bf16[256,1024]{1,0:T(8,128)(2,1)}, bf16[256,1024]{1,0:T(8,128)(2,1)}, u32[]{:S(2)}, u32[]{:S(2)}) collective-permute-start(bf16[256,1024]{1,0:T(8,128)(2,1)} %convolution_convert_fusion.4), channel_id=1, source_target_pairs={{0,1},{1,0},{2,3},{3,2},{4,5},{5,4},{6,7},{7,6},{8,9},{9,8},{10,11... | collective-permute-start | bytes 1572872 | tf_op jit(solution)/shard_map/ppermute | solution.py:26
  646.3 22.5 %collective-permute-start.64 = (bf16[1,64,1024]{2,1,0:T(8,128)(2,1)S(1)}, bf16[1,64,1024]{2,1,0:T(8,128)(2,1)S(1)}, u32[]{:S(2)}, u32[]{:S(2)}) collective-permute-start(bf16[1,64,1024]{2,1,0:T(8,128)(2,1)S(1)} %fusion.37), channel_id=1, source_target_pairs={{0,1},{1,0},{2,3},{3,2},{4,5},{5,4},{6,7},{7,6},{8,9},{9,8},{10,11... | collective-permute-start | bytes 393224 | tf_op jit(solution)/shard_map/ppermute | solution.py:26
  646.8 23.5 %collective-permute-start.63 = (bf16[1,64,1024]{2,1,0:T(8,128)(2,1)S(1)}, bf16[1,64,1024]{2,1,0:T(8,128)(2,1)}, u32[]{:S(2)}, u32[]{:S(2)}) collective-permute-start(bf16[1,64,1024]{2,1,0:T(8,128)(2,1)S(1)} %fusion.36), channel_id=1, source_target_pairs={{0,1},{1,0},{2,3},{3,2},{4,5},{5,4},{6,7},{7,6},{8,9},{9,8},{10,11... | collective-permute-start | bytes 393224 | tf_op jit(solution)/shard_map/ppermute | solution.py:26
  667.2 18.4 %collective-permute-start.56 = (bf16[256,1024]{1,0:T(8,128)(2,1)S(1)}, bf16[256,1024]{1,0:T(8,128)(2,1)S(1)}, u32[]{:S(2)}, u32[]{:S(2)}) collective-permute-start(bf16[256,1024]{1,0:T(8,128)(2,1)S(1)} %add_convert_fusion), channel_id=1, source_target_pairs={{0,2},{1,3},{2,0},{3,1},{4,6},{5,7},{6,4},{7,5},{8,10},{9,11},{10,... | collective-permute-start | bytes 1572872 | tf_op jit(solution)/shard_map/ppermute | solution.py:26
  (178 other events, 2693.7 us)
Sparse Core Ops, SparseCore 0:
  10.6 48.8 all-gather.4
  62.1 86.1 all-gather.6
  150.5 80.2 all-gather.8
  232.7 73.9 all-gather.10
  529.2 63.3 reduce-scatter.6
  596.3 64.3 reduce-scatter.12
  664.3 89.7 reduce-scatter.10
  758.1 87.7 reduce-scatter.8

commit v2 on v1

v2 whole, which is shorter than its diff:
```python
import functools

import jax
import jax.numpy as jnp
from jax import lax
from jax.experimental import pallas as pl
from jax.experimental.pallas import tpu as pltpu
from jax.sharding import PartitionSpec as P

HDIM = 64
SEQ = 8192
TILE = 512
norm_eps = 1e-05
neg_large = -1e30
f32 = jnp.float32
bf16 = jnp.bfloat16


def dot(left, right, left_dim, right_dim):
    return lax.dot_general(
        left, right, (((left_dim,), (right_dim,)), ((), ())), preferred_element_type=f32
    )


def swap(value, axis, mask):
    return lax.ppermute(value, axis, [(i, i ^ mask) for i in range(lax.axis_size(axis))])


def hd_masks():
    mask, masks = lax.axis_size("hd") // 2, []
    while mask:
        masks.append(mask)
        mask //= 2
    return masks


def gather_xor(value, first=lambda value: value):
    have = {0: value}
    for mask in hd_masks():
        for index in list(have):
            have[index ^ mask] = first(swap(have[index], "hd", mask))
        first = lambda value: value
    return [have[index] for index in range(len(have))]


def reduce_xor(parts, last=lambda value: value):
    have = dict(enumerate(parts))
    for mask in reversed(hd_masks()):
        for index in sorted(have, reverse=True):
            if index & mask:
                got = swap(have.pop(index).astype(bf16), "hd", mask)
                if len(have) == 1:
                    got = last(got)
                have[index ^ mask] = have[index ^ mask].astype(f32) + got.astype(f32)
    return have[0]


def pick(stacked, index):
    return lax.dynamic_index_in_dim(stacked, index, 0, keepdims=False)


def normalize(value):
    center = value - jnp.mean(value, axis=-1, keepdims=True)
    inverse = lax.rsqrt(jnp.mean(center * center, axis=-1, keepdims=True) + norm_eps)
    return center * inverse, inverse


def norm_backward(grad, unit, inverse, gain):
    scaled = grad * gain
    back = (
        scaled
        - jnp.mean(scaled, axis=-1, keepdims=True)
        - unit * jnp.mean(scaled * unit, axis=-1, keepdims=True)
    ) * inverse
    return back, jnp.sum(grad * unit, axis=0), jnp.sum(grad, axis=0)


def column(row, rows):
    return jnp.swapaxes(jnp.broadcast_to(row, (128, rows)), 0, 1)[:, :1]


VMEM = pl.BlockSpec(memory_space=pltpu.VMEM)
LIMIT = 48 * 2**20


ANY = pl.BlockSpec(memory_space=pl.ANY)


def tie(values, after):
    count = len(values)
    return pl.pallas_call(
        lambda *refs: None,
        in_specs=[ANY] * (count + len(after)),
        out_specs=[ANY] * count,
        out_shape=[jax.ShapeDtypeStruct(value.shape, value.dtype) for value in values],
        input_output_aliases={index: index for index in range(count)},
        name="tie",
    )(*values, *after)


def project_kernel(heads, group, info, *refs):
    refs = list(refs)
    w_ref, norm_ref, bias_ref = refs[:3]
    q_ref, k_ref, v_ref, h_ref = refs[-4:]
    x_refs = refs[3 : 3 + group]
    rows = x_refs[0].shape[0]
    for step, x_ref in enumerate(x_refs):
        start = pl.multiple_of(jnp.bitwise_xor(info[2], step) * rows, rows)
        cols = pl.ds(start, rows)
        x = x_ref[...].astype(f32)
        h = (normalize(x)[0] * norm_ref[0:1, :] + norm_ref[1:2, :]).astype(bf16)
        h_ref[cols, :] = h
        out = (dot(h, w_ref[...], 1, 0) + bias_ref[0:1, :]) * bias_ref[1:2, :]
        out = jnp.swapaxes(out.astype(bf16), 0, 1)
        for head in range(heads):
            for part, ref in enumerate((q_ref, k_ref, v_ref)):
                first = (head * 3 + part) * HDIM
                ref[head, :, cols] = out[first : first + HDIM]


def project(info, x, w, norm, bias, heads, after):
    rows, model = x[0].shape
    group = len(x)
    piece = rows * group
    width = w.shape[1]
    return pl.pallas_call(
        functools.partial(project_kernel, heads, group),
        grid_spec=pltpu.PrefetchScalarGridSpec(
            num_scalar_prefetch=1,
            grid=(1,),
            in_specs=[VMEM] * (group + 3) + [ANY] * len(after),
            out_specs=[VMEM] * 4,
        ),
        out_shape=[jax.ShapeDtypeStruct((heads, HDIM, piece), bf16)] * 3
        + [jax.ShapeDtypeStruct((piece, model), bf16)],
        compiler_params=pltpu.CompilerParams(vmem_limit_bytes=LIMIT),
        cost_estimate=pl.CostEstimate(
            flops=2 * piece * model * width, bytes_accessed=8 * 2**20, transcendentals=piece
        ),
        name="project",
    )(info, w, norm, bias, *x, *after)


def flip(place, others):
    return lax.rem(place, 2) * (others - 1)


def self_forward_kernel(heads, others, info, *refs):
    q_ref, id_ref = refs[:2]
    k_refs, v_refs = refs[2 : 2 + others], refs[2 + others : 2 + 2 * others]
    o_ref, l_ref, k_all, v_all = refs[-4:]
    beside = info[1]
    step = pl.program_id(0)
    piece_rows = q_ref.shape[2]
    per = piece_rows // TILE
    slot, tile = step // per, lax.rem(step, per)

    @pl.when(step == 0)
    def _():
        for other in range(others):
            for place in range(heads):
                k_all[other, place] = jnp.swapaxes(k_refs[other][place], 0, 1)
                v_all[other, place] = v_refs[other][place]

    piece = slot * others + jnp.bitwise_xor(beside, flip(slot, others))
    cols = pl.ds(pl.multiple_of(tile * TILE, TILE), TILE)
    q = q_ref[slot, :, cols]

    def update(state, k, v, mask):
        top, total, acc = state
        scores = dot(k, q, 1, 0)
        if mask is not None:
            scores = jnp.where(mask, scores, neg_large)
        new_top = jnp.maximum(top, jnp.max(scores, axis=0, keepdims=True))
        probs = jnp.exp(scores - new_top)
        fade = jnp.exp(top - new_top)
        total = total * fade + jnp.sum(probs, axis=0, keepdims=True)
        acc = acc * fade + dot(v, probs.astype(bf16), 1, 0)
        return new_top, total, acc

    def earlier_piece(index, state):
        place = index // others
        other = jnp.bitwise_xor(lax.rem(index, others), jnp.bitwise_xor(beside, flip(place, others)))
        return update(state, k_all[other, place], v_all[other, place], None)

    def earlier_tile(index, state):
        rows = pl.ds(pl.multiple_of(index * TILE, TILE), TILE)
        return update(state, k_all[0, slot, rows, :], v_all[0, slot, :, rows], None)

    state = (
        jnp.full((1, TILE), neg_large, f32),
        jnp.zeros((1, TILE), f32),
        jnp.zeros((HDIM, TILE), f32),
    )
    state = lax.fori_loop(0, piece, earlier_piece, state)
    state = lax.fori_loop(0, tile, earlier_tile, state)
    ids = id_ref[slot, :, cols]
    mask = column(ids, TILE) <= ids
    top, total, acc = update(state, k_all[0, slot, cols, :], v_all[0, slot, :, cols], mask)
    out = (acc / total).astype(o_ref.dtype)
    rows = o_ref.shape[2]
    for index in range(TILE // rows):
        place = (tile * (TILE // rows) + index) * heads + slot
        o_ref[place] = out[:, index * rows : (index + 1) * rows]
    l_ref[slot, :, cols] = top + jnp.log(total)


def self_forward(info, q, k, v, ids, rows, after):
    others = len(k)
    heads, depth, piece = q.shape
    area = heads * piece * heads * others * piece // 2
    return pl.pallas_call(
        functools.partial(self_forward_kernel, heads, others),
        grid_spec=pltpu.PrefetchScalarGridSpec(
            num_scalar_prefetch=1,
            grid=(heads * piece // TILE,),
            in_specs=[VMEM] * (2 + 2 * others) + [ANY] * len(after),
            out_specs=[VMEM] * 2,
            scratch_shapes=[
                pltpu.VMEM((others, heads, piece, depth), bf16),
                pltpu.VMEM((others, heads, depth, piece), bf16),
            ],
        ),
        out_shape=[
            jax.ShapeDtypeStruct((piece // rows * heads, depth, rows), bf16),
            jax.ShapeDtypeStruct((heads, 1, piece), f32),
        ],
        compiler_params=pltpu.CompilerParams(vmem_limit_bytes=LIMIT),
        cost_estimate=pl.CostEstimate(
            flops=area * 1024, bytes_accessed=8 * 2**20, transcendentals=area
        ),
        name="self_forward",
    )(info, q, ids, *k, *v, *after)


def self_backward_kernel(heads, sides, own, extra, info, *refs):
    refs = list(refs)
    q_ref, g_ref, o_ref, l_ref = refs[:4]
    k_refs, v_refs = refs[4 : 4 + sides], refs[4 + sides : 4 + 2 * sides]
    refs = refs[4 + 2 * sides :]
    id_ref, before_ref = (refs.pop(0), refs.pop(0)) if own else (None, None)
    dq_ref, dk_ref, dv_ref, g_all, inner_all, k_all, v_all, dk, dv = refs[extra:]
    beside = info[1]
    step = pl.program_id(0)
    piece_rows = q_ref.shape[2]
    per = piece_rows // TILE
    slot, tile = step // per, lax.rem(step, per)

    @pl.when(step == 0)
    def _():
        rows = g_ref.shape[2]
        for place in range(heads):
            for index in range(piece_rows // rows):
                at = slice(index * rows, (index + 1) * rows)
                grad = g_ref[index * heads + place]
                g_all[place, :, at] = grad
                inner_all[place, :, at] = jnp.sum(
                    o_ref[index * heads + place].astype(f32) * grad.astype(f32),
                    axis=0,
                    keepdims=True,
                )
            for side in range(sides):
                k_all[side, place] = jnp.swapaxes(k_refs[side][place], 0, 1)
                v_all[side, place] = jnp.swapaxes(v_refs[side][place], 0, 1)
        dk[...] = jnp.zeros_like(dk)
        dv[...] = jnp.zeros_like(dv)

    cols = pl.ds(pl.multiple_of(tile * TILE, TILE), TILE)
    q = q_ref[slot, :, cols]
    grad = g_all[slot, :, cols]
    q_rows = jnp.swapaxes(q, 0, 1)
    grad_rows = jnp.swapaxes(grad, 0, 1)
    log_total = l_ref[slot, :, cols]
    inner = inner_all[slot, :, cols]

    def update(dq, side, place, rows, mask):
        scores = dot(k_all[side, place, rows, :], q, 1, 0)
        if mask is not None:
            scores = jnp.where(mask, scores, neg_large)
        probs = jnp.exp(scores - log_total)
        grad_probs = dot(v_all[side, place, rows, :], grad, 1, 0)
        grad_scores = (probs * (grad_probs - inner)).astype(bf16)
        dv[side, place, rows, :] += dot(probs.astype(bf16), grad_rows, 1, 0)
        dk[side, place, rows, :] += dot(grad_scores, q_rows, 1, 0)
        return dq + dot(k_refs[side][place, :, rows], grad_scores, 1, 0)

    dq = before_ref[slot, :, cols] if own else jnp.zeros((HDIM, TILE), f32)
    for side in range(sides):

        def earlier(index, dq, side=side):
            rows = pl.ds(pl.multiple_of(lax.rem(index, per) * TILE, TILE), TILE)
            return update(dq, side, index // per, rows, None)

        if own:
            count = slot * per + tile
        else:
            here = jnp.bitwise_xor(beside, flip(slot, sides + 1))
            count = (slot + jnp.where(jnp.bitwise_xor(here, side + 1) < here, 1, 0)) * per
        dq = lax.fori_loop(0, count, earlier, dq)
    if own:
        ids = id_ref[slot, :, cols]
        mask = column(ids, TILE) <= ids
        dq = update(dq, 0, slot, cols, mask) * 0.125
    dq_ref[slot, :, cols] = dq.astype(dq_ref.dtype)

    @pl.when(step == heads * per - 1)
    def _():
        for side in range(sides):
            for place in range(heads):
                dk_ref[side, place] = jnp.swapaxes(dk[side, place], 0, 1).astype(dk_ref.dtype)
                dv_ref[side, place] = jnp.swapaxes(dv[side, place], 0, 1).astype(dv_ref.dtype)


def self_backward(info, q, k, v, ids, grad, context, log_total, before, after):
    own = ids is not None
    sides = len(k)
    heads, depth, piece = q.shape
    flat = [q, grad, context, log_total, *k, *v] + ([ids, before] if own else [])
    area = heads * piece * heads * sides * piece // 2
    return pl.pallas_call(
        functools.partial(self_backward_kernel, heads, sides, own, len(after)),
        grid_spec=pltpu.PrefetchScalarGridSpec(
            num_scalar_prefetch=1,
            grid=(heads * piece // TILE,),
            in_specs=[VMEM] * len(flat) + [ANY] * len(after),
            out_specs=[VMEM] * 3,
            scratch_shapes=[
                pltpu.VMEM((heads, depth, piece), bf16),
                pltpu.VMEM((heads, 1, piece), f32),
                pltpu.VMEM((sides, heads, piece, depth), bf16),
                pltpu.VMEM((sides, heads, piece, depth), bf16),
                pltpu.VMEM((sides, heads, piece, depth), f32),
                pltpu.VMEM((sides, heads, piece, depth), f32),
            ],
        ),
        out_shape=[jax.ShapeDtypeStruct((heads, depth, piece), bf16 if own else f32)]
        + [jax.ShapeDtypeStruct((sides, heads, depth, piece), f32 if own else bf16)] * 2,
        compiler_params=pltpu.CompilerParams(vmem_limit_bytes=LIMIT),
        cost_estimate=pl.CostEstimate(
            flops=area * 64, bytes_accessed=2**16, transcendentals=0
        ),
        name="self_backward",
    )(info, *flat, *after)


def gelu_parts(value):
    half = 0.5 * (1.0 + lax.erf(value * 0.7071067811865476))
    slope = half + value * jnp.exp(-0.5 * value * value) * 0.3989422804014327
    return value * half, slope


def middle_forward_kernel(group, heads, info, *refs):
    x_ref, ctx_ref, norm_ref, bias_ref = refs[:4]
    w_refs, kv_refs = refs[4 : 4 + group], refs[4 + group : 4 + 2 * group]
    x_two, unit_two, inv_two, unit_three, inv_three, h_two, h_three, ctx_xor, q, ctx, log = refs[-11:]
    width = heads * HDIM
    me = info[2]

    def natural(step):
        return pl.ds(pl.multiple_of(jnp.bitwise_xor(me, step) * width, width), width)

    resid = x_ref[...].astype(f32) + norm_ref[4:5, :]
    for step in range(group):
        part = ctx_ref[natural(step), :]
        ctx_xor[step * width : (step + 1) * width, :] = part
        resid = resid + dot(jnp.swapaxes(part, 0, 1), w_refs[step][0], 1, 1)
    unit, inverse = normalize(resid)
    unit_two[...] = unit
    inv_two[...] = inverse
    low = (unit * norm_ref[0:1, :] + norm_ref[1:2, :]).astype(bf16)
    h_two[...] = low
    for step in range(group):
        out = (dot(low, w_refs[step][2], 1, 0) + bias_ref[:, natural(step)]) * 0.125
        q[step * width : (step + 1) * width, :] = jnp.swapaxes(out.astype(bf16), 0, 1)
    resid = resid + norm_ref[5:6, :]
    for step in range(group):
        for head in range(heads):
            own = slice(head * HDIM, (head + 1) * HDIM)
            rows = slice(step * width + head * HDIM, step * width + (head + 1) * HDIM)
            scores = dot(jnp.swapaxes(kv_refs[step][0, own, :], 0, 1), q[rows, :], 1, 0)
            top = jnp.max(scores, axis=0, keepdims=True)
            probs = jnp.exp(scores - top)
            total = jnp.sum(probs, axis=0, keepdims=True)
            out = dot(kv_refs[step][1, own, :], probs.astype(bf16), 1, 0)
            ctx[rows, :] = (out / total).astype(bf16)
            log[step * heads + head] = top + jnp.log(total)
        part = ctx[step * width : (step + 1) * width, :]
        resid = resid + dot(jnp.swapaxes(part, 0, 1), w_refs[step][1], 1, 1)
    x_two[...] = resid
    unit, inverse = normalize(resid)
    unit_three[...] = unit
    inv_three[...] = inverse
    h_three[...] = (unit * norm_ref[2:3, :] + norm_ref[3:4, :]).astype(bf16)


def middle_forward(info, x, ctx, norm, bias, w, kv, heads, after):
    rows, model = x.shape
    group = len(w)
    total = ctx.shape[0]
    return pl.pallas_call(
        functools.partial(middle_forward_kernel, group, heads),
        grid_spec=pltpu.PrefetchScalarGridSpec(
            num_scalar_prefetch=1,
            grid=(1,),
            in_specs=[VMEM] * (4 + 2 * group) + [ANY] * len(after),
            out_specs=[VMEM] * 11,
        ),
        out_shape=[
            jax.ShapeDtypeStruct((rows, model), f32),
            jax.ShapeDtypeStruct((rows, model), f32),
            jax.ShapeDtypeStruct((rows, 1), f32),
            jax.ShapeDtypeStruct((rows, model), f32),
            jax.ShapeDtypeStruct((rows, 1), f32),
            jax.ShapeDtypeStruct((rows, model), bf16),
            jax.ShapeDtypeStruct((rows, model), bf16),
            jax.ShapeDtypeStruct((total, rows), bf16),
            jax.ShapeDtypeStruct((total, rows), bf16),
            jax.ShapeDtypeStruct((total, rows), bf16),
            jax.ShapeDtypeStruct((total // HDIM, 1, rows), f32),
        ],
        compiler_params=pltpu.CompilerParams(vmem_limit_bytes=LIMIT),
        cost_estimate=pl.CostEstimate(
            flops=6 * rows * model * total, bytes_accessed=12 * 2**20, transcendentals=2**20
        ),
        name="middle_forward",
    )(info, x, ctx, norm, bias, *w, *kv, *after)


def middle_backward_kernel(group, heads, extra, info, *refs):
    e_ref, cot_ref, unit_two, inv_two, unit_three, inv_three, norm_ref, q, ctx, log = refs[:10]
    w_refs, kv_refs = refs[10 : 10 + group], refs[10 + group : 10 + 2 * group]
    d_one, low_two, low_one, dq, dkv, d_ctx, sums = refs[10 + 2 * group + extra :]
    width = heads * HDIM
    me = info[2]

    def natural(step):
        return pl.ds(pl.multiple_of(jnp.bitwise_xor(me, step) * width, width), width)

    def add(row, value):
        sums[row : row + 1, :] = jnp.sum(value, axis=0, keepdims=True)

    def norm_back(grad, unit, inverse, gain, row):
        add(row, grad * unit)
        add(row + 1, grad)
        scaled = grad * gain
        return (
            scaled
            - jnp.mean(scaled, axis=-1, keepdims=True)
            - unit * jnp.mean(scaled * unit, axis=-1, keepdims=True)
        ) * inverse

    cot = cot_ref[...].astype(f32)
    d_two = cot + norm_back(e_ref[...], unit_three[...], inv_three[...], norm_ref[2:3, :], 0)
    low = d_two.astype(bf16)
    low_two[...] = low
    add(4, low.astype(f32))
    add(6, cot)
    e_two = jnp.zeros_like(d_two)
    for step in range(group):
        grads = jnp.swapaxes(dot(low, w_refs[step][1], 1, 0).astype(bf16), 0, 1)
        for head in range(heads):
            own = slice(head * HDIM, (head + 1) * HDIM)
            rows = slice(step * width + head * HDIM, step * width + (head + 1) * HDIM)
            grad = grads[own]
            inner = jnp.sum(ctx[rows, :].astype(f32) * grad.astype(f32), axis=0, keepdims=True)
            k_t = kv_refs[step][0, own, :]
            scores = dot(jnp.swapaxes(k_t, 0, 1), q[rows, :], 1, 0)
            probs = jnp.exp(scores - log[step * heads + head])
            grad_probs = dot(jnp.swapaxes(kv_refs[step][1, own, :], 0, 1), grad, 1, 0)
            grad_scores = (probs * (grad_probs - inner)).astype(bf16)
            dq[rows, :] = (dot(k_t, grad_scores, 1, 0) * 0.125).astype(bf16)
            dkv[step, 0, own, :] = dot(q[rows, :], grad_scores, 1, 1)
            dkv[step, 1, own, :] = dot(grad, probs.astype(bf16), 1, 1)
        part = jnp.swapaxes(dq[step * width : (step + 1) * width, :], 0, 1)
        sums[7:8, natural(step)] = jnp.sum(part.astype(f32), axis=0, keepdims=True)
        e_two = e_two + dot(part, w_refs[step][2], 1, 1)
    d_next = d_two + norm_back(e_two, unit_two[...], inv_two[...], norm_ref[0:1, :], 2)
    d_one[...] = d_next
    low = d_next.astype(bf16)
    low_one[...] = low
    add(5, low.astype(f32))
    for step in range(group):
        grads = dot(low, w_refs[step][0], 1, 0).astype(bf16)
        d_ctx[natural(step), :] = jnp.swapaxes(grads, 0, 1)


def middle_backward(info, e, cot, saved, norm, w, kv, heads, after):
    unit_two, inv_two, unit_three, inv_three, q, ctx, log = saved
    rows, model = cot.shape
    group = len(w)
    total = q.shape[0]
    enc = kv[0].shape[2]
    return pl.pallas_call(
        functools.partial(middle_backward_kernel, group, heads, len(after)),
        grid_spec=pltpu.PrefetchScalarGridSpec(
            num_scalar_prefetch=1,
            grid=(1,),
            in_specs=[VMEM] * (10 + 2 * group) + [ANY] * len(after),
            out_specs=[VMEM] * 7,
        ),
        out_shape=[
            jax.ShapeDtypeStruct((rows, model), f32),
            jax.ShapeDtypeStruct((rows, model), bf16),
            jax.ShapeDtypeStruct((rows, model), bf16),
            jax.ShapeDtypeStruct((total, rows), bf16),
            jax.ShapeDtypeStruct((group, 2, heads * HDIM, enc), f32),
            jax.ShapeDtypeStruct((total, rows), bf16),
            jax.ShapeDtypeStruct((8, model), f32),
        ],
        compiler_params=pltpu.CompilerParams(vmem_limit_bytes=LIMIT),
        cost_estimate=pl.CostEstimate(
            flops=6 * rows * model * total, bytes_accessed=16 * 2**20, transcendentals=2**20
        ),
        name="middle_backward",
    )(info, e, cot, unit_two, inv_two, unit_three, inv_three, norm, q, ctx, log, *w, *kv, *after)


CHUNK = 512


def grad_act_kernel(*refs):
    w_ref, out_ref = refs[-2:]
    rows = refs[0].shape[0]
    for index, ref in enumerate(refs[:-2]):
        for start in range(0, w_ref.shape[1], CHUNK):
            cols = slice(start, start + CHUNK)
            out_ref[index * rows : (index + 1) * rows, cols] = dot(
                ref[...], w_ref[:, cols], 1, 0
            ).astype(bf16)


def grad_act(cots, w):
    rows, ff = cots[0].shape[0] * len(cots), w.shape[1]
    return pl.pallas_call(
        grad_act_kernel,
        in_specs=[VMEM] * (len(cots) + 1),
        out_specs=VMEM,
        out_shape=jax.ShapeDtypeStruct((rows, ff), bf16),
        compiler_params=pltpu.CompilerParams(vmem_limit_bytes=LIMIT),
        cost_estimate=pl.CostEstimate(
            flops=2 * rows * ff * w.shape[0], bytes_accessed=10 * 2**20, transcendentals=0
        ),
        name="grad_act",
    )(*cots, w)


def feed_kernel(first, blocks, *refs):
    h_refs, (ga_ref, b_ref, w_ref) = refs[:blocks], refs[blocks : blocks + 3]
    refs = refs[blocks + 3 :]
    act_ref, du_ref, sum_ref, e_refs = refs[0], refs[1], refs[2], refs[3 : 3 + blocks]
    rows, ff = h_refs[0].shape[0], w_ref.shape[1]
    totals = [0.0] * blocks
    for start in range(0, ff, CHUNK):
        cols = slice(start, start + CHUNK)
        sums = 0.0
        for index in range(blocks):
            own = slice(index * rows, (index + 1) * rows)
            inner = dot(h_refs[index][...], w_ref[:, cols], 1, 0) + b_ref[:, cols]
            act, slope = gelu_parts(inner)
            act_ref[own, cols] = act.astype(bf16)
            there = slice((first + index) * rows, (first + index + 1) * rows)
            du = (slope * ga_ref[there, cols].astype(f32)).astype(bf16)
            du_ref[own, cols] = du
            sums = sums + jnp.sum(du.astype(f32), axis=0, keepdims=True)
            totals[index] = totals[index] + dot(du, w_ref[:, cols], 1, 1)
        sum_ref[:, cols] = sums
    for index in range(blocks):
        e_refs[index][...] = totals[index].astype(e_refs[index].dtype)


def feed(h, ga, w, bias, first):
    rows, model = h[0].shape
    ff = w.shape[1]
    blocks = len(h)
    return pl.pallas_call(
        functools.partial(feed_kernel, first, blocks),
        in_specs=[VMEM] * (blocks + 3),
        out_specs=[VMEM] * (3 + blocks),
        out_shape=[jax.ShapeDtypeStruct((blocks * rows, ff), bf16)] * 2
        + [jax.ShapeDtypeStruct((1, ff), f32)]
        + [
            jax.ShapeDtypeStruct((rows, model), bf16 if (first + index) % 2 else f32)
            for index in range(blocks)
        ],
        compiler_params=pltpu.CompilerParams(vmem_limit_bytes=LIMIT),
        cost_estimate=pl.CostEstimate(
            flops=4 * blocks * rows * ff * model, bytes_accessed=12 * 2**20, transcendentals=2**20
        ),
        name="feed",
    )(*h, ga, bias, w)


def outer_kernel(count, side, halves, extra, info, *refs):
    lefts, rights = refs[:count], refs[count : count + 2]
    got_ref = refs[count + 2] if extra else None
    out_ref, picked, turned = refs[-3:]
    rows, model = lefts[0].shape
    shard = out_ref.shape[0] // halves
    which = jnp.bitwise_xor(lax.rem(info[3], 2), side or 0)
    for index in range(count):
        own = slice(index * rows, (index + 1) * rows)
        if side is None:
            picked[:, own] = jnp.swapaxes(lefts[index][...], 0, 1)
            continue
        if shard % 128:
            turned[...] = jnp.swapaxes(lefts[index][...], 0, 1)
        for half in range(halves):
            start = pl.multiple_of((2 * half + which) * shard, shard)
            if shard % 128:
                part = turned[pl.ds(start, shard), :]
            else:
                part = jnp.swapaxes(lefts[index][:, pl.ds(start, shard)], 0, 1)
            picked[half * shard : (half + 1) * shard, own] = part
    middle = rights[0].shape[0]
    for start in range(0, out_ref.shape[1], CHUNK):
        cols = slice(start, start + CHUNK)
        out = dot(picked[:, :middle], rights[0][:, cols], 1, 0)
        out = out + dot(picked[:, middle:], rights[1][:, cols], 1, 0)
        if extra:
            out = out + got_ref[:, cols].astype(f32)
        out_ref[:, cols] = out.astype(bf16)


def outer(lefts, rights, info, side=None, halves=1, got=None):
    rows, model = lefts[0].shape
    count = len(lefts)
    ff = rights[0].shape[1]
    extra = [] if got is None else [got]
    size = model if side is None else model // 2
    return pl.pallas_call(
        functools.partial(outer_kernel, count, side, halves, len(extra)),
        grid_spec=pltpu.PrefetchScalarGridSpec(
            num_scalar_prefetch=1,
            grid=(1,),
            in_specs=[VMEM] * (count + 2 + len(extra)),
            out_specs=VMEM,
            scratch_shapes=[pltpu.VMEM((size, count * rows), bf16), pltpu.VMEM((model, rows), bf16)],
        ),
        out_shape=jax.ShapeDtypeStruct((size, ff), bf16),
        compiler_params=pltpu.CompilerParams(vmem_limit_bytes=LIMIT),
        cost_estimate=pl.CostEstimate(
            flops=2 * count * rows * ff * size, bytes_accessed=10 * 2**20, transcendentals=0
        ),
        name="outer",
    )(info, *lefts, *rights, *extra)


def local(
    hidden,
    encoder,
    cotangent,
    block_ids,
    self_qkv,
    self_out,
    cross_qkv,
    cross_out,
    up_weight,
    down_weight,
    proj_bias,
    up_bias,
    norm_gain,
    norm_shift,
):
    tok_size, group = lax.axis_size("tok"), lax.axis_size("hd")
    tok_index, me = lax.axis_index("tok"), lax.axis_index("hd")
    rows, model = hidden.shape
    shard = self_qkv.shape[0]
    width = self_qkv.shape[2]
    ff_local = up_weight.shape[1]
    piece_rows = rows * group
    span = SEQ // piece_rows
    heads = min(width // HDIM, span)
    others = span // heads
    assert heads * HDIM == width and heads * others == span
    seq_count, enc_rows, _ = encoder.shape
    enc_total = enc_rows * group
    own_seq = tok_index // span
    at = lax.rem(tok_index, span) // others
    beside = jnp.bitwise_xor(lax.rem(tok_index, others), lax.rem(at, 2) * (others - 1))
    info = jnp.stack([at, beside, me, tok_index]).astype(jnp.int32)

    def natural(blocks):
        stacked = jnp.stack(blocks)
        return [pick(stacked, me ^ index) for index in range(group)]

    even = lax.rem(tok_index, 2)
    halves = [[i for i in range(tok_size) if i % 2 == side] for side in range(2)]
    many = tok_size // 2

    def gather_half(block):
        return lax.all_gather(block, "tok", axis=0, tiled=True, axis_index_groups=halves)

    def gather_tok(block):
        return lax.all_gather(block, "tok", axis=0, tiled=True)

    def along_halves(block):
        return lax.all_to_all(
            jnp.broadcast_to(block[None], (many, *block.shape)),
            "tok", 0, 0, tiled=True, axis_index_groups=halves,
        )

    def merge_sides(own, got):
        sides = [jnp.where(even == 0, own, got), jnp.where(even == 0, got, own)]
        return jnp.stack(sides, 1).reshape(model, -1)

    w_self = self_qkv.reshape(shard, 3, heads, HDIM).transpose(0, 2, 1, 3)
    w_self = gather_tok(w_self.reshape(shard, 3 * width))
    w_mid = along_halves(
        jnp.concatenate([self_out.T, cross_out.T, cross_qkv.reshape(shard, 3 * width)], 1)
    )

    own_ids = lax.dynamic_slice_in_dim(block_ids, me * rows, rows).astype(bf16)
    small = jnp.concatenate(
        [
            proj_bias.T.reshape(-1),
            norm_gain.T.reshape(-1),
            norm_shift.T.reshape(-1),
            up_bias,
            own_ids,
        ]
    )
    total_devices = tok_size * group
    small_all = lax.all_to_all(
        jnp.broadcast_to(small[None], (total_devices, small.shape[0])),
        ("tok", "hd"), 0, 0, tiled=True,
    ).astype(f32)
    few = model // total_devices
    vectors = small_all[:, : 13 * few].reshape(total_devices, 13, few)
    vectors = vectors.transpose(1, 0, 2).reshape(13, model)
    bias, gain, shift = vectors[:7], vectors[7:10], vectors[10:13]
    few_up = up_bias.shape[0]
    bias_up = small_all[:, 13 * few : 13 * few + few_up].reshape(-1)
    bias_up = lax.dynamic_slice_in_dim(bias_up, me * ff_local, ff_local)
    ids = small_all[:, 13 * few + few_up :].reshape(tok_size, 1, piece_rows)
    ids = lax.dynamic_slice_in_dim(ids, own_seq * span, span).reshape(heads, others, 1, piece_rows)
    ids = jnp.stack([pick(ids[i], beside ^ (i % 2 * (others - 1))) for i in range(heads)])

    def own_columns(vector):
        return lax.dynamic_slice_in_dim(vector, me * width, width)

    hidden_blocks = gather_xor(hidden)
    self_bias = jnp.stack(
        [own_columns(bias[0]), jnp.zeros((width,), f32), own_columns(bias[1])]
    )
    scale = jnp.broadcast_to(jnp.array([0.125, 1.0, 1.0], f32)[:, None], (3, width))
    factors = jnp.stack([self_bias, scale]).reshape(2, 3, heads, HDIM)
    factors = factors.transpose(0, 2, 1, 3).reshape(2, 3 * width)

    lines = [
        [seq * span + i * others + (side ^ (i % 2 * (others - 1))) for i in range(heads)]
        for seq in range(tok_size // span)
        for side in range(others)
    ]
    wide_lines = [[i * group + h for h in range(group) for i in line] for line in lines]

    def across_lines(value):
        return lax.all_to_all(value, "tok", 0, 0, tiled=True, axis_index_groups=lines)

    def across_wide(value):
        return lax.all_to_all(
            value, ("tok", "hd"), 0, 0, tiled=True, axis_index_groups=wide_lines
        )

    q_out, k_out, v_out, h_one = project(
        info, hidden_blocks, w_self, jnp.stack([gain[0], shift[0]]), factors, heads, [w_mid]
    )
    w_up, w_down = tie([up_weight, down_weight.T], [h_one])
    w_up, w_down = gather_tok(w_up), gather_tok(w_down)
    w_mid = merge_sides(w_mid, swap(w_mid, "tok", 1))
    k = [across_lines(k_out)]
    v = [across_lines(v_out)]
    q = across_lines(q_out)
    k += [swap(k[0], "tok", other) for other in range(1, others)]
    v += [swap(v[0], "tok", other) for other in range(1, others)]
    w_cross_kv = w_mid[:, 3 * width :]
    enc_all = jnp.concatenate(natural(gather_xor(encoder)), 1)
    kv_bias = jnp.concatenate([jnp.zeros((width,), f32), own_columns(bias[4])])
    kv_two = dot(w_cross_kv, pick(enc_all, own_seq), 0, 1) + kv_bias[:, None]
    kv_two = kv_two.astype(bf16).reshape(2, width, enc_total)
    kv_two = gather_xor(kv_two)

    context, log_one = self_forward(info, q, k, v, ids, rows, kv_two)

    mid_block = jnp.stack(
        [w_mid[:, :width], w_mid[:, width : 2 * width], w_mid[:, 2 * width : 3 * width]]
    )
    w_blocks = gather_xor(mid_block, lambda value: tie([value], [log_one])[0])
    ctx_one = across_wide(context).reshape(model, rows)
    norm_rows = jnp.stack([gain[1], shift[1], gain[2], shift[2], bias[2], bias[5]])
    (
        resid_two, unit_two, inv_two, unit_three, inv_three,
        h_two, h_three, ctx_one, q_two, ctx_two, log_two,
    ) = middle_forward(
        info, hidden, ctx_one, norm_rows, bias[3:4], w_blocks, kv_two, heads, []
    )

    cot_blocks = gather_xor(cotangent)
    h_blocks = gather_xor(h_three)
    grad_a = grad_act(cot_blocks, w_down)
    near = group // 2
    bias_row = bias_up[None]
    near_out = feed(h_blocks[:near], grad_a, w_up, bias_row, 0)
    far_out = feed(h_blocks[near:], grad_a, w_up, bias_row, near)
    acts, grad_inners = [near_out[0], far_out[0]], [near_out[1], far_out[1]]
    up_sums = (near_out[2] + far_out[2])[0]
    grad_h_three = reduce_xor(list(near_out[3:]) + list(far_out[3:]))

    def half_columns(array, side):
        return jnp.concatenate(
            [
                lax.dynamic_slice_in_dim(array, (2 * i + side) * shard, shard, 1)
                for i in range(tok_size // 2)
            ],
            1,
        )

    def half_rows(array, side):
        return jnp.concatenate(
            [
                lax.dynamic_slice_in_dim(array, (2 * i + side) * shard, shard, 0)
                for i in range(tok_size // 2)
            ],
            0,
        )

    def reduce_tok(value):
        return lax.psum_scatter(value, "tok", scatter_dimension=0, tiled=True).astype(f32)

    def reduce_half(value):
        return lax.psum_scatter(
            value, "tok", scatter_dimension=0, tiled=True, axis_index_groups=halves
        ).astype(f32)

    grad_up = outer(h_blocks, grad_inners, info)
    down_away = outer(cot_blocks, acts, info, 1, many)
    sent_up = reduce_tok(grad_up)
    down_got = swap(down_away, "tok", 1)

    grad_one, grad_two_low, grad_one_low, grad_q_two, grad_kv_two, grad_ctx_one, sums = (
        middle_backward(
            info, grad_h_three, cotangent,
            (unit_two, inv_two, unit_three, inv_three, q_two, ctx_two, log_two),
            norm_rows, w_blocks, kv_two, heads, [grad_up, down_away],
        )
    )
    grad_heads = across_wide(grad_ctx_one.reshape(group * heads, HDIM, rows))
    grad_mid = [
        dot(grad_one_low, ctx_one, 0, 1),
        dot(grad_two_low, ctx_two, 0, 1),
        dot(h_two, grad_q_two, 0, 1),
    ]
    grad_mid = [
        jnp.concatenate([g[:, j * width : (j + 1) * width] for g in grad_mid], 1).astype(
            bf16 if j % 2 else f32
        )
        for j in range(group)
    ]
    masks = [1 << bit for bit in range(tok_size.bit_length() - 1)]

    def add_low(value, got):
        return (value.astype(f32) + got.astype(f32)).astype(bf16)

    grad_q_away, grad_k_away, grad_v_away = self_backward(
        info, q, k[1:], v[1:], None, grad_heads, context, log_one, None, grad_mid
    )
    grad_q_away, grad_k_away, grad_v_away, down_got = tie(
        [grad_q_away, grad_k_away, grad_v_away, down_got], []
    )
    down_sum = outer(cot_blocks, acts, info, 0, many, down_got)
    sent_down = reduce_half(tie([down_sum], [sent_up])[0]).T
    kv_total = reduce_xor(
        [grad_kv_two[j] for j in range(group)], lambda got: tie([got], [grad_q_away])[0]
    )
    seq_pick = jnp.arange(seq_count) == own_seq
    kv_total = jnp.where(seq_pick[:, None, None, None], kv_total[None], 0.0).astype(bf16)
    grad_mid = reduce_xor(grad_mid, lambda got: tie([got], [grad_q_away])[0])
    mid_got = swap(half_rows(grad_mid, 1 - even).astype(bf16), "tok", 1)
    mid_sum = (half_rows(grad_mid, even) + mid_got.astype(f32)).astype(bf16)
    sent_mid = reduce_half(tie([mid_sum], [sent_down])[0])
    grad_k_got = [swap(grad_k_away[i], "tok", i + 1) for i in range(others - 1)]
    grad_v_got = [swap(grad_v_away[i], "tok", i + 1) for i in range(others - 1)]
    grad_q, grad_k, grad_v = self_backward(
        info, q, k[:1], v[:1], ids, grad_heads, context, log_one, grad_q_away, [down_sum]
    )
    kv_got = swap(kv_total, "tok", masks[0])
    grad_q, grad_k, grad_v, sent_up, kv_got = tie([grad_q, grad_k, grad_v, sent_up, kv_got], [])
    kv_total = add_low(kv_total, kv_got)
    acts = tie(acts, [grad_q])
    def act_block(index):
        start = index % near * rows
        return acts[index // near][start : start + rows]

    final = reduce_xor([dot(act_block(j), w_down, 1, 1) for j in range(group)])
    output = (resid_two + final + bias[6]).astype(bf16)
    grad_k = grad_k[0] + sum(got.astype(f32) for got in grad_k_got)
    grad_v = grad_v[0] + sum(got.astype(f32) for got in grad_v_got)
    grad_qkv = jnp.stack([grad_q, grad_k.astype(bf16), grad_v.astype(bf16)], 1)
    grad_qkv = across_lines(grad_qkv).reshape(3 * width, piece_rows)
    kv_got = swap(kv_total, "tok", masks[1])
    grad_qkv, sent_down, kv_got = tie([grad_qkv, sent_down, kv_got], [])
    kv_total = add_low(kv_total, kv_got)
    for got_mask in masks[2:]:
        kv_total = add_low(kv_total, swap(kv_total, "tok", got_mask))
    kv_flat = kv_total.reshape(seq_count, 2 * width, enc_total)
    own_enc = lax.dynamic_slice_in_dim(enc_all, tok_index * shard, shard, 2)
    sent_cross_kv = sum(dot(own_enc[n], kv_flat[n], 0, 1) for n in range(seq_count))

    def encoder_part(index):
        start = (me ^ index) * enc_rows
        return jnp.stack(
            [
                dot(lax.dynamic_slice_in_dim(kv_flat[n], start, enc_rows, 1), w_cross_kv, 0, 1)
                for n in range(seq_count)
            ]
        )

    grad_encoder = reduce_xor([encoder_part(j) for j in range(group)])

    grad_h_one = reduce_xor(
        [
            dot(
                lax.dynamic_slice(grad_qkv, (0, (me ^ j) * rows), (3 * width, rows)), w_self, 0, 1
            )
            for j in range(group)
        ]
    )
    grad_self = dot(h_one, grad_qkv, 0, 1).astype(bf16)
    sent_self = lax.all_to_all(grad_self, "tok", 0, 0, tiled=True)
    ordered = sent_self
    sent_self = jnp.sum(sent_self.reshape(tok_size, shard, 3 * width).astype(f32), 0)
    sent_self = sent_self.reshape(shard, heads, 3, HDIM)
    sent_self = sent_self.transpose(0, 2, 1, 3).reshape(shard, 3, width)
    unit_one, inverse_one = normalize(hidden.astype(f32))
    back, gain_one, shift_one = norm_backward(grad_h_one, unit_one, inverse_one, gain[0])
    grad_hidden = grad_one + back

    def place(vector):
        return lax.dynamic_update_slice_in_dim(jnp.zeros((model,), f32), vector, me * width, 0)

    qkv_sums = jnp.sum(grad_qkv.astype(f32), 1).reshape(heads, 3, HDIM)
    once = (tok_index == 0).astype(f32)
    vectors = jnp.stack(
        [
            place(qkv_sums[:, 0].reshape(-1)),
            place(qkv_sums[:, 2].reshape(-1)),
            sums[5],
            sums[7],
            place(jnp.sum(kv_flat[:, width:].astype(f32), (0, 2)) * once),
            sums[4],
            sums[6],
            gain_one,
            sums[2],
            sums[0],
            shift_one,
            sums[3],
            sums[1],
        ]
    )
    vectors = vectors.reshape(13, total_devices, few).transpose(1, 0, 2).reshape(total_devices, -1)
    up_all = lax.dynamic_update_slice_in_dim(
        jnp.zeros((group * ff_local,), f32), up_sums, me * ff_local, 0
    )
    vectors = jnp.concatenate([vectors, up_all.reshape(total_devices, -1)], 1)
    vectors = tie([vectors], [ordered])[0]
    vectors = jnp.sum(lax.all_to_all(vectors, ("tok", "hd"), 0, 0, tiled=True), 0)
    columns = vectors[: 13 * few].reshape(13, few).T

    sent_mid = [sent_mid[:, j * width : (j + 1) * width] for j in range(3)]
    sent_cross = jnp.concatenate(
        [sent_mid[2][:, None], sent_cross_kv.reshape(shard, 2, width)], 1
    )
    return (
        output,
        grad_hidden,
        grad_encoder,
        sent_self,
        sent_mid[0].T,
        sent_cross,
        sent_mid[1].T,
        sent_up,
        sent_down,
        columns[:, :7],
        vectors[13 * few :],
        columns[:, 7:10],
        columns[:, 10:13],
    )


def solution(mesh):
    in_specs = (
        P(("tok", "hd"), None),
        P(None, "hd", None),
        P(("tok", "hd"), None),
        P("tok"),
        P("tok", None, "hd"),
        P("hd", "tok"),
        P("tok", None, "hd"),
        P("hd", "tok"),
        P("tok", "hd"),
        P("hd", "tok"),
        P(("tok", "hd"), None),
        P(("tok", "hd")),
        P(("tok", "hd"), None),
        P(("tok", "hd"), None),
    )
    out_specs = (
        P(("tok", "hd"), None),
        P(("tok", "hd"), None),
        P(None, "hd", None),
        P("tok", None, "hd"),
        P("hd", "tok"),
        P("tok", None, "hd"),
        P("hd", "tok"),
        P("tok", "hd"),
        P("hd", "tok"),
        P(("tok", "hd"), None),
        P(("tok", "hd")),
        P(("tok", "hd"), None),
        P(("tok", "hd"), None),
    )
    return jax.shard_map(local, mesh=mesh, in_specs=in_specs, out_specs=out_specs, check_vma=False)
```

time: 860 us -> 694 us (0.81)
  waiting for transfers between devices: 436 us -> 241 us
  Pallas kernels: 101 us -> 184 us
  matrix products: 88.2 us -> 37.9 us
    reduce_scatter x4 -> x1, waiting for transfers between devices: 134 us -> 0.01 us  [reduce_tok(): lax.psum_scatter(value, 'tok', scatter_dimension=0, tiled=True).astype(f32)]
    ppermute x69 -> x46, waiting for transfers between devices: 230 us -> 106 us  [swap(): lax.ppermute(value, axis, [(i, i ^ mask) for i in range(lax.axis_size(axi...]
    all_to_all x0 -> x8, waiting for transfers between devices: none -> 121 us  [the longest x2 51.8 us: across_wide(): lax.all_to_all(value, ('tok', 'hd'), 0, 0, tiled=True, axis_index_groups=...]
    pallas_call x3 -> x22, Pallas kernels: 67.1 us -> 145 us  [the longest x2 60.1 us: self_backward(): pl.pallas_call(functools.partial(self_backward_kernel, heads, sides, own,...]
    all_gather x4 -> x3, waiting for transfers between devices: 56 us -> 0.02 us  [gather_tok(): return lax.all_gather(block, 'tok', axis=0, tiled=True)]
    dot_general x33 -> x18, matrix products: 88.2 us -> 37.9 us  [dot(): lax.dot_general(left, right, (((left_dim,), (right_dim,)), ((), ())), pre...]
    ppermute x69 -> x46, starting transfers between devices: 76.2 us -> 26.6 us  [swap(): lax.ppermute(value, axis, [(i, i ^ mask) for i in range(lax.axis_size(axi...]
    all_to_all x0 -> x8, starting transfers between devices: none -> 32.6 us  [the longest x4 15.4 us: across_lines(): lax.all_to_all(value, 'tok', 0, 0, tiled=True, axis_index_groups=lines)]
  transfers between devices with their start and end apart: 79 -> 62, of which waited for: 34 -> 22; matrix products, arithmetic and copies ran while one was open for 21% -> 18% of each run, Pallas kernels for 5% -> 23%
where the time goes in v2:
time: 694 us; the launch traced here: 683 us
  waiting for transfers between devices  241 us (35%)
  Pallas kernels  184 us (27%)
  starting transfers between devices  80.5 us (12%)
  local copies, waits for them, and re-layouts  76.3 us (11%)
  other arithmetic  47.5 us (7%)
  matrix products  37.9 us (5%)
  between operations  16.1 us (2%)
    ppermute x46, waiting for transfers between devices, swap(): lax.ppermute(value, axis, [(i, i ^ mask) for i in range(lax.axis_size(axi...  106 us
    pallas_call x2, Pallas kernels, self_backward(): pl.pallas_call(functools.partial(self_backward_kernel, heads, sides, own,...  60.1 us
    all_to_all x2, waiting for transfers between devices, across_wide(): lax.all_to_all(value, ('tok', 'hd'), 0, 0, tiled=True, axis_index_groups=...  51.8 us
    all_to_all x4, waiting for transfers between devices, across_lines(): lax.all_to_all(value, 'tok', 0, 0, tiled=True, axis_index_groups=lines)  43.6 us
    unnamed x244, local copies, waits for them, and re-layouts  43 us
    pallas_call x1, Pallas kernels, self_forward(): pl.pallas_call(functools.partial(self_forward_kernel, heads, others), gri...  39.2 us
    dot_general x18, matrix products, dot(): lax.dot_general(left, right, (((left_dim,), (right_dim,)), ((), ())), pre...  37.9 us
    ppermute x46, starting transfers between devices, swap(): lax.ppermute(value, axis, [(i, i ^ mask) for i in range(lax.axis_size(axi...  26.6 us
  transfers between devices with their start and end apart: 62, of which 22 were waited for; matrix products, arithmetic and copies ran while one was open for 18% of the time, Pallas kernels for 23%

profile of v2, /device:TPU:0, one launch (start us, length us, event | category | flops | bytes accessed | tf_op | source)
XLA Modules:
  0.0 682.6 jit_solution(2115737908851693676)
XLA Ops:
  14.7 7.3 %all-to-all-start = ((bf16[32,2,464]{2,1,0:T(2,128)(2,1)}), bf16[32,2,464]{2,1,0:T(2,128)(2,1)S(1)}, u32[]{:S(2)}, u32[]{:S(2)}) async-start(bf16[32,2,464]{2,1,0:T(2,128)(2,1)} %reshape.392), calls=%async_computation | async-start | bytes 131072 | tf_op jit(solution)/shard_map/all_to_all | solution.py:723
  22.4 7.3 %all-to-all-done = bf16[32,2,464]{2,1,0:T(2,128)(2,1)S(1)} async-done(((bf16[32,2,464]{2,1,0:T(2,128)(2,1)}), bf16[32,2,464]{2,1,0:T(2,128)(2,1)S(1)}, u32[]{:S(2)}, u32[]{:S(2)}) %all-to-all-start) | async-done | bytes 59424 | tf_op jit(solution)/shard_map/all_to_all | solution.py:723
  30.9 3.7 all-to-all-start.1
  38.8 10.4 %collective-permute-done.1.refs_5_ = bf16[256,1024]{1,0:T(8,128)(2,1)S(1)} collective-permute-done((bf16[256,1024]{1,0:T(8,128)(2,1)S(1)}, bf16[256,1024]{1,0:T(8,128)(2,1)S(1)}, u32[]{:S(2)}, u32[]{:S(2)}) %collective-permute-start.1) | collective-permute-done | bytes 524320 | tf_op jit(solution)/shard_map/ppermute | solution.py:26
  49.1 3.6 slice_reduce_fusion
  53.6 25.9 %all-to-all-done.1.refs_7_ = bf16[4,128,1280]{2,1,0:T(8,128)(2,1)S(1)} async-done(((bf16[4,128,1280]{2,1,0:T(8,128)(2,1)}), bf16[4,128,1280]{2,1,0:T(8,128)(2,1)S(1)}, u32[]{:S(2)}, u32[]{:S(2)}) %all-to-all-start.1) | async-done | bytes 1310752 | tf_op jit(solution)/shard_map/all_to_all | solution.py:697
  79.6 6.4 project.1
  86.7 3.6 all-to-all-start.3
  90.7 4.8 collective-permute-done.7
  97.0 20.3 %all-to-all-done.3.refs_2_.refs_4_ = bf16[4,64,1024]{2,1,0:T(8,128)(2,1)S(1)} async-done(((bf16[4,64,1024]{2,1,0:T(8,128)(2,1)}), bf16[4,64,1024]{2,1,0:T(8,128)(2,1)S(1)}, u32[]{:S(2)}, u32[]{:S(2)}) %all-to-all-start.3) | async-done | bytes 524320 | tf_op jit(solution)/shard_map/all_to_all | solution.py:757
  117.4 3.6 all-to-all-start.4
  120.9 15.1 %collective-permute-done.5 = bf16[4,128,1280]{2,1,0:T(8,128)(2,1)} collective-permute-done((bf16[4,128,1280]{2,1,0:T(8,128)(2,1)S(1)}, bf16[4,128,1280]{2,1,0:T(8,128)(2,1)}, u32[]{:S(2)}, u32[]{:S(2)}) %collective-permute-start.5) | collective-permute-done | bytes 1310752 | tf_op jit(solution)/shard_map/ppermute | solution.py:26
  140.3 3.5 all-to-all-start.2
  148.0 4.1 collective-permute-done.10.refs_8_.refs_10_.refs_16_
  155.4 11.8 %all-to-all-done.2.refs_0_ = bf16[4,64,1024]{2,1,0:T(8,128)(2,1)S(1)} async-done(((bf16[4,64,1024]{2,1,0:T(8,128)(2,1)}), bf16[4,64,1024]{2,1,0:T(8,128)(2,1)S(1)}, u32[]{:S(2)}, u32[]{:S(2)}) %all-to-all-start.2) | async-done | bytes 524320 | tf_op jit(solution)/shard_map/all_to_all | solution.py:757
  167.2 6.5 collective-permute-done.3.refs_3_.refs_4_
  173.7 10.4 %collective-permute-done.4.refs_5_ = bf16[4,64,1024]{2,1,0:T(8,128)(2,1)} collective-permute-done((bf16[4,64,1024]{2,1,0:T(8,128)(2,1)S(1)}, bf16[4,64,1024]{2,1,0:T(8,128)(2,1)}, u32[]{:S(2)}, u32[]{:S(2)}) %collective-permute-start.4) | collective-permute-done | bytes 524320 | tf_op jit(solution)/shard_map/ppermute | solution.py:26
  184.1 39.2 %self_forward.1 = (bf16[16,64,256]{2,1,0:T(8,128)(2,1)}, f32[4,1,1024]{2,1,0:T(1,128)S(1)}) custom-call(s32[4]{0:T(128)S(1)} %pad_add_fusion.info, bf16[4,64,1024]{2,1,0:T(8,128)(2,1)S(1)} %all-to-all-done.2.refs_0_, f32[4,1,1024]{2,1,0:T(1,128)S(1)} %pad_maximum_fusion.13.refs_1_.refs_6_, bf16[4,64,1024]{2,1,0:T(8,128)(2,1)S(1)} %all-to-all-done.3.refs_2_.refs_4_, ...), custom_call_target="tpu_custom_call" | custom-call | flops 17179869184 | bytes 8388608 | tf_op jit(solution)/shard_map/self_forward/pallas_call | solution.py:212
  224.2 4.3 all-to-all-start.5
  231.5 27.4 %all-to-all-done.5 = bf16[16,64,256]{2,1,0:T(8,128)(2,1)S(1)} async-done(((bf16[16,64,256]{2,1,0:T(8,128)(2,1)}), bf16[16,64,256]{2,1,0:T(8,128)(2,1)S(1)}, u32[]{:S(2)}, u32[]{:S(2)}) %all-to-all-start.5) | async-done | bytes 524320 | tf_op jit(solution)/shard_map/all_to_all | solution.py:760
  261.7 12.1 %middle_forward.1 = (f32[256,1024]{1,0:T(8,128)S(1)}, f32[256,1024]{1,0:T(8,128)}, f32[256,1]{1,0:T(8,128)S(1)}, f32[256,1024]{1,0:T(8,128)}, f32[256,1]{1,0:T(8...) custom-call(s32[4]{0:T(128)S(1)} %pad_add_fusion.info, ...), custom_call_target="tpu_custom_call" | custom-call | flops 1610612736 | bytes 12582912 | tf_op jit(solution)/shard_map/middle_forward/pallas_call | solution.py:400
  280.6 11.4 %collective-permute-done.19.refs_0_.refs_2_ = bf16[256,1024]{1,0:T(8,128)(2,1)} collective-permute-done((bf16[256,1024]{1,0:T(8,128)(2,1)}, bf16[256,1024]{1,0:T(8,128)(2,1)}, u32[]{:S(2)}, u32[]{:S(2)}) %collective-permute-start.19) | collective-permute-done | bytes 524320 | tf_op jit(solution)/shard_map/ppermute | solution.py:26
  292.0 9.2 %grad_act.1.refs_2_ = bf16[1024,2048]{1,0:T(8,128)(2,1)} custom-call(bf16[256,1024]{1,0:T(8,128)(2,1)S(1)} %copy-done.11, bf16[256,1024]{1,0:T(8,128)(2,1)S(1)} %collective-permute-done.16.refs_1_, bf16[256,1024]{1,0:T(8,128)(2,1)S(1)} %collective-permute-done.17.refs_2_, bf16[256,1024]{1,0:T(8,128)(2,1)} %collective-permute-done.18.refs_3_, ...), custom_call_target="tpu_custom_call" | custom-call | flops 4294967296 | bytes 10485760 | tf_op jit(solution)/shard_map/grad_act/pallas_call | solution.py:534
  301.2 11.2 %feed.2 = (bf16[512,2048]{1,0:T(8,128)(2,1)S(1)}, bf16[512,2048]{1,0:T(8,128)(2,1)}, f32[1,2048]{1,0:T(1,128)S(1)}, f32[256,1024]{1,0:T(8,128)S(1)}, bf16[256,1024]{1,0:T(8,128)(2,1)S(1)}) custom-call(bf16[256,1024]{1,0:T(8,128)(2,1)} %get-tuple-element.75.refs_0_, bf16[256,1024]{1,0:T(8,128)(2,1)} %collective-permute-done.15.refs_1_, ...), custom_call_target="tpu_custom_call" | custom-call | flops 4294967296 | bytes 12582912 | tf_op jit(solution)/shard_map/feed/pallas_call | solution.py:575
  315.6 11.1 %feed.3 = (bf16[512,2048]{1,0:T(8,128)(2,1)S(1)}, bf16[512,2048]{1,0:T(8,128)(2,1)}, f32[1,2048]{1,0:T(1,128)S(1)}, f32[256,1024]{1,0:T(8,128)S(1)}, bf16[256,1024]{1,0:T(8,128)(2,1)S(1)}) custom-call(bf16[256,1024]{1,0:T(8,128)(2,1)} %collective-permute-done.19.refs_0_.refs_2_, bf16[256,1024]{1,0:T(8,128)(2,1)} %collective-permute-done.20.refs_1_.refs_3_, ...), custom_call_target="tpu_custom_call" | custom-call | flops 4294967296 | bytes 12582912 | tf_op jit(solution)/shard_map/feed/pallas_call | solution.py:575
  329.9 9.3 %outer.3.refs_18_ = bf16[1024,2048]{1,0:T(8,128)(2,1)} custom-call(s32[4]{0:T(128)S(1)} %pad_add_fusion.info, bf16[256,1024]{1,0:T(8,128)(2,1)} %get-tuple-element.75.refs_0_, bf16[256,1024]{1,0:T(8,128)(2,1)} %collective-permute-done.15.refs_1_, bf16[256,1024]{1,0:T(8,128)(2,1)} %collective-permute-done.19.refs_0_.refs_2_, ...), custom_call_target="tpu_custom_call" | custom-call | flops 4294967296 | bytes 10485760 | tf_op jit(solution)/shard_map/outer/pallas_call | solution.py:630
  344.6 5.7 outer.4.refs_19_
  351.7 5.5 collective-permute-done.23
  358.5 13.5 %middle_backward.1 = (f32[256,1024]{1,0:T(8,128)S(1)}, bf16[256,1024]{1,0:T(8,128)(2,1)S(1)}, bf16[256,1024]{1,0:T(8,128)(2,1)S(1)}, bf16[1024,256]{1,0:T(8,128)...) custom-call(s32[4]{0:T(128)S(1)} %pad_add_fusion.info, ...), custom_call_target="tpu_custom_call" | custom-call | flops 1610612736 | bytes 16777216 | tf_op jit(solution)/shard_map/middle_backward/pallas_call | solution.py:493
  388.3 4.4 all-to-all-start.6
  396.2 3.8 pad_maximum_fusion.refs_6_
  403.6 24.4 %all-to-all-done.6.refs_1_ = bf16[16,64,256]{2,1,0:T(8,128)(2,1)} async-done(((bf16[16,64,256]{2,1,0:T(8,128)(2,1)}), bf16[16,64,256]{2,1,0:T(8,128)(2,1)}, u32[]{:S(2)}, u32[]{:S(2)}) %all-to-all-start.6) | async-done | bytes 524320 | tf_op jit(solution)/shard_map/all_to_all | solution.py:760
  428.0 27.9 %self_backward.2 = (f32[4,64,1024]{2,1,0:T(8,128)S(1)}, bf16[1,4,64,1024]{3,2,1,0:T(8,128)(2,1)S(1)}, bf16[1,4,64,1024]{3,2,1,0:T(8,128)(2,1)S(1)}) custom-call(s32[4]{0:T(128)S(1)} %pad_add_fusion.info, bf16[4,64,1024]{2,1,0:T(8,128)(2,1)S(1)} %all-to-all-done.2.refs_0_, bf16[16,64,256]{2,1,0:T(8,128)(2,1)} %all-to-all-done.6.refs_1_, ...), custom_call_target="tpu_custom_call" | custom-call | flops 536870912 | bytes 65536 | tf_op jit(solution)/shard_map/self_backward/pallas_call | solution.py:320
  461.7 6.0 outer.5.refs_8_
  494.3 32.1 %self_backward.3 = (bf16[4,64,1024]{2,1,0:T(8,128)(2,1)S(1)}, f32[1,4,64,1024]{3,2,1,0:T(8,128)S(1)}, f32[1,4,64,1024]{3,2,1,0:T(8,128)S(1)}) custom-call(s32[4]{0:T(128)S(1)} %pad_add_fusion.info, bf16[4,64,1024]{2,1,0:T(8,128)(2,1)S(1)} %all-to-all-done.2.refs_0_, bf16[16,64,256]{2,1,0:T(8,128)(2,1)} %all-to-all-done.6.refs_1_, ...), custom_call_target="tpu_custom_call" | custom-call | flops 536870912 | bytes 65536 | tf_op jit(solution)/shard_map/self_backward/pallas_call | solution.py:320
  530.2 4.7 convolution_convert_fusion.3
  539.0 4.7 all-to-all-start.7
  543.8 3.6 convolution_convert_fusion.4
  555.5 9.0 %collective-permute-done.31 = bf16[256,1024]{1,0:T(8,128)(2,1)S(1)} collective-permute-done((bf16[256,1024]{1,0:T(8,128)(2,1)S(1)}, bf16[256,1024]{1,0:T(8,128)(2,1)S(1)}, u32[]{:S(2)}, u32[]{:S(2)}) %collective-permute-start.31) | collective-permute-done | bytes 524320 | tf_op jit(solution)/shard_map/ppermute | solution.py:26
  568.1 10.7 %collective-permute-done.34.refs_2_ = bf16[1,2,256,256]{3,2,1,0:T(8,128)(2,1)S(1)} collective-permute-done((bf16[1,2,256,256]{3,2,1,0:T(8,128)(2,1)S(1)}, bf16[1,2,256,256]{3,2,1,0:T(8,128)(2,1)S(1)}, u32[]{:S(2)}, u32[]{:S(2)}) %collective-permute-start.34) | collective-permute-done | bytes 262176 | tf_op jit(solution)/shard_map/ppermute | solution.py:26
  578.8 11.5 %all-to-all-done.7 = bf16[4,3,64,1024]{3,2,1,0:T(8,128)(2,1)} async-done(((bf16[4,3,64,1024]{3,2,1,0:T(8,128)(2,1)}), bf16[4,3,64,1024]{3,2,1,0:T(8,128)(2,1)}, u32[]{:S(2)}, u32[]{:S(2)}) %all-to-all-start.7) | async-done | bytes 1572896 | tf_op jit(solution)/shard_map/all_to_all | solution.py:757
  590.3 4.6 convolution_convert_fusion
  602.1 4.8 all-to-all-start.8
  610.5 6.3 collective-permute-done.38
  631.7 9.8 %collective-permute-done.37 = bf16[256,1024]{1,0:T(8,128)(2,1)} collective-permute-done((bf16[256,1024]{1,0:T(8,128)(2,1)}, bf16[256,1024]{1,0:T(8,128)(2,1)}, u32[]{:S(2)}, u32[]{:S(2)}) %collective-permute-start.37) | collective-permute-done | bytes 524320 | tf_op jit(solution)/shard_map/ppermute | solution.py:26
  641.5 2.9 fusion.15
  652.2 13.4 %all-to-all-start.9 = ((f32[32,1,672]{2,1,0:T(1,128)}), f32[32,1,672]{2,1,0:T(1,128)S(1)}, u32[]{:S(2)}, u32[]{:S(2)}) async-start(f32[32,1,672]{2,1,0:T(1,128)} %copy.137), calls=%async_computation.11 | async-start | bytes 196608 | tf_op jit(solution)/shard_map/all_to_all | solution.py:965
  668.3 5.0 all-to-all-done.9
  (516 shorter events, 168.5 us)
Async XLA Ops:
  7.3 72.3 %all-gather.4.cloned.1.call-start = ((), (), s32[]{:S(2)}) async-start(), calls=%async_computation.13 | async-start | bytes 1769472 | tf_op jit(solution)/shard_map/all_gather | solution.py:694
  14.7 15.0 %all-to-all-start = ((bf16[32,2,464]{2,1,0:T(2,128)(2,1)}), bf16[32,2,464]{2,1,0:T(2,128)(2,1)S(1)}, u32[]{:S(2)}, u32[]{:S(2)}) async-start(bf16[32,2,464]{2,1,0:T(2,128)(2,1)} %reshape.392), calls=%async_computation | async-start | bytes 131072 | tf_op jit(solution)/shard_map/all_to_all | solution.py:723
  30.9 48.7 %all-to-all-start.1 = ((bf16[4,128,1280]{2,1,0:T(8,128)(2,1)}), bf16[4,128,1280]{2,1,0:T(8,128)(2,1)S(1)}, u32[]{:S(2)}, u32[]{:S(2)}) async-start(bf16[4,128,1280]{2,1,0:T(8,128)(2,1)} %broadcast_in_dim.23), calls=%async_computation.1 | async-start | bytes 2621440 | tf_op jit(solution)/shard_map/all_to_all | solution.py:697
  34.6 257.5 %all-gather.6.cloned.1.call-start = ((), (), s32[]{:S(2)}) async-start(), calls=%async_computation.14 | async-start | bytes 4718592 | tf_op jit(solution)/shard_map/all_gather | solution.py:694
  34.6 14.5 %collective-permute-start.1 = (bf16[256,1024]{1,0:T(8,128)(2,1)S(1)}, bf16[256,1024]{1,0:T(8,128)(2,1)S(1)}, u32[]{:S(2)}, u32[]{:S(2)}) collective-permute-start(bf16[256,1024]{1,0:T(8,128)(2,1)S(1)} %copy-done.8), channel_id=1, source_target_pairs={{0,2},{1,3},{2,0},{3,1},{4,6},{5,7},{6,4},{7,5},{8,10},{9,11},{10,... | collective-permute-start | bytes 1572872 | tf_op jit(solution)/shard_map/ppermute | solution.py:26
  35.9 17.7 %collective-permute-start = (bf16[256,1024]{1,0:T(8,128)(2,1)S(1)}, bf16[256,1024]{1,0:T(8,128)(2,1)S(1)}, u32[]{:S(2)}, u32[]{:S(2)}) collective-permute-start(bf16[256,1024]{1,0:T(8,128)(2,1)S(1)} %copy-done.8), channel_id=1, source_target_pairs={{0,1},{1,0},{2,3},{3,2},{4,5},{5,4},{6,7},{7,6},{8,9},{9,8},{10,11... | collective-permute-start | bytes 1572872 | tf_op jit(solution)/shard_map/ppermute | solution.py:26
  86.0 215.3 %all-gather.8.cloned.1.call-start = ((), (), s32[]{:S(2)}) async-start(), calls=%async_computation.15 | async-start | bytes 4718592 | tf_op jit(solution)/shard_map/all_gather | solution.py:694
  86.0 50.0 %collective-permute-start.5 = (bf16[4,128,1280]{2,1,0:T(8,128)(2,1)S(1)}, bf16[4,128,1280]{2,1,0:T(8,128)(2,1)}, u32[]{:S(2)}, u32[]{:S(2)}) collective-permute-start(bf16[4,128,1280]{2,1,0:T(8,128)(2,1)S(1)} %all-to-all-done.1.refs_7_), channel_id=1, source_target_pairs={{0,4},{4,0},{8,12},{12,8},{16,20},{20,16},{24,28},{28,24},{1,5},{5... | collective-permute-start | bytes 3932168 | tf_op jit(solution)/shard_map/ppermute | solution.py:26
  86.7 30.7 %all-to-all-start.3 = ((bf16[4,64,1024]{2,1,0:T(8,128)(2,1)}), bf16[4,64,1024]{2,1,0:T(8,128)(2,1)S(1)}, u32[]{:S(2)}, u32[]{:S(2)}) async-start(bf16[4,64,1024]{2,1,0:T(8,128)(2,1)} %get-tuple-element.70), calls=%async_computation.3 | async-start | bytes 1048576 | tf_op jit(solution)/shard_map/all_to_all | solution.py:757
  117.4 22.1 %all-to-all-start.4 = ((bf16[4,64,1024]{2,1,0:T(8,128)(2,1)}), bf16[4,64,1024]{2,1,0:T(8,128)(2,1)S(1)}, u32[]{:S(2)}, u32[]{:S(2)}) async-start(bf16[4,64,1024]{2,1,0:T(8,128)(2,1)} %get-tuple-element.71), calls=%async_computation.4 | async-start | bytes 1048576 | tf_op jit(solution)/shard_map/all_to_all | solution.py:757
  140.3 26.8 %all-to-all-start.2 = ((bf16[4,64,1024]{2,1,0:T(8,128)(2,1)}), bf16[4,64,1024]{2,1,0:T(8,128)(2,1)S(1)}, u32[]{:S(2)}, u32[]{:S(2)}) async-start(bf16[4,64,1024]{2,1,0:T(8,128)(2,1)} %get-tuple-element.69), calls=%async_computation.2 | async-start | bytes 1048576 | tf_op jit(solution)/shard_map/all_to_all | solution.py:757
  145.8 27.9 %collective-permute-start.3 = (bf16[4,64,1024]{2,1,0:T(8,128)(2,1)S(1)}, bf16[4,64,1024]{2,1,0:T(8,128)(2,1)}, u32[]{:S(2)}, u32[]{:S(2)}) collective-permute-start(bf16[4,64,1024]{2,1,0:T(8,128)(2,1)S(1)} %all-to-all-done.3.refs_2_.refs_4_), channel_id=1, source_target_pairs={{0,4},{4,0},{8,12},{12,8},{16,20},{20,16},{24,28},{28,24},{1,5},{5... | collective-permute-start | bytes 1572872 | tf_op jit(solution)/shard_map/ppermute | solution.py:26
  145.9 38.3 %collective-permute-start.4 = (bf16[4,64,1024]{2,1,0:T(8,128)(2,1)S(1)}, bf16[4,64,1024]{2,1,0:T(8,128)(2,1)}, u32[]{:S(2)}, u32[]{:S(2)}) collective-permute-start(bf16[4,64,1024]{2,1,0:T(8,128)(2,1)S(1)} %copy-done.20), channel_id=1, source_target_pairs={{0,4},{4,0},{8,12},{12,8},{16,20},{20,16},{24,28},{28,24},{1,5},{5... | collective-permute-start | bytes 1572872 | tf_op jit(solution)/shard_map/ppermute | solution.py:26
  152.1 15.1 %collective-permute-start.11 = (bf16[2,256,256]{2,1,0:T(8,128)(2,1)S(1)}, bf16[2,256,256]{2,1,0:T(8,128)(2,1)S(1)}, u32[]{:S(2)}, u32[]{:S(2)}) collective-permute-start(bf16[2,256,256]{2,1,0:T(8,128)(2,1)S(1)} %collective-permute-done.10.refs_8_.refs_10_.refs_16_), channel_id=1, source_target_pairs={{0,1},{1,0},{2,3},{3,2},{4,5},{5,4},{6,7},{7,6},{8,9},{9,8},{10,11... | collective-permute-start | bytes 786440 | tf_op jit(solution)/shard_map/ppermute | solution.py:26
  155.0 76.6 %collective-permute-start.12 = (bf16[3,1024,256]{2,1,0:T(8,128)(2,1)}, bf16[3,1024,256]{2,1,0:T(8,128)(2,1)}, u32[]{:S(2)}, u32[]{:S(2)}) collective-permute-start(bf16[3,1024,256]{2,1,0:T(8,128)(2,1)} %pad_maximum_fusion.3.refs_4_.refs_10_), channel_id=1, source_target_pairs={{0,1},{1,0},{2,3},{3,2},{4,5},{5,4},{6,7},{7,6},{8,9},{9,8},{10,11... | collective-permute-start | bytes 4718600 | tf_op jit(solution)/shard_map/ppermute | solution.py:26
  155.4 68.6 %collective-permute-start.13 = (bf16[3,1024,256]{2,1,0:T(8,128)(2,1)}, bf16[3,1024,256]{2,1,0:T(8,128)(2,1)}, u32[]{:S(2)}, u32[]{:S(2)}) collective-permute-start(bf16[3,1024,256]{2,1,0:T(8,128)(2,1)} %pad_maximum_fusion.3.refs_4_.refs_10_), channel_id=1, source_target_pairs={{0,2},{1,3},{2,0},{3,1},{4,6},{5,7},{6,4},{7,5},{8,10},{9,11},{10,... | collective-permute-start | bytes 4718600 | tf_op jit(solution)/shard_map/ppermute | solution.py:26
  224.1 34.8 %collective-permute-start.14 = (bf16[3,1024,256]{2,1,0:T(8,128)(2,1)}, bf16[3,1024,256]{2,1,0:T(8,128)(2,1)}, u32[]{:S(2)}, u32[]{:S(2)}) collective-permute-start(bf16[3,1024,256]{2,1,0:T(8,128)(2,1)} %tie.11.refs_6_.refs_12_), channel_id=1, source_target_pairs={{0,1},{1,0},{2,3},{3,2},{4,5},{5,4},{6,7},{7,6},{8,9},{9,8},{10,11... | collective-permute-start | bytes 4718600 | tf_op jit(solution)/shard_map/ppermute | solution.py:26
  224.2 34.7 %all-to-all-start.5 = ((bf16[16,64,256]{2,1,0:T(8,128)(2,1)}), bf16[16,64,256]{2,1,0:T(8,128)(2,1)S(1)}, u32[]{:S(2)}, u32[]{:S(2)}) async-start(bf16[16,64,256]{2,1,0:T(8,128)(2,1)} %get-tuple-element.72.refs_2_), calls=%async_computation.5 | async-start | bytes 1048576 | tf_op jit(solution)/shard_map/all_to_all | solution.py:760
  228.5 249.0 %reduce-scatter.6.cloned.1.call-start = ((), (), s32[]{:S(2)}) async-start(), calls=%async_computation.16 | async-start | bytes 4718592 | tf_op jit(solution)/shard_map/reduce_scatter | solution.py:827
  228.9 50.3 %collective-permute-start.17 = (bf16[256,1024]{1,0:T(8,128)(2,1)S(1)}, bf16[256,1024]{1,0:T(8,128)(2,1)S(1)}, u32[]{:S(2)}, u32[]{:S(2)}) collective-permute-start(bf16[256,1024]{1,0:T(8,128)(2,1)S(1)} %copy-done.11), channel_id=1, source_target_pairs={{0,2},{1,3},{2,0},{3,1},{4,6},{5,7},{6,4},{7,5},{8,10},{9,11},{10,... | collective-permute-start | bytes 1572872 | tf_op jit(solution)/shard_map/ppermute | solution.py:26
  278.5 13.5 %collective-permute-start.19 = (bf16[256,1024]{1,0:T(8,128)(2,1)}, bf16[256,1024]{1,0:T(8,128)(2,1)}, u32[]{:S(2)}, u32[]{:S(2)}) collective-permute-start(bf16[256,1024]{1,0:T(8,128)(2,1)} %get-tuple-element.75.refs_0_), channel_id=1, source_target_pairs={{0,2},{1,3},{2,0},{3,1},{4,6},{5,7},{6,4},{7,5},{8,10},{9,11},{10,... | collective-permute-start | bytes 1572872 | tf_op jit(solution)/shard_map/ppermute | solution.py:26
  278.9 13.1 %collective-permute-start.16 = (bf16[256,1024]{1,0:T(8,128)(2,1)S(1)}, bf16[256,1024]{1,0:T(8,128)(2,1)S(1)}, u32[]{:S(2)}, u32[]{:S(2)}) collective-permute-start(bf16[256,1024]{1,0:T(8,128)(2,1)S(1)} %copy-done.11), channel_id=1, source_target_pairs={{0,1},{1,0},{2,3},{3,2},{4,5},{5,4},{6,7},{7,6},{8,9},{9,8},{10,11... | collective-permute-start | bytes 1572872 | tf_op jit(solution)/shard_map/ppermute | solution.py:26
  279.2 12.8 %collective-permute-start.18 = (bf16[256,1024]{1,0:T(8,128)(2,1)S(1)}, bf16[256,1024]{1,0:T(8,128)(2,1)}, u32[]{:S(2)}, u32[]{:S(2)}) collective-permute-start(bf16[256,1024]{1,0:T(8,128)(2,1)S(1)} %collective-permute-done.17.refs_2_), channel_id=1, source_target_pairs={{0,1},{1,0},{2,3},{3,2},{4,5},{5,4},{6,7},{7,6},{8,9},{9,8},{10,11... | collective-permute-start | bytes 1572872 | tf_op jit(solution)/shard_map/ppermute | solution.py:26
  279.4 21.9 %collective-permute-start.15 = (bf16[256,1024]{1,0:T(8,128)(2,1)}, bf16[256,1024]{1,0:T(8,128)(2,1)}, u32[]{:S(2)}, u32[]{:S(2)}) collective-permute-start(bf16[256,1024]{1,0:T(8,128)(2,1)} %get-tuple-element.75.refs_0_), channel_id=1, source_target_pairs={{0,1},{1,0},{2,3},{3,2},{4,5},{5,4},{6,7},{7,6},{8,9},{9,8},{10,11... | collective-permute-start | bytes 1572872 | tf_op jit(solution)/shard_map/ppermute | solution.py:26
  292.0 23.6 %collective-permute-start.20 = (bf16[256,1024]{1,0:T(8,128)(2,1)}, bf16[256,1024]{1,0:T(8,128)(2,1)}, u32[]{:S(2)}, u32[]{:S(2)}) collective-permute-start(bf16[256,1024]{1,0:T(8,128)(2,1)} %collective-permute-done.19.refs_0_.refs_2_), channel_id=1, source_target_pairs={{0,1},{1,0},{2,3},{3,2},{4,5},{5,4},{6,7},{7,6},{8,9},{9,8},{10,11... | collective-permute-start | bytes 1572872 | tf_op jit(solution)/shard_map/ppermute | solution.py:26
  342.9 14.3 %collective-permute-start.23 = (bf16[256,1024]{1,0:T(8,128)(2,1)S(1)}, bf16[256,1024]{1,0:T(8,128)(2,1)S(1)}, u32[]{:S(2)}, u32[]{:S(2)}) collective-permute-start(bf16[256,1024]{1,0:T(8,128)(2,1)S(1)} %add_convert_fusion.3), channel_id=1, source_target_pairs={{0,2},{1,3},{2,0},{3,1},{4,6},{5,7},{6,4},{7,5},{8,10},{9,11},{10,... | collective-permute-start | bytes 1572872 | tf_op jit(solution)/shard_map/ppermute | solution.py:26
  378.0 80.6 %collective-permute-start.24 = (bf16[512,2048]{1,0:T(8,128)(2,1)S(1)}, bf16[512,2048]{1,0:T(8,128)(2,1)}, u32[]{:S(2)}, u32[]{:S(2)}) collective-permute-start(bf16[512,2048]{1,0:T(8,128)(2,1)S(1)} %copy-done.7), channel_id=1, source_target_pairs={{0,4},{4,0},{8,12},{12,8},{16,20},{20,16},{24,28},{28,24},{1,5},{5... | collective-permute-start | bytes 6291464 | tf_op jit(solution)/shard_map/ppermute | solution.py:26
  385.5 84.2 %collective-permute-start.44 = (bf16[1024,768]{1,0:T(8,128)(2,1)}, bf16[1024,768]{1,0:T(8,128)(2,1)}, u32[]{:S(2)}, u32[]{:S(2)}) collective-permute-start(bf16[1024,768]{1,0:T(8,128)(2,1)} %get-tuple-element.205), channel_id=1, source_target_pairs={{0,2},{1,3},{2,0},{3,1},{4,6},{5,7},{6,4},{7,5},{8,10},{9,11},{10,... | collective-permute-start | bytes 4718600 | tf_op jit(solution)/shard_map/ppermute | solution.py:26
  388.2 81.5 %collective-permute-start.42 = (bf16[1024,768]{1,0:T(8,128)(2,1)}, bf16[1024,768]{1,0:T(8,128)(2,1)}, u32[]{:S(2)}, u32[]{:S(2)}) collective-permute-start(bf16[1024,768]{1,0:T(8,128)(2,1)} %pad_maximum_fusion.4.refs_7_), channel_id=1, source_target_pairs={{0,1},{1,0},{2,3},{3,2},{4,5},{5,4},{6,7},{7,6},{8,9},{9,8},{10,11... | collective-permute-start | bytes 4718600 | tf_op jit(solution)/shard_map/ppermute | solution.py:26
  388.3 39.7 %all-to-all-start.6 = ((bf16[16,64,256]{2,1,0:T(8,128)(2,1)}), bf16[16,64,256]{2,1,0:T(8,128)(2,1)}, u32[]{:S(2)}, u32[]{:S(2)}) async-start(bf16[16,64,256]{2,1,0:T(8,128)(2,1)} %bitcast.173), calls=%async_computation.6 | async-start | bytes 1048576 | tf_op jit(solution)/shard_map/all_to_all | solution.py:760
  392.8 172.9 %reduce-scatter.10.cloned.1.call-start = ((), (), s32[]{:S(2)}) async-start(), calls=%async_computation.18 | async-start | bytes 2621440
  396.0 93.7 %collective-permute-start.25 = (bf16[2,256,256]{2,1,0:T(8,128)(2,1)}, bf16[2,256,256]{2,1,0:T(8,128)(2,1)}, u32[]{:S(2)}, u32[]{:S(2)}) collective-permute-start(bf16[2,256,256]{2,1,0:T(8,128)(2,1)} %get-tuple-element.218), channel_id=1, source_target_pairs={{0,1},{1,0},{2,3},{3,2},{4,5},{5,4},{6,7},{7,6},{8,9},{9,8},{10,11... | collective-permute-start | bytes 786440 | tf_op jit(solution)/shard_map/ppermute | solution.py:26
  401.8 87.1 %collective-permute-start.27 = (bf16[2,256,256]{2,1,0:T(8,128)(2,1)}, bf16[2,256,256]{2,1,0:T(8,128)(2,1)S(1)}, u32[]{:S(2)}, u32[]{:S(2)}) collective-permute-start(bf16[2,256,256]{2,1,0:T(8,128)(2,1)} %fusion.46), channel_id=1, source_target_pairs={{0,2},{1,3},{2,0},{3,1},{4,6},{5,7},{6,4},{7,5},{8,10},{9,11},{10,... | collective-permute-start | bytes 786440 | tf_op jit(solution)/shard_map/ppermute | solution.py:26
  476.7 50.0 %collective-permute-start.45 = (bf16[512,768]{1,0:T(8,128)(2,1)}, bf16[512,768]{1,0:T(8,128)(2,1)}, u32[]{:S(2)}, u32[]{:S(2)}) collective-permute-start(bf16[512,768]{1,0:T(8,128)(2,1)} %pad_maximum_fusion.7), channel_id=1, source_target_pairs={{0,4},{4,0},{8,12},{12,8},{16,20},{20,16},{24,28},{28,24},{1,5},{5... | collective-permute-start | bytes 2359304 | tf_op jit(solution)/shard_map/ppermute | solution.py:26
  491.0 38.5 %collective-permute-start.28 = (bf16[1,2,256,256]{3,2,1,0:T(8,128)(2,1)S(1)}, bf16[1,2,256,256]{3,2,1,0:T(8,128)(2,1)S(1)}, u32[]{:S(2)}, u32[]{:S(2)}) collective-permute-start(bf16[1,2,256,256]{3,2,1,0:T(8,128)(2,1)S(1)} %fusion.55), channel_id=1, source_target_pairs={{0,4},{4,0},{8,12},{12,8},{16,20},{20,16},{24,28},{28,24},{1,5},{5... | collective-permute-start | bytes 786440 | tf_op jit(solution)/shard_map/ppermute | solution.py:26
  492.3 42.6 %collective-permute-start.33 = (bf16[4,64,1024]{2,1,0:T(8,128)(2,1)S(1)}, bf16[4,64,1024]{2,1,0:T(8,128)(2,1)}, u32[]{:S(2)}, u32[]{:S(2)}) collective-permute-start(bf16[4,64,1024]{2,1,0:T(8,128)(2,1)S(1)} %bitcast.175), channel_id=1, source_target_pairs={{0,4},{4,0},{8,12},{12,8},{16,20},{20,16},{24,28},{28,24},{1,5},{5... | collective-permute-start | bytes 1572872 | tf_op jit(solution)/shard_map/ppermute | solution.py:26
  493.1 43.2 %collective-permute-start.32 = (bf16[4,64,1024]{2,1,0:T(8,128)(2,1)S(1)}, bf16[4,64,1024]{2,1,0:T(8,128)(2,1)}, u32[]{:S(2)}, u32[]{:S(2)}) collective-permute-start(bf16[4,64,1024]{2,1,0:T(8,128)(2,1)S(1)} %bitcast.174), channel_id=1, source_target_pairs={{0,4},{4,0},{8,12},{12,8},{16,20},{20,16},{24,28},{28,24},{1,5},{5... | collective-permute-start | bytes 1572872 | tf_op jit(solution)/shard_map/ppermute | solution.py:26
  534.9 13.1 %collective-permute-start.30 = (bf16[256,1024]{1,0:T(8,128)(2,1)}, bf16[256,1024]{1,0:T(8,128)(2,1)}, u32[]{:S(2)}, u32[]{:S(2)}) collective-permute-start(bf16[256,1024]{1,0:T(8,128)(2,1)} %convolution_convert_fusion.3), channel_id=1, source_target_pairs={{0,1},{1,0},{2,3},{3,2},{4,5},{5,4},{6,7},{7,6},{8,9},{9,8},{10,11... | collective-permute-start | bytes 1572872 | tf_op jit(solution)/shard_map/ppermute | solution.py:26
  539.0 51.2 %all-to-all-start.7 = ((bf16[4,3,64,1024]{3,2,1,0:T(8,128)(2,1)}), bf16[4,3,64,1024]{3,2,1,0:T(8,128)(2,1)}, u32[]{:S(2)}, u32[]{:S(2)}) async-start(bf16[4,3,64,1024]{3,2,1,0:T(8,128)(2,1)} %copy.124), calls=%async_computation.8 | async-start | bytes 3145728 | tf_op jit(solution)/shard_map/all_to_all | solution.py:757
  543.8 103.5 %reduce-scatter.8.cloned.1.call-start = ((), (), s32[]{:S(2)}) async-start(), calls=%async_computation.17 | async-start | bytes 983040 | tf_op jit(solution)/shard_map/reduce_scatter | solution.py:830
  550.3 14.2 %collective-permute-start.31 = (bf16[256,1024]{1,0:T(8,128)(2,1)S(1)}, bf16[256,1024]{1,0:T(8,128)(2,1)S(1)}, u32[]{:S(2)}, u32[]{:S(2)}) collective-permute-start(bf16[256,1024]{1,0:T(8,128)(2,1)S(1)} %add_convert_fusion.2), channel_id=1, source_target_pairs={{0,2},{1,3},{2,0},{3,1},{4,6},{5,7},{6,4},{7,5},{8,10},{9,11},{10,... | collective-permute-start | bytes 1572872 | tf_op jit(solution)/shard_map/ppermute | solution.py:26
  551.9 26.8 %collective-permute-start.34 = (bf16[1,2,256,256]{3,2,1,0:T(8,128)(2,1)S(1)}, bf16[1,2,256,256]{3,2,1,0:T(8,128)(2,1)S(1)}, u32[]{:S(2)}, u32[]{:S(2)}) collective-permute-start(bf16[1,2,256,256]{3,2,1,0:T(8,128)(2,1)S(1)} %add_convert_fusion.6), channel_id=1, source_target_pairs={{0,8},{4,12},{8,0},{12,4},{16,24},{20,28},{24,16},{28,20},{1,9},{5... | collective-permute-start | bytes 786440 | tf_op jit(solution)/shard_map/ppermute | solution.py:26
  599.0 26.0 %collective-permute-start.36 = (bf16[256,1024]{1,0:T(8,128)(2,1)}, bf16[256,1024]{1,0:T(8,128)(2,1)}, u32[]{:S(2)}, u32[]{:S(2)}) collective-permute-start(bf16[256,1024]{1,0:T(8,128)(2,1)} %convolution_convert_fusion.1), channel_id=1, source_target_pairs={{0,1},{1,0},{2,3},{3,2},{4,5},{5,4},{6,7},{7,6},{8,9},{9,8},{10,11... | collective-permute-start | bytes 1572872 | tf_op jit(solution)/shard_map/ppermute | solution.py:26
  601.5 30.2 %collective-permute-start.35 = (bf16[256,1024]{1,0:T(8,128)(2,1)}, bf16[256,1024]{1,0:T(8,128)(2,1)}, u32[]{:S(2)}, u32[]{:S(2)}) collective-permute-start(bf16[256,1024]{1,0:T(8,128)(2,1)} %convolution_convert_fusion.2), channel_id=1, source_target_pairs={{0,1},{1,0},{2,3},{3,2},{4,5},{5,4},{6,7},{7,6},{8,9},{9,8},{10,11... | collective-permute-start | bytes 1572872 | tf_op jit(solution)/shard_map/ppermute | solution.py:26
  602.1 14.7 %collective-permute-start.38 = (bf16[1,2,256,256]{3,2,1,0:T(8,128)(2,1)S(1)}, bf16[1,2,256,256]{3,2,1,0:T(8,128)(2,1)}, u32[]{:S(2)}, u32[]{:S(2)}) collective-permute-start(bf16[1,2,256,256]{3,2,1,0:T(8,128)(2,1)S(1)} %add_convert_fusion.5), channel_id=1, source_target_pairs={{0,16},{4,20},{8,24},{12,28},{16,0},{20,4},{24,8},{28,12},{1,17},{... | collective-permute-start | bytes 786440 | tf_op jit(solution)/shard_map/ppermute | solution.py:26
  602.1 48.4 %all-to-all-start.8 = ((bf16[8,128,768]{2,1,0:T(8,128)(2,1)}), bf16[8,128,768]{2,1,0:T(8,128)(2,1)}, u32[]{:S(2)}, u32[]{:S(2)}) async-start(bf16[8,128,768]{2,1,0:T(8,128)(2,1)} %bitcast.190), calls=%async_computation.9 | async-start | bytes 3145728 | tf_op jit(solution)/shard_map/all_to_all | solution.py:928
  627.6 13.9 %collective-permute-start.37 = (bf16[256,1024]{1,0:T(8,128)(2,1)}, bf16[256,1024]{1,0:T(8,128)(2,1)}, u32[]{:S(2)}, u32[]{:S(2)}) collective-permute-start(bf16[256,1024]{1,0:T(8,128)(2,1)} %fusion.2), channel_id=1, source_target_pairs={{0,2},{1,3},{2,0},{3,1},{4,6},{5,7},{6,4},{7,5},{8,10},{9,11},{10,... | collective-permute-start | bytes 1572872 | tf_op jit(solution)/shard_map/ppermute | solution.py:26
  652.2 21.2 %all-to-all-start.9 = ((f32[32,1,672]{2,1,0:T(1,128)}), f32[32,1,672]{2,1,0:T(1,128)S(1)}, u32[]{:S(2)}, u32[]{:S(2)}) async-start(f32[32,1,672]{2,1,0:T(1,128)} %copy.137), calls=%async_computation.11 | async-start | bytes 196608 | tf_op jit(solution)/shard_map/all_to_all | solution.py:965
  (129 other events, 1336.8 us)
Sparse Core Ops, SparseCore 0:
  11.3 62.2 all-gather.3
  86.1 98.1 all-gather.5
  187.0 81.6 all-gather.7
  339.3 108.4 reduce-scatter.5
  479.7 42.2 reduce-scatter.9
  568.2 26.9 reduce-scatter.7

commit v3 on v2

--- a/solution.py
+++ b/solution.py
@@ -51,7 +51,8 @@
                 got = swap(have.pop(index).astype(bf16), "hd", mask)
                 if len(have) == 1:
                     got = last(got)
-                have[index ^ mask] = have[index ^ mask].astype(f32) + got.astype(f32)
+                total = have[index ^ mask].astype(f32) + got.astype(f32)
+                have[index ^ mask] = total if len(have) == 1 else total.astype(bf16)
     return have[0]
 
 
@@ -397,27 +398,31 @@
     rows, model = x.shape
     group = len(w)
     total = ctx.shape[0]
+    shapes = [
+        jax.ShapeDtypeStruct((rows, model), f32),
+        jax.ShapeDtypeStruct((rows, model), f32),
+        jax.ShapeDtypeStruct((rows, 1), f32),
+        jax.ShapeDtypeStruct((rows, model), f32),
+        jax.ShapeDtypeStruct((rows, 1), f32),
+        jax.ShapeDtypeStruct((rows, model), bf16),
+        jax.ShapeDtypeStruct((rows, model), bf16),
+        jax.ShapeDtypeStruct((total, rows), bf16),
+        jax.ShapeDtypeStruct((total, rows), bf16),
+        jax.ShapeDtypeStruct((total, rows), bf16),
+        jax.ShapeDtypeStruct((total // HDIM, 1, rows), f32),
+    ]
     return pl.pallas_call(
         functools.partial(middle_forward_kernel, group, heads),
         grid_spec=pltpu.PrefetchScalarGridSpec(
             num_scalar_prefetch=1,
             grid=(1,),
             in_specs=[VMEM] * (4 + 2 * group) + [ANY] * len(after),
-            out_specs=[VMEM] * 11,
-        ),
-        out_shape=[
-            jax.ShapeDtypeStruct((rows, model), f32),
-            jax.ShapeDtypeStruct((rows, model), f32),
-            jax.ShapeDtypeStruct((rows, 1), f32),
-            jax.ShapeDtypeStruct((rows, model), f32),
-            jax.ShapeDtypeStruct((rows, 1), f32),
-            jax.ShapeDtypeStruct((rows, model), bf16),
-            jax.ShapeDtypeStruct((rows, model), bf16),
-            jax.ShapeDtypeStruct((total, rows), bf16),
-            jax.ShapeDtypeStruct((total, rows), bf16),
-            jax.ShapeDtypeStruct((total, rows), bf16),
-            jax.ShapeDtypeStruct((total // HDIM, 1, rows), f32),
-        ],
+            out_specs=[
+                VMEM if index == 6 else pl.BlockSpec(shape.shape, lambda *_, n=len(shape.shape): (0,) * n)
+                for index, shape in enumerate(shapes)
+            ],
+        ),
+        out_shape=shapes,
         compiler_params=pltpu.CompilerParams(vmem_limit_bytes=LIMIT),
         cost_estimate=pl.CostEstimate(
             flops=6 * rows * model * total, bytes_accessed=12 * 2**20, transcendentals=2**20
@@ -645,6 +650,60 @@
     )(info, *lefts, *rights, *extra)
 
 
+def middle_outer_kernel(group, *refs):
+    one, ctx_one, two, ctx_two, h, dq = refs[:6]
+    outs = refs[6:]
+    width = dq.shape[0] // group
+    for index, (left, right) in enumerate(((one, ctx_one), (two, ctx_two), (h, dq))):
+        turned = jnp.swapaxes(left[...], 0, 1)
+        cols = slice(index * width, (index + 1) * width)
+        for step in range(group):
+            part = right[step * width : (step + 1) * width, :]
+            outs[step][:, cols] = dot(turned, part, 1, 1).astype(bf16)
+
+
+def middle_outer(one, ctx_one, two, ctx_two, h, dq, group):
+    rows, model = one.shape
+    width = dq.shape[0] // group
+    return pl.pallas_call(
+        functools.partial(middle_outer_kernel, group),
+        in_specs=[VMEM] * 6,
+        out_specs=[VMEM] * group,
+        out_shape=[jax.ShapeDtypeStruct((model, 3 * width), bf16)] * group,
+        compiler_params=pltpu.CompilerParams(vmem_limit_bytes=LIMIT),
+        cost_estimate=pl.CostEstimate(
+            flops=6 * rows * model * model, bytes_accessed=9 * 2**20, transcendentals=0
+        ),
+        name="middle_outer",
+    )(one, ctx_one, two, ctx_two, h, dq)
+
+
+def combine_kernel(extra, *refs):
+    dq, dk, dv = refs[:3]
+    gots, out = refs[3:-1], refs[-1]
+    gots = gots[: len(gots) - extra]
+    out[:, 0] = dq[...]
+    for index, value in enumerate((dk, dv)):
+        total = value[0]
+        for got in gots[index::2]:
+            total = total + got[...].astype(f32)
+        out[:, 1 + index] = total.astype(bf16)
+
+
+def combine(dq, dk, dv, got_k, got_v, after):
+    heads, depth, piece = dq.shape
+    gots = [got for pair in zip(got_k, got_v) for got in pair]
+    return pl.pallas_call(
+        functools.partial(combine_kernel, len(after)),
+        in_specs=[VMEM] * (3 + len(gots)) + [ANY] * len(after),
+        out_specs=VMEM,
+        out_shape=jax.ShapeDtypeStruct((heads, 3, depth, piece), bf16),
+        compiler_params=pltpu.CompilerParams(vmem_limit_bytes=LIMIT),
+        cost_estimate=pl.CostEstimate(flops=2**20, bytes_accessed=5 * 2**20, transcendentals=0),
+        name="combine",
+    )(dq, dk, dv, *gots, *after)
+
+
 def local(
     hidden,
     encoder,
@@ -764,8 +823,8 @@
     q_out, k_out, v_out, h_one = project(
         info, hidden_blocks, w_self, jnp.stack([gain[0], shift[0]]), factors, heads, [w_mid]
     )
-    w_up, w_down = tie([up_weight, down_weight.T], [h_one])
-    w_up, w_down = gather_tok(w_up), gather_tok(w_down)
+    w_up, w_down = tie([up_weight, down_weight], [h_one])
+    w_up, w_down = gather_tok(w_up), gather_tok(w_down.T)
     w_mid = merge_sides(w_mid, swap(w_mid, "tok", 1))
     k = [across_lines(k_out)]
     v = [across_lines(v_out)]
@@ -844,17 +903,9 @@
         )
     )
     grad_heads = across_wide(grad_ctx_one.reshape(group * heads, HDIM, rows))
-    grad_mid = [
-        dot(grad_one_low, ctx_one, 0, 1),
-        dot(grad_two_low, ctx_two, 0, 1),
-        dot(h_two, grad_q_two, 0, 1),
-    ]
-    grad_mid = [
-        jnp.concatenate([g[:, j * width : (j + 1) * width] for g in grad_mid], 1).astype(
-            bf16 if j % 2 else f32
-        )
-        for j in range(group)
-    ]
+    grad_mid = middle_outer(
+        grad_one_low, ctx_one, grad_two_low, ctx_two, h_two, grad_q_two, group
+    )
     masks = [1 << bit for bit in range(tok_size.bit_length() - 1)]
 
     def add_low(value, got):
@@ -863,9 +914,7 @@
     grad_q_away, grad_k_away, grad_v_away = self_backward(
         info, q, k[1:], v[1:], None, grad_heads, context, log_one, None, grad_mid
     )
-    grad_q_away, grad_k_away, grad_v_away, down_got = tie(
-        [grad_q_away, grad_k_away, grad_v_away, down_got], []
-    )
+    down_got = tie([down_got], [grad_q_away])[0]
     down_sum = outer(cot_blocks, acts, info, 0, many, down_got)
     sent_down = reduce_half(tie([down_sum], [sent_up])[0]).T
     kv_total = reduce_xor(
@@ -883,7 +932,7 @@
         info, q, k[:1], v[:1], ids, grad_heads, context, log_one, grad_q_away, [down_sum]
     )
     kv_got = swap(kv_total, "tok", masks[0])
-    grad_q, grad_k, grad_v, sent_up, kv_got = tie([grad_q, grad_k, grad_v, sent_up, kv_got], [])
+    grad_qkv = combine(grad_q, grad_k, grad_v, grad_k_got, grad_v_got, [sent_up, kv_got])
     kv_total = add_low(kv_total, kv_got)
     acts = tie(acts, [grad_q])
     def act_block(index):
@@ -892,9 +941,6 @@
 
     final = reduce_xor([dot(act_block(j), w_down, 1, 1) for j in range(group)])
     output = (resid_two + final + bias[6]).astype(bf16)
-    grad_k = grad_k[0] + sum(got.astype(f32) for got in grad_k_got)
-    grad_v = grad_v[0] + sum(got.astype(f32) for got in grad_v_got)
-    grad_qkv = jnp.stack([grad_q, grad_k.astype(bf16), grad_v.astype(bf16)], 1)
     grad_qkv = across_lines(grad_qkv).reshape(3 * width, piece_rows)
     kv_got = swap(kv_total, "tok", masks[1])
     grad_qkv, sent_down, kv_got = tie([grad_qkv, sent_down, kv_got], [])
@@ -939,23 +985,16 @@
 
     qkv_sums = jnp.sum(grad_qkv.astype(f32), 1).reshape(heads, 3, HDIM)
     once = (tok_index == 0).astype(f32)
-    vectors = jnp.stack(
+    late = jnp.concatenate(
         [
             place(qkv_sums[:, 0].reshape(-1)),
             place(qkv_sums[:, 2].reshape(-1)),
-            sums[5],
-            sums[7],
             place(jnp.sum(kv_flat[:, width:].astype(f32), (0, 2)) * once),
-            sums[4],
-            sums[6],
             gain_one,
-            sums[2],
-            sums[0],
             shift_one,
-            sums[3],
-            sums[1],
         ]
     )
+    vectors = jnp.concatenate([sums, late.reshape(5, model)], 0)
     vectors = vectors.reshape(13, total_devices, few).transpose(1, 0, 2).reshape(total_devices, -1)
     up_all = lax.dynamic_update_slice_in_dim(
         jnp.zeros((group * ff_local,), f32), up_sums, me * ff_local, 0
@@ -963,7 +1002,8 @@
     vectors = jnp.concatenate([vectors, up_all.reshape(total_devices, -1)], 1)
     vectors = tie([vectors], [ordered])[0]
     vectors = jnp.sum(lax.all_to_all(vectors, ("tok", "hd"), 0, 0, tiled=True), 0)
-    columns = vectors[: 13 * few].reshape(13, few).T
+    columns = vectors[: 13 * few].reshape(13, few)
+    columns = columns[jnp.array([8, 9, 5, 7, 10, 4, 6, 11, 2, 0, 12, 3, 1])].T
 
     sent_mid = [sent_mid[:, j * width : (j + 1) * width] for j in range(3)]
     sent_cross = jnp.concatenate(

time: 694 us -> 664 us (0.957)
  waiting for transfers between devices: 241 us -> 220 us
  other arithmetic: 47.5 us -> 35.7 us
  Pallas kernels: 184 us -> 191 us
    all_to_all x2, waiting for transfers between devices: 51.8 us -> 26.5 us  [across_wide(): lax.all_to_all(value, ('tok', 'hd'), 0, 0, tiled=True, axis_index_groups=...]
    all_to_all x4, waiting for transfers between devices: 43.6 us -> 29.8 us  [across_lines(): lax.all_to_all(value, 'tok', 0, 0, tiled=True, axis_index_groups=lines)]
    another operation x21 -> x6, local copies, waits for them, and re-layouts: 9.47 us -> 0.85 us  [the longest x19 8.08 us: local(): jnp.stack([place(qkv_sums[:, 0].reshape(-1)), place(qkv_sums[:, 2].reshap...]
    reduce_scatter x1, waiting for transfers between devices: 0.01 us -> 8.56 us  [reduce_tok(): lax.psum_scatter(value, 'tok', scatter_dimension=0, tiled=True).astype(f32)]
    unnamed x244 -> x254, local copies, waits for them, and re-layouts: 43 us -> 47.9 us
    dot_general x18 -> x15, matrix products: 37.9 us -> 35.9 us  [dot(): lax.dot_general(left, right, (((left_dim,), (right_dim,)), ((), ())), pre...]
  transfers between devices with their start and end apart: 62 -> 62, of which waited for: 22 -> 23; matrix products, arithmetic and copies ran while one was open for 18% -> 15% of each run, Pallas kernels for 23% -> 25%
where the time goes in v3:
time: 664 us; the launch traced here: 653 us
  waiting for transfers between devices  220 us (33%)
  Pallas kernels  191 us (29%)
  starting transfers between devices  80.8 us (12%)
  local copies, waits for them, and re-layouts  74.2 us (11%)
  matrix products  35.9 us (5%)
  other arithmetic  35.7 us (5%)
  between operations  15.7 us (2%)
    ppermute x46, waiting for transfers between devices, swap(): lax.ppermute(value, axis, [(i, i ^ mask) for i in range(lax.axis_size(axi...  113 us
    pallas_call x2, Pallas kernels, self_backward(): pl.pallas_call(functools.partial(self_backward_kernel, heads, sides, own,...  61.3 us
    unnamed x254, local copies, waits for them, and re-layouts  47.9 us
    pallas_call x1, Pallas kernels, self_forward(): pl.pallas_call(functools.partial(self_forward_kernel, heads, others), gri...  39.1 us
    dot_general x15, matrix products, dot(): lax.dot_general(left, right, (((left_dim,), (right_dim,)), ((), ())), pre...  35.9 us
    all_to_all x4, waiting for transfers between devices, across_lines(): lax.all_to_all(value, 'tok', 0, 0, tiled=True, axis_index_groups=lines)  29.8 us
    all_to_all x1, waiting for transfers between devices, along_halves(): lax.all_to_all(jnp.broadcast_to(block[None], (many, *block.shape)), 'tok'...  28 us
    ppermute x46, starting transfers between devices, swap(): lax.ppermute(value, axis, [(i, i ^ mask) for i in range(lax.axis_size(axi...  27.6 us
  transfers between devices with their start and end apart: 62, of which 23 were waited for; matrix products, arithmetic and copies ran while one was open for 15% of the time, Pallas kernels for 25%

profile of v3, /device:TPU:0, one launch (start us, length us, event | category | flops | bytes accessed | tf_op | source)
XLA Modules:
  0.0 652.8 jit_solution(12516201805712005366)
XLA Ops:
  15.7 7.3 %all-to-all-start = ((bf16[32,2,464]{2,1,0:T(2,128)(2,1)}), bf16[32,2,464]{2,1,0:T(2,128)(2,1)S(1)}, u32[]{:S(2)}, u32[]{:S(2)}) async-start(bf16[32,2,464]{2,1,0:T(2,128)(2,1)} %reshape.316), calls=%async_computation | async-start | bytes 131072 | tf_op jit(solution)/shard_map/all_to_all | solution.py:782
  23.4 7.3 %all-to-all-done = bf16[32,2,464]{2,1,0:T(2,128)(2,1)S(1)} async-done(((bf16[32,2,464]{2,1,0:T(2,128)(2,1)}), bf16[32,2,464]{2,1,0:T(2,128)(2,1)S(1)}, u32[]{:S(2)}, u32[]{:S(2)}) %all-to-all-start) | async-done | bytes 59424 | tf_op jit(solution)/shard_map/all_to_all | solution.py:782
  31.9 3.7 all-to-all-start.1
  37.4 12.7 %collective-permute-done.1.refs_5_ = bf16[256,1024]{1,0:T(8,128)(2,1)S(1)} collective-permute-done((bf16[256,1024]{1,0:T(8,128)(2,1)S(1)}, bf16[256,1024]{1,0:T(8,128)(2,1)S(1)}, u32[]{:S(2)}, u32[]{:S(2)}) %collective-permute-start.1) | collective-permute-done | bytes 524320 | tf_op jit(solution)/shard_map/ppermute | solution.py:26
  52.6 28.0 %all-to-all-done.1.refs_7_ = bf16[4,128,1280]{2,1,0:T(8,128)(2,1)S(1)} async-done(((bf16[4,128,1280]{2,1,0:T(8,128)(2,1)}), bf16[4,128,1280]{2,1,0:T(8,128)(2,1)S(1)}, u32[]{:S(2)}, u32[]{:S(2)}) %all-to-all-start.1) | async-done | bytes 1310752 | tf_op jit(solution)/shard_map/all_to_all | solution.py:756
  80.6 6.4 project.1
  90.6 3.6 all-to-all-start.3
  94.8 4.6 collective-permute-done.7
  103.2 18.1 %all-to-all-done.3.refs_2_.refs_4_ = bf16[4,64,1024]{2,1,0:T(8,128)(2,1)S(1)} async-done(((bf16[4,64,1024]{2,1,0:T(8,128)(2,1)}), bf16[4,64,1024]{2,1,0:T(8,128)(2,1)S(1)}, u32[]{:S(2)}, u32[]{:S(2)}) %all-to-all-start.3) | async-done | bytes 524320 | tf_op jit(solution)/shard_map/all_to_all | solution.py:816
  121.3 3.5 all-to-all-start.4
  124.8 15.2 %collective-permute-done.5 = bf16[4,128,1280]{2,1,0:T(8,128)(2,1)} collective-permute-done((bf16[4,128,1280]{2,1,0:T(8,128)(2,1)S(1)}, bf16[4,128,1280]{2,1,0:T(8,128)(2,1)}, u32[]{:S(2)}, u32[]{:S(2)}) %collective-permute-start.5) | collective-permute-done | bytes 1310752 | tf_op jit(solution)/shard_map/ppermute | solution.py:26
  144.2 3.5 all-to-all-start.2
  151.9 4.1 collective-permute-done.10.refs_8_.refs_10_.refs_16_
  159.3 11.7 %all-to-all-done.2.refs_0_ = bf16[4,64,1024]{2,1,0:T(8,128)(2,1)S(1)} async-done(((bf16[4,64,1024]{2,1,0:T(8,128)(2,1)}), bf16[4,64,1024]{2,1,0:T(8,128)(2,1)S(1)}, u32[]{:S(2)}, u32[]{:S(2)}) %all-to-all-start.2) | async-done | bytes 524320 | tf_op jit(solution)/shard_map/all_to_all | solution.py:816
  171.1 6.5 %collective-permute-done.3.refs_3_.refs_4_ = bf16[4,64,1024]{2,1,0:T(8,128)(2,1)} collective-permute-done((bf16[4,64,1024]{2,1,0:T(8,128)(2,1)S(1)}, bf16[4,64,1024]{2,1,0:T(8,128)(2,1)}, u32[]{:S(2)}, u32[]{:S(2)}) %collective-permute-start.3) | collective-permute-done | bytes 524320 | tf_op jit(solution)/shard_map/ppermute | solution.py:26
  177.6 10.4 %collective-permute-done.4.refs_5_ = bf16[4,64,1024]{2,1,0:T(8,128)(2,1)} collective-permute-done((bf16[4,64,1024]{2,1,0:T(8,128)(2,1)S(1)}, bf16[4,64,1024]{2,1,0:T(8,128)(2,1)}, u32[]{:S(2)}, u32[]{:S(2)}) %collective-permute-start.4) | collective-permute-done | bytes 524320 | tf_op jit(solution)/shard_map/ppermute | solution.py:26
  188.0 39.1 %self_forward.1 = (bf16[16,64,256]{2,1,0:T(8,128)(2,1)}, f32[4,1,1024]{2,1,0:T(1,128)S(1)}) custom-call(s32[4]{0:T(128)S(1)} %pad_add_fusion.info, bf16[4,64,1024]{2,1,0:T(8,128)(2,1)S(1)} %all-to-all-done.2.refs_0_, f32[4,1,1024]{2,1,0:T(1,128)S(1)} %pad_maximum_fusion.8.refs_1_.refs_6_, bf16[4,64,1024]{2,1,0:T(8,128)(2,1)S(1)} %all-to-all-done.3.refs_2_.refs_4_, ...), custom_call_target="tpu_custom_call" | custom-call | flops 17179869184 | bytes 8388608 | tf_op jit(solution)/shard_map/self_forward/pallas_call | solution.py:213
  227.8 4.3 all-to-all-start.5
  236.6 25.8 %all-to-all-done.5 = bf16[16,64,256]{2,1,0:T(8,128)(2,1)S(1)} async-done(((bf16[16,64,256]{2,1,0:T(8,128)(2,1)}), bf16[16,64,256]{2,1,0:T(8,128)(2,1)S(1)}, u32[]{:S(2)}, u32[]{:S(2)}) %all-to-all-start.5) | async-done | bytes 524320 | tf_op jit(solution)/shard_map/all_to_all | solution.py:819
  263.3 12.1 %middle_forward.1 = (f32[256,1024]{1,0:T(8,128)S(1)}, f32[256,1024]{1,0:T(8,128)}, f32[256,1]{1,0:T(8,128)S(1)}, f32[256,1024]{1,0:T(8,128)}, f32[256,1]{1,0:T(8...) custom-call(s32[4]{0:T(128)S(1)} %pad_add_fusion.info, ...), custom_call_target="tpu_custom_call" | custom-call | flops 1610612736 | bytes 12582912 | tf_op jit(solution)/shard_map/middle_forward/pallas_call | solution.py:414
  282.0 12.8 %collective-permute-done.19.refs_0_.refs_2_ = bf16[256,1024]{1,0:T(8,128)(2,1)} collective-permute-done((bf16[256,1024]{1,0:T(8,128)(2,1)}, bf16[256,1024]{1,0:T(8,128)(2,1)}, u32[]{:S(2)}, u32[]{:S(2)}) %collective-permute-start.19) | collective-permute-done | bytes 524320 | tf_op jit(solution)/shard_map/ppermute | solution.py:26
  296.4 9.1 %grad_act.1.refs_2_ = bf16[1024,2048]{1,0:T(8,128)(2,1)} custom-call(bf16[256,1024]{1,0:T(8,128)(2,1)S(1)} %copy-done.13, bf16[256,1024]{1,0:T(8,128)(2,1)S(1)} %collective-permute-done.16.refs_1_, bf16[256,1024]{1,0:T(8,128)(2,1)S(1)} %collective-permute-done.17.refs_2_, bf16[256,1024]{1,0:T(8,128)(2,1)S(1)} %collective-permute-done.18.refs_3_, ...), custom_call_target="tpu_custom_call" | custom-call | flops 4294967296 | bytes 10485760 | tf_op jit(solution)/shard_map/grad_act/pallas_call | solution.py:539
  305.5 11.2 %feed.3 = (bf16[512,2048]{1,0:T(8,128)(2,1)S(1)}, bf16[512,2048]{1,0:T(8,128)(2,1)}, f32[1,2048]{1,0:T(1,128)S(1)}, f32[256,1024]{1,0:T(8,128)S(1)}, bf16[256,1024]{1,0:T(8,128)(2,1)S(1)}) custom-call(bf16[256,1024]{1,0:T(8,128)(2,1)} %collective-permute-done.19.refs_0_.refs_2_, bf16[256,1024]{1,0:T(8,128)(2,1)} %collective-permute-done.20.refs_1_.refs_3_, ...), custom_call_target="tpu_custom_call" | custom-call | flops 4294967296 | bytes 12582912 | tf_op jit(solution)/shard_map/feed/pallas_call | solution.py:580
  318.1 11.2 %feed.2 = (bf16[512,2048]{1,0:T(8,128)(2,1)S(1)}, bf16[512,2048]{1,0:T(8,128)(2,1)}, f32[1,2048]{1,0:T(1,128)S(1)}, f32[256,1024]{1,0:T(8,128)S(1)}, bf16[256,1024]{1,0:T(8,128)(2,1)}) custom-call(bf16[256,1024]{1,0:T(8,128)(2,1)} %get-tuple-element.70.refs_0_, bf16[256,1024]{1,0:T(8,128)(2,1)} %collective-permute-done.15.refs_1_, ...), custom_call_target="tpu_custom_call" | custom-call | flops 4294967296 | bytes 12582912 | tf_op jit(solution)/shard_map/feed/pallas_call | solution.py:580
  333.2 9.4 %outer.3.refs_18_ = bf16[1024,2048]{1,0:T(8,128)(2,1)} custom-call(s32[4]{0:T(128)S(1)} %pad_add_fusion.info, bf16[256,1024]{1,0:T(8,128)(2,1)} %get-tuple-element.70.refs_0_, bf16[256,1024]{1,0:T(8,128)(2,1)} %collective-permute-done.15.refs_1_, bf16[256,1024]{1,0:T(8,128)(2,1)} %collective-permute-done.19.refs_0_.refs_2_, ...), custom_call_target="tpu_custom_call" | custom-call | flops 4294967296 | bytes 10485760 | tf_op jit(solution)/shard_map/outer/pallas_call | solution.py:635
  346.1 5.7 outer.4.refs_19_
  353.5 5.3 collective-permute-done.23
  360.6 13.3 %middle_backward.1 = (f32[256,1024]{1,0:T(8,128)S(1)}, bf16[256,1024]{1,0:T(8,128)(2,1)S(1)}, bf16[256,1024]{1,0:T(8,128)(2,1)S(1)}, bf16[1024,256]{1,0:T(8,128)...) custom-call(s32[4]{0:T(128)S(1)} %pad_add_fusion.info, ...), custom_call_target="tpu_custom_call" | custom-call | flops 1610612736 | bytes 16777216 | tf_op jit(solution)/shard_map/middle_backward/pallas_call | solution.py:498
  378.2 4.2 all-to-all-start.6
  388.8 3.7 middle_outer.1
  401.3 29.3 %self_backward.2 = (f32[4,64,1024]{2,1,0:T(8,128)S(1)}, bf16[1,4,64,1024]{3,2,1,0:T(8,128)(2,1)}, bf16[1,4,64,1024]{3,2,1,0:T(8,128)(2,1)}) custom-call(s32[4]{0:T(128)S(1)} %pad_add_fusion.info, bf16[4,64,1024]{2,1,0:T(8,128)(2,1)S(1)} %all-to-all-done.2.refs_0_, bf16[16,64,256]{2,1,0:T(8,128)(2,1)} %all-to-all-done.6.refs_1_, ...), custom_call_target="tpu_custom_call" | custom-call | flops 536870912 | bytes 65536 | tf_op jit(solution)/shard_map/self_backward/pallas_call | solution.py:321
  435.9 5.8 outer.5.refs_8_
  443.8 8.6 %reduce-scatter.6.cloned.1.call-done = bf16[128,2048]{1,0:T(8,128)(2,1)} async-done(((bf16[1024,2048]{1,0:T(8,128)(2,1)}), bf16[128,2048]{1,0:T(8,128)(2,1)}) %reduce-scatter.6.cloned.1.call-update) | async-done | bytes 524304 | tf_op jit(solution)/shard_map/reduce_scatter | solution.py:886
  463.8 3.0 add_convert_fusion
  468.3 32.0 %self_backward.3 = (bf16[4,64,1024]{2,1,0:T(8,128)(2,1)S(1)}, f32[1,4,64,1024]{3,2,1,0:T(8,128)S(1)}, f32[1,4,64,1024]{3,2,1,0:T(8,128)S(1)}) custom-call(s32[4]{0:T(128)S(1)} %pad_add_fusion.info, bf16[4,64,1024]{2,1,0:T(8,128)(2,1)S(1)} %all-to-all-done.2.refs_0_, bf16[16,64,256]{2,1,0:T(8,128)(2,1)} %all-to-all-done.6.refs_1_, ...), custom_call_target="tpu_custom_call" | custom-call | flops 536870912 | bytes 65536 | tf_op jit(solution)/shard_map/self_backward/pallas_call | solution.py:321
  501.1 4.8 convolution_convert_fusion.3
  511.0 2.6 combine.1
  513.6 4.5 all-to-all-start.7
  518.3 3.6 add_convert_fusion.3
  529.9 5.7 collective-permute-done.27
  536.8 18.5 %collective-permute-done.45 = bf16[512,768]{1,0:T(8,128)(2,1)S(1)} collective-permute-done((bf16[512,768]{1,0:T(8,128)(2,1)S(1)}, bf16[512,768]{1,0:T(8,128)(2,1)S(1)}, u32[]{:S(2)}, u32[]{:S(2)}) %collective-permute-start.45) | collective-permute-done | bytes 786464 | tf_op jit(solution)/shard_map/ppermute | solution.py:26
  570.5 4.4 convolution_convert_fusion
  574.9 4.8 all-to-all-start.8
  579.7 4.5 collective-permute-done.38
  589.5 2.6 fusion.2
  598.7 10.4 %collective-permute-done.41 = bf16[1,64,1024]{2,1,0:T(8,128)(2,1)} collective-permute-done((bf16[1,64,1024]{2,1,0:T(8,128)(2,1)}, bf16[1,64,1024]{2,1,0:T(8,128)(2,1)}, u32[]{:S(2)}, u32[]{:S(2)}) %collective-permute-start.41) | collective-permute-done | bytes 131104 | tf_op jit(solution)/shard_map/ppermute | solution.py:26
  622.2 13.1 %all-to-all-start.9 = ((f32[32,1,672]{2,1,0:T(1,128)}), f32[32,1,672]{2,1,0:T(1,128)S(1)}, u32[]{:S(2)}, u32[]{:S(2)}) async-start(f32[32,1,672]{2,1,0:T(1,128)} %copy.79), calls=%async_computation.11 | async-start | bytes 196608 | tf_op jit(solution)/shard_map/all_to_all | solution.py:1004
  638.0 5.0 all-to-all-done.9
  (502 shorter events, 160.2 us)
Async XLA Ops:
  7.2 73.3 %all-gather.4.cloned.1.call-start = ((), (), s32[]{:S(2)}) async-start(), calls=%async_computation.13 | async-start | bytes 1769472 | tf_op jit(solution)/shard_map/all_gather | solution.py:753
  15.7 15.0 %all-to-all-start = ((bf16[32,2,464]{2,1,0:T(2,128)(2,1)}), bf16[32,2,464]{2,1,0:T(2,128)(2,1)S(1)}, u32[]{:S(2)}, u32[]{:S(2)}) async-start(bf16[32,2,464]{2,1,0:T(2,128)(2,1)} %reshape.316), calls=%async_computation | async-start | bytes 131072 | tf_op jit(solution)/shard_map/all_to_all | solution.py:782
  31.9 48.7 %all-to-all-start.1 = ((bf16[4,128,1280]{2,1,0:T(8,128)(2,1)}), bf16[4,128,1280]{2,1,0:T(8,128)(2,1)S(1)}, u32[]{:S(2)}, u32[]{:S(2)}) async-start(bf16[4,128,1280]{2,1,0:T(8,128)(2,1)} %broadcast_in_dim.25), calls=%async_computation.1 | async-start | bytes 2621440 | tf_op jit(solution)/shard_map/all_to_all | solution.py:756
  35.6 260.8 %all-gather.6.cloned.1.call-start = ((), (), s32[]{:S(2)}) async-start(), calls=%async_computation.14 | async-start | bytes 4718592 | tf_op jit(solution)/shard_map/all_gather | solution.py:753
  35.6 14.5 %collective-permute-start.1 = (bf16[256,1024]{1,0:T(8,128)(2,1)S(1)}, bf16[256,1024]{1,0:T(8,128)(2,1)S(1)}, u32[]{:S(2)}, u32[]{:S(2)}) collective-permute-start(bf16[256,1024]{1,0:T(8,128)(2,1)S(1)} %copy-done.9), channel_id=1, source_target_pairs={{0,2},{1,3},{2,0},{3,1},{4,6},{5,7},{6,4},{7,5},{8,10},{9,11},{10,... | collective-permute-start | bytes 1572872 | tf_op jit(solution)/shard_map/ppermute | solution.py:26
  36.9 15.6 %collective-permute-start = (bf16[256,1024]{1,0:T(8,128)(2,1)S(1)}, bf16[256,1024]{1,0:T(8,128)(2,1)S(1)}, u32[]{:S(2)}, u32[]{:S(2)}) collective-permute-start(bf16[256,1024]{1,0:T(8,128)(2,1)S(1)} %copy-done.9), channel_id=1, source_target_pairs={{0,1},{1,0},{2,3},{3,2},{4,5},{5,4},{6,7},{7,6},{8,9},{9,8},{10,11... | collective-permute-start | bytes 1572872 | tf_op jit(solution)/shard_map/ppermute | solution.py:26
  89.9 215.6 %all-gather.8.cloned.1.call-start = ((), (), s32[]{:S(2)}) async-start(), calls=%async_computation.15 | async-start | bytes 4718592 | tf_op jit(solution)/shard_map/all_gather | solution.py:753
  89.9 50.0 %collective-permute-start.5 = (bf16[4,128,1280]{2,1,0:T(8,128)(2,1)S(1)}, bf16[4,128,1280]{2,1,0:T(8,128)(2,1)}, u32[]{:S(2)}, u32[]{:S(2)}) collective-permute-start(bf16[4,128,1280]{2,1,0:T(8,128)(2,1)S(1)} %all-to-all-done.1.refs_7_), channel_id=1, source_target_pairs={{0,4},{4,0},{8,12},{12,8},{16,20},{20,16},{24,28},{28,24},{1,5},{5... | collective-permute-start | bytes 3932168 | tf_op jit(solution)/shard_map/ppermute | solution.py:26
  90.6 30.7 %all-to-all-start.3 = ((bf16[4,64,1024]{2,1,0:T(8,128)(2,1)}), bf16[4,64,1024]{2,1,0:T(8,128)(2,1)S(1)}, u32[]{:S(2)}, u32[]{:S(2)}) async-start(bf16[4,64,1024]{2,1,0:T(8,128)(2,1)} %get-tuple-element.65), calls=%async_computation.3 | async-start | bytes 1048576 | tf_op jit(solution)/shard_map/all_to_all | solution.py:816
  121.3 22.1 %all-to-all-start.4 = ((bf16[4,64,1024]{2,1,0:T(8,128)(2,1)}), bf16[4,64,1024]{2,1,0:T(8,128)(2,1)S(1)}, u32[]{:S(2)}, u32[]{:S(2)}) async-start(bf16[4,64,1024]{2,1,0:T(8,128)(2,1)} %copy-done.52), calls=%async_computation.4 | async-start | bytes 1048576 | tf_op jit(solution)/shard_map/all_to_all | solution.py:816
  144.2 26.9 %all-to-all-start.2 = ((bf16[4,64,1024]{2,1,0:T(8,128)(2,1)}), bf16[4,64,1024]{2,1,0:T(8,128)(2,1)S(1)}, u32[]{:S(2)}, u32[]{:S(2)}) async-start(bf16[4,64,1024]{2,1,0:T(8,128)(2,1)} %get-tuple-element.64), calls=%async_computation.2 | async-start | bytes 1048576 | tf_op jit(solution)/shard_map/all_to_all | solution.py:816
  149.7 28.0 %collective-permute-start.3 = (bf16[4,64,1024]{2,1,0:T(8,128)(2,1)S(1)}, bf16[4,64,1024]{2,1,0:T(8,128)(2,1)}, u32[]{:S(2)}, u32[]{:S(2)}) collective-permute-start(bf16[4,64,1024]{2,1,0:T(8,128)(2,1)S(1)} %all-to-all-done.3.refs_2_.refs_4_), channel_id=1, source_target_pairs={{0,4},{4,0},{8,12},{12,8},{16,20},{20,16},{24,28},{28,24},{1,5},{5... | collective-permute-start | bytes 1572872 | tf_op jit(solution)/shard_map/ppermute | solution.py:26
  149.8 38.3 %collective-permute-start.4 = (bf16[4,64,1024]{2,1,0:T(8,128)(2,1)S(1)}, bf16[4,64,1024]{2,1,0:T(8,128)(2,1)}, u32[]{:S(2)}, u32[]{:S(2)}) collective-permute-start(bf16[4,64,1024]{2,1,0:T(8,128)(2,1)S(1)} %copy-done.21), channel_id=1, source_target_pairs={{0,4},{4,0},{8,12},{12,8},{16,20},{20,16},{24,28},{28,24},{1,5},{5... | collective-permute-start | bytes 1572872 | tf_op jit(solution)/shard_map/ppermute | solution.py:26
  155.9 15.1 %collective-permute-start.11 = (bf16[2,256,256]{2,1,0:T(8,128)(2,1)S(1)}, bf16[2,256,256]{2,1,0:T(8,128)(2,1)S(1)}, u32[]{:S(2)}, u32[]{:S(2)}) collective-permute-start(bf16[2,256,256]{2,1,0:T(8,128)(2,1)S(1)} %collective-permute-done.10.refs_8_.refs_10_.refs_16_), channel_id=1, source_target_pairs={{0,1},{1,0},{2,3},{3,2},{4,5},{5,4},{6,7},{7,6},{8,9},{9,8},{10,11... | collective-permute-start | bytes 786440 | tf_op jit(solution)/shard_map/ppermute | solution.py:26
  158.8 68.9 %collective-permute-start.13 = (bf16[3,1024,256]{2,1,0:T(8,128)(2,1)}, bf16[3,1024,256]{2,1,0:T(8,128)(2,1)}, u32[]{:S(2)}, u32[]{:S(2)}) collective-permute-start(bf16[3,1024,256]{2,1,0:T(8,128)(2,1)} %pad_maximum_fusion.1.refs_4_.refs_10_), channel_id=1, source_target_pairs={{0,2},{1,3},{2,0},{3,1},{4,6},{5,7},{6,4},{7,5},{8,10},{9,11},{10,... | collective-permute-start | bytes 4718600 | tf_op jit(solution)/shard_map/ppermute | solution.py:26
  158.8 77.7 %collective-permute-start.12 = (bf16[3,1024,256]{2,1,0:T(8,128)(2,1)}, bf16[3,1024,256]{2,1,0:T(8,128)(2,1)}, u32[]{:S(2)}, u32[]{:S(2)}) collective-permute-start(bf16[3,1024,256]{2,1,0:T(8,128)(2,1)} %pad_maximum_fusion.1.refs_4_.refs_10_), channel_id=1, source_target_pairs={{0,1},{1,0},{2,3},{3,2},{4,5},{5,4},{6,7},{7,6},{8,9},{9,8},{10,11... | collective-permute-start | bytes 4718600 | tf_op jit(solution)/shard_map/ppermute | solution.py:26
  227.7 34.6 %collective-permute-start.14 = (bf16[3,1024,256]{2,1,0:T(8,128)(2,1)}, bf16[3,1024,256]{2,1,0:T(8,128)(2,1)}, u32[]{:S(2)}, u32[]{:S(2)}) collective-permute-start(bf16[3,1024,256]{2,1,0:T(8,128)(2,1)} %tie.10.refs_6_.refs_12_), channel_id=1, source_target_pairs={{0,1},{1,0},{2,3},{3,2},{4,5},{5,4},{6,7},{7,6},{8,9},{9,8},{10,11... | collective-permute-start | bytes 4718600 | tf_op jit(solution)/shard_map/ppermute | solution.py:26
  227.8 34.5 %all-to-all-start.5 = ((bf16[16,64,256]{2,1,0:T(8,128)(2,1)}), bf16[16,64,256]{2,1,0:T(8,128)(2,1)S(1)}, u32[]{:S(2)}, u32[]{:S(2)}) async-start(bf16[16,64,256]{2,1,0:T(8,128)(2,1)} %get-tuple-element.67.refs_2_), calls=%async_computation.5 | async-start | bytes 1048576 | tf_op jit(solution)/shard_map/all_to_all | solution.py:819
  232.1 220.2 %reduce-scatter.6.cloned.1.call-start = ((), (), s32[]{:S(2)}) async-start(), calls=%async_computation.16 | async-start | bytes 4718592 | tf_op jit(solution)/shard_map/reduce_scatter | solution.py:886
  232.5 49.1 %collective-permute-start.17 = (bf16[256,1024]{1,0:T(8,128)(2,1)S(1)}, bf16[256,1024]{1,0:T(8,128)(2,1)S(1)}, u32[]{:S(2)}, u32[]{:S(2)}) collective-permute-start(bf16[256,1024]{1,0:T(8,128)(2,1)S(1)} %copy-done.13), channel_id=1, source_target_pairs={{0,2},{1,3},{2,0},{3,1},{4,6},{5,7},{6,4},{7,5},{8,10},{9,11},{10,... | collective-permute-start | bytes 1572872 | tf_op jit(solution)/shard_map/ppermute | solution.py:26
  280.9 13.9 %collective-permute-start.19 = (bf16[256,1024]{1,0:T(8,128)(2,1)}, bf16[256,1024]{1,0:T(8,128)(2,1)}, u32[]{:S(2)}, u32[]{:S(2)}) collective-permute-start(bf16[256,1024]{1,0:T(8,128)(2,1)} %get-tuple-element.70.refs_0_), channel_id=1, source_target_pairs={{0,2},{1,3},{2,0},{3,1},{4,6},{5,7},{6,4},{7,5},{8,10},{9,11},{10,... | collective-permute-start | bytes 1572872 | tf_op jit(solution)/shard_map/ppermute | solution.py:26
  281.5 14.8 %collective-permute-start.16 = (bf16[256,1024]{1,0:T(8,128)(2,1)S(1)}, bf16[256,1024]{1,0:T(8,128)(2,1)S(1)}, u32[]{:S(2)}, u32[]{:S(2)}) collective-permute-start(bf16[256,1024]{1,0:T(8,128)(2,1)S(1)} %copy-done.13), channel_id=1, source_target_pairs={{0,1},{1,0},{2,3},{3,2},{4,5},{5,4},{6,7},{7,6},{8,9},{9,8},{10,11... | collective-permute-start | bytes 1572872 | tf_op jit(solution)/shard_map/ppermute | solution.py:26
  281.7 14.7 %collective-permute-start.18 = (bf16[256,1024]{1,0:T(8,128)(2,1)S(1)}, bf16[256,1024]{1,0:T(8,128)(2,1)S(1)}, u32[]{:S(2)}, u32[]{:S(2)}) collective-permute-start(bf16[256,1024]{1,0:T(8,128)(2,1)S(1)} %collective-permute-done.17.refs_2_), channel_id=1, source_target_pairs={{0,1},{1,0},{2,3},{3,2},{4,5},{5,4},{6,7},{7,6},{8,9},{9,8},{10,11... | collective-permute-start | bytes 1572872 | tf_op jit(solution)/shard_map/ppermute | solution.py:26
  295.7 22.3 %collective-permute-start.15 = (bf16[256,1024]{1,0:T(8,128)(2,1)}, bf16[256,1024]{1,0:T(8,128)(2,1)}, u32[]{:S(2)}, u32[]{:S(2)}) collective-permute-start(bf16[256,1024]{1,0:T(8,128)(2,1)} %get-tuple-element.70.refs_0_), channel_id=1, source_target_pairs={{0,1},{1,0},{2,3},{3,2},{4,5},{5,4},{6,7},{7,6},{8,9},{9,8},{10,11... | collective-permute-start | bytes 1572872 | tf_op jit(solution)/shard_map/ppermute | solution.py:26
  344.7 14.0 %collective-permute-start.23 = (bf16[256,1024]{1,0:T(8,128)(2,1)S(1)}, bf16[256,1024]{1,0:T(8,128)(2,1)S(1)}, u32[]{:S(2)}, u32[]{:S(2)}) collective-permute-start(bf16[256,1024]{1,0:T(8,128)(2,1)S(1)} %add_convert_fusion.5), channel_id=1, source_target_pairs={{0,2},{1,3},{2,0},{3,1},{4,6},{5,7},{6,4},{7,5},{8,10},{9,11},{10,... | collective-permute-start | bytes 1572872 | tf_op jit(solution)/shard_map/ppermute | solution.py:26
  351.8 79.7 %collective-permute-start.24 = (bf16[512,2048]{1,0:T(8,128)(2,1)S(1)}, bf16[512,2048]{1,0:T(8,128)(2,1)}, u32[]{:S(2)}, u32[]{:S(2)}) collective-permute-start(bf16[512,2048]{1,0:T(8,128)(2,1)S(1)} %outer.4.refs_19_), channel_id=1, source_target_pairs={{0,4},{4,0},{8,12},{12,8},{16,20},{20,16},{24,28},{28,24},{1,5},{5... | collective-permute-start | bytes 6291464 | tf_op jit(solution)/shard_map/ppermute | solution.py:26
  378.2 23.1 %all-to-all-start.6 = ((bf16[16,64,256]{2,1,0:T(8,128)(2,1)}), bf16[16,64,256]{2,1,0:T(8,128)(2,1)}, u32[]{:S(2)}, u32[]{:S(2)}) async-start(bf16[16,64,256]{2,1,0:T(8,128)(2,1)} %bitcast.140), calls=%async_computation.6 | async-start | bytes 1048576 | tf_op jit(solution)/shard_map/all_to_all | solution.py:819
  382.4 173.9 %reduce-scatter.10.cloned.1.call-start = ((), (), s32[]{:S(2)}) async-start(), calls=%async_computation.18 | async-start | bytes 2621440
  392.4 71.3 %collective-permute-start.43 = (bf16[1024,768]{1,0:T(8,128)(2,1)}, bf16[1024,768]{1,0:T(8,128)(2,1)}, u32[]{:S(2)}, u32[]{:S(2)}) collective-permute-start(bf16[1024,768]{1,0:T(8,128)(2,1)} %get-tuple-element.98.refs_9_), channel_id=1, source_target_pairs={{0,1},{1,0},{2,3},{3,2},{4,5},{5,4},{6,7},{7,6},{8,9},{9,8},{10,11... | collective-permute-start | bytes 4718600 | tf_op jit(solution)/shard_map/ppermute | solution.py:26
  396.6 62.3 %collective-permute-start.30 = (bf16[2,256,256]{2,1,0:T(8,128)(2,1)}, bf16[2,256,256]{2,1,0:T(8,128)(2,1)}, u32[]{:S(2)}, u32[]{:S(2)}) collective-permute-start(bf16[2,256,256]{2,1,0:T(8,128)(2,1)} %get-tuple-element.186), channel_id=1, source_target_pairs={{0,1},{1,0},{2,3},{3,2},{4,5},{5,4},{6,7},{7,6},{8,9},{9,8},{10,11... | collective-permute-start | bytes 786440 | tf_op jit(solution)/shard_map/ppermute | solution.py:26
  398.6 59.5 %collective-permute-start.32 = (bf16[2,256,256]{2,1,0:T(8,128)(2,1)}, bf16[2,256,256]{2,1,0:T(8,128)(2,1)S(1)}, u32[]{:S(2)}, u32[]{:S(2)}) collective-permute-start(bf16[2,256,256]{2,1,0:T(8,128)(2,1)} %fusion.52), channel_id=1, source_target_pairs={{0,2},{1,3},{2,0},{3,1},{4,6},{5,7},{6,4},{7,5},{8,10},{9,11},{10,... | collective-permute-start | bytes 786440 | tf_op jit(solution)/shard_map/ppermute | solution.py:26
  457.3 65.2 %collective-permute-start.42 = (bf16[1024,768]{1,0:T(8,128)(2,1)}, bf16[1024,768]{1,0:T(8,128)(2,1)}, u32[]{:S(2)}, u32[]{:S(2)}) collective-permute-start(bf16[1024,768]{1,0:T(8,128)(2,1)} %get-tuple-element.96.refs_7_), channel_id=1, source_target_pairs={{0,1},{1,0},{2,3},{3,2},{4,5},{5,4},{6,7},{7,6},{8,9},{9,8},{10,11... | collective-permute-start | bytes 4718600 | tf_op jit(solution)/shard_map/ppermute | solution.py:26
  460.2 45.6 %collective-permute-start.33 = (bf16[1,2,256,256]{3,2,1,0:T(8,128)(2,1)S(1)}, bf16[1,2,256,256]{3,2,1,0:T(8,128)(2,1)S(1)}, u32[]{:S(2)}, u32[]{:S(2)}) collective-permute-start(bf16[1,2,256,256]{3,2,1,0:T(8,128)(2,1)S(1)} %fusion.59), channel_id=1, source_target_pairs={{0,4},{4,0},{8,12},{12,8},{16,20},{20,16},{24,28},{28,24},{1,5},{5... | collective-permute-start | bytes 786440 | tf_op jit(solution)/shard_map/ppermute | solution.py:26
  461.7 47.0 %collective-permute-start.28 = (bf16[4,64,1024]{2,1,0:T(8,128)(2,1)}, bf16[4,64,1024]{2,1,0:T(8,128)(2,1)}, u32[]{:S(2)}, u32[]{:S(2)}) collective-permute-start(bf16[4,64,1024]{2,1,0:T(8,128)(2,1)} %bitcast.35), channel_id=1, source_target_pairs={{0,4},{4,0},{8,12},{12,8},{16,20},{20,16},{24,28},{28,24},{1,5},{5... | collective-permute-start | bytes 1572872 | tf_op jit(solution)/shard_map/ppermute | solution.py:26
  462.3 46.9 %collective-permute-start.29 = (bf16[4,64,1024]{2,1,0:T(8,128)(2,1)}, bf16[4,64,1024]{2,1,0:T(8,128)(2,1)}, u32[]{:S(2)}, u32[]{:S(2)}) collective-permute-start(bf16[4,64,1024]{2,1,0:T(8,128)(2,1)} %bitcast.36), channel_id=1, source_target_pairs={{0,4},{4,0},{8,12},{12,8},{16,20},{20,16},{24,28},{28,24},{1,5},{5... | collective-permute-start | bytes 1572872 | tf_op jit(solution)/shard_map/ppermute | solution.py:26
  466.8 55.7 %collective-permute-start.44 = (bf16[1024,768]{1,0:T(8,128)(2,1)}, bf16[1024,768]{1,0:T(8,128)(2,1)}, u32[]{:S(2)}, u32[]{:S(2)}) collective-permute-start(bf16[1024,768]{1,0:T(8,128)(2,1)} %add_convert_fusion), channel_id=1, source_target_pairs={{0,2},{1,3},{2,0},{3,1},{4,6},{5,7},{6,4},{7,5},{8,10},{9,11},{10,... | collective-permute-start | bytes 4718600 | tf_op jit(solution)/shard_map/ppermute | solution.py:26
  508.8 17.9 %collective-permute-start.25 = (bf16[256,1024]{1,0:T(8,128)(2,1)}, bf16[256,1024]{1,0:T(8,128)(2,1)}, u32[]{:S(2)}, u32[]{:S(2)}) collective-permute-start(bf16[256,1024]{1,0:T(8,128)(2,1)} %convolution_convert_fusion.4), channel_id=1, source_target_pairs={{0,1},{1,0},{2,3},{3,2},{4,5},{5,4},{6,7},{7,6},{8,9},{9,8},{10,11... | collective-permute-start | bytes 1572872 | tf_op jit(solution)/shard_map/ppermute | solution.py:26
  509.2 49.5 %collective-permute-start.34 = (bf16[1,2,256,256]{3,2,1,0:T(8,128)(2,1)}, bf16[1,2,256,256]{3,2,1,0:T(8,128)(2,1)}, u32[]{:S(2)}, u32[]{:S(2)}) collective-permute-start(bf16[1,2,256,256]{3,2,1,0:T(8,128)(2,1)} %add_convert_fusion.9), channel_id=1, source_target_pairs={{0,8},{4,12},{8,0},{12,4},{16,24},{20,28},{24,16},{28,20},{1,9},{5... | collective-permute-start | bytes 786440 | tf_op jit(solution)/shard_map/ppermute | solution.py:26
  513.6 45.2 %all-to-all-start.7 = ((bf16[4,3,64,1024]{3,2,1,0:T(8,128)(2,1)}), bf16[4,3,64,1024]{3,2,1,0:T(8,128)(2,1)}, u32[]{:S(2)}, u32[]{:S(2)}) async-start(bf16[4,3,64,1024]{3,2,1,0:T(8,128)(2,1)} %combine.1), calls=%async_computation.8 | async-start | bytes 3145728 | tf_op jit(solution)/shard_map/all_to_all | solution.py:816
  518.1 98.3 %reduce-scatter.8.cloned.1.call-start = ((), (), s32[]{:S(2)}) async-start(), calls=%async_computation.17 | async-start | bytes 983040 | tf_op jit(solution)/shard_map/reduce_scatter | solution.py:889
  526.1 29.2 %collective-permute-start.45 = (bf16[512,768]{1,0:T(8,128)(2,1)S(1)}, bf16[512,768]{1,0:T(8,128)(2,1)S(1)}, u32[]{:S(2)}, u32[]{:S(2)}) collective-permute-start(bf16[512,768]{1,0:T(8,128)(2,1)S(1)} %pad_maximum_fusion.2), channel_id=1, source_target_pairs={{0,4},{4,0},{8,12},{12,8},{16,20},{20,16},{24,28},{28,24},{1,5},{5... | collective-permute-start | bytes 2359304 | tf_op jit(solution)/shard_map/ppermute | solution.py:26
  560.0 24.2 %collective-permute-start.38 = (bf16[1,2,256,256]{3,2,1,0:T(8,128)(2,1)S(1)}, bf16[1,2,256,256]{3,2,1,0:T(8,128)(2,1)}, u32[]{:S(2)}, u32[]{:S(2)}) collective-permute-start(bf16[1,2,256,256]{3,2,1,0:T(8,128)(2,1)S(1)} %add_convert_fusion.8), channel_id=1, source_target_pairs={{0,16},{4,20},{8,24},{12,28},{16,0},{20,4},{24,8},{28,12},{1,17},{... | collective-permute-start | bytes 786440 | tf_op jit(solution)/shard_map/ppermute | solution.py:26
  566.1 23.3 %collective-permute-start.36 = (bf16[256,1024]{1,0:T(8,128)(2,1)}, bf16[256,1024]{1,0:T(8,128)(2,1)}, u32[]{:S(2)}, u32[]{:S(2)}) collective-permute-start(bf16[256,1024]{1,0:T(8,128)(2,1)} %convolution_convert_fusion.1), channel_id=1, source_target_pairs={{0,1},{1,0},{2,3},{3,2},{4,5},{5,4},{6,7},{7,6},{8,9},{9,8},{10,11... | collective-permute-start | bytes 1572872 | tf_op jit(solution)/shard_map/ppermute | solution.py:26
  568.7 42.6 %collective-permute-start.35 = (bf16[256,1024]{1,0:T(8,128)(2,1)}, bf16[256,1024]{1,0:T(8,128)(2,1)}, u32[]{:S(2)}, u32[]{:S(2)}) collective-permute-start(bf16[256,1024]{1,0:T(8,128)(2,1)} %convolution_convert_fusion.2), channel_id=1, source_target_pairs={{0,1},{1,0},{2,3},{3,2},{4,5},{5,4},{6,7},{7,6},{8,9},{9,8},{10,11... | collective-permute-start | bytes 1572872 | tf_op jit(solution)/shard_map/ppermute | solution.py:26
  574.9 45.6 %all-to-all-start.8 = ((bf16[8,128,768]{2,1,0:T(8,128)(2,1)}), bf16[8,128,768]{2,1,0:T(8,128)(2,1)}, u32[]{:S(2)}, u32[]{:S(2)}) async-start(bf16[8,128,768]{2,1,0:T(8,128)(2,1)} %bitcast.155), calls=%async_computation.9 | async-start | bytes 3145728 | tf_op jit(solution)/shard_map/all_to_all | solution.py:974
  592.1 19.2 %collective-permute-start.37 = (bf16[256,1024]{1,0:T(8,128)(2,1)}, bf16[256,1024]{1,0:T(8,128)(2,1)}, u32[]{:S(2)}, u32[]{:S(2)}) collective-permute-start(bf16[256,1024]{1,0:T(8,128)(2,1)} %fusion.2), channel_id=1, source_target_pairs={{0,2},{1,3},{2,0},{3,1},{4,6},{5,7},{6,4},{7,5},{8,10},{9,11},{10,... | collective-permute-start | bytes 1572872 | tf_op jit(solution)/shard_map/ppermute | solution.py:26
  593.3 15.8 %collective-permute-start.41 = (bf16[1,64,1024]{2,1,0:T(8,128)(2,1)}, bf16[1,64,1024]{2,1,0:T(8,128)(2,1)}, u32[]{:S(2)}, u32[]{:S(2)}) collective-permute-start(bf16[1,64,1024]{2,1,0:T(8,128)(2,1)} %fusion.40), channel_id=1, source_target_pairs={{0,2},{1,3},{2,0},{3,1},{4,6},{5,7},{6,4},{7,5},{8,10},{9,11},{10,... | collective-permute-start | bytes 393224 | tf_op jit(solution)/shard_map/ppermute | solution.py:26
  622.2 20.9 %all-to-all-start.9 = ((f32[32,1,672]{2,1,0:T(1,128)}), f32[32,1,672]{2,1,0:T(1,128)S(1)}, u32[]{:S(2)}, u32[]{:S(2)}) async-start(f32[32,1,672]{2,1,0:T(1,128)} %copy.79), calls=%async_computation.11 | async-start | bytes 196608 | tf_op jit(solution)/shard_map/all_to_all | solution.py:1004
  (134 other events, 1084.2 us)
Sparse Core Ops, SparseCore 0:
  12.3 62.2 all-gather.3
  90.0 98.2 all-gather.5
  191.0 81.5 all-gather.7
  342.7 109.6 reduce-scatter.5
  454.6 43.6 reduce-scatter.9
  558.9 35.8 reduce-scatter.7

commit v4 on v3

--- a/solution.py
+++ b/solution.py
@@ -149,10 +149,11 @@
 def self_forward_kernel(heads, others, info, *refs):
     q_ref, id_ref = refs[:2]
     k_refs, v_refs = refs[2 : 2 + others], refs[2 + others : 2 + 2 * others]
-    o_ref, l_ref, k_all, v_all = refs[-4:]
+    o_ref, l_ref, k_all, v_all, wait_a, wait_b = refs[-6:]
     beside = info[1]
     step = pl.program_id(0)
     piece_rows = q_ref.shape[2]
+    assert piece_rows == 2 * TILE
     per = piece_rows // TILE
     slot, tile = step // per, lax.rem(step, per)
 
@@ -167,37 +168,58 @@
     cols = pl.ds(pl.multiple_of(tile * TILE, TILE), TILE)
     q = q_ref[slot, :, cols]
 
-    def update(state, k, v, mask):
-        top, total, acc = state
-        scores = dot(k, q, 1, 0)
+    def ahead(wait, keys, top, mask=None):
+        scores = dot(keys, q, 1, 0)
         if mask is not None:
             scores = jnp.where(mask, scores, neg_large)
-        new_top = jnp.maximum(top, jnp.max(scores, axis=0, keepdims=True))
-        probs = jnp.exp(scores - new_top)
-        fade = jnp.exp(top - new_top)
+        wait[...] = scores
+        return jnp.maximum(top, jnp.max(scores, axis=0, keepdims=True))
+
+    def finish(wait, values, top, fade, total, acc):
+        probs = jnp.exp(wait[...] - top)
         total = total * fade + jnp.sum(probs, axis=0, keepdims=True)
-        acc = acc * fade + dot(v, probs.astype(bf16), 1, 0)
-        return new_top, total, acc
+        return total, acc * fade + dot(values, probs.astype(bf16), 1, 0)
+
+    def locate(index):
+        place = index // others
+        side = jnp.bitwise_xor(beside, flip(place, others))
+        return jnp.bitwise_xor(lax.rem(index, others), side), place
+
+    def waiting(index):
+        other, place = locate(jnp.maximum(index - 1, 0))
+        other, place = jnp.where(index == 0, 0, other), jnp.where(index == 0, slot, place)
+        start = jnp.where(index == 0, 0, TILE)
+        return v_all[other, place, :, pl.ds(pl.multiple_of(start, TILE), TILE)]
+
+    def earlier_tile(state):
+        top, fade, total, acc = state
+        new_top = ahead(wait_b, k_all[0, slot, :TILE, :], top)
+        total, acc = finish(wait_a, v_all[0, slot, :, cols], top, fade, total, acc)
+        wait_a[...] = wait_b[...]
+        return new_top, jnp.exp(top - new_top), total, acc
 
     def earlier_piece(index, state):
-        place = index // others
-        other = jnp.bitwise_xor(lax.rem(index, others), jnp.bitwise_xor(beside, flip(place, others)))
-        return update(state, k_all[other, place], v_all[other, place], None)
-
-    def earlier_tile(index, state):
-        rows = pl.ds(pl.multiple_of(index * TILE, TILE), TILE)
-        return update(state, k_all[0, slot, rows, :], v_all[0, slot, :, rows], None)
-
+        top, fade, total, acc = state
+        other, place = locate(index)
+        new_top = ahead(wait_b, k_all[other, place, :TILE, :], top)
+        total, acc = finish(wait_a, waiting(index), top, fade, total, acc)
+        fade, top = jnp.exp(top - new_top), new_top
+        new_top = ahead(wait_a, k_all[other, place, TILE:, :], top)
+        total, acc = finish(wait_b, v_all[other, place, :, :TILE], top, fade, total, acc)
+        return new_top, jnp.exp(top - new_top), total, acc
+
+    ids = id_ref[slot, :, cols]
+    mask = column(ids, TILE) <= ids
+    top = ahead(wait_a, k_all[0, slot, cols, :], jnp.full((1, TILE), neg_large, f32), mask)
     state = (
-        jnp.full((1, TILE), neg_large, f32),
+        top,
+        jnp.ones((1, TILE), f32),
         jnp.zeros((1, TILE), f32),
         jnp.zeros((HDIM, TILE), f32),
     )
-    state = lax.fori_loop(0, piece, earlier_piece, state)
-    state = lax.fori_loop(0, tile, earlier_tile, state)
-    ids = id_ref[slot, :, cols]
-    mask = column(ids, TILE) <= ids
-    top, total, acc = update(state, k_all[0, slot, cols, :], v_all[0, slot, :, cols], mask)
+    state = lax.cond(tile == 1, earlier_tile, lambda state: state, state)
+    top, fade, total, acc = lax.fori_loop(0, piece, earlier_piece, state)
+    total, acc = finish(wait_a, waiting(piece), top, fade, total, acc)
     out = (acc / total).astype(o_ref.dtype)
     rows = o_ref.shape[2]
     for index in range(TILE // rows):
@@ -220,6 +242,8 @@
             scratch_shapes=[
                 pltpu.VMEM((others, heads, piece, depth), bf16),
                 pltpu.VMEM((others, heads, depth, piece), bf16),
+                pltpu.VMEM((TILE, TILE), f32),
+                pltpu.VMEM((TILE, TILE), f32),
             ],
         ),
         out_shape=[
@@ -962,6 +986,13 @@
 
     grad_encoder = reduce_xor([encoder_part(j) for j in range(group)])
 
+    grad_self = dot(h_one, grad_qkv, 0, 1).astype(bf16)
+    sent_self = lax.all_to_all(grad_self, "tok", 0, 0, tiled=True)
+    ordered = sent_self
+    sent_self = jnp.sum(sent_self.reshape(tok_size, shard, 3 * width).astype(f32), 0)
+    sent_self = sent_self.reshape(shard, heads, 3, HDIM)
+    sent_self = sent_self.transpose(0, 2, 1, 3).reshape(shard, 3, width)
+    grad_qkv = tie([grad_qkv], [grad_self])[0]
     grad_h_one = reduce_xor(
         [
             dot(
@@ -970,12 +1001,6 @@
             for j in range(group)
         ]
     )
-    grad_self = dot(h_one, grad_qkv, 0, 1).astype(bf16)
-    sent_self = lax.all_to_all(grad_self, "tok", 0, 0, tiled=True)
-    ordered = sent_self
-    sent_self = jnp.sum(sent_self.reshape(tok_size, shard, 3 * width).astype(f32), 0)
-    sent_self = sent_self.reshape(shard, heads, 3, HDIM)
-    sent_self = sent_self.transpose(0, 2, 1, 3).reshape(shard, 3, width)
     unit_one, inverse_one = normalize(hidden.astype(f32))
     back, gain_one, shift_one = norm_backward(grad_h_one, unit_one, inverse_one, gain[0])
     grad_hidden = grad_one + back

time: 664 us -> 653 us (0.983)
  waiting for transfers between devices: 220 us -> 208 us
  starting transfers between devices: 80.8 us -> 92.2 us
  Pallas kernels: 191 us -> 180 us
    pallas_call x1, Pallas kernels: 39.1 us -> 28 us  [self_forward(): pl.pallas_call(functools.partial(self_forward_kernel, heads, others), gri...]
  transfers between devices with their start and end apart: 62 -> 62, of which waited for: 23 -> 23; matrix products, arithmetic and copies ran while one was open for 15% -> 15% of each run, Pallas kernels for 25% -> 24%
where the time goes in v4:
time: 653 us; the launch traced here: 642 us
  waiting for transfers between devices  208 us (32%)
  Pallas kernels  180 us (28%)
  starting transfers between devices  92.2 us (14%)
  local copies, waits for them, and re-layouts  75.4 us (12%)
  other arithmetic  35.8 us (5%)
  matrix products  35.7 us (5%)
  between operations  15.9 us (2%)
    ppermute x46, waiting for transfers between devices, swap(): lax.ppermute(value, axis, [(i, i ^ mask) for i in range(lax.axis_size(axi...  107 us
    pallas_call x2, Pallas kernels, self_backward(): pl.pallas_call(functools.partial(self_backward_kernel, heads, sides, own,...  61.1 us
    unnamed x254, local copies, waits for them, and re-layouts  49.1 us
    dot_general x15, matrix products, dot(): lax.dot_general(left, right, (((left_dim,), (right_dim,)), ((), ())), pre...  35.7 us
    ppermute x46, starting transfers between devices, swap(): lax.ppermute(value, axis, [(i, i ^ mask) for i in range(lax.axis_size(axi...  32.8 us
    all_to_all x4, waiting for transfers between devices, across_lines(): lax.all_to_all(value, 'tok', 0, 0, tiled=True, axis_index_groups=lines)  29.8 us
    pallas_call x1, Pallas kernels, self_forward(): pl.pallas_call(functools.partial(self_forward_kernel, heads, others), gri...  28 us
    all_to_all x1, waiting for transfers between devices, along_halves(): lax.all_to_all(jnp.broadcast_to(block[None], (many, *block.shape)), 'tok'...  28 us
  transfers between devices with their start and end apart: 62, of which 23 were waited for; matrix products, arithmetic and copies ran while one was open for 15% of the time, Pallas kernels for 24%

profile of v4, /device:TPU:0, one launch (start us, length us, event | category | flops | bytes accessed | tf_op | source)
XLA Modules:
  0.0 642.1 jit_solution(10118022303451431825)
XLA Ops:
  15.7 7.3 %all-to-all-start = ((bf16[32,2,464]{2,1,0:T(2,128)(2,1)}), bf16[32,2,464]{2,1,0:T(2,128)(2,1)S(1)}, u32[]{:S(2)}, u32[]{:S(2)}) async-start(bf16[32,2,464]{2,1,0:T(2,128)(2,1)} %reshape.316), calls=%async_computation | async-start | bytes 131072 | tf_op jit(solution)/shard_map/all_to_all | solution.py:806
  23.4 7.3 %all-to-all-done = bf16[32,2,464]{2,1,0:T(2,128)(2,1)S(1)} async-done(((bf16[32,2,464]{2,1,0:T(2,128)(2,1)}), bf16[32,2,464]{2,1,0:T(2,128)(2,1)S(1)}, u32[]{:S(2)}, u32[]{:S(2)}) %all-to-all-start) | async-done | bytes 59424 | tf_op jit(solution)/shard_map/all_to_all | solution.py:806
  31.9 3.7 all-to-all-start.1
  37.4 12.7 %collective-permute-done.1.refs_5_ = bf16[256,1024]{1,0:T(8,128)(2,1)S(1)} collective-permute-done((bf16[256,1024]{1,0:T(8,128)(2,1)S(1)}, bf16[256,1024]{1,0:T(8,128)(2,1)S(1)}, u32[]{:S(2)}, u32[]{:S(2)}) %collective-permute-start.1) | collective-permute-done | bytes 524320 | tf_op jit(solution)/shard_map/ppermute | solution.py:26
  52.6 28.0 %all-to-all-done.1.refs_7_ = bf16[4,128,1280]{2,1,0:T(8,128)(2,1)S(1)} async-done(((bf16[4,128,1280]{2,1,0:T(8,128)(2,1)}), bf16[4,128,1280]{2,1,0:T(8,128)(2,1)S(1)}, u32[]{:S(2)}, u32[]{:S(2)}) %all-to-all-start.1) | async-done | bytes 1310752 | tf_op jit(solution)/shard_map/all_to_all | solution.py:780
  80.6 6.4 %project.1 = (bf16[4,64,1024]{2,1,0:T(8,128)(2,1)}, bf16[4,64,1024]{2,1,0:T(8,128)(2,1)}, bf16[4,64,1024]{2,1,0:T(8,128)(2,1)S(1)}, bf16[1024,1024]{1,0:T(8,128)(2,1)}) custom-call(s32[4]{0:T(128)S(1)} %pad_add_fusion.info, bf16[1024,768]{1,0:T(8,128)(2,1)} %all-gather.4.cloned.1.call-done.refs_0_, f32[2,1024]{1,0:T(2,128)S(1)} %pad_maximum_fusion.9.refs_1_, ...), custom_call_target="tpu_custom_call" | custom-call | flops 1610612736 | bytes 8388608 | tf_op jit(solution)/shard_map/project/pallas_call | solution.py:127
  90.6 3.6 all-to-all-start.3
  94.8 4.6 collective-permute-done.7
  103.2 18.1 %all-to-all-done.3.refs_2_.refs_4_ = bf16[4,64,1024]{2,1,0:T(8,128)(2,1)S(1)} async-done(((bf16[4,64,1024]{2,1,0:T(8,128)(2,1)}), bf16[4,64,1024]{2,1,0:T(8,128)(2,1)S(1)}, u32[]{:S(2)}, u32[]{:S(2)}) %all-to-all-start.3) | async-done | bytes 524320 | tf_op jit(solution)/shard_map/all_to_all | solution.py:840
  121.3 3.5 all-to-all-start.4
  124.8 15.1 %collective-permute-done.5 = bf16[4,128,1280]{2,1,0:T(8,128)(2,1)} collective-permute-done((bf16[4,128,1280]{2,1,0:T(8,128)(2,1)S(1)}, bf16[4,128,1280]{2,1,0:T(8,128)(2,1)}, u32[]{:S(2)}, u32[]{:S(2)}) %collective-permute-start.5) | collective-permute-done | bytes 1310752 | tf_op jit(solution)/shard_map/ppermute | solution.py:26
  144.2 3.5 all-to-all-start.2
  151.8 4.1 collective-permute-done.10.refs_8_.refs_10_.refs_16_
  159.3 11.8 %all-to-all-done.2.refs_0_ = bf16[4,64,1024]{2,1,0:T(8,128)(2,1)S(1)} async-done(((bf16[4,64,1024]{2,1,0:T(8,128)(2,1)}), bf16[4,64,1024]{2,1,0:T(8,128)(2,1)S(1)}, u32[]{:S(2)}, u32[]{:S(2)}) %all-to-all-start.2) | async-done | bytes 524320 | tf_op jit(solution)/shard_map/all_to_all | solution.py:840
  171.1 6.5 %collective-permute-done.3.refs_3_.refs_4_ = bf16[4,64,1024]{2,1,0:T(8,128)(2,1)} collective-permute-done((bf16[4,64,1024]{2,1,0:T(8,128)(2,1)S(1)}, bf16[4,64,1024]{2,1,0:T(8,128)(2,1)}, u32[]{:S(2)}, u32[]{:S(2)}) %collective-permute-start.3) | collective-permute-done | bytes 524320 | tf_op jit(solution)/shard_map/ppermute | solution.py:26
  177.6 10.4 %collective-permute-done.4.refs_5_ = bf16[4,64,1024]{2,1,0:T(8,128)(2,1)} collective-permute-done((bf16[4,64,1024]{2,1,0:T(8,128)(2,1)S(1)}, bf16[4,64,1024]{2,1,0:T(8,128)(2,1)}, u32[]{:S(2)}, u32[]{:S(2)}) %collective-permute-start.4) | collective-permute-done | bytes 524320 | tf_op jit(solution)/shard_map/ppermute | solution.py:26
  188.0 28.0 %self_forward.1 = (bf16[16,64,256]{2,1,0:T(8,128)(2,1)}, f32[4,1,1024]{2,1,0:T(1,128)S(1)}) custom-call(s32[4]{0:T(128)S(1)} %pad_add_fusion.info, bf16[4,64,1024]{2,1,0:T(8,128)(2,1)S(1)} %all-to-all-done.2.refs_0_, f32[4,1,1024]{2,1,0:T(1,128)S(1)} %pad_maximum_fusion.8.refs_1_.refs_6_, bf16[4,64,1024]{2,1,0:T(8,128)(2,1)S(1)} %all-to-all-done.3.refs_2_.refs_4_, ...), custom_call_target="tpu_custom_call" | custom-call | flops 17179869184 | bytes 8388608 | tf_op jit(solution)/shard_map/self_forward/pallas_call | solution.py:235
  216.8 4.3 all-to-all-start.5
  225.4 18.8 %all-to-all-done.5 = bf16[16,64,256]{2,1,0:T(8,128)(2,1)S(1)} async-done(((bf16[16,64,256]{2,1,0:T(8,128)(2,1)}), bf16[16,64,256]{2,1,0:T(8,128)(2,1)S(1)}, u32[]{:S(2)}, u32[]{:S(2)}) %all-to-all-start.5) | async-done | bytes 524320 | tf_op jit(solution)/shard_map/all_to_all | solution.py:843
  245.2 12.1 %middle_forward.1 = (f32[256,1024]{1,0:T(8,128)S(1)}, f32[256,1024]{1,0:T(8,128)}, f32[256,1]{1,0:T(8,128)S(1)}, f32[256,1024]{1,0:T(8,128)}, f32[256,1]{1,0:T(8...) custom-call(s32[4]{0:T(128)S(1)} %pad_add_fusion.info, ...), custom_call_target="tpu_custom_call" | custom-call | flops 1610612736 | bytes 12582912 | tf_op jit(solution)/shard_map/middle_forward/pallas_call | solution.py:438
  263.4 2.8 collective-permute-start.16
  266.3 10.4 %collective-permute-done.19.refs_0_.refs_2_ = bf16[256,1024]{1,0:T(8,128)(2,1)} collective-permute-done((bf16[256,1024]{1,0:T(8,128)(2,1)}, bf16[256,1024]{1,0:T(8,128)(2,1)}, u32[]{:S(2)}, u32[]{:S(2)}) %collective-permute-start.19) | collective-permute-done | bytes 524320 | tf_op jit(solution)/shard_map/ppermute | solution.py:26
  278.8 9.1 %grad_act.1.refs_2_ = bf16[1024,2048]{1,0:T(8,128)(2,1)} custom-call(bf16[256,1024]{1,0:T(8,128)(2,1)S(1)} %copy-done.13, bf16[256,1024]{1,0:T(8,128)(2,1)S(1)} %collective-permute-done.16.refs_1_, bf16[256,1024]{1,0:T(8,128)(2,1)S(1)} %collective-permute-done.17.refs_2_, bf16[256,1024]{1,0:T(8,128)(2,1)S(1)} %collective-permute-done.18.refs_3_, ...), custom_call_target="tpu_custom_call" | custom-call | flops 4294967296 | bytes 10485760 | tf_op jit(solution)/shard_map/grad_act/pallas_call | solution.py:563
  288.0 11.2 %feed.3 = (bf16[512,2048]{1,0:T(8,128)(2,1)S(1)}, bf16[512,2048]{1,0:T(8,128)(2,1)}, f32[1,2048]{1,0:T(1,128)S(1)}, f32[256,1024]{1,0:T(8,128)S(1)}, bf16[256,1024]{1,0:T(8,128)(2,1)S(1)}) custom-call(bf16[256,1024]{1,0:T(8,128)(2,1)} %collective-permute-done.19.refs_0_.refs_2_, bf16[256,1024]{1,0:T(8,128)(2,1)} %collective-permute-done.20.refs_1_.refs_3_, ...), custom_call_target="tpu_custom_call" | custom-call | flops 4294967296 | bytes 12582912 | tf_op jit(solution)/shard_map/feed/pallas_call | solution.py:604
  300.5 11.2 %feed.2 = (bf16[512,2048]{1,0:T(8,128)(2,1)S(1)}, bf16[512,2048]{1,0:T(8,128)(2,1)}, f32[1,2048]{1,0:T(1,128)S(1)}, f32[256,1024]{1,0:T(8,128)S(1)}, bf16[256,1024]{1,0:T(8,128)(2,1)}) custom-call(bf16[256,1024]{1,0:T(8,128)(2,1)} %get-tuple-element.70.refs_0_, bf16[256,1024]{1,0:T(8,128)(2,1)} %collective-permute-done.15.refs_1_, ...), custom_call_target="tpu_custom_call" | custom-call | flops 4294967296 | bytes 12582912 | tf_op jit(solution)/shard_map/feed/pallas_call | solution.py:604
  315.6 9.3 %outer.3.refs_18_ = bf16[1024,2048]{1,0:T(8,128)(2,1)} custom-call(s32[4]{0:T(128)S(1)} %pad_add_fusion.info, bf16[256,1024]{1,0:T(8,128)(2,1)} %get-tuple-element.70.refs_0_, bf16[256,1024]{1,0:T(8,128)(2,1)} %collective-permute-done.15.refs_1_, bf16[256,1024]{1,0:T(8,128)(2,1)} %collective-permute-done.19.refs_0_.refs_2_, ...), custom_call_target="tpu_custom_call" | custom-call | flops 4294967296 | bytes 10485760 | tf_op jit(solution)/shard_map/outer/pallas_call | solution.py:659
  328.0 5.6 outer.4.refs_19_
  333.5 3.9 collective-permute-start.24
  337.6 3.9 collective-permute-done.23
  343.5 13.3 %middle_backward.1 = (f32[256,1024]{1,0:T(8,128)S(1)}, bf16[256,1024]{1,0:T(8,128)(2,1)S(1)}, bf16[256,1024]{1,0:T(8,128)(2,1)S(1)}, bf16[1024,256]{1,0:T(8,128)...) custom-call(s32[4]{0:T(128)S(1)} %pad_add_fusion.info, ...), custom_call_target="tpu_custom_call" | custom-call | flops 1610612736 | bytes 16777216 | tf_op jit(solution)/shard_map/middle_backward/pallas_call | solution.py:522
  361.0 10.1 %all-to-all-start.6 = ((bf16[16,64,256]{2,1,0:T(8,128)(2,1)}), bf16[16,64,256]{2,1,0:T(8,128)(2,1)}, u32[]{:S(2)}, u32[]{:S(2)}) async-start(bf16[16,64,256]{2,1,0:T(8,128)(2,1)} %bitcast.140), calls=%async_computation.6 | async-start | bytes 1048576 | tf_op jit(solution)/shard_map/all_to_all | solution.py:843
  377.4 3.7 middle_outer.1
  390.4 29.1 %self_backward.2 = (f32[4,64,1024]{2,1,0:T(8,128)S(1)}, bf16[1,4,64,1024]{3,2,1,0:T(8,128)(2,1)}, bf16[1,4,64,1024]{3,2,1,0:T(8,128)(2,1)}) custom-call(s32[4]{0:T(128)S(1)} %pad_add_fusion.info, bf16[4,64,1024]{2,1,0:T(8,128)(2,1)S(1)} %all-to-all-done.2.refs_0_, bf16[16,64,256]{2,1,0:T(8,128)(2,1)} %all-to-all-done.6.refs_1_, ...), custom_call_target="tpu_custom_call" | custom-call | flops 536870912 | bytes 65536 | tf_op jit(solution)/shard_map/self_backward/pallas_call | solution.py:345
  424.8 5.8 outer.5.refs_8_
  432.7 8.6 %reduce-scatter.6.cloned.1.call-done = bf16[128,2048]{1,0:T(8,128)(2,1)} async-done(((bf16[1024,2048]{1,0:T(8,128)(2,1)}), bf16[128,2048]{1,0:T(8,128)(2,1)}) %reduce-scatter.6.cloned.1.call-update) | async-done | bytes 524304 | tf_op jit(solution)/shard_map/reduce_scatter | solution.py:910
  452.8 3.0 add_convert_fusion
  457.3 32.0 %self_backward.3 = (bf16[4,64,1024]{2,1,0:T(8,128)(2,1)S(1)}, f32[1,4,64,1024]{3,2,1,0:T(8,128)S(1)}, f32[1,4,64,1024]{3,2,1,0:T(8,128)S(1)}) custom-call(s32[4]{0:T(128)S(1)} %pad_add_fusion.info, bf16[4,64,1024]{2,1,0:T(8,128)(2,1)S(1)} %all-to-all-done.2.refs_0_, bf16[16,64,256]{2,1,0:T(8,128)(2,1)} %all-to-all-done.6.refs_1_, ...), custom_call_target="tpu_custom_call" | custom-call | flops 536870912 | bytes 65536 | tf_op jit(solution)/shard_map/self_backward/pallas_call | solution.py:345
  490.1 4.8 convolution_convert_fusion.3
  502.6 4.5 all-to-all-start.7
  507.4 3.6 add_convert_fusion.3
  519.0 5.7 collective-permute-done.27
  525.8 18.4 %collective-permute-done.45 = bf16[512,768]{1,0:T(8,128)(2,1)S(1)} collective-permute-done((bf16[512,768]{1,0:T(8,128)(2,1)S(1)}, bf16[512,768]{1,0:T(8,128)(2,1)S(1)}, u32[]{:S(2)}, u32[]{:S(2)}) %collective-permute-start.45) | collective-permute-done | bytes 786464 | tf_op jit(solution)/shard_map/ppermute | solution.py:26
  551.1 4.4 convolution_convert_fusion.refs_1_
  565.4 4.8 all-to-all-start.8
  577.9 2.6 fusion.2
  587.1 10.4 %collective-permute-done.41 = bf16[1,64,1024]{2,1,0:T(8,128)(2,1)} collective-permute-done((bf16[1,64,1024]{2,1,0:T(8,128)(2,1)}, bf16[1,64,1024]{2,1,0:T(8,128)(2,1)}, u32[]{:S(2)}, u32[]{:S(2)}) %collective-permute-start.41) | collective-permute-done | bytes 131104 | tf_op jit(solution)/shard_map/ppermute | solution.py:26
  610.9 13.4 %all-to-all-start.9 = ((f32[32,1,672]{2,1,0:T(1,128)}), f32[32,1,672]{2,1,0:T(1,128)S(1)}, u32[]{:S(2)}, u32[]{:S(2)}) async-start(f32[32,1,672]{2,1,0:T(1,128)} %copy.80), calls=%async_computation.11 | async-start | bytes 196608 | tf_op jit(solution)/shard_map/all_to_all | solution.py:1029
  627.1 5.0 all-to-all-done.9
  (503 shorter events, 165.4 us)
Async XLA Ops:
  7.2 73.3 %all-gather.4.cloned.1.call-start = ((), (), s32[]{:S(2)}) async-start(), calls=%async_computation.13 | async-start | bytes 1769472 | tf_op jit(solution)/shard_map/all_gather | solution.py:777
  15.7 15.0 %all-to-all-start = ((bf16[32,2,464]{2,1,0:T(2,128)(2,1)}), bf16[32,2,464]{2,1,0:T(2,128)(2,1)S(1)}, u32[]{:S(2)}, u32[]{:S(2)}) async-start(bf16[32,2,464]{2,1,0:T(2,128)(2,1)} %reshape.316), calls=%async_computation | async-start | bytes 131072 | tf_op jit(solution)/shard_map/all_to_all | solution.py:806
  31.9 48.7 %all-to-all-start.1 = ((bf16[4,128,1280]{2,1,0:T(8,128)(2,1)}), bf16[4,128,1280]{2,1,0:T(8,128)(2,1)S(1)}, u32[]{:S(2)}, u32[]{:S(2)}) async-start(bf16[4,128,1280]{2,1,0:T(8,128)(2,1)} %broadcast_in_dim.25), calls=%async_computation.1 | async-start | bytes 2621440 | tf_op jit(solution)/shard_map/all_to_all | solution.py:780
  35.6 243.3 %all-gather.6.cloned.1.call-start = ((), (), s32[]{:S(2)}) async-start(), calls=%async_computation.14 | async-start | bytes 4718592 | tf_op jit(solution)/shard_map/all_gather | solution.py:777
  35.6 14.5 %collective-permute-start.1 = (bf16[256,1024]{1,0:T(8,128)(2,1)S(1)}, bf16[256,1024]{1,0:T(8,128)(2,1)S(1)}, u32[]{:S(2)}, u32[]{:S(2)}) collective-permute-start(bf16[256,1024]{1,0:T(8,128)(2,1)S(1)} %copy-done.9), channel_id=1, source_target_pairs={{0,2},{1,3},{2,0},{3,1},{4,6},{5,7},{6,4},{7,5},{8,10},{9,11},{10,... | collective-permute-start | bytes 1572872 | tf_op jit(solution)/shard_map/ppermute | solution.py:26
  36.9 15.6 %collective-permute-start = (bf16[256,1024]{1,0:T(8,128)(2,1)S(1)}, bf16[256,1024]{1,0:T(8,128)(2,1)S(1)}, u32[]{:S(2)}, u32[]{:S(2)}) collective-permute-start(bf16[256,1024]{1,0:T(8,128)(2,1)S(1)} %copy-done.9), channel_id=1, source_target_pairs={{0,1},{1,0},{2,3},{3,2},{4,5},{5,4},{6,7},{7,6},{8,9},{9,8},{10,11... | collective-permute-start | bytes 1572872 | tf_op jit(solution)/shard_map/ppermute | solution.py:26
  89.9 198.1 %all-gather.8.cloned.1.call-start = ((), (), s32[]{:S(2)}) async-start(), calls=%async_computation.15 | async-start | bytes 4718592 | tf_op jit(solution)/shard_map/all_gather | solution.py:777
  89.9 50.0 %collective-permute-start.5 = (bf16[4,128,1280]{2,1,0:T(8,128)(2,1)S(1)}, bf16[4,128,1280]{2,1,0:T(8,128)(2,1)}, u32[]{:S(2)}, u32[]{:S(2)}) collective-permute-start(bf16[4,128,1280]{2,1,0:T(8,128)(2,1)S(1)} %all-to-all-done.1.refs_7_), channel_id=1, source_target_pairs={{0,4},{4,0},{8,12},{12,8},{16,20},{20,16},{24,28},{28,24},{1,5},{5... | collective-permute-start | bytes 3932168 | tf_op jit(solution)/shard_map/ppermute | solution.py:26
  90.6 30.7 %all-to-all-start.3 = ((bf16[4,64,1024]{2,1,0:T(8,128)(2,1)}), bf16[4,64,1024]{2,1,0:T(8,128)(2,1)S(1)}, u32[]{:S(2)}, u32[]{:S(2)}) async-start(bf16[4,64,1024]{2,1,0:T(8,128)(2,1)} %get-tuple-element.65), calls=%async_computation.3 | async-start | bytes 1048576 | tf_op jit(solution)/shard_map/all_to_all | solution.py:840
  121.3 22.1 %all-to-all-start.4 = ((bf16[4,64,1024]{2,1,0:T(8,128)(2,1)}), bf16[4,64,1024]{2,1,0:T(8,128)(2,1)S(1)}, u32[]{:S(2)}, u32[]{:S(2)}) async-start(bf16[4,64,1024]{2,1,0:T(8,128)(2,1)} %copy-done.52), calls=%async_computation.4 | async-start | bytes 1048576 | tf_op jit(solution)/shard_map/all_to_all | solution.py:840
  144.2 26.9 %all-to-all-start.2 = ((bf16[4,64,1024]{2,1,0:T(8,128)(2,1)}), bf16[4,64,1024]{2,1,0:T(8,128)(2,1)S(1)}, u32[]{:S(2)}, u32[]{:S(2)}) async-start(bf16[4,64,1024]{2,1,0:T(8,128)(2,1)} %get-tuple-element.64), calls=%async_computation.2 | async-start | bytes 1048576 | tf_op jit(solution)/shard_map/all_to_all | solution.py:840
  149.7 28.0 %collective-permute-start.3 = (bf16[4,64,1024]{2,1,0:T(8,128)(2,1)S(1)}, bf16[4,64,1024]{2,1,0:T(8,128)(2,1)}, u32[]{:S(2)}, u32[]{:S(2)}) collective-permute-start(bf16[4,64,1024]{2,1,0:T(8,128)(2,1)S(1)} %all-to-all-done.3.refs_2_.refs_4_), channel_id=1, source_target_pairs={{0,4},{4,0},{8,12},{12,8},{16,20},{20,16},{24,28},{28,24},{1,5},{5... | collective-permute-start | bytes 1572872 | tf_op jit(solution)/shard_map/ppermute | solution.py:26
  149.7 38.3 %collective-permute-start.4 = (bf16[4,64,1024]{2,1,0:T(8,128)(2,1)S(1)}, bf16[4,64,1024]{2,1,0:T(8,128)(2,1)}, u32[]{:S(2)}, u32[]{:S(2)}) collective-permute-start(bf16[4,64,1024]{2,1,0:T(8,128)(2,1)S(1)} %copy-done.21), channel_id=1, source_target_pairs={{0,4},{4,0},{8,12},{12,8},{16,20},{20,16},{24,28},{28,24},{1,5},{5... | collective-permute-start | bytes 1572872 | tf_op jit(solution)/shard_map/ppermute | solution.py:26
  155.9 15.1 %collective-permute-start.11 = (bf16[2,256,256]{2,1,0:T(8,128)(2,1)S(1)}, bf16[2,256,256]{2,1,0:T(8,128)(2,1)S(1)}, u32[]{:S(2)}, u32[]{:S(2)}) collective-permute-start(bf16[2,256,256]{2,1,0:T(8,128)(2,1)S(1)} %collective-permute-done.10.refs_8_.refs_10_.refs_16_), channel_id=1, source_target_pairs={{0,1},{1,0},{2,3},{3,2},{4,5},{5,4},{6,7},{7,6},{8,9},{9,8},{10,11... | collective-permute-start | bytes 786440 | tf_op jit(solution)/shard_map/ppermute | solution.py:26
  158.8 57.9 %collective-permute-start.13 = (bf16[3,1024,256]{2,1,0:T(8,128)(2,1)}, bf16[3,1024,256]{2,1,0:T(8,128)(2,1)}, u32[]{:S(2)}, u32[]{:S(2)}) collective-permute-start(bf16[3,1024,256]{2,1,0:T(8,128)(2,1)} %pad_maximum_fusion.1.refs_4_.refs_10_), channel_id=1, source_target_pairs={{0,2},{1,3},{2,0},{3,1},{4,6},{5,7},{6,4},{7,5},{8,10},{9,11},{10,... | collective-permute-start | bytes 4718600 | tf_op jit(solution)/shard_map/ppermute | solution.py:26
  158.8 66.5 %collective-permute-start.12 = (bf16[3,1024,256]{2,1,0:T(8,128)(2,1)}, bf16[3,1024,256]{2,1,0:T(8,128)(2,1)}, u32[]{:S(2)}, u32[]{:S(2)}) collective-permute-start(bf16[3,1024,256]{2,1,0:T(8,128)(2,1)} %pad_maximum_fusion.1.refs_4_.refs_10_), channel_id=1, source_target_pairs={{0,1},{1,0},{2,3},{3,2},{4,5},{5,4},{6,7},{7,6},{8,9},{9,8},{10,11... | collective-permute-start | bytes 4718600 | tf_op jit(solution)/shard_map/ppermute | solution.py:26
  216.7 27.5 %collective-permute-start.14 = (bf16[3,1024,256]{2,1,0:T(8,128)(2,1)}, bf16[3,1024,256]{2,1,0:T(8,128)(2,1)}, u32[]{:S(2)}, u32[]{:S(2)}) collective-permute-start(bf16[3,1024,256]{2,1,0:T(8,128)(2,1)} %tie.11.refs_6_.refs_12_), channel_id=1, source_target_pairs={{0,1},{1,0},{2,3},{3,2},{4,5},{5,4},{6,7},{7,6},{8,9},{9,8},{10,11... | collective-permute-start | bytes 4718600 | tf_op jit(solution)/shard_map/ppermute | solution.py:26
  216.8 27.4 %all-to-all-start.5 = ((bf16[16,64,256]{2,1,0:T(8,128)(2,1)}), bf16[16,64,256]{2,1,0:T(8,128)(2,1)S(1)}, u32[]{:S(2)}, u32[]{:S(2)}) async-start(bf16[16,64,256]{2,1,0:T(8,128)(2,1)} %get-tuple-element.67.refs_2_), calls=%async_computation.5 | async-start | bytes 1048576 | tf_op jit(solution)/shard_map/all_to_all | solution.py:843
  221.1 220.2 %reduce-scatter.6.cloned.1.call-start = ((), (), s32[]{:S(2)}) async-start(), calls=%async_computation.16 | async-start | bytes 4718592 | tf_op jit(solution)/shard_map/reduce_scatter | solution.py:910
  221.3 44.9 %collective-permute-start.17 = (bf16[256,1024]{1,0:T(8,128)(2,1)S(1)}, bf16[256,1024]{1,0:T(8,128)(2,1)S(1)}, u32[]{:S(2)}, u32[]{:S(2)}) collective-permute-start(bf16[256,1024]{1,0:T(8,128)(2,1)S(1)} %copy-done.13), channel_id=1, source_target_pairs={{0,2},{1,3},{2,0},{3,1},{4,6},{5,7},{6,4},{7,5},{8,10},{9,11},{10,... | collective-permute-start | bytes 1572872 | tf_op jit(solution)/shard_map/ppermute | solution.py:26
  262.8 13.8 %collective-permute-start.19 = (bf16[256,1024]{1,0:T(8,128)(2,1)}, bf16[256,1024]{1,0:T(8,128)(2,1)}, u32[]{:S(2)}, u32[]{:S(2)}) collective-permute-start(bf16[256,1024]{1,0:T(8,128)(2,1)} %get-tuple-element.70.refs_0_), channel_id=1, source_target_pairs={{0,2},{1,3},{2,0},{3,1},{4,6},{5,7},{6,4},{7,5},{8,10},{9,11},{10,... | collective-permute-start | bytes 1572872 | tf_op jit(solution)/shard_map/ppermute | solution.py:26
  263.4 15.4 %collective-permute-start.16 = (bf16[256,1024]{1,0:T(8,128)(2,1)S(1)}, bf16[256,1024]{1,0:T(8,128)(2,1)S(1)}, u32[]{:S(2)}, u32[]{:S(2)}) collective-permute-start(bf16[256,1024]{1,0:T(8,128)(2,1)S(1)} %copy-done.13), channel_id=1, source_target_pairs={{0,1},{1,0},{2,3},{3,2},{4,5},{5,4},{6,7},{7,6},{8,9},{9,8},{10,11... | collective-permute-start | bytes 1572872 | tf_op jit(solution)/shard_map/ppermute | solution.py:26
  278.7 21.9 %collective-permute-start.15 = (bf16[256,1024]{1,0:T(8,128)(2,1)}, bf16[256,1024]{1,0:T(8,128)(2,1)}, u32[]{:S(2)}, u32[]{:S(2)}) collective-permute-start(bf16[256,1024]{1,0:T(8,128)(2,1)} %get-tuple-element.70.refs_0_), channel_id=1, source_target_pairs={{0,1},{1,0},{2,3},{3,2},{4,5},{5,4},{6,7},{7,6},{8,9},{9,8},{10,11... | collective-permute-start | bytes 1572872 | tf_op jit(solution)/shard_map/ppermute | solution.py:26
  327.3 14.3 %collective-permute-start.23 = (bf16[256,1024]{1,0:T(8,128)(2,1)S(1)}, bf16[256,1024]{1,0:T(8,128)(2,1)S(1)}, u32[]{:S(2)}, u32[]{:S(2)}) collective-permute-start(bf16[256,1024]{1,0:T(8,128)(2,1)S(1)} %add_convert_fusion.5), channel_id=1, source_target_pairs={{0,2},{1,3},{2,0},{3,1},{4,6},{5,7},{6,4},{7,5},{8,10},{9,11},{10,... | collective-permute-start | bytes 1572872 | tf_op jit(solution)/shard_map/ppermute | solution.py:26
  333.5 86.9 %collective-permute-start.24 = (bf16[512,2048]{1,0:T(8,128)(2,1)S(1)}, bf16[512,2048]{1,0:T(8,128)(2,1)}, u32[]{:S(2)}, u32[]{:S(2)}) collective-permute-start(bf16[512,2048]{1,0:T(8,128)(2,1)S(1)} %outer.4.refs_19_), channel_id=1, source_target_pairs={{0,4},{4,0},{8,12},{12,8},{16,20},{20,16},{24,28},{28,24},{1,5},{5... | collective-permute-start | bytes 6291464 | tf_op jit(solution)/shard_map/ppermute | solution.py:26
  361.0 29.5 %all-to-all-start.6 = ((bf16[16,64,256]{2,1,0:T(8,128)(2,1)}), bf16[16,64,256]{2,1,0:T(8,128)(2,1)}, u32[]{:S(2)}, u32[]{:S(2)}) async-start(bf16[16,64,256]{2,1,0:T(8,128)(2,1)} %bitcast.140), calls=%async_computation.6 | async-start | bytes 1048576 | tf_op jit(solution)/shard_map/all_to_all | solution.py:843
  371.1 174.2 %reduce-scatter.10.cloned.1.call-start = ((), (), s32[]{:S(2)}) async-start(), calls=%async_computation.18 | async-start | bytes 2621440
  381.1 71.7 %collective-permute-start.43 = (bf16[1024,768]{1,0:T(8,128)(2,1)}, bf16[1024,768]{1,0:T(8,128)(2,1)}, u32[]{:S(2)}, u32[]{:S(2)}) collective-permute-start(bf16[1024,768]{1,0:T(8,128)(2,1)} %get-tuple-element.98.refs_9_), channel_id=1, source_target_pairs={{0,1},{1,0},{2,3},{3,2},{4,5},{5,4},{6,7},{7,6},{8,9},{9,8},{10,11... | collective-permute-start | bytes 4718600 | tf_op jit(solution)/shard_map/ppermute | solution.py:26
  385.4 62.5 %collective-permute-start.30 = (bf16[2,256,256]{2,1,0:T(8,128)(2,1)}, bf16[2,256,256]{2,1,0:T(8,128)(2,1)}, u32[]{:S(2)}, u32[]{:S(2)}) collective-permute-start(bf16[2,256,256]{2,1,0:T(8,128)(2,1)} %get-tuple-element.186), channel_id=1, source_target_pairs={{0,1},{1,0},{2,3},{3,2},{4,5},{5,4},{6,7},{7,6},{8,9},{9,8},{10,11... | collective-permute-start | bytes 786440 | tf_op jit(solution)/shard_map/ppermute | solution.py:26
  387.4 59.8 %collective-permute-start.32 = (bf16[2,256,256]{2,1,0:T(8,128)(2,1)}, bf16[2,256,256]{2,1,0:T(8,128)(2,1)S(1)}, u32[]{:S(2)}, u32[]{:S(2)}) collective-permute-start(bf16[2,256,256]{2,1,0:T(8,128)(2,1)} %fusion.52), channel_id=1, source_target_pairs={{0,2},{1,3},{2,0},{3,1},{4,6},{5,7},{6,4},{7,5},{8,10},{9,11},{10,... | collective-permute-start | bytes 786440 | tf_op jit(solution)/shard_map/ppermute | solution.py:26
  446.4 65.2 %collective-permute-start.42 = (bf16[1024,768]{1,0:T(8,128)(2,1)}, bf16[1024,768]{1,0:T(8,128)(2,1)}, u32[]{:S(2)}, u32[]{:S(2)}) collective-permute-start(bf16[1024,768]{1,0:T(8,128)(2,1)} %get-tuple-element.96.refs_7_), channel_id=1, source_target_pairs={{0,1},{1,0},{2,3},{3,2},{4,5},{5,4},{6,7},{7,6},{8,9},{9,8},{10,11... | collective-permute-start | bytes 4718600 | tf_op jit(solution)/shard_map/ppermute | solution.py:26
  449.2 45.7 %collective-permute-start.33 = (bf16[1,2,256,256]{3,2,1,0:T(8,128)(2,1)S(1)}, bf16[1,2,256,256]{3,2,1,0:T(8,128)(2,1)S(1)}, u32[]{:S(2)}, u32[]{:S(2)}) collective-permute-start(bf16[1,2,256,256]{3,2,1,0:T(8,128)(2,1)S(1)} %fusion.59), channel_id=1, source_target_pairs={{0,4},{4,0},{8,12},{12,8},{16,20},{20,16},{24,28},{28,24},{1,5},{5... | collective-permute-start | bytes 786440 | tf_op jit(solution)/shard_map/ppermute | solution.py:26
  450.8 47.0 %collective-permute-start.28 = (bf16[4,64,1024]{2,1,0:T(8,128)(2,1)}, bf16[4,64,1024]{2,1,0:T(8,128)(2,1)}, u32[]{:S(2)}, u32[]{:S(2)}) collective-permute-start(bf16[4,64,1024]{2,1,0:T(8,128)(2,1)} %bitcast.35), channel_id=1, source_target_pairs={{0,4},{4,0},{8,12},{12,8},{16,20},{20,16},{24,28},{28,24},{1,5},{5... | collective-permute-start | bytes 1572872 | tf_op jit(solution)/shard_map/ppermute | solution.py:26
  451.3 47.0 %collective-permute-start.29 = (bf16[4,64,1024]{2,1,0:T(8,128)(2,1)}, bf16[4,64,1024]{2,1,0:T(8,128)(2,1)}, u32[]{:S(2)}, u32[]{:S(2)}) collective-permute-start(bf16[4,64,1024]{2,1,0:T(8,128)(2,1)} %bitcast.36), channel_id=1, source_target_pairs={{0,4},{4,0},{8,12},{12,8},{16,20},{20,16},{24,28},{28,24},{1,5},{5... | collective-permute-start | bytes 1572872 | tf_op jit(solution)/shard_map/ppermute | solution.py:26
  455.8 55.8 %collective-permute-start.44 = (bf16[1024,768]{1,0:T(8,128)(2,1)}, bf16[1024,768]{1,0:T(8,128)(2,1)}, u32[]{:S(2)}, u32[]{:S(2)}) collective-permute-start(bf16[1024,768]{1,0:T(8,128)(2,1)} %add_convert_fusion), channel_id=1, source_target_pairs={{0,2},{1,3},{2,0},{3,1},{4,6},{5,7},{6,4},{7,5},{8,10},{9,11},{10,... | collective-permute-start | bytes 4718600 | tf_op jit(solution)/shard_map/ppermute | solution.py:26
  497.8 17.9 %collective-permute-start.25 = (bf16[256,1024]{1,0:T(8,128)(2,1)}, bf16[256,1024]{1,0:T(8,128)(2,1)}, u32[]{:S(2)}, u32[]{:S(2)}) collective-permute-start(bf16[256,1024]{1,0:T(8,128)(2,1)} %convolution_convert_fusion.4), channel_id=1, source_target_pairs={{0,1},{1,0},{2,3},{3,2},{4,5},{5,4},{6,7},{7,6},{8,9},{9,8},{10,11... | collective-permute-start | bytes 1572872 | tf_op jit(solution)/shard_map/ppermute | solution.py:26
  498.3 49.5 %collective-permute-start.34 = (bf16[1,2,256,256]{3,2,1,0:T(8,128)(2,1)}, bf16[1,2,256,256]{3,2,1,0:T(8,128)(2,1)}, u32[]{:S(2)}, u32[]{:S(2)}) collective-permute-start(bf16[1,2,256,256]{3,2,1,0:T(8,128)(2,1)} %add_convert_fusion.9), channel_id=1, source_target_pairs={{0,8},{4,12},{8,0},{12,4},{16,24},{20,28},{24,16},{28,20},{1,9},{5... | collective-permute-start | bytes 786440 | tf_op jit(solution)/shard_map/ppermute | solution.py:26
  502.6 45.2 %all-to-all-start.7 = ((bf16[4,3,64,1024]{3,2,1,0:T(8,128)(2,1)}), bf16[4,3,64,1024]{3,2,1,0:T(8,128)(2,1)}, u32[]{:S(2)}, u32[]{:S(2)}) async-start(bf16[4,3,64,1024]{3,2,1,0:T(8,128)(2,1)} %combine.1), calls=%async_computation.8 | async-start | bytes 3145728 | tf_op jit(solution)/shard_map/all_to_all | solution.py:840
  507.1 97.7 %reduce-scatter.8.cloned.1.call-start = ((), (), s32[]{:S(2)}) async-start(), calls=%async_computation.17 | async-start | bytes 983040 | tf_op jit(solution)/shard_map/reduce_scatter | solution.py:913
  511.0 13.7 %collective-permute-start.27 = (bf16[256,1024]{1,0:T(8,128)(2,1)S(1)}, bf16[256,1024]{1,0:T(8,128)(2,1)S(1)}, u32[]{:S(2)}, u32[]{:S(2)}) collective-permute-start(bf16[256,1024]{1,0:T(8,128)(2,1)S(1)} %add_convert_fusion.3), channel_id=1, source_target_pairs={{0,2},{1,3},{2,0},{3,1},{4,6},{5,7},{6,4},{7,5},{8,10},{9,11},{10,... | collective-permute-start | bytes 1572872 | tf_op jit(solution)/shard_map/ppermute | solution.py:26
  515.1 29.1 %collective-permute-start.45 = (bf16[512,768]{1,0:T(8,128)(2,1)S(1)}, bf16[512,768]{1,0:T(8,128)(2,1)S(1)}, u32[]{:S(2)}, u32[]{:S(2)}) collective-permute-start(bf16[512,768]{1,0:T(8,128)(2,1)S(1)} %pad_maximum_fusion.2), channel_id=1, source_target_pairs={{0,4},{4,0},{8,12},{12,8},{16,20},{20,16},{24,28},{28,24},{1,5},{5... | collective-permute-start | bytes 2359304 | tf_op jit(solution)/shard_map/ppermute | solution.py:26
  549.0 23.6 %collective-permute-start.38 = (bf16[1,2,256,256]{3,2,1,0:T(8,128)(2,1)S(1)}, bf16[1,2,256,256]{3,2,1,0:T(8,128)(2,1)}, u32[]{:S(2)}, u32[]{:S(2)}) collective-permute-start(bf16[1,2,256,256]{3,2,1,0:T(8,128)(2,1)S(1)} %add_convert_fusion.8), channel_id=1, source_target_pairs={{0,16},{4,20},{8,24},{12,28},{16,0},{20,4},{24,8},{28,12},{1,17},{... | collective-permute-start | bytes 786440 | tf_op jit(solution)/shard_map/ppermute | solution.py:26
  559.3 18.6 %collective-permute-start.36 = (bf16[256,1024]{1,0:T(8,128)(2,1)}, bf16[256,1024]{1,0:T(8,128)(2,1)}, u32[]{:S(2)}, u32[]{:S(2)}) collective-permute-start(bf16[256,1024]{1,0:T(8,128)(2,1)} %convolution_convert_fusion.1), channel_id=1, source_target_pairs={{0,1},{1,0},{2,3},{3,2},{4,5},{5,4},{6,7},{7,6},{8,9},{9,8},{10,11... | collective-permute-start | bytes 1572872 | tf_op jit(solution)/shard_map/ppermute | solution.py:26
  561.8 38.0 %collective-permute-start.35 = (bf16[256,1024]{1,0:T(8,128)(2,1)}, bf16[256,1024]{1,0:T(8,128)(2,1)}, u32[]{:S(2)}, u32[]{:S(2)}) collective-permute-start(bf16[256,1024]{1,0:T(8,128)(2,1)} %convolution_convert_fusion.2), channel_id=1, source_target_pairs={{0,1},{1,0},{2,3},{3,2},{4,5},{5,4},{6,7},{7,6},{8,9},{9,8},{10,11... | collective-permute-start | bytes 1572872 | tf_op jit(solution)/shard_map/ppermute | solution.py:26
  565.4 43.9 %all-to-all-start.8 = ((bf16[8,128,768]{2,1,0:T(8,128)(2,1)}), bf16[8,128,768]{2,1,0:T(8,128)(2,1)}, u32[]{:S(2)}, u32[]{:S(2)}) async-start(bf16[8,128,768]{2,1,0:T(8,128)(2,1)} %bitcast.149), calls=%async_computation.9 | async-start | bytes 3145728 | tf_op jit(solution)/shard_map/all_to_all | solution.py:990
  580.5 19.2 %collective-permute-start.37 = (bf16[256,1024]{1,0:T(8,128)(2,1)}, bf16[256,1024]{1,0:T(8,128)(2,1)}, u32[]{:S(2)}, u32[]{:S(2)}) collective-permute-start(bf16[256,1024]{1,0:T(8,128)(2,1)} %fusion.2), channel_id=1, source_target_pairs={{0,2},{1,3},{2,0},{3,1},{4,6},{5,7},{6,4},{7,5},{8,10},{9,11},{10,... | collective-permute-start | bytes 1572872 | tf_op jit(solution)/shard_map/ppermute | solution.py:26
  582.1 15.4 %collective-permute-start.41 = (bf16[1,64,1024]{2,1,0:T(8,128)(2,1)}, bf16[1,64,1024]{2,1,0:T(8,128)(2,1)}, u32[]{:S(2)}, u32[]{:S(2)}) collective-permute-start(bf16[1,64,1024]{2,1,0:T(8,128)(2,1)} %fusion.40), channel_id=1, source_target_pairs={{0,2},{1,3},{2,0},{3,1},{4,6},{5,7},{6,4},{7,5},{8,10},{9,11},{10,... | collective-permute-start | bytes 393224 | tf_op jit(solution)/shard_map/ppermute | solution.py:26
  610.9 21.3 %all-to-all-start.9 = ((f32[32,1,672]{2,1,0:T(1,128)}), f32[32,1,672]{2,1,0:T(1,128)S(1)}, u32[]{:S(2)}, u32[]{:S(2)}) async-start(f32[32,1,672]{2,1,0:T(1,128)} %copy.80), calls=%async_computation.11 | async-start | bytes 196608 | tf_op jit(solution)/shard_map/all_to_all | solution.py:1029
  (134 other events, 1032.8 us)
Sparse Core Ops, SparseCore 0:
  12.3 62.2 all-gather.3
  90.0 98.1 all-gather.5
  191.0 79.7 all-gather.7
  325.1 116.1 reduce-scatter.5
  443.6 43.6 reduce-scatter.9
  547.8 28.2 reduce-scatter.7

commit v5 on v4

--- a/solution.py
+++ b/solution.py
@@ -878,8 +878,8 @@
     )
 
     cot_blocks = gather_xor(cotangent)
-    h_blocks = gather_xor(h_three)
     grad_a = grad_act(cot_blocks, w_down)
+    h_blocks = gather_xor(h_three, lambda got: tie([got], [grad_a])[0])
     near = group // 2
     bias_row = bias_up[None]
     near_out = feed(h_blocks[:near], grad_a, w_up, bias_row, 0)
@@ -907,12 +907,12 @@
         )
 
     def reduce_tok(value):
-        return lax.psum_scatter(value, "tok", scatter_dimension=0, tiled=True).astype(f32)
+        return lax.psum_scatter(value, "tok", scatter_dimension=0, tiled=True)
 
     def reduce_half(value):
         return lax.psum_scatter(
             value, "tok", scatter_dimension=0, tiled=True, axis_index_groups=halves
-        ).astype(f32)
+        )
 
     grad_up = outer(h_blocks, grad_inners, info)
     down_away = outer(cot_blocks, acts, info, 1, many)
@@ -940,7 +940,7 @@
     )
     down_got = tie([down_got], [grad_q_away])[0]
     down_sum = outer(cot_blocks, acts, info, 0, many, down_got)
-    sent_down = reduce_half(tie([down_sum], [sent_up])[0]).T
+    sent_down = reduce_half(tie([down_sum], [sent_up])[0])
     kv_total = reduce_xor(
         [grad_kv_two[j] for j in range(group)], lambda got: tie([got], [grad_q_away])[0]
     )
@@ -1030,6 +1030,7 @@
     columns = vectors[: 13 * few].reshape(13, few)
     columns = columns[jnp.array([8, 9, 5, 7, 10, 4, 6, 11, 2, 0, 12, 3, 1])].T
 
+    sent_mid = sent_mid.astype(f32)
     sent_mid = [sent_mid[:, j * width : (j + 1) * width] for j in range(3)]
     sent_cross = jnp.concatenate(
         [sent_mid[2][:, None], sent_cross_kv.reshape(shard, 2, width)], 1
@@ -1042,8 +1043,8 @@
         sent_mid[0].T,
         sent_cross,
         sent_mid[1].T,
-        sent_up,
-        sent_down,
+        sent_up.astype(f32),
+        sent_down.astype(f32).T,
         columns[:, :7],
         vectors[13 * few :],
         columns[:, 7:10],

time: 653 us -> 641 us (0.982)
  waiting for transfers between devices: 208 us -> 188 us
  local copies, waits for them, and re-layouts: 75.4 us -> 84 us
    all_to_all x2, waiting for transfers between devices: 20 us -> 4.46 us  [across_wide(): lax.all_to_all(value, ('tok', 'hd'), 0, 0, tiled=True, axis_index_groups=...]
    unnamed x254 -> x250, local copies, waits for them, and re-layouts: 49.1 us -> 51.8 us
  transfers between devices with their start and end apart: 62 -> 62, of which waited for: 23 -> 22; matrix products, arithmetic and copies ran while one was open for 15% -> 17% of each run, Pallas kernels for 24% -> 24%
where the time goes in v5:
time: 641 us; the launch traced here: 629 us
  waiting for transfers between devices  188 us (29%)
  Pallas kernels  178 us (28%)
  starting transfers between devices  87.6 us (14%)
  local copies, waits for them, and re-layouts  84 us (13%)
  other arithmetic  38.3 us (6%)
  matrix products  36.9 us (6%)
  between operations  15.8 us (2%)
    ppermute x46, waiting for transfers between devices, swap(): lax.ppermute(value, axis, [(i, i ^ mask) for i in range(lax.axis_size(axi...  112 us
    pallas_call x2, Pallas kernels, self_backward(): pl.pallas_call(functools.partial(self_backward_kernel, heads, sides, own,...  61 us
    unnamed x250, local copies, waits for them, and re-layouts  51.8 us
    dot_general x15, matrix products, dot(): lax.dot_general(left, right, (((left_dim,), (right_dim,)), ((), ())), pre...  36.9 us
    ppermute x46, starting transfers between devices, swap(): lax.ppermute(value, axis, [(i, i ^ mask) for i in range(lax.axis_size(axi...  31.4 us
    all_to_all x4, waiting for transfers between devices, across_lines(): lax.all_to_all(value, 'tok', 0, 0, tiled=True, axis_index_groups=lines)  31.4 us
    pallas_call x1, Pallas kernels, self_forward(): pl.pallas_call(functools.partial(self_forward_kernel, heads, others), gri...  28 us
    pallas_call x2, Pallas kernels, feed(): pl.pallas_call(functools.partial(feed_kernel, first, blocks), in_specs=[V...  22.6 us
  transfers between devices with their start and end apart: 62, of which 22 were waited for; matrix products, arithmetic and copies ran while one was open for 17% of the time, Pallas kernels for 24%

profile of v5, /device:TPU:0, one launch (start us, length us, event | category | flops | bytes accessed | tf_op | source)
XLA Modules:
  0.0 629.1 jit_solution(12035227086752155355)
XLA Ops:
  15.7 7.3 %all-to-all-start = ((bf16[32,2,464]{2,1,0:T(2,128)(2,1)}), bf16[32,2,464]{2,1,0:T(2,128)(2,1)S(1)}, u32[]{:S(2)}, u32[]{:S(2)}) async-start(bf16[32,2,464]{2,1,0:T(2,128)(2,1)} %reshape.314), calls=%async_computation | async-start | bytes 131072 | tf_op jit(solution)/shard_map/all_to_all | solution.py:806
  23.4 7.3 %all-to-all-done = bf16[32,2,464]{2,1,0:T(2,128)(2,1)S(1)} async-done(((bf16[32,2,464]{2,1,0:T(2,128)(2,1)}), bf16[32,2,464]{2,1,0:T(2,128)(2,1)S(1)}, u32[]{:S(2)}, u32[]{:S(2)}) %all-to-all-start) | async-done | bytes 59424 | tf_op jit(solution)/shard_map/all_to_all | solution.py:806
  31.9 3.7 all-to-all-start.1
  38.1 12.0 %collective-permute-done.1.refs_5_ = bf16[256,1024]{1,0:T(8,128)(2,1)S(1)} collective-permute-done((bf16[256,1024]{1,0:T(8,128)(2,1)S(1)}, bf16[256,1024]{1,0:T(8,128)(2,1)S(1)}, u32[]{:S(2)}, u32[]{:S(2)}) %collective-permute-start.1) | collective-permute-done | bytes 524320 | tf_op jit(solution)/shard_map/ppermute | solution.py:26
  50.1 3.8 slice_reduce_fusion
  58.9 21.6 %all-to-all-done.1.refs_7_ = bf16[4,128,1280]{2,1,0:T(8,128)(2,1)S(1)} async-done(((bf16[4,128,1280]{2,1,0:T(8,128)(2,1)}), bf16[4,128,1280]{2,1,0:T(8,128)(2,1)S(1)}, u32[]{:S(2)}, u32[]{:S(2)}) %all-to-all-start.1) | async-done | bytes 1310752 | tf_op jit(solution)/shard_map/all_to_all | solution.py:780
  80.5 6.4 %project.1 = (bf16[4,64,1024]{2,1,0:T(8,128)(2,1)}, bf16[4,64,1024]{2,1,0:T(8,128)(2,1)}, bf16[4,64,1024]{2,1,0:T(8,128)(2,1)}, bf16[1024,1024]{1,0:T(8,128)(2,1)}) custom-call(s32[4]{0:T(128)S(1)} %pad_add_fusion.info, bf16[1024,768]{1,0:T(8,128)(2,1)} %all-gather.4.cloned.1.call-done.refs_0_, f32[2,1024]{1,0:T(2,128)S(1)} %pad_maximum_fusion.9.refs_1_, ...), custom_call_target="tpu_custom_call" | custom-call | flops 1610612736 | bytes 8388608 | tf_op jit(solution)/shard_map/project/pallas_call | solution.py:127
  89.8 3.6 all-to-all-start.3
  93.9 4.6 collective-permute-done.7
  100.8 19.7 %all-to-all-done.3.refs_2_.refs_4_ = bf16[4,64,1024]{2,1,0:T(8,128)(2,1)S(1)} async-done(((bf16[4,64,1024]{2,1,0:T(8,128)(2,1)}), bf16[4,64,1024]{2,1,0:T(8,128)(2,1)S(1)}, u32[]{:S(2)}, u32[]{:S(2)}) %all-to-all-start.3) | async-done | bytes 524320 | tf_op jit(solution)/shard_map/all_to_all | solution.py:840
  120.4 3.5 all-to-all-start.4
  123.9 15.2 %collective-permute-done.5 = bf16[4,128,1280]{2,1,0:T(8,128)(2,1)} collective-permute-done((bf16[4,128,1280]{2,1,0:T(8,128)(2,1)S(1)}, bf16[4,128,1280]{2,1,0:T(8,128)(2,1)}, u32[]{:S(2)}, u32[]{:S(2)}) %collective-permute-start.5) | collective-permute-done | bytes 1310752 | tf_op jit(solution)/shard_map/ppermute | solution.py:26
  143.4 3.5 all-to-all-start.2
  151.0 4.1 collective-permute-done.10.refs_8_.refs_10_.refs_16_
  158.5 11.7 %all-to-all-done.2.refs_0_ = bf16[4,64,1024]{2,1,0:T(8,128)(2,1)S(1)} async-done(((bf16[4,64,1024]{2,1,0:T(8,128)(2,1)}), bf16[4,64,1024]{2,1,0:T(8,128)(2,1)S(1)}, u32[]{:S(2)}, u32[]{:S(2)}) %all-to-all-start.2) | async-done | bytes 524320 | tf_op jit(solution)/shard_map/all_to_all | solution.py:840
  170.2 6.5 %collective-permute-done.3.refs_3_.refs_4_ = bf16[4,64,1024]{2,1,0:T(8,128)(2,1)} collective-permute-done((bf16[4,64,1024]{2,1,0:T(8,128)(2,1)S(1)}, bf16[4,64,1024]{2,1,0:T(8,128)(2,1)}, u32[]{:S(2)}, u32[]{:S(2)}) %collective-permute-start.3) | collective-permute-done | bytes 524320 | tf_op jit(solution)/shard_map/ppermute | solution.py:26
  176.8 10.4 %collective-permute-done.4.refs_5_ = bf16[4,64,1024]{2,1,0:T(8,128)(2,1)} collective-permute-done((bf16[4,64,1024]{2,1,0:T(8,128)(2,1)S(1)}, bf16[4,64,1024]{2,1,0:T(8,128)(2,1)}, u32[]{:S(2)}, u32[]{:S(2)}) %collective-permute-start.4) | collective-permute-done | bytes 524320 | tf_op jit(solution)/shard_map/ppermute | solution.py:26
  187.2 28.0 %self_forward.1 = (bf16[16,64,256]{2,1,0:T(8,128)(2,1)}, f32[4,1,1024]{2,1,0:T(1,128)S(1)}) custom-call(s32[4]{0:T(128)S(1)} %pad_add_fusion.info, bf16[4,64,1024]{2,1,0:T(8,128)(2,1)S(1)} %all-to-all-done.2.refs_0_, f32[4,1,1024]{2,1,0:T(1,128)S(1)} %pad_maximum_fusion.8.refs_1_.refs_6_, bf16[4,64,1024]{2,1,0:T(8,128)(2,1)S(1)} %all-to-all-done.3.refs_2_.refs_4_, ...), custom_call_target="tpu_custom_call" | custom-call | flops 17179869184 | bytes 8388608 | tf_op jit(solution)/shard_map/self_forward/pallas_call | solution.py:235
  215.9 4.4 all-to-all-start.5
  222.5 17.4 %collective-permute-done.17.refs_2_ = bf16[256,1024]{1,0:T(8,128)(2,1)S(1)} collective-permute-done((bf16[256,1024]{1,0:T(8,128)(2,1)S(1)}, bf16[256,1024]{1,0:T(8,128)(2,1)S(1)}, u32[]{:S(2)}, u32[]{:S(2)}) %collective-permute-start.17) | collective-permute-done | bytes 524320 | tf_op jit(solution)/shard_map/ppermute | solution.py:26
  241.2 4.5 all-to-all-done.5
  248.5 12.2 %middle_forward.1 = (f32[256,1024]{1,0:T(8,128)S(1)}, f32[256,1024]{1,0:T(8,128)}, f32[256,1]{1,0:T(8,128)S(1)}, f32[256,1024]{1,0:T(8,128)}, f32[256,1]{1,0:T(8...) custom-call(s32[4]{0:T(128)S(1)} %pad_add_fusion.info, ...), custom_call_target="tpu_custom_call" | custom-call | flops 1610612736 | bytes 12582912 | tf_op jit(solution)/shard_map/middle_forward/pallas_call | solution.py:438
  269.5 9.1 %grad_act.1.refs_2_.refs_1_ = bf16[1024,2048]{1,0:T(8,128)(2,1)} custom-call(bf16[256,1024]{1,0:T(8,128)(2,1)S(1)} %copy-done.10, bf16[256,1024]{1,0:T(8,128)(2,1)S(1)} %collective-permute-done.16.refs_1_, bf16[256,1024]{1,0:T(8,128)(2,1)S(1)} %collective-permute-done.17.refs_2_, bf16[256,1024]{1,0:T(8,128)(2,1)S(1)} %collective-permute-done.18.refs_3_, ...), custom_call_target="tpu_custom_call" | custom-call | flops 4294967296 | bytes 10485760 | tf_op jit(solution)/shard_map/grad_act/pallas_call | solution.py:563
  282.2 11.5 %feed.2 = (bf16[512,2048]{1,0:T(8,128)(2,1)S(1)}, bf16[512,2048]{1,0:T(8,128)(2,1)}, f32[1,2048]{1,0:T(1,128)S(1)}, f32[256,1024]{1,0:T(8,128)S(1)}, bf16[256,1024]{1,0:T(8,128)(2,1)}) custom-call(bf16[256,1024]{1,0:T(8,128)(2,1)} %get-tuple-element.70.refs_0_, bf16[256,1024]{1,0:T(8,128)(2,1)} %collective-permute-done.15.refs_1_, ...), custom_call_target="tpu_custom_call" | custom-call | flops 4294967296 | bytes 12582912 | tf_op jit(solution)/shard_map/feed/pallas_call | solution.py:604
  296.0 11.2 %feed.3 = (bf16[512,2048]{1,0:T(8,128)(2,1)S(1)}, bf16[512,2048]{1,0:T(8,128)(2,1)}, f32[1,2048]{1,0:T(1,128)S(1)}, f32[256,1024]{1,0:T(8,128)S(1)}, bf16[256,1024]{1,0:T(8,128)(2,1)S(1)}) custom-call(bf16[256,1024]{1,0:T(8,128)(2,1)} %tie.14.refs_0_.refs_2_, bf16[256,1024]{1,0:T(8,128)(2,1)} %collective-permute-done.20.refs_1_.refs_3_, ...), custom_call_target="tpu_custom_call" | custom-call | flops 4294967296 | bytes 12582912 | tf_op jit(solution)/shard_map/feed/pallas_call | solution.py:604
  309.3 9.3 %outer.3.refs_18_ = bf16[1024,2048]{1,0:T(8,128)(2,1)} custom-call(s32[4]{0:T(128)S(1)} %pad_add_fusion.info, bf16[256,1024]{1,0:T(8,128)(2,1)} %get-tuple-element.70.refs_0_, bf16[256,1024]{1,0:T(8,128)(2,1)} %collective-permute-done.15.refs_1_, bf16[256,1024]{1,0:T(8,128)(2,1)} %tie.14.refs_0_.refs_2_, ...), custom_call_target="tpu_custom_call" | custom-call | flops 4294967296 | bytes 10485760 | tf_op jit(solution)/shard_map/outer/pallas_call | solution.py:659
  323.1 5.6 outer.4.refs_19_
  330.4 5.9 collective-permute-done.23
  338.2 13.3 %middle_backward.1 = (f32[256,1024]{1,0:T(8,128)S(1)}, bf16[256,1024]{1,0:T(8,128)(2,1)S(1)}, bf16[256,1024]{1,0:T(8,128)(2,1)S(1)}, bf16[1024,256]{1,0:T(8,128)...) custom-call(s32[4]{0:T(128)S(1)} %pad_add_fusion.info, ...), custom_call_target="tpu_custom_call" | custom-call | flops 1610612736 | bytes 16777216 | tf_op jit(solution)/shard_map/middle_backward/pallas_call | solution.py:522
  355.6 8.1 %all-to-all-start.6 = ((bf16[16,64,256]{2,1,0:T(8,128)(2,1)}), bf16[16,64,256]{2,1,0:T(8,128)(2,1)}, u32[]{:S(2)}, u32[]{:S(2)}) async-start(bf16[16,64,256]{2,1,0:T(8,128)(2,1)} %bitcast.138), calls=%async_computation.6 | async-start | bytes 1048576 | tf_op jit(solution)/shard_map/all_to_all | solution.py:843
  370.1 3.7 middle_outer.1
  381.9 29.1 %self_backward.2 = (f32[4,64,1024]{2,1,0:T(8,128)S(1)}, bf16[1,4,64,1024]{3,2,1,0:T(8,128)(2,1)}, bf16[1,4,64,1024]{3,2,1,0:T(8,128)(2,1)}) custom-call(s32[4]{0:T(128)S(1)} %pad_add_fusion.info, bf16[4,64,1024]{2,1,0:T(8,128)(2,1)S(1)} %all-to-all-done.2.refs_0_, bf16[16,64,256]{2,1,0:T(8,128)(2,1)} %all-to-all-done.6.refs_1_, ...), custom_call_target="tpu_custom_call" | custom-call | flops 536870912 | bytes 65536 | tf_op jit(solution)/shard_map/self_backward/pallas_call | solution.py:345
  416.1 5.8 outer.5.refs_8_
  424.0 5.4 reduce-scatter.4.cloned.1.call-done.refs_5_.refs_1_
  439.4 3.4 add_convert_fusion
  444.2 32.0 %self_backward.3 = (bf16[4,64,1024]{2,1,0:T(8,128)(2,1)S(1)}, f32[1,4,64,1024]{3,2,1,0:T(8,128)S(1)}, f32[1,4,64,1024]{3,2,1,0:T(8,128)S(1)}) custom-call(s32[4]{0:T(128)S(1)} %pad_add_fusion.info, bf16[4,64,1024]{2,1,0:T(8,128)(2,1)S(1)} %all-to-all-done.2.refs_0_, bf16[16,64,256]{2,1,0:T(8,128)(2,1)} %all-to-all-done.6.refs_1_, ...), custom_call_target="tpu_custom_call" | custom-call | flops 536870912 | bytes 65536 | tf_op jit(solution)/shard_map/self_backward/pallas_call | solution.py:345
  479.0 4.7 convolution_convert_fusion.3
  489.1 4.4 all-to-all-start.7
  497.4 4.7 add_convert_fusion.3
  502.7 3.0 convert_add_fusion
  509.7 6.0 collective-permute-done.27
  517.9 12.9 %collective-permute-done.45 = bf16[512,768]{1,0:T(8,128)(2,1)S(1)} collective-permute-done((bf16[512,768]{1,0:T(8,128)(2,1)S(1)}, bf16[512,768]{1,0:T(8,128)(2,1)S(1)}, u32[]{:S(2)}, u32[]{:S(2)}) %collective-permute-start.45) | collective-permute-done | bytes 786464 | tf_op jit(solution)/shard_map/ppermute | solution.py:26
  535.0 2.7 collective-permute-start.38
  537.8 4.5 convolution_convert_fusion.refs_1_
  551.0 4.7 all-to-all-start.8
  576.4 10.4 %collective-permute-done.41 = bf16[1,64,1024]{2,1,0:T(8,128)(2,1)} collective-permute-done((bf16[1,64,1024]{2,1,0:T(8,128)(2,1)}, bf16[1,64,1024]{2,1,0:T(8,128)(2,1)}, u32[]{:S(2)}, u32[]{:S(2)}) %collective-permute-start.41) | collective-permute-done | bytes 131104 | tf_op jit(solution)/shard_map/ppermute | solution.py:26
  599.0 12.4 %all-to-all-start.9 = ((f32[32,1,672]{2,1,0:T(1,128)}), f32[32,1,672]{2,1,0:T(1,128)S(1)}, u32[]{:S(2)}, u32[]{:S(2)}) async-start(f32[32,1,672]{2,1,0:T(1,128)} %copy.80), calls=%async_computation.12 | async-start | bytes 196608 | tf_op jit(solution)/shard_map/all_to_all | solution.py:1029
  614.2 5.0 all-to-all-done.9
  (500 shorter events, 173.1 us)
Async XLA Ops:
  7.2 73.3 %all-gather.4.cloned.1.call-start = ((), (), s32[]{:S(2)}) async-start(), calls=%async_computation.13 | async-start | bytes 1769472 | tf_op jit(solution)/shard_map/all_gather | solution.py:777
  15.7 15.0 %all-to-all-start = ((bf16[32,2,464]{2,1,0:T(2,128)(2,1)}), bf16[32,2,464]{2,1,0:T(2,128)(2,1)S(1)}, u32[]{:S(2)}, u32[]{:S(2)}) async-start(bf16[32,2,464]{2,1,0:T(2,128)(2,1)} %reshape.314), calls=%async_computation | async-start | bytes 131072 | tf_op jit(solution)/shard_map/all_to_all | solution.py:806
  31.9 48.7 %all-to-all-start.1 = ((bf16[4,128,1280]{2,1,0:T(8,128)(2,1)}), bf16[4,128,1280]{2,1,0:T(8,128)(2,1)S(1)}, u32[]{:S(2)}, u32[]{:S(2)}) async-start(bf16[4,128,1280]{2,1,0:T(8,128)(2,1)} %broadcast_in_dim.25), calls=%async_computation.1 | async-start | bytes 2621440 | tf_op jit(solution)/shard_map/all_to_all | solution.py:780
  35.5 233.9 %all-gather.6.cloned.1.call-start = ((), (), s32[]{:S(2)}) async-start(), calls=%async_computation.14 | async-start | bytes 4718592 | tf_op jit(solution)/shard_map/all_gather | solution.py:777
  35.6 14.5 %collective-permute-start.1 = (bf16[256,1024]{1,0:T(8,128)(2,1)S(1)}, bf16[256,1024]{1,0:T(8,128)(2,1)S(1)}, u32[]{:S(2)}, u32[]{:S(2)}) collective-permute-start(bf16[256,1024]{1,0:T(8,128)(2,1)S(1)} %copy-done.6), channel_id=1, source_target_pairs={{0,2},{1,3},{2,0},{3,1},{4,6},{5,7},{6,4},{7,5},{8,10},{9,11},{10,... | collective-permute-start | bytes 1572872 | tf_op jit(solution)/shard_map/ppermute | solution.py:26
  36.9 22.0 %collective-permute-start = (bf16[256,1024]{1,0:T(8,128)(2,1)S(1)}, bf16[256,1024]{1,0:T(8,128)(2,1)S(1)}, u32[]{:S(2)}, u32[]{:S(2)}) collective-permute-start(bf16[256,1024]{1,0:T(8,128)(2,1)S(1)} %copy-done.6), channel_id=1, source_target_pairs={{0,1},{1,0},{2,3},{3,2},{4,5},{5,4},{6,7},{7,6},{8,9},{9,8},{10,11... | collective-permute-start | bytes 1572872 | tf_op jit(solution)/shard_map/ppermute | solution.py:26
  89.0 193.1 %all-gather.8.cloned.1.call-start = ((), (), s32[]{:S(2)}) async-start(), calls=%async_computation.15 | async-start | bytes 4718592 | tf_op jit(solution)/shard_map/all_gather | solution.py:777
  89.1 50.0 %collective-permute-start.5 = (bf16[4,128,1280]{2,1,0:T(8,128)(2,1)S(1)}, bf16[4,128,1280]{2,1,0:T(8,128)(2,1)}, u32[]{:S(2)}, u32[]{:S(2)}) collective-permute-start(bf16[4,128,1280]{2,1,0:T(8,128)(2,1)S(1)} %all-to-all-done.1.refs_7_), channel_id=1, source_target_pairs={{0,4},{4,0},{8,12},{12,8},{16,20},{20,16},{24,28},{28,24},{1,5},{5... | collective-permute-start | bytes 3932168 | tf_op jit(solution)/shard_map/ppermute | solution.py:26
  89.8 30.7 %all-to-all-start.3 = ((bf16[4,64,1024]{2,1,0:T(8,128)(2,1)}), bf16[4,64,1024]{2,1,0:T(8,128)(2,1)S(1)}, u32[]{:S(2)}, u32[]{:S(2)}) async-start(bf16[4,64,1024]{2,1,0:T(8,128)(2,1)} %get-tuple-element.65), calls=%async_computation.3 | async-start | bytes 1048576 | tf_op jit(solution)/shard_map/all_to_all | solution.py:840
  120.4 22.1 %all-to-all-start.4 = ((bf16[4,64,1024]{2,1,0:T(8,128)(2,1)}), bf16[4,64,1024]{2,1,0:T(8,128)(2,1)S(1)}, u32[]{:S(2)}, u32[]{:S(2)}) async-start(bf16[4,64,1024]{2,1,0:T(8,128)(2,1)} %get-tuple-element.66), calls=%async_computation.4 | async-start | bytes 1048576 | tf_op jit(solution)/shard_map/all_to_all | solution.py:840
  143.4 26.8 %all-to-all-start.2 = ((bf16[4,64,1024]{2,1,0:T(8,128)(2,1)}), bf16[4,64,1024]{2,1,0:T(8,128)(2,1)S(1)}, u32[]{:S(2)}, u32[]{:S(2)}) async-start(bf16[4,64,1024]{2,1,0:T(8,128)(2,1)} %get-tuple-element.64), calls=%async_computation.2 | async-start | bytes 1048576 | tf_op jit(solution)/shard_map/all_to_all | solution.py:840
  148.8 27.9 %collective-permute-start.3 = (bf16[4,64,1024]{2,1,0:T(8,128)(2,1)S(1)}, bf16[4,64,1024]{2,1,0:T(8,128)(2,1)}, u32[]{:S(2)}, u32[]{:S(2)}) collective-permute-start(bf16[4,64,1024]{2,1,0:T(8,128)(2,1)S(1)} %all-to-all-done.3.refs_2_.refs_4_), channel_id=1, source_target_pairs={{0,4},{4,0},{8,12},{12,8},{16,20},{20,16},{24,28},{28,24},{1,5},{5... | collective-permute-start | bytes 1572872 | tf_op jit(solution)/shard_map/ppermute | solution.py:26
  148.9 38.3 %collective-permute-start.4 = (bf16[4,64,1024]{2,1,0:T(8,128)(2,1)S(1)}, bf16[4,64,1024]{2,1,0:T(8,128)(2,1)}, u32[]{:S(2)}, u32[]{:S(2)}) collective-permute-start(bf16[4,64,1024]{2,1,0:T(8,128)(2,1)S(1)} %copy-done.18), channel_id=1, source_target_pairs={{0,4},{4,0},{8,12},{12,8},{16,20},{20,16},{24,28},{28,24},{1,5},{5... | collective-permute-start | bytes 1572872 | tf_op jit(solution)/shard_map/ppermute | solution.py:26
  155.1 15.1 %collective-permute-start.11 = (bf16[2,256,256]{2,1,0:T(8,128)(2,1)S(1)}, bf16[2,256,256]{2,1,0:T(8,128)(2,1)S(1)}, u32[]{:S(2)}, u32[]{:S(2)}) collective-permute-start(bf16[2,256,256]{2,1,0:T(8,128)(2,1)S(1)} %collective-permute-done.10.refs_8_.refs_10_.refs_16_), channel_id=1, source_target_pairs={{0,1},{1,0},{2,3},{3,2},{4,5},{5,4},{6,7},{7,6},{8,9},{9,8},{10,11... | collective-permute-start | bytes 786440 | tf_op jit(solution)/shard_map/ppermute | solution.py:26
  158.0 57.8 %collective-permute-start.13 = (bf16[3,1024,256]{2,1,0:T(8,128)(2,1)}, bf16[3,1024,256]{2,1,0:T(8,128)(2,1)}, u32[]{:S(2)}, u32[]{:S(2)}) collective-permute-start(bf16[3,1024,256]{2,1,0:T(8,128)(2,1)} %pad_maximum_fusion.1.refs_4_.refs_10_), channel_id=1, source_target_pairs={{0,2},{1,3},{2,0},{3,1},{4,6},{5,7},{6,4},{7,5},{8,10},{9,11},{10,... | collective-permute-start | bytes 4718600 | tf_op jit(solution)/shard_map/ppermute | solution.py:26
  158.0 83.2 %collective-permute-start.12 = (bf16[3,1024,256]{2,1,0:T(8,128)(2,1)}, bf16[3,1024,256]{2,1,0:T(8,128)(2,1)}, u32[]{:S(2)}, u32[]{:S(2)}) collective-permute-start(bf16[3,1024,256]{2,1,0:T(8,128)(2,1)} %pad_maximum_fusion.1.refs_4_.refs_10_), channel_id=1, source_target_pairs={{0,1},{1,0},{2,3},{3,2},{4,5},{5,4},{6,7},{7,6},{8,9},{9,8},{10,11... | collective-permute-start | bytes 4718600 | tf_op jit(solution)/shard_map/ppermute | solution.py:26
  215.9 29.8 %collective-permute-start.14 = (bf16[3,1024,256]{2,1,0:T(8,128)(2,1)}, bf16[3,1024,256]{2,1,0:T(8,128)(2,1)}, u32[]{:S(2)}, u32[]{:S(2)}) collective-permute-start(bf16[3,1024,256]{2,1,0:T(8,128)(2,1)} %tie.12.refs_6_.refs_12_), channel_id=1, source_target_pairs={{0,1},{1,0},{2,3},{3,2},{4,5},{5,4},{6,7},{7,6},{8,9},{9,8},{10,11... | collective-permute-start | bytes 4718600 | tf_op jit(solution)/shard_map/ppermute | solution.py:26
  215.9 29.7 %all-to-all-start.5 = ((bf16[16,64,256]{2,1,0:T(8,128)(2,1)}), bf16[16,64,256]{2,1,0:T(8,128)(2,1)}, u32[]{:S(2)}, u32[]{:S(2)}) async-start(bf16[16,64,256]{2,1,0:T(8,128)(2,1)} %get-tuple-element.67.refs_2_), calls=%async_computation.5 | async-start | bytes 1048576 | tf_op jit(solution)/shard_map/all_to_all | solution.py:843
  220.3 209.1 %reduce-scatter.4.cloned.1.call-start = ((), (), s32[]{:S(2)}) async-start(), calls=%async_computation.16 | async-start | bytes 4718592 | tf_op jit(solution)/shard_map/reduce_scatter | solution.py:910
  220.6 19.3 %collective-permute-start.17 = (bf16[256,1024]{1,0:T(8,128)(2,1)S(1)}, bf16[256,1024]{1,0:T(8,128)(2,1)S(1)}, u32[]{:S(2)}, u32[]{:S(2)}) collective-permute-start(bf16[256,1024]{1,0:T(8,128)(2,1)S(1)} %copy-done.10), channel_id=1, source_target_pairs={{0,2},{1,3},{2,0},{3,1},{4,6},{5,7},{6,4},{7,5},{8,10},{9,11},{10,... | collective-permute-start | bytes 1572872 | tf_op jit(solution)/shard_map/ppermute | solution.py:26
  222.5 47.0 %collective-permute-start.16 = (bf16[256,1024]{1,0:T(8,128)(2,1)S(1)}, bf16[256,1024]{1,0:T(8,128)(2,1)S(1)}, u32[]{:S(2)}, u32[]{:S(2)}) collective-permute-start(bf16[256,1024]{1,0:T(8,128)(2,1)S(1)} %copy-done.10), channel_id=1, source_target_pairs={{0,1},{1,0},{2,3},{3,2},{4,5},{5,4},{6,7},{7,6},{8,9},{9,8},{10,11... | collective-permute-start | bytes 1572872 | tf_op jit(solution)/shard_map/ppermute | solution.py:26
  239.9 29.6 %collective-permute-start.18 = (bf16[256,1024]{1,0:T(8,128)(2,1)S(1)}, bf16[256,1024]{1,0:T(8,128)(2,1)S(1)}, u32[]{:S(2)}, u32[]{:S(2)}) collective-permute-start(bf16[256,1024]{1,0:T(8,128)(2,1)S(1)} %collective-permute-done.17.refs_2_), channel_id=1, source_target_pairs={{0,1},{1,0},{2,3},{3,2},{4,5},{5,4},{6,7},{7,6},{8,9},{9,8},{10,11... | collective-permute-start | bytes 1572872 | tf_op jit(solution)/shard_map/ppermute | solution.py:26
  266.3 14.1 %collective-permute-start.19 = (bf16[256,1024]{1,0:T(8,128)(2,1)}, bf16[256,1024]{1,0:T(8,128)(2,1)}, u32[]{:S(2)}, u32[]{:S(2)}) collective-permute-start(bf16[256,1024]{1,0:T(8,128)(2,1)} %get-tuple-element.70.refs_0_), channel_id=1, source_target_pairs={{0,2},{1,3},{2,0},{3,1},{4,6},{5,7},{6,4},{7,5},{8,10},{9,11},{10,... | collective-permute-start | bytes 1572872 | tf_op jit(solution)/shard_map/ppermute | solution.py:26
  266.8 15.3 %collective-permute-start.15 = (bf16[256,1024]{1,0:T(8,128)(2,1)}, bf16[256,1024]{1,0:T(8,128)(2,1)}, u32[]{:S(2)}, u32[]{:S(2)}) collective-permute-start(bf16[256,1024]{1,0:T(8,128)(2,1)} %get-tuple-element.70.refs_0_), channel_id=1, source_target_pairs={{0,1},{1,0},{2,3},{3,2},{4,5},{5,4},{6,7},{7,6},{8,9},{9,8},{10,11... | collective-permute-start | bytes 1572872 | tf_op jit(solution)/shard_map/ppermute | solution.py:26
  280.4 15.6 %collective-permute-start.20 = (bf16[256,1024]{1,0:T(8,128)(2,1)}, bf16[256,1024]{1,0:T(8,128)(2,1)}, u32[]{:S(2)}, u32[]{:S(2)}) collective-permute-start(bf16[256,1024]{1,0:T(8,128)(2,1)} %tie.14.refs_0_.refs_2_), channel_id=1, source_target_pairs={{0,1},{1,0},{2,3},{3,2},{4,5},{5,4},{6,7},{7,6},{8,9},{9,8},{10,11... | collective-permute-start | bytes 1572872 | tf_op jit(solution)/shard_map/ppermute | solution.py:26
  328.7 83.3 %collective-permute-start.24 = (bf16[512,2048]{1,0:T(8,128)(2,1)S(1)}, bf16[512,2048]{1,0:T(8,128)(2,1)}, u32[]{:S(2)}, u32[]{:S(2)}) collective-permute-start(bf16[512,2048]{1,0:T(8,128)(2,1)S(1)} %outer.4.refs_19_), channel_id=1, source_target_pairs={{0,4},{4,0},{8,12},{12,8},{16,20},{20,16},{24,28},{28,24},{1,5},{5... | collective-permute-start | bytes 6291464 | tf_op jit(solution)/shard_map/ppermute | solution.py:26
  355.6 26.3 %all-to-all-start.6 = ((bf16[16,64,256]{2,1,0:T(8,128)(2,1)}), bf16[16,64,256]{2,1,0:T(8,128)(2,1)}, u32[]{:S(2)}, u32[]{:S(2)}) async-start(bf16[16,64,256]{2,1,0:T(8,128)(2,1)} %bitcast.138), calls=%async_computation.6 | async-start | bytes 1048576 | tf_op jit(solution)/shard_map/all_to_all | solution.py:843
  363.7 169.3 %reduce-scatter.6.cloned.1.call-start = ((), (), s32[]{:S(2)}) async-start(), calls=%async_computation.17 | async-start | bytes 2621440 | tf_op jit(solution)/shard_map/reduce_scatter | solution.py:913
  373.8 65.6 %collective-permute-start.43 = (bf16[1024,768]{1,0:T(8,128)(2,1)}, bf16[1024,768]{1,0:T(8,128)(2,1)}, u32[]{:S(2)}, u32[]{:S(2)}) collective-permute-start(bf16[1024,768]{1,0:T(8,128)(2,1)} %get-tuple-element.98.refs_9_), channel_id=1, source_target_pairs={{0,1},{1,0},{2,3},{3,2},{4,5},{5,4},{6,7},{7,6},{8,9},{9,8},{10,11... | collective-permute-start | bytes 4718600 | tf_op jit(solution)/shard_map/ppermute | solution.py:26
  378.0 55.8 %collective-permute-start.30 = (bf16[2,256,256]{2,1,0:T(8,128)(2,1)}, bf16[2,256,256]{2,1,0:T(8,128)(2,1)}, u32[]{:S(2)}, u32[]{:S(2)}) collective-permute-start(bf16[2,256,256]{2,1,0:T(8,128)(2,1)} %get-tuple-element.186), channel_id=1, source_target_pairs={{0,1},{1,0},{2,3},{3,2},{4,5},{5,4},{6,7},{7,6},{8,9},{9,8},{10,11... | collective-permute-start | bytes 786440 | tf_op jit(solution)/shard_map/ppermute | solution.py:26
  380.1 53.1 %collective-permute-start.32 = (bf16[2,256,256]{2,1,0:T(8,128)(2,1)}, bf16[2,256,256]{2,1,0:T(8,128)(2,1)S(1)}, u32[]{:S(2)}, u32[]{:S(2)}) collective-permute-start(bf16[2,256,256]{2,1,0:T(8,128)(2,1)} %fusion.52), channel_id=1, source_target_pairs={{0,2},{1,3},{2,0},{3,1},{4,6},{5,7},{6,4},{7,5},{8,10},{9,11},{10,... | collective-permute-start | bytes 786440 | tf_op jit(solution)/shard_map/ppermute | solution.py:26
  432.3 70.4 %collective-permute-start.42 = (bf16[1024,768]{1,0:T(8,128)(2,1)}, bf16[1024,768]{1,0:T(8,128)(2,1)}, u32[]{:S(2)}, u32[]{:S(2)}) collective-permute-start(bf16[1024,768]{1,0:T(8,128)(2,1)} %get-tuple-element.96.refs_7_), channel_id=1, source_target_pairs={{0,1},{1,0},{2,3},{3,2},{4,5},{5,4},{6,7},{7,6},{8,9},{9,8},{10,11... | collective-permute-start | bytes 4718600 | tf_op jit(solution)/shard_map/ppermute | solution.py:26
  435.9 47.9 %collective-permute-start.33 = (bf16[1,2,256,256]{3,2,1,0:T(8,128)(2,1)}, bf16[1,2,256,256]{3,2,1,0:T(8,128)(2,1)S(1)}, u32[]{:S(2)}, u32[]{:S(2)}) collective-permute-start(bf16[1,2,256,256]{3,2,1,0:T(8,128)(2,1)} %fusion.59), channel_id=1, source_target_pairs={{0,4},{4,0},{8,12},{12,8},{16,20},{20,16},{24,28},{28,24},{1,5},{5... | collective-permute-start | bytes 786440 | tf_op jit(solution)/shard_map/ppermute | solution.py:26
  437.3 48.5 %collective-permute-start.28 = (bf16[4,64,1024]{2,1,0:T(8,128)(2,1)}, bf16[4,64,1024]{2,1,0:T(8,128)(2,1)}, u32[]{:S(2)}, u32[]{:S(2)}) collective-permute-start(bf16[4,64,1024]{2,1,0:T(8,128)(2,1)} %bitcast.35), channel_id=1, source_target_pairs={{0,4},{4,0},{8,12},{12,8},{16,20},{20,16},{24,28},{28,24},{1,5},{5... | collective-permute-start | bytes 1572872 | tf_op jit(solution)/shard_map/ppermute | solution.py:26
  437.9 48.5 %collective-permute-start.29 = (bf16[4,64,1024]{2,1,0:T(8,128)(2,1)}, bf16[4,64,1024]{2,1,0:T(8,128)(2,1)}, u32[]{:S(2)}, u32[]{:S(2)}) collective-permute-start(bf16[4,64,1024]{2,1,0:T(8,128)(2,1)} %bitcast.36), channel_id=1, source_target_pairs={{0,4},{4,0},{8,12},{12,8},{16,20},{20,16},{24,28},{28,24},{1,5},{5... | collective-permute-start | bytes 1572872 | tf_op jit(solution)/shard_map/ppermute | solution.py:26
  442.8 59.9 %collective-permute-start.44 = (bf16[1024,768]{1,0:T(8,128)(2,1)}, bf16[1024,768]{1,0:T(8,128)(2,1)}, u32[]{:S(2)}, u32[]{:S(2)}) collective-permute-start(bf16[1024,768]{1,0:T(8,128)(2,1)} %add_convert_fusion), channel_id=1, source_target_pairs={{0,2},{1,3},{2,0},{3,1},{4,6},{5,7},{6,4},{7,5},{8,10},{9,11},{10,... | collective-permute-start | bytes 4718600 | tf_op jit(solution)/shard_map/ppermute | solution.py:26
  485.9 21.5 %collective-permute-start.25 = (bf16[256,1024]{1,0:T(8,128)(2,1)}, bf16[256,1024]{1,0:T(8,128)(2,1)}, u32[]{:S(2)}, u32[]{:S(2)}) collective-permute-start(bf16[256,1024]{1,0:T(8,128)(2,1)} %convolution_convert_fusion.4), channel_id=1, source_target_pairs={{0,1},{1,0},{2,3},{3,2},{4,5},{5,4},{6,7},{7,6},{8,9},{9,8},{10,11... | collective-permute-start | bytes 1572872 | tf_op jit(solution)/shard_map/ppermute | solution.py:26
  489.1 44.0 %all-to-all-start.7 = ((bf16[4,3,64,1024]{3,2,1,0:T(8,128)(2,1)}), bf16[4,3,64,1024]{3,2,1,0:T(8,128)(2,1)}, u32[]{:S(2)}, u32[]{:S(2)}) async-start(bf16[4,3,64,1024]{3,2,1,0:T(8,128)(2,1)} %copy-done.7), calls=%async_computation.8 | async-start | bytes 3145728 | tf_op jit(solution)/shard_map/all_to_all | solution.py:840
  493.4 100.6 %reduce-scatter.8.cloned.1.call-start = ((), (), s32[]{:S(2)}) async-start(), calls=%async_computation.18 | async-start | bytes 983040 | tf_op jit(solution)/shard_map/reduce_scatter | solution.py:913
  495.4 37.6 %collective-permute-start.34 = (bf16[1,2,256,256]{3,2,1,0:T(8,128)(2,1)}, bf16[1,2,256,256]{3,2,1,0:T(8,128)(2,1)S(1)}, u32[]{:S(2)}, u32[]{:S(2)}) collective-permute-start(bf16[1,2,256,256]{3,2,1,0:T(8,128)(2,1)} %add_convert_fusion.9), channel_id=1, source_target_pairs={{0,8},{4,12},{8,0},{12,4},{16,24},{20,28},{24,16},{28,20},{1,9},{5... | collective-permute-start | bytes 786440 | tf_op jit(solution)/shard_map/ppermute | solution.py:26
  505.9 25.0 %collective-permute-start.45 = (bf16[512,768]{1,0:T(8,128)(2,1)S(1)}, bf16[512,768]{1,0:T(8,128)(2,1)S(1)}, u32[]{:S(2)}, u32[]{:S(2)}) collective-permute-start(bf16[512,768]{1,0:T(8,128)(2,1)S(1)} %pad_maximum_fusion.2), channel_id=1, source_target_pairs={{0,4},{4,0},{8,12},{12,8},{16,20},{20,16},{24,28},{28,24},{1,5},{5... | collective-permute-start | bytes 2359304 | tf_op jit(solution)/shard_map/ppermute | solution.py:26
  535.0 26.8 %collective-permute-start.38 = (bf16[1,2,256,256]{3,2,1,0:T(8,128)(2,1)S(1)}, bf16[1,2,256,256]{3,2,1,0:T(8,128)(2,1)}, u32[]{:S(2)}, u32[]{:S(2)}) collective-permute-start(bf16[1,2,256,256]{3,2,1,0:T(8,128)(2,1)S(1)} %add_convert_fusion.8), channel_id=1, source_target_pairs={{0,16},{4,20},{8,24},{12,28},{16,0},{20,4},{24,8},{28,12},{1,17},{... | collective-permute-start | bytes 786440 | tf_op jit(solution)/shard_map/ppermute | solution.py:26
  546.6 20.5 %collective-permute-start.36 = (bf16[256,1024]{1,0:T(8,128)(2,1)}, bf16[256,1024]{1,0:T(8,128)(2,1)}, u32[]{:S(2)}, u32[]{:S(2)}) collective-permute-start(bf16[256,1024]{1,0:T(8,128)(2,1)} %convolution_convert_fusion.1), channel_id=1, source_target_pairs={{0,1},{1,0},{2,3},{3,2},{4,5},{5,4},{6,7},{7,6},{8,9},{9,8},{10,11... | collective-permute-start | bytes 1572872 | tf_op jit(solution)/shard_map/ppermute | solution.py:26
  549.0 39.9 %collective-permute-start.35 = (bf16[256,1024]{1,0:T(8,128)(2,1)}, bf16[256,1024]{1,0:T(8,128)(2,1)}, u32[]{:S(2)}, u32[]{:S(2)}) collective-permute-start(bf16[256,1024]{1,0:T(8,128)(2,1)} %convolution_convert_fusion.2), channel_id=1, source_target_pairs={{0,1},{1,0},{2,3},{3,2},{4,5},{5,4},{6,7},{7,6},{8,9},{9,8},{10,11... | collective-permute-start | bytes 1572872 | tf_op jit(solution)/shard_map/ppermute | solution.py:26
  551.0 46.4 %all-to-all-start.8 = ((bf16[8,128,768]{2,1,0:T(8,128)(2,1)}), bf16[8,128,768]{2,1,0:T(8,128)(2,1)}, u32[]{:S(2)}, u32[]{:S(2)}) async-start(bf16[8,128,768]{2,1,0:T(8,128)(2,1)} %bitcast.48), calls=%async_computation.10 | async-start | bytes 3145728 | tf_op jit(solution)/shard_map/all_to_all | solution.py:990
  569.8 19.2 %collective-permute-start.37 = (bf16[256,1024]{1,0:T(8,128)(2,1)}, bf16[256,1024]{1,0:T(8,128)(2,1)}, u32[]{:S(2)}, u32[]{:S(2)}) collective-permute-start(bf16[256,1024]{1,0:T(8,128)(2,1)} %fusion.2), channel_id=1, source_target_pairs={{0,2},{1,3},{2,0},{3,1},{4,6},{5,7},{6,4},{7,5},{8,10},{9,11},{10,... | collective-permute-start | bytes 1572872 | tf_op jit(solution)/shard_map/ppermute | solution.py:26
  571.7 15.1 %collective-permute-start.41 = (bf16[1,64,1024]{2,1,0:T(8,128)(2,1)}, bf16[1,64,1024]{2,1,0:T(8,128)(2,1)}, u32[]{:S(2)}, u32[]{:S(2)}) collective-permute-start(bf16[1,64,1024]{2,1,0:T(8,128)(2,1)} %fusion.40), channel_id=1, source_target_pairs={{0,2},{1,3},{2,0},{3,1},{4,6},{5,7},{6,4},{7,5},{8,10},{9,11},{10,... | collective-permute-start | bytes 393224 | tf_op jit(solution)/shard_map/ppermute | solution.py:26
  599.0 20.2 %all-to-all-start.9 = ((f32[32,1,672]{2,1,0:T(1,128)}), f32[32,1,672]{2,1,0:T(1,128)S(1)}, u32[]{:S(2)}, u32[]{:S(2)}) async-start(f32[32,1,672]{2,1,0:T(1,128)} %copy.80), calls=%async_computation.12 | async-start | bytes 196608 | tf_op jit(solution)/shard_map/all_to_all | solution.py:1029
  (132 other events, 891.3 us)
Sparse Core Ops, SparseCore 0:
  12.3 62.2 all-gather.3
  89.2 98.1 all-gather.5
  189.5 80.4 all-gather.7
  318.8 110.5 reduce-scatter.3
  431.7 43.6 reduce-scatter.5
  533.2 38.2 reduce-scatter.7

commit v6 on v5

--- a/solution.py
+++ b/solution.py
@@ -312,16 +312,24 @@
     dq = before_ref[slot, :, cols] if own else jnp.zeros((HDIM, TILE), f32)
     for side in range(sides):
 
-        def earlier(index, dq, side=side):
-            rows = pl.ds(pl.multiple_of(lax.rem(index, per) * TILE, TILE), TILE)
-            return update(dq, side, index // per, rows, None)
+        def earlier(place, dq, side=side):
+            for start in range(0, piece_rows, TILE):
+                dq = update(dq, side, place, slice(start, start + TILE), None)
+            return dq
 
         if own:
-            count = slot * per + tile
+            count = slot
         else:
             here = jnp.bitwise_xor(beside, flip(slot, sides + 1))
-            count = (slot + jnp.where(jnp.bitwise_xor(here, side + 1) < here, 1, 0)) * per
+            count = slot + jnp.where(jnp.bitwise_xor(here, side + 1) < here, 1, 0)
         dq = lax.fori_loop(0, count, earlier, dq)
+    if own:
+
+        def earlier_tile(index, dq):
+            rows = pl.ds(pl.multiple_of(index * TILE, TILE), TILE)
+            return update(dq, 0, slot, rows, None)
+
+        dq = lax.fori_loop(0, tile, earlier_tile, dq)
     if own:
         ids = id_ref[slot, :, cols]
         mask = column(ids, TILE) <= ids

time: 641 us -> 640 us (level)
  no operation moved by 1% of the time
where the time goes in v6:
time: 640 us; the launch traced here: 628 us
  waiting for transfers between devices  190 us (30%)
  Pallas kernels  176 us (28%)
  starting transfers between devices  87.3 us (14%)
  local copies, waits for them, and re-layouts  84 us (13%)
  other arithmetic  38.3 us (6%)
  matrix products  36.9 us (6%)
  between operations  15.8 us (2%)
    ppermute x46, waiting for transfers between devices, swap(): lax.ppermute(value, axis, [(i, i ^ mask) for i in range(lax.axis_size(axi...  112 us
    pallas_call x2, Pallas kernels, self_backward(): pl.pallas_call(functools.partial(self_backward_kernel, heads, sides, own,...  58.2 us
    unnamed x250, local copies, waits for them, and re-layouts  51.8 us
    dot_general x15, matrix products, dot(): lax.dot_general(left, right, (((left_dim,), (right_dim,)), ((), ())), pre...  36.9 us
    ppermute x46, starting transfers between devices, swap(): lax.ppermute(value, axis, [(i, i ^ mask) for i in range(lax.axis_size(axi...  31.4 us
    all_to_all x4, waiting for transfers between devices, across_lines(): lax.all_to_all(value, 'tok', 0, 0, tiled=True, axis_index_groups=lines)  31.4 us
    pallas_call x1, Pallas kernels, self_forward(): pl.pallas_call(functools.partial(self_forward_kernel, heads, others), gri...  28 us
    pallas_call x2, Pallas kernels, feed(): pl.pallas_call(functools.partial(feed_kernel, first, blocks), in_specs=[V...  22.6 us
  transfers between devices with their start and end apart: 62, of which 22 were waited for; matrix products, arithmetic and copies ran while one was open for 17% of the time, Pallas kernels for 24%

profile of v6, /device:TPU:0, one launch (start us, length us, event | category | flops | bytes accessed | tf_op | source)
XLA Modules:
  0.0 628.1 jit_solution(5653345271447297766)
XLA Ops:
  15.7 7.3 %all-to-all-start = ((bf16[32,2,464]{2,1,0:T(2,128)(2,1)}), bf16[32,2,464]{2,1,0:T(2,128)(2,1)S(1)}, u32[]{:S(2)}, u32[]{:S(2)}) async-start(bf16[32,2,464]{2,1,0:T(2,128)(2,1)} %reshape.314), calls=%async_computation | async-start | bytes 131072 | tf_op jit(solution)/shard_map/all_to_all | solution.py:814
  23.4 7.3 %all-to-all-done = bf16[32,2,464]{2,1,0:T(2,128)(2,1)S(1)} async-done(((bf16[32,2,464]{2,1,0:T(2,128)(2,1)}), bf16[32,2,464]{2,1,0:T(2,128)(2,1)S(1)}, u32[]{:S(2)}, u32[]{:S(2)}) %all-to-all-start) | async-done | bytes 59424 | tf_op jit(solution)/shard_map/all_to_all | solution.py:814
  31.9 3.7 all-to-all-start.1
  38.1 12.0 %collective-permute-done.1.refs_5_ = bf16[256,1024]{1,0:T(8,128)(2,1)S(1)} collective-permute-done((bf16[256,1024]{1,0:T(8,128)(2,1)S(1)}, bf16[256,1024]{1,0:T(8,128)(2,1)S(1)}, u32[]{:S(2)}, u32[]{:S(2)}) %collective-permute-start.1) | collective-permute-done | bytes 524320 | tf_op jit(solution)/shard_map/ppermute | solution.py:26
  50.1 3.8 slice_reduce_fusion
  58.9 21.6 %all-to-all-done.1.refs_7_ = bf16[4,128,1280]{2,1,0:T(8,128)(2,1)S(1)} async-done(((bf16[4,128,1280]{2,1,0:T(8,128)(2,1)}), bf16[4,128,1280]{2,1,0:T(8,128)(2,1)S(1)}, u32[]{:S(2)}, u32[]{:S(2)}) %all-to-all-start.1) | async-done | bytes 1310752 | tf_op jit(solution)/shard_map/all_to_all | solution.py:788
  80.5 6.4 %project.1 = (bf16[4,64,1024]{2,1,0:T(8,128)(2,1)}, bf16[4,64,1024]{2,1,0:T(8,128)(2,1)}, bf16[4,64,1024]{2,1,0:T(8,128)(2,1)}, bf16[1024,1024]{1,0:T(8,128)(2,1)}) custom-call(s32[4]{0:T(128)S(1)} %pad_add_fusion.info, bf16[1024,768]{1,0:T(8,128)(2,1)} %all-gather.4.cloned.1.call-done.refs_0_, f32[2,1024]{1,0:T(2,128)S(1)} %pad_maximum_fusion.9.refs_1_, ...), custom_call_target="tpu_custom_call" | custom-call | flops 1610612736 | bytes 8388608 | tf_op jit(solution)/shard_map/project/pallas_call | solution.py:127
  89.8 3.6 all-to-all-start.3
  93.9 4.6 collective-permute-done.7
  100.8 19.7 %all-to-all-done.3.refs_2_.refs_4_ = bf16[4,64,1024]{2,1,0:T(8,128)(2,1)S(1)} async-done(((bf16[4,64,1024]{2,1,0:T(8,128)(2,1)}), bf16[4,64,1024]{2,1,0:T(8,128)(2,1)S(1)}, u32[]{:S(2)}, u32[]{:S(2)}) %all-to-all-start.3) | async-done | bytes 524320 | tf_op jit(solution)/shard_map/all_to_all | solution.py:848
  120.4 3.5 all-to-all-start.4
  123.9 15.2 %collective-permute-done.5 = bf16[4,128,1280]{2,1,0:T(8,128)(2,1)} collective-permute-done((bf16[4,128,1280]{2,1,0:T(8,128)(2,1)S(1)}, bf16[4,128,1280]{2,1,0:T(8,128)(2,1)}, u32[]{:S(2)}, u32[]{:S(2)}) %collective-permute-start.5) | collective-permute-done | bytes 1310752 | tf_op jit(solution)/shard_map/ppermute | solution.py:26
  143.4 3.5 all-to-all-start.2
  151.0 4.1 collective-permute-done.10.refs_8_.refs_10_.refs_16_
  158.5 11.7 %all-to-all-done.2.refs_0_ = bf16[4,64,1024]{2,1,0:T(8,128)(2,1)S(1)} async-done(((bf16[4,64,1024]{2,1,0:T(8,128)(2,1)}), bf16[4,64,1024]{2,1,0:T(8,128)(2,1)S(1)}, u32[]{:S(2)}, u32[]{:S(2)}) %all-to-all-start.2) | async-done | bytes 524320 | tf_op jit(solution)/shard_map/all_to_all | solution.py:848
  170.2 6.5 %collective-permute-done.3.refs_3_.refs_4_ = bf16[4,64,1024]{2,1,0:T(8,128)(2,1)} collective-permute-done((bf16[4,64,1024]{2,1,0:T(8,128)(2,1)S(1)}, bf16[4,64,1024]{2,1,0:T(8,128)(2,1)}, u32[]{:S(2)}, u32[]{:S(2)}) %collective-permute-start.3) | collective-permute-done | bytes 524320 | tf_op jit(solution)/shard_map/ppermute | solution.py:26
  176.8 10.4 %collective-permute-done.4.refs_5_ = bf16[4,64,1024]{2,1,0:T(8,128)(2,1)} collective-permute-done((bf16[4,64,1024]{2,1,0:T(8,128)(2,1)S(1)}, bf16[4,64,1024]{2,1,0:T(8,128)(2,1)}, u32[]{:S(2)}, u32[]{:S(2)}) %collective-permute-start.4) | collective-permute-done | bytes 524320 | tf_op jit(solution)/shard_map/ppermute | solution.py:26
  187.2 28.0 %self_forward.1 = (bf16[16,64,256]{2,1,0:T(8,128)(2,1)}, f32[4,1,1024]{2,1,0:T(1,128)S(1)}) custom-call(s32[4]{0:T(128)S(1)} %pad_add_fusion.info, bf16[4,64,1024]{2,1,0:T(8,128)(2,1)S(1)} %all-to-all-done.2.refs_0_, f32[4,1,1024]{2,1,0:T(1,128)S(1)} %pad_maximum_fusion.8.refs_1_.refs_6_, bf16[4,64,1024]{2,1,0:T(8,128)(2,1)S(1)} %all-to-all-done.3.refs_2_.refs_4_, ...), custom_call_target="tpu_custom_call" | custom-call | flops 17179869184 | bytes 8388608 | tf_op jit(solution)/shard_map/self_forward/pallas_call | solution.py:235
  215.9 4.4 all-to-all-start.5
  222.5 17.4 %collective-permute-done.17.refs_2_ = bf16[256,1024]{1,0:T(8,128)(2,1)S(1)} collective-permute-done((bf16[256,1024]{1,0:T(8,128)(2,1)S(1)}, bf16[256,1024]{1,0:T(8,128)(2,1)S(1)}, u32[]{:S(2)}, u32[]{:S(2)}) %collective-permute-start.17) | collective-permute-done | bytes 524320 | tf_op jit(solution)/shard_map/ppermute | solution.py:26
  241.2 4.5 all-to-all-done.5
  248.5 12.2 %middle_forward.1 = (f32[256,1024]{1,0:T(8,128)S(1)}, f32[256,1024]{1,0:T(8,128)}, f32[256,1]{1,0:T(8,128)S(1)}, f32[256,1024]{1,0:T(8,128)}, f32[256,1]{1,0:T(8...) custom-call(s32[4]{0:T(128)S(1)} %pad_add_fusion.info, ...), custom_call_target="tpu_custom_call" | custom-call | flops 1610612736 | bytes 12582912 | tf_op jit(solution)/shard_map/middle_forward/pallas_call | solution.py:446
  269.5 9.1 %grad_act.1.refs_2_.refs_1_ = bf16[1024,2048]{1,0:T(8,128)(2,1)} custom-call(bf16[256,1024]{1,0:T(8,128)(2,1)S(1)} %copy-done.10, bf16[256,1024]{1,0:T(8,128)(2,1)S(1)} %collective-permute-done.16.refs_1_, bf16[256,1024]{1,0:T(8,128)(2,1)S(1)} %collective-permute-done.17.refs_2_, bf16[256,1024]{1,0:T(8,128)(2,1)S(1)} %collective-permute-done.18.refs_3_, ...), custom_call_target="tpu_custom_call" | custom-call | flops 4294967296 | bytes 10485760 | tf_op jit(solution)/shard_map/grad_act/pallas_call | solution.py:571
  282.2 11.5 %feed.2 = (bf16[512,2048]{1,0:T(8,128)(2,1)S(1)}, bf16[512,2048]{1,0:T(8,128)(2,1)}, f32[1,2048]{1,0:T(1,128)S(1)}, f32[256,1024]{1,0:T(8,128)S(1)}, bf16[256,1024]{1,0:T(8,128)(2,1)}) custom-call(bf16[256,1024]{1,0:T(8,128)(2,1)} %get-tuple-element.70.refs_0_, bf16[256,1024]{1,0:T(8,128)(2,1)} %collective-permute-done.15.refs_1_, ...), custom_call_target="tpu_custom_call" | custom-call | flops 4294967296 | bytes 12582912 | tf_op jit(solution)/shard_map/feed/pallas_call | solution.py:612
  296.0 11.2 %feed.3 = (bf16[512,2048]{1,0:T(8,128)(2,1)S(1)}, bf16[512,2048]{1,0:T(8,128)(2,1)}, f32[1,2048]{1,0:T(1,128)S(1)}, f32[256,1024]{1,0:T(8,128)S(1)}, bf16[256,1024]{1,0:T(8,128)(2,1)S(1)}) custom-call(bf16[256,1024]{1,0:T(8,128)(2,1)} %tie.14.refs_0_.refs_2_, bf16[256,1024]{1,0:T(8,128)(2,1)} %collective-permute-done.20.refs_1_.refs_3_, ...), custom_call_target="tpu_custom_call" | custom-call | flops 4294967296 | bytes 12582912 | tf_op jit(solution)/shard_map/feed/pallas_call | solution.py:612
  309.3 9.3 %outer.3.refs_18_ = bf16[1024,2048]{1,0:T(8,128)(2,1)} custom-call(s32[4]{0:T(128)S(1)} %pad_add_fusion.info, bf16[256,1024]{1,0:T(8,128)(2,1)} %get-tuple-element.70.refs_0_, bf16[256,1024]{1,0:T(8,128)(2,1)} %collective-permute-done.15.refs_1_, bf16[256,1024]{1,0:T(8,128)(2,1)} %tie.14.refs_0_.refs_2_, ...), custom_call_target="tpu_custom_call" | custom-call | flops 4294967296 | bytes 10485760 | tf_op jit(solution)/shard_map/outer/pallas_call | solution.py:667
  323.1 5.6 outer.4.refs_19_
  330.4 5.9 collective-permute-done.23
  338.2 13.3 %middle_backward.1 = (f32[256,1024]{1,0:T(8,128)S(1)}, bf16[256,1024]{1,0:T(8,128)(2,1)S(1)}, bf16[256,1024]{1,0:T(8,128)(2,1)S(1)}, bf16[1024,256]{1,0:T(8,128)...) custom-call(s32[4]{0:T(128)S(1)} %pad_add_fusion.info, ...), custom_call_target="tpu_custom_call" | custom-call | flops 1610612736 | bytes 16777216 | tf_op jit(solution)/shard_map/middle_backward/pallas_call | solution.py:530
  355.6 8.1 %all-to-all-start.6 = ((bf16[16,64,256]{2,1,0:T(8,128)(2,1)}), bf16[16,64,256]{2,1,0:T(8,128)(2,1)}, u32[]{:S(2)}, u32[]{:S(2)}) async-start(bf16[16,64,256]{2,1,0:T(8,128)(2,1)} %bitcast.138), calls=%async_computation.6 | async-start | bytes 1048576 | tf_op jit(solution)/shard_map/all_to_all | solution.py:851
  370.1 3.7 middle_outer.1
  381.9 27.3 %self_backward.2 = (f32[4,64,1024]{2,1,0:T(8,128)S(1)}, bf16[1,4,64,1024]{3,2,1,0:T(8,128)(2,1)}, bf16[1,4,64,1024]{3,2,1,0:T(8,128)(2,1)}) custom-call(s32[4]{0:T(128)S(1)} %pad_add_fusion.info, bf16[4,64,1024]{2,1,0:T(8,128)(2,1)S(1)} %all-to-all-done.2.refs_0_, bf16[16,64,256]{2,1,0:T(8,128)(2,1)} %all-to-all-done.6.refs_1_, ...), custom_call_target="tpu_custom_call" | custom-call | flops 536870912 | bytes 65536 | tf_op jit(solution)/shard_map/self_backward/pallas_call | solution.py:353
  414.3 5.8 outer.5.refs_8_
  422.2 7.2 %reduce-scatter.4.cloned.1.call-done.refs_5_.refs_1_ = bf16[128,2048]{1,0:T(8,128)(2,1)} async-done(((bf16[1024,2048]{1,0:T(8,128)(2,1)}), bf16[128,2048]{1,0:T(8,128)(2,1)}) %reduce-scatter.4.cloned.1.call-update) | async-done | bytes 524304 | tf_op jit(solution)/shard_map/reduce_scatter | solution.py:918
  439.4 3.4 add_convert_fusion
  444.2 30.9 %self_backward.3 = (bf16[4,64,1024]{2,1,0:T(8,128)(2,1)S(1)}, f32[1,4,64,1024]{3,2,1,0:T(8,128)S(1)}, f32[1,4,64,1024]{3,2,1,0:T(8,128)S(1)}) custom-call(s32[4]{0:T(128)S(1)} %pad_add_fusion.info, bf16[4,64,1024]{2,1,0:T(8,128)(2,1)S(1)} %all-to-all-done.2.refs_0_, bf16[16,64,256]{2,1,0:T(8,128)(2,1)} %all-to-all-done.6.refs_1_, ...), custom_call_target="tpu_custom_call" | custom-call | flops 536870912 | bytes 65536 | tf_op jit(solution)/shard_map/self_backward/pallas_call | solution.py:353
  477.9 4.7 convolution_convert_fusion.3
  488.0 4.4 all-to-all-start.7
  496.1 4.7 add_convert_fusion.3
  501.4 3.0 convert_add_fusion
  508.4 6.0 collective-permute-done.27
  516.6 13.1 %collective-permute-done.45 = bf16[512,768]{1,0:T(8,128)(2,1)S(1)} collective-permute-done((bf16[512,768]{1,0:T(8,128)(2,1)S(1)}, bf16[512,768]{1,0:T(8,128)(2,1)S(1)}, u32[]{:S(2)}, u32[]{:S(2)}) %collective-permute-start.45) | collective-permute-done | bytes 786464 | tf_op jit(solution)/shard_map/ppermute | solution.py:26
  533.9 2.7 collective-permute-start.38
  536.7 4.5 convolution_convert_fusion.refs_1_
  549.9 4.7 all-to-all-start.8
  575.3 10.4 %collective-permute-done.41 = bf16[1,64,1024]{2,1,0:T(8,128)(2,1)} collective-permute-done((bf16[1,64,1024]{2,1,0:T(8,128)(2,1)}, bf16[1,64,1024]{2,1,0:T(8,128)(2,1)}, u32[]{:S(2)}, u32[]{:S(2)}) %collective-permute-start.41) | collective-permute-done | bytes 131104 | tf_op jit(solution)/shard_map/ppermute | solution.py:26
  598.0 12.4 %all-to-all-start.9 = ((f32[32,1,672]{2,1,0:T(1,128)}), f32[32,1,672]{2,1,0:T(1,128)S(1)}, u32[]{:S(2)}, u32[]{:S(2)}) async-start(f32[32,1,672]{2,1,0:T(1,128)} %copy.80), calls=%async_computation.12 | async-start | bytes 196608 | tf_op jit(solution)/shard_map/all_to_all | solution.py:1037
  613.1 5.0 all-to-all-done.9
  (500 shorter events, 172.9 us)
Async XLA Ops:
  7.2 73.3 %all-gather.4.cloned.1.call-start = ((), (), s32[]{:S(2)}) async-start(), calls=%async_computation.13 | async-start | bytes 1769472 | tf_op jit(solution)/shard_map/all_gather | solution.py:785
  15.7 15.0 %all-to-all-start = ((bf16[32,2,464]{2,1,0:T(2,128)(2,1)}), bf16[32,2,464]{2,1,0:T(2,128)(2,1)S(1)}, u32[]{:S(2)}, u32[]{:S(2)}) async-start(bf16[32,2,464]{2,1,0:T(2,128)(2,1)} %reshape.314), calls=%async_computation | async-start | bytes 131072 | tf_op jit(solution)/shard_map/all_to_all | solution.py:814
  31.9 48.7 %all-to-all-start.1 = ((bf16[4,128,1280]{2,1,0:T(8,128)(2,1)}), bf16[4,128,1280]{2,1,0:T(8,128)(2,1)S(1)}, u32[]{:S(2)}, u32[]{:S(2)}) async-start(bf16[4,128,1280]{2,1,0:T(8,128)(2,1)} %broadcast_in_dim.25), calls=%async_computation.1 | async-start | bytes 2621440 | tf_op jit(solution)/shard_map/all_to_all | solution.py:788
  35.5 233.9 %all-gather.6.cloned.1.call-start = ((), (), s32[]{:S(2)}) async-start(), calls=%async_computation.14 | async-start | bytes 4718592 | tf_op jit(solution)/shard_map/all_gather | solution.py:785
  35.6 14.5 %collective-permute-start.1 = (bf16[256,1024]{1,0:T(8,128)(2,1)S(1)}, bf16[256,1024]{1,0:T(8,128)(2,1)S(1)}, u32[]{:S(2)}, u32[]{:S(2)}) collective-permute-start(bf16[256,1024]{1,0:T(8,128)(2,1)S(1)} %copy-done.6), channel_id=1, source_target_pairs={{0,2},{1,3},{2,0},{3,1},{4,6},{5,7},{6,4},{7,5},{8,10},{9,11},{10,... | collective-permute-start | bytes 1572872 | tf_op jit(solution)/shard_map/ppermute | solution.py:26
  36.9 22.0 %collective-permute-start = (bf16[256,1024]{1,0:T(8,128)(2,1)S(1)}, bf16[256,1024]{1,0:T(8,128)(2,1)S(1)}, u32[]{:S(2)}, u32[]{:S(2)}) collective-permute-start(bf16[256,1024]{1,0:T(8,128)(2,1)S(1)} %copy-done.6), channel_id=1, source_target_pairs={{0,1},{1,0},{2,3},{3,2},{4,5},{5,4},{6,7},{7,6},{8,9},{9,8},{10,11... | collective-permute-start | bytes 1572872 | tf_op jit(solution)/shard_map/ppermute | solution.py:26
  89.0 193.1 %all-gather.8.cloned.1.call-start = ((), (), s32[]{:S(2)}) async-start(), calls=%async_computation.15 | async-start | bytes 4718592 | tf_op jit(solution)/shard_map/all_gather | solution.py:785
  89.1 50.0 %collective-permute-start.5 = (bf16[4,128,1280]{2,1,0:T(8,128)(2,1)S(1)}, bf16[4,128,1280]{2,1,0:T(8,128)(2,1)}, u32[]{:S(2)}, u32[]{:S(2)}) collective-permute-start(bf16[4,128,1280]{2,1,0:T(8,128)(2,1)S(1)} %all-to-all-done.1.refs_7_), channel_id=1, source_target_pairs={{0,4},{4,0},{8,12},{12,8},{16,20},{20,16},{24,28},{28,24},{1,5},{5... | collective-permute-start | bytes 3932168 | tf_op jit(solution)/shard_map/ppermute | solution.py:26
  89.8 30.7 %all-to-all-start.3 = ((bf16[4,64,1024]{2,1,0:T(8,128)(2,1)}), bf16[4,64,1024]{2,1,0:T(8,128)(2,1)S(1)}, u32[]{:S(2)}, u32[]{:S(2)}) async-start(bf16[4,64,1024]{2,1,0:T(8,128)(2,1)} %get-tuple-element.65), calls=%async_computation.3 | async-start | bytes 1048576 | tf_op jit(solution)/shard_map/all_to_all | solution.py:848
  120.4 22.1 %all-to-all-start.4 = ((bf16[4,64,1024]{2,1,0:T(8,128)(2,1)}), bf16[4,64,1024]{2,1,0:T(8,128)(2,1)S(1)}, u32[]{:S(2)}, u32[]{:S(2)}) async-start(bf16[4,64,1024]{2,1,0:T(8,128)(2,1)} %get-tuple-element.66), calls=%async_computation.4 | async-start | bytes 1048576 | tf_op jit(solution)/shard_map/all_to_all | solution.py:848
  143.4 26.8 %all-to-all-start.2 = ((bf16[4,64,1024]{2,1,0:T(8,128)(2,1)}), bf16[4,64,1024]{2,1,0:T(8,128)(2,1)S(1)}, u32[]{:S(2)}, u32[]{:S(2)}) async-start(bf16[4,64,1024]{2,1,0:T(8,128)(2,1)} %get-tuple-element.64), calls=%async_computation.2 | async-start | bytes 1048576 | tf_op jit(solution)/shard_map/all_to_all | solution.py:848
  148.8 27.9 %collective-permute-start.3 = (bf16[4,64,1024]{2,1,0:T(8,128)(2,1)S(1)}, bf16[4,64,1024]{2,1,0:T(8,128)(2,1)}, u32[]{:S(2)}, u32[]{:S(2)}) collective-permute-start(bf16[4,64,1024]{2,1,0:T(8,128)(2,1)S(1)} %all-to-all-done.3.refs_2_.refs_4_), channel_id=1, source_target_pairs={{0,4},{4,0},{8,12},{12,8},{16,20},{20,16},{24,28},{28,24},{1,5},{5... | collective-permute-start | bytes 1572872 | tf_op jit(solution)/shard_map/ppermute | solution.py:26
  148.9 38.3 %collective-permute-start.4 = (bf16[4,64,1024]{2,1,0:T(8,128)(2,1)S(1)}, bf16[4,64,1024]{2,1,0:T(8,128)(2,1)}, u32[]{:S(2)}, u32[]{:S(2)}) collective-permute-start(bf16[4,64,1024]{2,1,0:T(8,128)(2,1)S(1)} %copy-done.18), channel_id=1, source_target_pairs={{0,4},{4,0},{8,12},{12,8},{16,20},{20,16},{24,28},{28,24},{1,5},{5... | collective-permute-start | bytes 1572872 | tf_op jit(solution)/shard_map/ppermute | solution.py:26
  155.1 15.1 %collective-permute-start.11 = (bf16[2,256,256]{2,1,0:T(8,128)(2,1)S(1)}, bf16[2,256,256]{2,1,0:T(8,128)(2,1)S(1)}, u32[]{:S(2)}, u32[]{:S(2)}) collective-permute-start(bf16[2,256,256]{2,1,0:T(8,128)(2,1)S(1)} %collective-permute-done.10.refs_8_.refs_10_.refs_16_), channel_id=1, source_target_pairs={{0,1},{1,0},{2,3},{3,2},{4,5},{5,4},{6,7},{7,6},{8,9},{9,8},{10,11... | collective-permute-start | bytes 786440 | tf_op jit(solution)/shard_map/ppermute | solution.py:26
  158.0 57.8 %collective-permute-start.13 = (bf16[3,1024,256]{2,1,0:T(8,128)(2,1)}, bf16[3,1024,256]{2,1,0:T(8,128)(2,1)}, u32[]{:S(2)}, u32[]{:S(2)}) collective-permute-start(bf16[3,1024,256]{2,1,0:T(8,128)(2,1)} %pad_maximum_fusion.1.refs_4_.refs_10_), channel_id=1, source_target_pairs={{0,2},{1,3},{2,0},{3,1},{4,6},{5,7},{6,4},{7,5},{8,10},{9,11},{10,... | collective-permute-start | bytes 4718600 | tf_op jit(solution)/shard_map/ppermute | solution.py:26
  158.0 83.2 %collective-permute-start.12 = (bf16[3,1024,256]{2,1,0:T(8,128)(2,1)}, bf16[3,1024,256]{2,1,0:T(8,128)(2,1)}, u32[]{:S(2)}, u32[]{:S(2)}) collective-permute-start(bf16[3,1024,256]{2,1,0:T(8,128)(2,1)} %pad_maximum_fusion.1.refs_4_.refs_10_), channel_id=1, source_target_pairs={{0,1},{1,0},{2,3},{3,2},{4,5},{5,4},{6,7},{7,6},{8,9},{9,8},{10,11... | collective-permute-start | bytes 4718600 | tf_op jit(solution)/shard_map/ppermute | solution.py:26
  215.9 29.8 %collective-permute-start.14 = (bf16[3,1024,256]{2,1,0:T(8,128)(2,1)}, bf16[3,1024,256]{2,1,0:T(8,128)(2,1)}, u32[]{:S(2)}, u32[]{:S(2)}) collective-permute-start(bf16[3,1024,256]{2,1,0:T(8,128)(2,1)} %tie.12.refs_6_.refs_12_), channel_id=1, source_target_pairs={{0,1},{1,0},{2,3},{3,2},{4,5},{5,4},{6,7},{7,6},{8,9},{9,8},{10,11... | collective-permute-start | bytes 4718600 | tf_op jit(solution)/shard_map/ppermute | solution.py:26
  215.9 29.7 %all-to-all-start.5 = ((bf16[16,64,256]{2,1,0:T(8,128)(2,1)}), bf16[16,64,256]{2,1,0:T(8,128)(2,1)}, u32[]{:S(2)}, u32[]{:S(2)}) async-start(bf16[16,64,256]{2,1,0:T(8,128)(2,1)} %get-tuple-element.67.refs_2_), calls=%async_computation.5 | async-start | bytes 1048576 | tf_op jit(solution)/shard_map/all_to_all | solution.py:851
  220.3 209.1 %reduce-scatter.4.cloned.1.call-start = ((), (), s32[]{:S(2)}) async-start(), calls=%async_computation.16 | async-start | bytes 4718592 | tf_op jit(solution)/shard_map/reduce_scatter | solution.py:918
  220.6 19.3 %collective-permute-start.17 = (bf16[256,1024]{1,0:T(8,128)(2,1)S(1)}, bf16[256,1024]{1,0:T(8,128)(2,1)S(1)}, u32[]{:S(2)}, u32[]{:S(2)}) collective-permute-start(bf16[256,1024]{1,0:T(8,128)(2,1)S(1)} %copy-done.10), channel_id=1, source_target_pairs={{0,2},{1,3},{2,0},{3,1},{4,6},{5,7},{6,4},{7,5},{8,10},{9,11},{10,... | collective-permute-start | bytes 1572872 | tf_op jit(solution)/shard_map/ppermute | solution.py:26
  222.5 47.0 %collective-permute-start.16 = (bf16[256,1024]{1,0:T(8,128)(2,1)S(1)}, bf16[256,1024]{1,0:T(8,128)(2,1)S(1)}, u32[]{:S(2)}, u32[]{:S(2)}) collective-permute-start(bf16[256,1024]{1,0:T(8,128)(2,1)S(1)} %copy-done.10), channel_id=1, source_target_pairs={{0,1},{1,0},{2,3},{3,2},{4,5},{5,4},{6,7},{7,6},{8,9},{9,8},{10,11... | collective-permute-start | bytes 1572872 | tf_op jit(solution)/shard_map/ppermute | solution.py:26
  239.9 29.6 %collective-permute-start.18 = (bf16[256,1024]{1,0:T(8,128)(2,1)S(1)}, bf16[256,1024]{1,0:T(8,128)(2,1)S(1)}, u32[]{:S(2)}, u32[]{:S(2)}) collective-permute-start(bf16[256,1024]{1,0:T(8,128)(2,1)S(1)} %collective-permute-done.17.refs_2_), channel_id=1, source_target_pairs={{0,1},{1,0},{2,3},{3,2},{4,5},{5,4},{6,7},{7,6},{8,9},{9,8},{10,11... | collective-permute-start | bytes 1572872 | tf_op jit(solution)/shard_map/ppermute | solution.py:26
  266.3 14.1 %collective-permute-start.19 = (bf16[256,1024]{1,0:T(8,128)(2,1)}, bf16[256,1024]{1,0:T(8,128)(2,1)}, u32[]{:S(2)}, u32[]{:S(2)}) collective-permute-start(bf16[256,1024]{1,0:T(8,128)(2,1)} %get-tuple-element.70.refs_0_), channel_id=1, source_target_pairs={{0,2},{1,3},{2,0},{3,1},{4,6},{5,7},{6,4},{7,5},{8,10},{9,11},{10,... | collective-permute-start | bytes 1572872 | tf_op jit(solution)/shard_map/ppermute | solution.py:26
  266.8 15.3 %collective-permute-start.15 = (bf16[256,1024]{1,0:T(8,128)(2,1)}, bf16[256,1024]{1,0:T(8,128)(2,1)}, u32[]{:S(2)}, u32[]{:S(2)}) collective-permute-start(bf16[256,1024]{1,0:T(8,128)(2,1)} %get-tuple-element.70.refs_0_), channel_id=1, source_target_pairs={{0,1},{1,0},{2,3},{3,2},{4,5},{5,4},{6,7},{7,6},{8,9},{9,8},{10,11... | collective-permute-start | bytes 1572872 | tf_op jit(solution)/shard_map/ppermute | solution.py:26
  280.4 15.6 %collective-permute-start.20 = (bf16[256,1024]{1,0:T(8,128)(2,1)}, bf16[256,1024]{1,0:T(8,128)(2,1)}, u32[]{:S(2)}, u32[]{:S(2)}) collective-permute-start(bf16[256,1024]{1,0:T(8,128)(2,1)} %tie.14.refs_0_.refs_2_), channel_id=1, source_target_pairs={{0,1},{1,0},{2,3},{3,2},{4,5},{5,4},{6,7},{7,6},{8,9},{9,8},{10,11... | collective-permute-start | bytes 1572872 | tf_op jit(solution)/shard_map/ppermute | solution.py:26
  328.7 81.5 %collective-permute-start.24 = (bf16[512,2048]{1,0:T(8,128)(2,1)S(1)}, bf16[512,2048]{1,0:T(8,128)(2,1)}, u32[]{:S(2)}, u32[]{:S(2)}) collective-permute-start(bf16[512,2048]{1,0:T(8,128)(2,1)S(1)} %outer.4.refs_19_), channel_id=1, source_target_pairs={{0,4},{4,0},{8,12},{12,8},{16,20},{20,16},{24,28},{28,24},{1,5},{5... | collective-permute-start | bytes 6291464 | tf_op jit(solution)/shard_map/ppermute | solution.py:26
  355.6 26.3 %all-to-all-start.6 = ((bf16[16,64,256]{2,1,0:T(8,128)(2,1)}), bf16[16,64,256]{2,1,0:T(8,128)(2,1)}, u32[]{:S(2)}, u32[]{:S(2)}) async-start(bf16[16,64,256]{2,1,0:T(8,128)(2,1)} %bitcast.138), calls=%async_computation.6 | async-start | bytes 1048576 | tf_op jit(solution)/shard_map/all_to_all | solution.py:851
  363.7 168.2 %reduce-scatter.6.cloned.1.call-start = ((), (), s32[]{:S(2)}) async-start(), calls=%async_computation.17 | async-start | bytes 2621440 | tf_op jit(solution)/shard_map/reduce_scatter | solution.py:921
  373.8 65.6 %collective-permute-start.43 = (bf16[1024,768]{1,0:T(8,128)(2,1)}, bf16[1024,768]{1,0:T(8,128)(2,1)}, u32[]{:S(2)}, u32[]{:S(2)}) collective-permute-start(bf16[1024,768]{1,0:T(8,128)(2,1)} %get-tuple-element.98.refs_9_), channel_id=1, source_target_pairs={{0,1},{1,0},{2,3},{3,2},{4,5},{5,4},{6,7},{7,6},{8,9},{9,8},{10,11... | collective-permute-start | bytes 4718600 | tf_op jit(solution)/shard_map/ppermute | solution.py:26
  378.0 55.8 %collective-permute-start.30 = (bf16[2,256,256]{2,1,0:T(8,128)(2,1)}, bf16[2,256,256]{2,1,0:T(8,128)(2,1)}, u32[]{:S(2)}, u32[]{:S(2)}) collective-permute-start(bf16[2,256,256]{2,1,0:T(8,128)(2,1)} %get-tuple-element.186), channel_id=1, source_target_pairs={{0,1},{1,0},{2,3},{3,2},{4,5},{5,4},{6,7},{7,6},{8,9},{9,8},{10,11... | collective-permute-start | bytes 786440 | tf_op jit(solution)/shard_map/ppermute | solution.py:26
  380.1 53.1 %collective-permute-start.32 = (bf16[2,256,256]{2,1,0:T(8,128)(2,1)}, bf16[2,256,256]{2,1,0:T(8,128)(2,1)S(1)}, u32[]{:S(2)}, u32[]{:S(2)}) collective-permute-start(bf16[2,256,256]{2,1,0:T(8,128)(2,1)} %fusion.52), channel_id=1, source_target_pairs={{0,2},{1,3},{2,0},{3,1},{4,6},{5,7},{6,4},{7,5},{8,10},{9,11},{10,... | collective-permute-start | bytes 786440 | tf_op jit(solution)/shard_map/ppermute | solution.py:26
  432.3 69.1 %collective-permute-start.42 = (bf16[1024,768]{1,0:T(8,128)(2,1)}, bf16[1024,768]{1,0:T(8,128)(2,1)}, u32[]{:S(2)}, u32[]{:S(2)}) collective-permute-start(bf16[1024,768]{1,0:T(8,128)(2,1)} %get-tuple-element.96.refs_7_), channel_id=1, source_target_pairs={{0,1},{1,0},{2,3},{3,2},{4,5},{5,4},{6,7},{7,6},{8,9},{9,8},{10,11... | collective-permute-start | bytes 4718600 | tf_op jit(solution)/shard_map/ppermute | solution.py:26
  435.9 46.8 %collective-permute-start.33 = (bf16[1,2,256,256]{3,2,1,0:T(8,128)(2,1)}, bf16[1,2,256,256]{3,2,1,0:T(8,128)(2,1)S(1)}, u32[]{:S(2)}, u32[]{:S(2)}) collective-permute-start(bf16[1,2,256,256]{3,2,1,0:T(8,128)(2,1)} %fusion.59), channel_id=1, source_target_pairs={{0,4},{4,0},{8,12},{12,8},{16,20},{20,16},{24,28},{28,24},{1,5},{5... | collective-permute-start | bytes 786440 | tf_op jit(solution)/shard_map/ppermute | solution.py:26
  437.3 47.5 %collective-permute-start.28 = (bf16[4,64,1024]{2,1,0:T(8,128)(2,1)}, bf16[4,64,1024]{2,1,0:T(8,128)(2,1)}, u32[]{:S(2)}, u32[]{:S(2)}) collective-permute-start(bf16[4,64,1024]{2,1,0:T(8,128)(2,1)} %bitcast.35), channel_id=1, source_target_pairs={{0,4},{4,0},{8,12},{12,8},{16,20},{20,16},{24,28},{28,24},{1,5},{5... | collective-permute-start | bytes 1572872 | tf_op jit(solution)/shard_map/ppermute | solution.py:26
  437.9 47.4 %collective-permute-start.29 = (bf16[4,64,1024]{2,1,0:T(8,128)(2,1)}, bf16[4,64,1024]{2,1,0:T(8,128)(2,1)}, u32[]{:S(2)}, u32[]{:S(2)}) collective-permute-start(bf16[4,64,1024]{2,1,0:T(8,128)(2,1)} %bitcast.36), channel_id=1, source_target_pairs={{0,4},{4,0},{8,12},{12,8},{16,20},{20,16},{24,28},{28,24},{1,5},{5... | collective-permute-start | bytes 1572872 | tf_op jit(solution)/shard_map/ppermute | solution.py:26
  442.8 58.6 %collective-permute-start.44 = (bf16[1024,768]{1,0:T(8,128)(2,1)}, bf16[1024,768]{1,0:T(8,128)(2,1)}, u32[]{:S(2)}, u32[]{:S(2)}) collective-permute-start(bf16[1024,768]{1,0:T(8,128)(2,1)} %add_convert_fusion), channel_id=1, source_target_pairs={{0,2},{1,3},{2,0},{3,1},{4,6},{5,7},{6,4},{7,5},{8,10},{9,11},{10,... | collective-permute-start | bytes 4718600 | tf_op jit(solution)/shard_map/ppermute | solution.py:26
  484.8 21.3 %collective-permute-start.25 = (bf16[256,1024]{1,0:T(8,128)(2,1)}, bf16[256,1024]{1,0:T(8,128)(2,1)}, u32[]{:S(2)}, u32[]{:S(2)}) collective-permute-start(bf16[256,1024]{1,0:T(8,128)(2,1)} %convolution_convert_fusion.4), channel_id=1, source_target_pairs={{0,1},{1,0},{2,3},{3,2},{4,5},{5,4},{6,7},{7,6},{8,9},{9,8},{10,11... | collective-permute-start | bytes 1572872 | tf_op jit(solution)/shard_map/ppermute | solution.py:26
  488.0 44.0 %all-to-all-start.7 = ((bf16[4,3,64,1024]{3,2,1,0:T(8,128)(2,1)}), bf16[4,3,64,1024]{3,2,1,0:T(8,128)(2,1)}, u32[]{:S(2)}, u32[]{:S(2)}) async-start(bf16[4,3,64,1024]{3,2,1,0:T(8,128)(2,1)} %copy-done.7), calls=%async_computation.8 | async-start | bytes 3145728 | tf_op jit(solution)/shard_map/all_to_all | solution.py:848
  492.4 100.6 %reduce-scatter.8.cloned.1.call-start = ((), (), s32[]{:S(2)}) async-start(), calls=%async_computation.18 | async-start | bytes 983040 | tf_op jit(solution)/shard_map/reduce_scatter | solution.py:921
  494.1 37.8 %collective-permute-start.34 = (bf16[1,2,256,256]{3,2,1,0:T(8,128)(2,1)}, bf16[1,2,256,256]{3,2,1,0:T(8,128)(2,1)S(1)}, u32[]{:S(2)}, u32[]{:S(2)}) collective-permute-start(bf16[1,2,256,256]{3,2,1,0:T(8,128)(2,1)} %add_convert_fusion.9), channel_id=1, source_target_pairs={{0,8},{4,12},{8,0},{12,4},{16,24},{20,28},{24,16},{28,20},{1,9},{5... | collective-permute-start | bytes 786440 | tf_op jit(solution)/shard_map/ppermute | solution.py:26
  504.6 25.2 %collective-permute-start.45 = (bf16[512,768]{1,0:T(8,128)(2,1)S(1)}, bf16[512,768]{1,0:T(8,128)(2,1)S(1)}, u32[]{:S(2)}, u32[]{:S(2)}) collective-permute-start(bf16[512,768]{1,0:T(8,128)(2,1)S(1)} %pad_maximum_fusion.2), channel_id=1, source_target_pairs={{0,4},{4,0},{8,12},{12,8},{16,20},{20,16},{24,28},{28,24},{1,5},{5... | collective-permute-start | bytes 2359304 | tf_op jit(solution)/shard_map/ppermute | solution.py:26
  533.9 26.8 %collective-permute-start.38 = (bf16[1,2,256,256]{3,2,1,0:T(8,128)(2,1)S(1)}, bf16[1,2,256,256]{3,2,1,0:T(8,128)(2,1)}, u32[]{:S(2)}, u32[]{:S(2)}) collective-permute-start(bf16[1,2,256,256]{3,2,1,0:T(8,128)(2,1)S(1)} %add_convert_fusion.8), channel_id=1, source_target_pairs={{0,16},{4,20},{8,24},{12,28},{16,0},{20,4},{24,8},{28,12},{1,17},{... | collective-permute-start | bytes 786440 | tf_op jit(solution)/shard_map/ppermute | solution.py:26
  545.6 20.6 %collective-permute-start.36 = (bf16[256,1024]{1,0:T(8,128)(2,1)}, bf16[256,1024]{1,0:T(8,128)(2,1)}, u32[]{:S(2)}, u32[]{:S(2)}) collective-permute-start(bf16[256,1024]{1,0:T(8,128)(2,1)} %convolution_convert_fusion.1), channel_id=1, source_target_pairs={{0,1},{1,0},{2,3},{3,2},{4,5},{5,4},{6,7},{7,6},{8,9},{9,8},{10,11... | collective-permute-start | bytes 1572872 | tf_op jit(solution)/shard_map/ppermute | solution.py:26
  548.0 40.0 %collective-permute-start.35 = (bf16[256,1024]{1,0:T(8,128)(2,1)}, bf16[256,1024]{1,0:T(8,128)(2,1)}, u32[]{:S(2)}, u32[]{:S(2)}) collective-permute-start(bf16[256,1024]{1,0:T(8,128)(2,1)} %convolution_convert_fusion.2), channel_id=1, source_target_pairs={{0,1},{1,0},{2,3},{3,2},{4,5},{5,4},{6,7},{7,6},{8,9},{9,8},{10,11... | collective-permute-start | bytes 1572872 | tf_op jit(solution)/shard_map/ppermute | solution.py:26
  549.9 46.4 %all-to-all-start.8 = ((bf16[8,128,768]{2,1,0:T(8,128)(2,1)}), bf16[8,128,768]{2,1,0:T(8,128)(2,1)}, u32[]{:S(2)}, u32[]{:S(2)}) async-start(bf16[8,128,768]{2,1,0:T(8,128)(2,1)} %bitcast.48), calls=%async_computation.10 | async-start | bytes 3145728 | tf_op jit(solution)/shard_map/all_to_all | solution.py:998
  568.7 19.2 %collective-permute-start.37 = (bf16[256,1024]{1,0:T(8,128)(2,1)}, bf16[256,1024]{1,0:T(8,128)(2,1)}, u32[]{:S(2)}, u32[]{:S(2)}) collective-permute-start(bf16[256,1024]{1,0:T(8,128)(2,1)} %fusion.2), channel_id=1, source_target_pairs={{0,2},{1,3},{2,0},{3,1},{4,6},{5,7},{6,4},{7,5},{8,10},{9,11},{10,... | collective-permute-start | bytes 1572872 | tf_op jit(solution)/shard_map/ppermute | solution.py:26
  570.3 15.4 %collective-permute-start.41 = (bf16[1,64,1024]{2,1,0:T(8,128)(2,1)}, bf16[1,64,1024]{2,1,0:T(8,128)(2,1)}, u32[]{:S(2)}, u32[]{:S(2)}) collective-permute-start(bf16[1,64,1024]{2,1,0:T(8,128)(2,1)} %fusion.40), channel_id=1, source_target_pairs={{0,2},{1,3},{2,0},{3,1},{4,6},{5,7},{6,4},{7,5},{8,10},{9,11},{10,... | collective-permute-start | bytes 393224 | tf_op jit(solution)/shard_map/ppermute | solution.py:26
  598.0 20.2 %all-to-all-start.9 = ((f32[32,1,672]{2,1,0:T(1,128)}), f32[32,1,672]{2,1,0:T(1,128)S(1)}, u32[]{:S(2)}, u32[]{:S(2)}) async-start(f32[32,1,672]{2,1,0:T(1,128)} %copy.80), calls=%async_computation.12 | async-start | bytes 196608 | tf_op jit(solution)/shard_map/all_to_all | solution.py:1037
  (132 other events, 890.8 us)
Sparse Core Ops, SparseCore 0:
  12.3 62.2 all-gather.3
  89.2 98.1 all-gather.5
  189.5 80.4 all-gather.7
  318.8 110.5 reduce-scatter.3
  431.7 43.6 reduce-scatter.5
  532.1 38.2 reduce-scatter.7
